TPU v7x, 32 devices: a whole 2x2x4 slice. The times are simulated.
32 devices in a mesh: head: 4 (over y, x), blk: 8 (over z, core).
Axes of the slice: x: 2, y: 2, z: 4, core: 2. Of those that a mesh axis runs over, the one named last changes fastest.
Arguments:
- layer_input: bfloat16 [2, 8, 256, 512], P(None, 'blk', 'head'), may hold values from -6 to 6
- segments: int32 [2, 2048], replicated, may hold values from 0 to 16, as said below
- token_valid: int32 [2, 2048], replicated, may hold values from 0 to 1, as said below
- attention_gain: bfloat16 [512], P(('head', 'blk')), may hold values from 0.5 to 1.5
- attention_shift: bfloat16 [512], P(('head', 'blk')), may hold values from -1.25 to 1.25
- project_weight: bfloat16 [512, 1536], P(('head', 'blk')), may hold values from -0.25 to 0.25
- project_bias: bfloat16 [1024], P(('head', 'blk')), may hold values from -1.25 to 1.25
- output_weight: bfloat16 [512, 512], P(('head', 'blk')), may hold values from -1.5 to 1.5
- output_bias: bfloat16 [512], P(('head', 'blk')), may hold values from -1.25 to 1.25
- feed_gain: bfloat16 [512], P(('head', 'blk')), may hold values from 0.5 to 1.5
- feed_shift: bfloat16 [512], P(('head', 'blk')), may hold values from -1.25 to 1.25
- up_weight: bfloat16 [512, 2048], P(('head', 'blk')), may hold values from -0.25 to 0.25
- up_bias: bfloat16 [2048], P(('head', 'blk')), may hold values from -1.25 to 1.25
- down_weight: bfloat16 [2048, 512], P(('head', 'blk')), may hold values from -0.125 to 0.125
- down_bias: bfloat16 [512], P(('head', 'blk')), may hold values from -1.25 to 1.25
- cotangent: bfloat16 [2, 8, 256, 512], P(None, 'blk', 'head'), may hold values from -6 to 6
Outputs:
- layer_output: bfloat16 [2, 8, 256, 512], P(None, 'blk', 'head')
- input_grad: bfloat16 [2, 8, 256, 512], P(None, 'blk', 'head')
- attention_gain_grad: float32 [512], P(('head', 'blk'))
- attention_shift_grad: float32 [512], P(('head', 'blk'))
- project_weight_grad: float32 [512, 1536], P(('head', 'blk'))
- project_bias_grad: float32 [1024], P(('head', 'blk'))
- output_weight_grad: float32 [512, 512], P(('head', 'blk'))
- output_bias_grad: float32 [512], P(('head', 'blk'))
- feed_gain_grad: float32 [512], P(('head', 'blk'))
- feed_shift_grad: float32 [512], P(('head', 'blk'))
- up_weight_grad: float32 [512, 2048], P(('head', 'blk'))
- up_bias_grad: float32 [2048], P(('head', 'blk'))
- down_weight_grad: float32 [2048, 512], P(('head', 'blk'))
- down_bias_grad: float32 [512], P(('head', 'blk'))
Inputs may be any that keep to these rules, and one draw needn't show every extreme that they name: `segments`: in each sequence segment numbers start at 0 and never fall. In one sequence, drawn from the seed, segment 1 starts within its first 256 positions and runs to its end; in the others every segment but the last holds 12 to 127 positions, and the last segment number is the most. `token_valid`: each sequence is ones followed by zeros; its last 1 to 256 positions are zeros, and fewer than 128 of them in the sequence whose segment 1 runs to its end.
All inputs are finite; a program needn't handle non-finite values.
Results may differ from a plain program's by a relative error of at most 0.018.
Values may be sent and summed in bfloat16 or wider, within the bound.
No kernel may reach another device: no remote copies, remote signals or barrier semaphores. Data moves between devices by JAX's collectives and lax.ppermute only.
A program may use at most 128 MiB of HBM per device.

v0:
```python
import jax
import jax.numpy as jnp
from jax import lax
from jax.sharding import PartitionSpec as P

H = 8
HD = 64


EPSILON = 1e-05
NEG_FILL = -1e30


def shifted(x, axis, by):
    peers = lax.axis_size(axis)
    pairs = [(i, i + by) for i in range(peers) if 0 <= i + by < peers]
    return lax.ppermute(x, axis, pairs)


def from_behind(x, axis, by):
    peers = lax.axis_size(axis)
    return lax.ppermute(x, axis, [(i, (i + by) % peers) for i in range(peers)])


def norm_forward(values, gain, shift):
    centred = values - jnp.mean(values, axis=-1, keepdims=True)
    variance = jnp.mean(centred * centred, axis=-1, keepdims=True)
    inverse_root = lax.rsqrt(variance + EPSILON)
    unit_value = centred * inverse_root
    return (unit_value * gain + shift, unit_value, inverse_root)


def norm_backward(upstream, unit_value, inverse_root, gain):
    scaled = upstream * gain
    inner = scaled - jnp.mean(scaled, axis=-1, keepdims=True)
    inner = inner - unit_value * jnp.mean(scaled * unit_value, axis=-1, keepdims=True)
    return (inverse_root * inner, jnp.sum(upstream * unit_value, axis=0), jnp.sum(upstream, axis=0))


def on_device(
    layer_input,
    segments,
    token_valid,
    attention_gain,
    attention_shift,
    project_weight,
    project_bias,
    output_weight,
    output_bias,
    feed_gain,
    feed_shift,
    up_weight,
    up_bias,
    down_weight,
    down_bias,
    cotangent,
):
    head_count = lax.axis_size("head")
    cycle_count = lax.axis_size("blk")
    cycle_index = lax.axis_index("blk")
    seq_count = layer_input.shape[0]
    sub_rows = layer_input.shape[2]
    width = layer_input.shape[3]
    block_rows = sub_rows * head_count
    local_width = width // head_count
    local_heads = H // head_count
    token_rows = seq_count * sub_rows
    scale = HD ** (-0.5)
    bf16 = jnp.bfloat16
    f32 = jnp.float32
    gathered = (
        lax.all_gather(attention_gain, ("head", "blk"), axis=0, tiled=True),
        lax.all_gather(attention_shift, ("head", "blk"), axis=0, tiled=True),
        lax.all_gather(project_weight, ("head", "blk"), axis=0, tiled=True),
        lax.all_gather(project_bias, ("head", "blk"), axis=0, tiled=True),
        lax.all_gather(output_weight, ("head", "blk"), axis=0, tiled=True),
        lax.all_gather(output_bias, ("head", "blk"), axis=0, tiled=True),
        lax.all_gather(feed_gain, ("head", "blk"), axis=0, tiled=True),
        lax.all_gather(feed_shift, ("head", "blk"), axis=0, tiled=True),
        lax.all_gather(up_weight, ("head", "blk"), axis=0, tiled=True),
        lax.all_gather(up_bias, ("head", "blk"), axis=0, tiled=True),
        lax.all_gather(down_weight, ("head", "blk"), axis=0, tiled=True),
        lax.all_gather(down_bias, ("head", "blk"), axis=0, tiled=True),
    )
    (
        gain_one,
        shift_one,
        w_project,
        b_project,
        w_output,
        b_output,
        gain_two,
        shift_two,
        w_up,
        b_up,
        w_down,
        b_down,
    ) = gathered
    gain_one = gain_one.astype(f32)
    shift_one = shift_one.astype(f32)
    gain_two = gain_two.astype(f32)
    shift_two = shift_two.astype(f32)
    b_project = b_project.astype(f32)
    b_output = b_output.astype(f32)
    b_up = b_up.astype(f32)
    b_down = b_down.astype(f32)
    inputs_f32 = layer_input.reshape(token_rows, width).astype(f32)
    normed_one, unit_one, root_one = norm_forward(inputs_f32, gain_one, shift_one)
    normed_bf = normed_one.astype(bf16)
    bias_full = jnp.concatenate([b_project[:width], jnp.zeros((width,), f32), b_project[width:]])
    projected = jnp.dot(normed_bf, w_project, preferred_element_type=f32) + bias_full
    query_tok = projected[:, :width].astype(bf16).reshape(seq_count, sub_rows, width)
    key_tok = projected[:, width : 2 * width].astype(bf16).reshape(seq_count, sub_rows, width)
    value_tok = projected[:, 2 * width :].astype(bf16).reshape(seq_count, sub_rows, width)
    head_q, head_k, head_v = (
        lax.all_to_all(query_tok, "head", split_axis=2, concat_axis=1, tiled=True),
        lax.all_to_all(key_tok, "head", split_axis=2, concat_axis=1, tiled=True),
        lax.all_to_all(value_tok, "head", split_axis=2, concat_axis=1, tiled=True),
    )
    head_shape = (seq_count, block_rows, local_heads, HD)
    head_q = head_q.reshape(head_shape)
    head_k = head_k.reshape(head_shape)
    head_v = head_v.reshape(head_shape)
    local_rows = jnp.arange(block_rows, dtype=jnp.int32)

    def allowed_pairs(query_block, key_block):
        query_seg = lax.dynamic_slice_in_dim(segments, query_block * block_rows, block_rows, axis=1)
        key_seg = lax.dynamic_slice_in_dim(segments, key_block * block_rows, block_rows, axis=1)
        key_live = lax.dynamic_slice_in_dim(token_valid, key_block * block_rows, block_rows, axis=1)
        query_pos = query_block * block_rows + local_rows
        key_pos = key_block * block_rows + local_rows
        same_doc = query_seg[:, :, None] == key_seg[:, None, :]
        causal = (key_pos[None, :] <= query_pos[:, None])[None]
        diagonal = (key_pos[None, :] == query_pos[:, None])[None]
        allowed = same_doc & causal & ((key_live[:, None, :] == 1) | diagonal)
        return allowed[:, :, None, :]

    def any_pairs(query_block, key_block):
        last_key = lax.dynamic_slice_in_dim(
            segments, key_block * block_rows + block_rows - 1, 1, axis=1
        )
        first_query = lax.dynamic_slice_in_dim(segments, query_block * block_rows, 1, axis=1)
        earlier = (key_block < query_block) & jnp.any(last_key == first_query)
        return (key_block == query_block) | earlier

    def forward_block(key_block, key_rows, value_rows, state):

        def forward_compute(carried):
            run_max, run_sum, weighted = carried
            allowed = allowed_pairs(cycle_index, key_block)
            scores = (
                jnp.einsum("sqhd,skhd->sqhk", head_q, key_rows, preferred_element_type=f32) * scale
            )
            masked = jnp.where(allowed, scores, NEG_FILL)
            new_max = jnp.maximum(run_max, jnp.max(masked, axis=-1))
            factor = jnp.exp(run_max - new_max)
            probs = jnp.where(allowed, jnp.exp(masked - new_max[..., None]), 0.0)
            new_sum = run_sum * factor + jnp.sum(probs, axis=-1)
            new_weighted = weighted * factor[..., None] + jnp.einsum(
                "sqhk,skhd->sqhd", probs.astype(bf16), value_rows, preferred_element_type=f32
            )
            return (new_max, new_sum, new_weighted)

        return lax.cond(
            any_pairs(cycle_index, key_block), forward_compute, lambda carried: carried, state
        )

    def forward_turn(turn_index, carry):
        key_rows, value_rows, state = carry
        key_block = (cycle_index - turn_index) % cycle_count
        state = forward_block(key_block, key_rows, value_rows, state)
        key_rows, value_rows = shifted((key_rows, value_rows), "blk", 1)
        return (key_rows, value_rows, state)

    stat_shape = (seq_count, block_rows, local_heads)
    start_state = (
        jnp.full(stat_shape, NEG_FILL, f32),
        jnp.zeros(stat_shape, f32),
        jnp.zeros(head_shape, f32),
    )
    key_rows, value_rows, state = lax.fori_loop(
        0, cycle_count - 1, forward_turn, (head_k, head_v, start_state)
    )
    last_block = (cycle_index - (cycle_count - 1)) % cycle_count
    run_max, run_sum, weighted = forward_block(last_block, key_rows, value_rows, state)
    log_total = run_max + jnp.log(run_sum)
    attended = weighted / run_sum[..., None]
    attended_bf = attended.astype(bf16).reshape(seq_count, block_rows, local_width)
    mixed_tok = lax.all_to_all(
        attended_bf, "head", split_axis=1, concat_axis=2, tiled=True
    ).reshape(token_rows, width)
    branch = jnp.dot(mixed_tok, w_output, preferred_element_type=f32) + b_output
    middle = inputs_f32 + branch
    normed_two, unit_two, root_two = norm_forward(middle, gain_two, shift_two)
    second_bf = normed_two.astype(bf16)
    hidden = jnp.dot(second_bf, w_up, preferred_element_type=f32) + b_up
    sigma = jax.nn.sigmoid(1.702 * hidden)
    activated = (hidden * sigma).astype(bf16)
    feed_out = jnp.dot(activated, w_down, preferred_element_type=f32) + b_down
    layer_output = middle + feed_out
    grad_out_bf = cotangent.reshape(token_rows, width)
    grad_out = grad_out_bf.astype(f32)
    grad_down = jnp.einsum("tf,td->fd", activated, grad_out_bf, preferred_element_type=f32)
    grad_down_bias = jnp.sum(grad_out, axis=0)
    grad_act = jnp.einsum("td,fd->tf", grad_out_bf, w_down, preferred_element_type=f32)
    grad_hidden = (grad_act * (sigma + 1.702 * hidden * sigma * (1.0 - sigma))).astype(bf16)
    grad_up = jnp.einsum("td,tf->df", second_bf, grad_hidden, preferred_element_type=f32)
    grad_up_bias = jnp.sum(grad_hidden.astype(f32), axis=0)
    grad_second = jnp.einsum("tf,df->td", grad_hidden, w_up, preferred_element_type=f32)
    grad_middle_norm, grad_gain_two, grad_shift_two = norm_backward(
        grad_second, unit_two, root_two, gain_two
    )
    grad_middle = grad_out + grad_middle_norm
    grad_branch = grad_middle.astype(bf16)
    grad_output = jnp.einsum("te,td->ed", mixed_tok, grad_branch, preferred_element_type=f32)
    grad_output_bias = jnp.sum(grad_branch.astype(f32), axis=0)
    grad_mixed = jnp.einsum("td,ed->te", grad_branch, w_output, preferred_element_type=f32)
    grad_mixed = grad_mixed.astype(bf16).reshape(seq_count, sub_rows, width)
    head_grad = lax.all_to_all(grad_mixed, "head", split_axis=2, concat_axis=1, tiled=True).reshape(
        head_shape
    )
    delta = jnp.sum(head_grad.astype(f32) * attended, axis=-1)

    def block_terms(
        query_block, key_block, query_rows, grad_rows, log_rows, delta_rows, key_rows, value_rows
    ):

        def block_compute():
            allowed = allowed_pairs(query_block, key_block)
            scores = (
                jnp.einsum("sqhd,skhd->sqhk", query_rows, key_rows, preferred_element_type=f32)
                * scale
            )
            probs = jnp.where(allowed, jnp.exp(scores - log_rows[..., None]), 0.0)
            grad_probs = jnp.einsum(
                "sqhd,skhd->sqhk", grad_rows, value_rows, preferred_element_type=f32
            )
            grad_scores = (probs * (grad_probs - delta_rows[..., None])).astype(bf16)
            part_query = scale * jnp.einsum(
                "sqhk,skhd->sqhd", grad_scores, key_rows, preferred_element_type=f32
            )
            part_key = scale * jnp.einsum(
                "sqhk,sqhd->skhd", grad_scores, query_rows, preferred_element_type=f32
            )
            part_value = jnp.einsum(
                "sqhk,sqhd->skhd", probs.astype(bf16), grad_rows, preferred_element_type=f32
            )
            return (part_query, part_key, part_value)

        def nothing():
            return (
                jnp.zeros(head_shape, f32),
                jnp.zeros(head_shape, f32),
                jnp.zeros(head_shape, f32),
            )

        return lax.cond(any_pairs(query_block, key_block), block_compute, nothing)

    zero_field = jnp.zeros(head_shape, f32)

    def key_turn(turn_index, carry):
        key_rows, value_rows, key_grad, value_grad, query_grad = carry
        key_block = (cycle_index - turn_index) % cycle_count
        part_query, part_key, part_value = block_terms(
            cycle_index, key_block, head_q, head_grad, log_total, delta, key_rows, value_rows
        )
        key_grad = key_grad + part_key
        value_grad = value_grad + part_value
        query_grad = query_grad + part_query
        key_rows, value_rows = shifted((key_rows, value_rows), "blk", 1)
        key_grad, value_grad = (
            from_behind(key_grad.astype(jnp.bfloat16), "blk", 1).astype(key_grad.dtype),
            from_behind(value_grad.astype(jnp.bfloat16), "blk", 1).astype(value_grad.dtype),
        )
        return (key_rows, value_rows, key_grad, value_grad, query_grad)

    finished = lax.fori_loop(
        0, cycle_count, key_turn, (head_k, head_v, zero_field, zero_field, zero_field)
    )
    key_grad, value_grad, query_grad = (finished[2], finished[3], finished[4])
    flat_shape = (seq_count, block_rows, local_width)
    grad_q_tok, grad_k_tok, grad_v_tok = (
        lax.all_to_all(
            query_grad.astype(bf16).reshape(flat_shape),
            "head",
            split_axis=1,
            concat_axis=2,
            tiled=True,
        ),
        lax.all_to_all(
            key_grad.astype(bf16).reshape(flat_shape),
            "head",
            split_axis=1,
            concat_axis=2,
            tiled=True,
        ),
        lax.all_to_all(
            value_grad.astype(bf16).reshape(flat_shape),
            "head",
            split_axis=1,
            concat_axis=2,
            tiled=True,
        ),
    )
    grad_q_tok = grad_q_tok.reshape(token_rows, width)
    grad_k_tok = grad_k_tok.reshape(token_rows, width)
    grad_v_tok = grad_v_tok.reshape(token_rows, width)
    grad_project_rows = jnp.concatenate([grad_q_tok, grad_k_tok, grad_v_tok], axis=1)
    grad_project = jnp.einsum("td,te->de", normed_bf, grad_project_rows, preferred_element_type=f32)
    grad_project_bias = jnp.concatenate(
        [jnp.sum(grad_q_tok.astype(f32), axis=0), jnp.sum(grad_v_tok.astype(f32), axis=0)]
    )
    grad_normed = jnp.einsum("te,de->td", grad_project_rows, w_project, preferred_element_type=f32)
    grad_input_norm, grad_gain_one, grad_shift_one = norm_backward(
        grad_normed, unit_one, root_one, gain_one
    )
    grad_input = grad_middle + grad_input_norm
    owned = (
        lax.psum_scatter(grad_gain_one, ("head", "blk"), scatter_dimension=0, tiled=True),
        lax.psum_scatter(grad_shift_one, ("head", "blk"), scatter_dimension=0, tiled=True),
        lax.psum_scatter(grad_project, ("head", "blk"), scatter_dimension=0, tiled=True),
        lax.psum_scatter(grad_project_bias, ("head", "blk"), scatter_dimension=0, tiled=True),
        lax.psum_scatter(grad_output, ("head", "blk"), scatter_dimension=0, tiled=True),
        lax.psum_scatter(grad_output_bias, ("head", "blk"), scatter_dimension=0, tiled=True),
        lax.psum_scatter(grad_gain_two, ("head", "blk"), scatter_dimension=0, tiled=True),
        lax.psum_scatter(grad_shift_two, ("head", "blk"), scatter_dimension=0, tiled=True),
        lax.psum_scatter(grad_up, ("head", "blk"), scatter_dimension=0, tiled=True),
        lax.psum_scatter(grad_up_bias, ("head", "blk"), scatter_dimension=0, tiled=True),
        lax.psum_scatter(grad_down, ("head", "blk"), scatter_dimension=0, tiled=True),
        lax.psum_scatter(grad_down_bias, ("head", "blk"), scatter_dimension=0, tiled=True),
    )
    return (
        layer_output.astype(bf16).reshape(layer_input.shape),
        grad_input.astype(bf16).reshape(layer_input.shape),
        owned[0],
        owned[1],
        owned[2],
        owned[3],
        owned[4],
        owned[5],
        owned[6],
        owned[7],
        owned[8],
        owned[9],
        owned[10],
        owned[11],
    )


def solution(mesh):
    placed = (
        P(None, "blk", "head", None),
        P(),
        P(),
        P(("head", "blk")),
        P(("head", "blk")),
        P(("head", "blk"), None),
        P(("head", "blk")),
        P(("head", "blk"), None),
        P(("head", "blk")),
        P(("head", "blk")),
        P(("head", "blk")),
        P(("head", "blk"), None),
        P(("head", "blk")),
        P(("head", "blk"), None),
        P(("head", "blk")),
        P(None, "blk", "head", None),
    )
    return jax.shard_map(
        on_device,
        mesh=mesh,
        in_specs=placed,
        out_specs=(
            P(None, "blk", "head", None),
            P(None, "blk", "head", None),
            P(("head", "blk")),
            P(("head", "blk")),
            P(("head", "blk"), None),
            P(("head", "blk")),
            P(("head", "blk"), None),
            P(("head", "blk")),
            P(("head", "blk")),
            P(("head", "blk")),
            P(("head", "blk"), None),
            P(("head", "blk")),
            P(("head", "blk"), None),
            P(("head", "blk")),
        ),
        check_vma=False,
    )
```

profile of v0, /device:TPU:0, one launch (start us, length us, event | category | flops | bytes accessed | tf_op | source)
XLA Modules:
  0.0 812.0 jit_solution(15571114791368626788)
XLA Ops:
  18.4 42.4 %all-reduce.17 = (bf16[1024]{0:T(1024)(128)(2,1)S(1)}, bf16[512]{0:T(512)(128)(2,1)S(1)}, bf16[512]{0:T(512)(128)(2,1)S(1)}, bf16[512]{0:T(512)(128)(2,1)S(1)}, ...) all-reduce(bf16[1024]{0:T(1024)(128)(2,1)S(1)} %dynamic-update-slic, ...), channel_id=1, replica_groups=mesh['head'=4,'blk'=8] {'head','blk'}, use_global_device_ids=true, to_apply=%add.2 | all-reduce | flops 6144 | bytes 24576
  61.9 7.3 all-gather.4.cloned.1.call-done
  72.1 3.3 all-to-all-start
  76.6 3.9 all-to-all-done
  80.5 3.3 all-to-all-start.1
  84.9 3.9 all-to-all-done.1
  88.8 3.3 all-to-all-start.2
  94.8 2.3 all-to-all-done.2
  97.9 73.0 %while.54 = (s32[]{:T(128)}, bf16[2,256,2,64]{1,3,2,0:T(8,128)(2,1)S(1)}, bf16[2,256,2,64]{1,3,2,0:T(8,128)(2,1)S(1)}, f32[2,256,2]{1,2,0:T(2,128)S(1)}, f32[2,2...) while((s32[]{:T(128)}, ...), condition=%wide.region_9.10_spmd.clone.clone, body=%wide.region_3.9_spmd.clone.clone.sunk | while | flops 70257696 | bytes 6511330 | solution.py:181
  100.5 3.2 collective-permute-start.1
  105.1 3.9 conditional.10
  112.3 2.6 collective-permute-start.1
  117.0 5.8 collective-permute-start
  123.5 4.1 collective-permute-start.1
  129.8 2.7 collective-permute-start
  133.1 6.0 collective-permute-start.1
  141.3 2.7 collective-permute-start
  144.6 4.2 collective-permute-start.1
  151.0 3.5 collective-permute-start
  155.2 4.2 collective-permute-start.1
  161.5 3.0 collective-permute-start
  165.1 4.3 collective-permute-start.1
  171.8 3.3 all-to-all-start.3
  175.1 44.3 %all_gather.40 = bf16[512,512]{1,0:T(8,128)(2,1)S(1)} all-gather(bf16[16,512]{1,0:T(8,128)(2,1)S(1)} %copy-done.13), channel_id=1, replica_groups=mesh['head'=4,'blk'=8] {'head','blk'}, dimensions={0}, use_global_device_ids=true | all-gather | bytes 540672 | tf_op jit(solution)/shard_map/all_gather | solution.py:76
  224.0 3.5 convert_reduce_fusion
  230.1 3.3 all-to-all-start.4
  234.8 3.7 all-to-all-done.4
  239.2 148.6 %while.55 = (s32[]{:T(128)}, bf16[2,256,2,64]{1,3,2,0:T(8,128)(2,1)S(1)}, bf16[2,256,2,64]{1,3,2,0:T(8,128)(2,1)S(1)}, f32[2,256,2,64]{1,3,2,0:T(8,128)S(1)}, f3...) while((s32[]{:T(128)}, ...), condition=%wide.region_23.24_spmd.clone.clone, body=%wide.region_19.0_spmd.clone.clone.sunk | while | flops 171050016 | bytes 12483382 | solution.py:277
  245.6 6.1 conditional.11
  252.1 6.2 collective-permute-done.4
  265.9 5.2 collective-permute-start.4
  271.6 2.3 collective-permute-done.4
  273.9 3.6 collective-permute-done.5
  280.2 2.8 collective-permute-start.3
  285.3 7.1 collective-permute-start.5
  294.2 4.1 collective-permute-start.2
  298.9 4.4 collective-permute-start.3
  307.6 4.5 collective-permute-done.4
  314.3 4.0 collective-permute-start.2
  319.0 4.4 collective-permute-start.3
  327.0 5.0 collective-permute-done.4
  336.3 2.8 collective-permute-start.3
  341.3 2.6 collective-permute-start.4
  344.0 2.5 collective-permute-start.5
  347.9 2.4 collective-permute-done.5
  353.6 4.4 collective-permute-start.3
  362.2 2.5 collective-permute-start.5
  371.3 4.4 collective-permute-start.3
  378.0 2.5 collective-permute-start.5
  380.6 5.8 collective-permute-done.4
  388.6 3.3 all-to-all-start.5
  392.8 4.2 all-to-all-done.5
  397.0 3.3 all-to-all-start.6
  401.1 4.2 all-to-all-done.6
  405.3 3.3 all-to-all-start.7
  408.9 4.7 all-to-all-done.7
  413.8 2.3 fusion.58
  417.2 2.8 fusion.51
  421.2 2.7 fusion.52
  424.6 2.9 fusion.41
  428.4 39.6 %all-reduce.16 = (f32[512]{0:T(512)S(1)}, f32[512]{0:T(512)S(1)}, f32[1024]{0:T(1024)S(1)}, f32[512]{0:T(512)S(1)}, f32[512]{0:T(512)S(1)}, /*index=5*/f32[512]{0:T(512)S(1)}, f32[2048]{0:T(1024)S(1)}, f32[512]{0:T(512)S(1)}) all-reduce(f32[512]{0:T(512)S(1)} %get-tuple-element.1356, ...), channel_id=2, replica_groups=mesh['head'=4,'blk'=8] {'head','blk'}, use_global_device_ids=true, to_apply=%region_27.28.clone | all-reduce | flops 6144 | bytes 49152
  473.5 44.7 %reduce-scatter.5.cloned.1.call-done = f32[16,1536]{1,0:T(8,128)} async-done(((f32[512,1536]{1,0:T(8,128)}), f32[16,1536]{1,0:T(8,128)}) %reduce-scatter.5.cloned.1.call-update) | async-done | bytes 98320 | tf_op jit(solution)/shard_map/reduce_scatter | solution.py:321
  518.2 144.5 %reduce-scatter.9.cloned.1.call-done = f32[16,2048]{1,0:T(8,128)} async-done(((f32[512,2048]{1,0:T(8,128)}), f32[16,2048]{1,0:T(8,128)}) %reduce-scatter.9.cloned.1.call-update) | async-done | bytes 131088 | tf_op jit(solution)/shard_map/reduce_scatter | solution.py:327
  662.7 142.5 %reduce-scatter.11.cloned.1.call-done = f32[64,512]{1,0:T(8,128)} async-done(((f32[2048,512]{1,0:T(8,128)}), f32[64,512]{1,0:T(8,128)}) %reduce-scatter.11.cloned.1.call-update) | async-done | bytes 131088 | tf_op jit(solution)/shard_map/reduce_scatter | solution.py:329
  (401 shorter events, 122.4 us)
Async XLA Ops:
  7.2 62.0 %all-gather.4.cloned.1.call-start = ((), (), s32[]{:S(2)}) async-start(), calls=%async_computation.12 | async-start | bytes 1622016 | tf_op jit(solution)/shard_map/all_gather | solution.py:74
  7.9 213.9 %all-gather.6.cloned.1.call-start = ((), (), s32[]{:S(2)}) async-start(), calls=%async_computation.13 | async-start | bytes 2162688 | tf_op jit(solution)/shard_map/all_gather | solution.py:80
  8.7 215.3 %all-gather.8.cloned.1.call-start = ((), (), s32[]{:S(2)}) async-start(), calls=%async_computation.14 | async-start | bytes 2162688 | tf_op jit(solution)/shard_map/all_gather | solution.py:82
  11.6 59.5 %copy-start.20 = (f32[128]{0:T(128)}, f32[128]{0:T(128)S(1)}, u32[]{:S(2)}) copy-start(f32[128]{0:T(128)S(1)} %div.38) | copy-start | bytes 1540
  72.1 8.3 %all-to-all-start = ((bf16[4,2,8192]{2,1,0:T(2,128)(2,1)}), bf16[4,2,8192]{2,1,0:T(2,128)(2,1)S(1)}, u32[]{:S(2)}, u32[]{:S(2)}) async-start(bf16[4,2,8192]{2,1,0:T(2,128)(2,1)} %reshape.392), calls=%async_computation | async-start | bytes 262144 | tf_op jit(solution)/shard_map/all_to_all | solution.py:117
  80.5 8.3 %all-to-all-start.1 = ((bf16[4,2,8192]{2,1,0:T(2,128)(2,1)}), bf16[4,2,8192]{2,1,0:T(2,128)(2,1)S(1)}, u32[]{:S(2)}, u32[]{:S(2)}) async-start(bf16[4,2,8192]{2,1,0:T(2,128)(2,1)} %reshape.394), calls=%async_computation.1 | async-start | bytes 262144 | tf_op jit(solution)/shard_map/all_to_all | solution.py:118
  88.8 8.3 %all-to-all-start.2 = ((bf16[4,2,8192]{2,1,0:T(2,128)(2,1)}), bf16[4,2,8192]{2,1,0:T(2,128)(2,1)S(1)}, u32[]{:S(2)}, u32[]{:S(2)}) async-start(bf16[4,2,8192]{2,1,0:T(2,128)(2,1)} %reshape.396), calls=%async_computation.2 | async-start | bytes 262144 | tf_op jit(solution)/shard_map/all_to_all | solution.py:116
  98.5 10.5 %collective-permute-start = (bf16[2,256,2,64]{1,3,2,0:T(8,128)(2,1)}, bf16[2,256,2,64]{1,3,2,0:T(8,128)(2,1)S(1)}, u32[]{:S(2)}, u32[]{:S(2)}) collective-permute-start(bf16[2,256,2,64]{1,3,2,0:T(8,128)(2,1)} %copy.205), channel_id=1, source_target_pairs={{0,1},{1,2},{2,3},{3,4},{4,5},{5,6},{6,7},{8,9},{9,10},{10,11},{11... | collective-permute-start | bytes 393224 | tf_op jit(solution)/shard_map/while/body/eval_jaxpr/ppermute | solution.py:17
  100.5 8.5 %collective-permute-start.1 = (bf16[2,256,2,64]{1,3,2,0:T(8,128)(2,1)}, bf16[2,256,2,64]{1,3,2,0:T(8,128)(2,1)S(1)}, u32[]{:S(2)}, u32[]{:S(2)}) collective-permute-start(bf16[2,256,2,64]{1,3,2,0:T(8,128)(2,1)} %copy.206), channel_id=1, source_target_pairs={{0,1},{1,2},{2,3},{3,4},{4,5},{5,6},{6,7},{8,9},{9,10},{10,11},{11... | collective-permute-start | bytes 393224 | tf_op jit(solution)/shard_map/while/body/eval_jaxpr/ppermute | solution.py:17
  109.7 6.7 collective-permute-start
  112.3 4.1 collective-permute-start.1
  117.0 12.1 %collective-permute-start = (bf16[2,256,2,64]{1,3,2,0:T(8,128)(2,1)}, bf16[2,256,2,64]{1,3,2,0:T(8,128)(2,1)S(1)}, u32[]{:S(2)}, u32[]{:S(2)}) collective-permute-start(bf16[2,256,2,64]{1,3,2,0:T(8,128)(2,1)} %copy.205), channel_id=1, source_target_pairs={{0,1},{1,2},{2,3},{3,4},{4,5},{5,6},{6,7},{8,9},{9,10},{10,11},{11... | collective-permute-start | bytes 393224 | tf_op jit(solution)/shard_map/while/body/eval_jaxpr/ppermute | solution.py:17
  123.5 5.6 collective-permute-start.1
  129.8 10.8 %collective-permute-start = (bf16[2,256,2,64]{1,3,2,0:T(8,128)(2,1)}, bf16[2,256,2,64]{1,3,2,0:T(8,128)(2,1)S(1)}, u32[]{:S(2)}, u32[]{:S(2)}) collective-permute-start(bf16[2,256,2,64]{1,3,2,0:T(8,128)(2,1)} %copy.205), channel_id=1, source_target_pairs={{0,1},{1,2},{2,3},{3,4},{4,5},{5,6},{6,7},{8,9},{9,10},{10,11},{11... | collective-permute-start | bytes 393224 | tf_op jit(solution)/shard_map/while/body/eval_jaxpr/ppermute | solution.py:17
  133.1 7.5 collective-permute-start.1
  141.3 9.0 %collective-permute-start = (bf16[2,256,2,64]{1,3,2,0:T(8,128)(2,1)}, bf16[2,256,2,64]{1,3,2,0:T(8,128)(2,1)S(1)}, u32[]{:S(2)}, u32[]{:S(2)}) collective-permute-start(bf16[2,256,2,64]{1,3,2,0:T(8,128)(2,1)} %copy.205), channel_id=1, source_target_pairs={{0,1},{1,2},{2,3},{3,4},{4,5},{5,6},{6,7},{8,9},{9,10},{10,11},{11... | collective-permute-start | bytes 393224 | tf_op jit(solution)/shard_map/while/body/eval_jaxpr/ppermute | solution.py:17
  144.6 5.7 collective-permute-start.1
  151.0 9.8 %collective-permute-start = (bf16[2,256,2,64]{1,3,2,0:T(8,128)(2,1)}, bf16[2,256,2,64]{1,3,2,0:T(8,128)(2,1)S(1)}, u32[]{:S(2)}, u32[]{:S(2)}) collective-permute-start(bf16[2,256,2,64]{1,3,2,0:T(8,128)(2,1)} %copy.205), channel_id=1, source_target_pairs={{0,1},{1,2},{2,3},{3,4},{4,5},{5,6},{6,7},{8,9},{9,10},{10,11},{11... | collective-permute-start | bytes 393224 | tf_op jit(solution)/shard_map/while/body/eval_jaxpr/ppermute | solution.py:17
  155.2 5.7 collective-permute-start.1
  161.5 9.3 %collective-permute-start = (bf16[2,256,2,64]{1,3,2,0:T(8,128)(2,1)}, bf16[2,256,2,64]{1,3,2,0:T(8,128)(2,1)S(1)}, u32[]{:S(2)}, u32[]{:S(2)}) collective-permute-start(bf16[2,256,2,64]{1,3,2,0:T(8,128)(2,1)} %copy.205), channel_id=1, source_target_pairs={{0,1},{1,2},{2,3},{3,4},{4,5},{5,6},{6,7},{8,9},{9,10},{10,11},{11... | collective-permute-start | bytes 393224 | tf_op jit(solution)/shard_map/while/body/eval_jaxpr/ppermute | solution.py:17
  165.1 5.7 collective-permute-start.1
  171.0 48.5 %copy-start.24 = (f32[2,256,2]{1,2,0:T(2,128)}, f32[2,256,2]{1,2,0:T(2,128)S(1)}, u32[]{:S(2)}) copy-start(f32[2,256,2]{1,2,0:T(2,128)S(1)} %get-tuple-element.1719) | copy-start | bytes 12292
  171.0 49.8 %copy-start.2 = (bf16[2,1,64,512]{3,2,1,0:T(8,128)(2,1)S(1)}, bf16[2,1,64,512]{3,2,1,0:T(8,128)(2,1)}, u32[]{:S(2)}) copy-start(bf16[2,1,64,512]{3,2,1,0:T(8,128)(2,1)} %param.26) | copy-start | bytes 393220
  171.8 48.8 %all-to-all-start.3 = ((bf16[2,256,128]{2,0,1:T(2,128)(2,1)}), bf16[2,256,128]{2,0,1:T(2,128)(2,1)S(1)}, u32[]{:S(2)}, u32[]{:S(2)}) async-start(bf16[2,256,128]{2,0,1:T(2,128)(2,1)} %copy.111), calls=%async_computation.3 | async-start | bytes 262144 | tf_op jit(solution)/shard_map/all_to_all | solution.py:189
  230.1 8.4 %all-to-all-start.4 = ((bf16[4,2,8192]{2,1,0:T(2,128)(2,1)}), bf16[4,2,8192]{2,1,0:T(2,128)(2,1)S(1)}, u32[]{:S(2)}, u32[]{:S(2)}) async-start(bf16[4,2,8192]{2,1,0:T(2,128)(2,1)} %reshape.398), calls=%async_computation.4 | async-start | bytes 262144 | tf_op jit(solution)/shard_map/all_to_all | solution.py:219
  233.4 240.1 %reduce-scatter.7.cloned.1.call-start = ((), (), s32[]{:S(2)}) async-start(), calls=%async_computation.16 | async-start | bytes 1081344 | tf_op jit(solution)/shard_map/reduce_scatter | solution.py:323
  239.9 19.8 %collective-permute-start.2 = (bf16[2,256,2,64]{1,3,2,0:T(8,128)(2,1)}, bf16[2,256,2,64]{1,3,2,0:T(8,128)(2,1)S(1)}, u32[]{:S(2)}, u32[]{:S(2)}) collective-permute-start(bf16[2,256,2,64]{1,3,2,0:T(8,128)(2,1)} %copy.229), channel_id=1, source_target_pairs={{0,1},{1,2},{2,3},{3,4},{4,5},{5,6},{6,7},{8,9},{9,10},{10,11},{11... | collective-permute-start | bytes 393224 | tf_op jit(solution)/shard_map/while/body/eval_jaxpr/ppermute | solution.py:17
  241.8 17.9 %collective-permute-start.3 = (bf16[2,256,2,64]{1,3,2,0:T(8,128)(2,1)}, bf16[2,256,2,64]{1,3,2,0:T(8,128)(2,1)S(1)}, u32[]{:S(2)}, u32[]{:S(2)}) collective-permute-start(bf16[2,256,2,64]{1,3,2,0:T(8,128)(2,1)} %copy.230), channel_id=1, source_target_pairs={{0,1},{1,2},{2,3},{3,4},{4,5},{5,6},{6,7},{8,9},{9,10},{10,11},{11... | collective-permute-start | bytes 393224 | tf_op jit(solution)/shard_map/while/body/eval_jaxpr/ppermute | solution.py:17
  251.8 6.5 collective-permute-start.4
  251.9 7.8 collective-permute-start.5
  260.4 17.2 %collective-permute-start.2 = (bf16[2,256,2,64]{1,3,2,0:T(8,128)(2,1)}, bf16[2,256,2,64]{1,3,2,0:T(8,128)(2,1)S(1)}, u32[]{:S(2)}, u32[]{:S(2)}) collective-permute-start(bf16[2,256,2,64]{1,3,2,0:T(8,128)(2,1)} %copy.229), channel_id=1, source_target_pairs={{0,1},{1,2},{2,3},{3,4},{4,5},{5,6},{6,7},{8,9},{9,10},{10,11},{11... | collective-permute-start | bytes 393224 | tf_op jit(solution)/shard_map/while/body/eval_jaxpr/ppermute | solution.py:17
  262.4 15.2 %collective-permute-start.3 = (bf16[2,256,2,64]{1,3,2,0:T(8,128)(2,1)}, bf16[2,256,2,64]{1,3,2,0:T(8,128)(2,1)S(1)}, u32[]{:S(2)}, u32[]{:S(2)}) collective-permute-start(bf16[2,256,2,64]{1,3,2,0:T(8,128)(2,1)} %copy.230), channel_id=1, source_target_pairs={{0,1},{1,2},{2,3},{3,4},{4,5},{5,6},{6,7},{8,9},{9,10},{10,11},{11... | collective-permute-start | bytes 393224 | tf_op jit(solution)/shard_map/while/body/eval_jaxpr/ppermute | solution.py:17
  265.9 8.0 collective-permute-start.4
  271.2 6.4 collective-permute-start.5
  278.3 15.2 %collective-permute-start.2 = (bf16[2,256,2,64]{1,3,2,0:T(8,128)(2,1)}, bf16[2,256,2,64]{1,3,2,0:T(8,128)(2,1)S(1)}, u32[]{:S(2)}, u32[]{:S(2)}) collective-permute-start(bf16[2,256,2,64]{1,3,2,0:T(8,128)(2,1)} %copy.229), channel_id=1, source_target_pairs={{0,1},{1,2},{2,3},{3,4},{4,5},{5,6},{6,7},{8,9},{9,10},{10,11},{11... | collective-permute-start | bytes 393224 | tf_op jit(solution)/shard_map/while/body/eval_jaxpr/ppermute | solution.py:17
  280.2 13.3 %collective-permute-start.3 = (bf16[2,256,2,64]{1,3,2,0:T(8,128)(2,1)}, bf16[2,256,2,64]{1,3,2,0:T(8,128)(2,1)S(1)}, u32[]{:S(2)}, u32[]{:S(2)}) collective-permute-start(bf16[2,256,2,64]{1,3,2,0:T(8,128)(2,1)} %copy.230), channel_id=1, source_target_pairs={{0,1},{1,2},{2,3},{3,4},{4,5},{5,6},{6,7},{8,9},{9,10},{10,11},{11... | collective-permute-start | bytes 393224 | tf_op jit(solution)/shard_map/while/body/eval_jaxpr/ppermute | solution.py:17
  285.2 7.3 collective-permute-start.4
  285.3 8.1 %collective-permute-start.5 = (bf16[2,256,2,64]{1,3,2,0:T(8,128)(2,1)S(1)}, bf16[2,256,2,64]{1,3,2,0:T(8,128)(2,1)S(1)}, u32[]{:S(2)}, u32[]{:S(2)}) collective-permute-start(bf16[2,256,2,64]{1,3,2,0:T(8,128)(2,1)S(1)} %fusion.92), channel_id=1, source_target_pairs={{0,1},{1,2},{2,3},{3,4},{4,5},{5,6},{6,7},{7,0},{8,9},{9,10},{10,1... | collective-permute-start | bytes 393224 | tf_op jit(solution)/shard_map/while/body/eval_jaxpr/ppermute | solution.py:22
  294.2 19.4 %collective-permute-start.2 = (bf16[2,256,2,64]{1,3,2,0:T(8,128)(2,1)}, bf16[2,256,2,64]{1,3,2,0:T(8,128)(2,1)S(1)}, u32[]{:S(2)}, u32[]{:S(2)}) collective-permute-start(bf16[2,256,2,64]{1,3,2,0:T(8,128)(2,1)} %copy.229), channel_id=1, source_target_pairs={{0,1},{1,2},{2,3},{3,4},{4,5},{5,6},{6,7},{8,9},{9,10},{10,11},{11... | collective-permute-start | bytes 393224 | tf_op jit(solution)/shard_map/while/body/eval_jaxpr/ppermute | solution.py:17
  298.9 14.7 %collective-permute-start.3 = (bf16[2,256,2,64]{1,3,2,0:T(8,128)(2,1)}, bf16[2,256,2,64]{1,3,2,0:T(8,128)(2,1)S(1)}, u32[]{:S(2)}, u32[]{:S(2)}) collective-permute-start(bf16[2,256,2,64]{1,3,2,0:T(8,128)(2,1)} %copy.230), channel_id=1, source_target_pairs={{0,1},{1,2},{2,3},{3,4},{4,5},{5,6},{6,7},{8,9},{9,10},{10,11},{11... | collective-permute-start | bytes 393224 | tf_op jit(solution)/shard_map/while/body/eval_jaxpr/ppermute | solution.py:17
  305.6 6.5 collective-permute-start.4
  305.7 7.9 collective-permute-start.5
  314.3 19.3 %collective-permute-start.2 = (bf16[2,256,2,64]{1,3,2,0:T(8,128)(2,1)}, bf16[2,256,2,64]{1,3,2,0:T(8,128)(2,1)S(1)}, u32[]{:S(2)}, u32[]{:S(2)}) collective-permute-start(bf16[2,256,2,64]{1,3,2,0:T(8,128)(2,1)} %copy.229), channel_id=1, source_target_pairs={{0,1},{1,2},{2,3},{3,4},{4,5},{5,6},{6,7},{8,9},{9,10},{10,11},{11... | collective-permute-start | bytes 393224 | tf_op jit(solution)/shard_map/while/body/eval_jaxpr/ppermute | solution.py:17
  319.0 14.6 %collective-permute-start.3 = (bf16[2,256,2,64]{1,3,2,0:T(8,128)(2,1)}, bf16[2,256,2,64]{1,3,2,0:T(8,128)(2,1)S(1)}, u32[]{:S(2)}, u32[]{:S(2)}) collective-permute-start(bf16[2,256,2,64]{1,3,2,0:T(8,128)(2,1)} %copy.230), channel_id=1, source_target_pairs={{0,1},{1,2},{2,3},{3,4},{4,5},{5,6},{6,7},{8,9},{9,10},{10,11},{11... | collective-permute-start | bytes 393224 | tf_op jit(solution)/shard_map/while/body/eval_jaxpr/ppermute | solution.py:17
  325.7 6.3 collective-permute-start.4
  325.8 7.8 collective-permute-start.5
  334.3 16.0 %collective-permute-start.2 = (bf16[2,256,2,64]{1,3,2,0:T(8,128)(2,1)}, bf16[2,256,2,64]{1,3,2,0:T(8,128)(2,1)S(1)}, u32[]{:S(2)}, u32[]{:S(2)}) collective-permute-start(bf16[2,256,2,64]{1,3,2,0:T(8,128)(2,1)} %copy.229), channel_id=1, source_target_pairs={{0,1},{1,2},{2,3},{3,4},{4,5},{5,6},{6,7},{8,9},{9,10},{10,11},{11... | collective-permute-start | bytes 393224 | tf_op jit(solution)/shard_map/while/body/eval_jaxpr/ppermute | solution.py:17
  336.3 14.1 %collective-permute-start.3 = (bf16[2,256,2,64]{1,3,2,0:T(8,128)(2,1)}, bf16[2,256,2,64]{1,3,2,0:T(8,128)(2,1)S(1)}, u32[]{:S(2)}, u32[]{:S(2)}) collective-permute-start(bf16[2,256,2,64]{1,3,2,0:T(8,128)(2,1)} %copy.230), channel_id=1, source_target_pairs={{0,1},{1,2},{2,3},{3,4},{4,5},{5,6},{6,7},{8,9},{9,10},{10,11},{11... | collective-permute-start | bytes 393224 | tf_op jit(solution)/shard_map/while/body/eval_jaxpr/ppermute | solution.py:17
  341.3 6.5 collective-permute-start.4
  344.0 6.3 collective-permute-start.5
  351.0 17.5 %collective-permute-start.2 = (bf16[2,256,2,64]{1,3,2,0:T(8,128)(2,1)}, bf16[2,256,2,64]{1,3,2,0:T(8,128)(2,1)S(1)}, u32[]{:S(2)}, u32[]{:S(2)}) collective-permute-start(bf16[2,256,2,64]{1,3,2,0:T(8,128)(2,1)} %copy.229), channel_id=1, source_target_pairs={{0,1},{1,2},{2,3},{3,4},{4,5},{5,6},{6,7},{8,9},{9,10},{10,11},{11... | collective-permute-start | bytes 393224 | tf_op jit(solution)/shard_map/while/body/eval_jaxpr/ppermute | solution.py:17
  353.6 14.9 %collective-permute-start.3 = (bf16[2,256,2,64]{1,3,2,0:T(8,128)(2,1)}, bf16[2,256,2,64]{1,3,2,0:T(8,128)(2,1)S(1)}, u32[]{:S(2)}, u32[]{:S(2)}) collective-permute-start(bf16[2,256,2,64]{1,3,2,0:T(8,128)(2,1)} %copy.230), channel_id=1, source_target_pairs={{0,1},{1,2},{2,3},{3,4},{4,5},{5,6},{6,7},{8,9},{9,10},{10,11},{11... | collective-permute-start | bytes 393224 | tf_op jit(solution)/shard_map/while/body/eval_jaxpr/ppermute | solution.py:17
  360.3 6.8 collective-permute-start.4
  362.2 6.3 collective-permute-start.5
  369.2 18.6 %collective-permute-start.2 = (bf16[2,256,2,64]{1,3,2,0:T(8,128)(2,1)}, bf16[2,256,2,64]{1,3,2,0:T(8,128)(2,1)S(1)}, u32[]{:S(2)}, u32[]{:S(2)}) collective-permute-start(bf16[2,256,2,64]{1,3,2,0:T(8,128)(2,1)} %copy.229), channel_id=1, source_target_pairs={{0,1},{1,2},{2,3},{3,4},{4,5},{5,6},{6,7},{8,9},{9,10},{10,11},{11... | collective-permute-start | bytes 393224 | tf_op jit(solution)/shard_map/while/body/eval_jaxpr/ppermute | solution.py:17
  371.3 16.6 %collective-permute-start.3 = (bf16[2,256,2,64]{1,3,2,0:T(8,128)(2,1)}, bf16[2,256,2,64]{1,3,2,0:T(8,128)(2,1)S(1)}, u32[]{:S(2)}, u32[]{:S(2)}) collective-permute-start(bf16[2,256,2,64]{1,3,2,0:T(8,128)(2,1)} %copy.230), channel_id=1, source_target_pairs={{0,1},{1,2},{2,3},{3,4},{4,5},{5,6},{6,7},{8,9},{9,10},{10,11},{11... | collective-permute-start | bytes 393224 | tf_op jit(solution)/shard_map/while/body/eval_jaxpr/ppermute | solution.py:17
  377.9 8.5 %collective-permute-start.4 = (bf16[2,256,2,64]{1,3,2,0:T(8,128)(2,1)S(1)}, bf16[2,256,2,64]{1,3,2,0:T(8,128)(2,1)S(1)}, u32[]{:S(2)}, u32[]{:S(2)}) collective-permute-start(bf16[2,256,2,64]{1,3,2,0:T(8,128)(2,1)S(1)} %fusion.91), channel_id=1, source_target_pairs={{0,1},{1,2},{2,3},{3,4},{4,5},{5,6},{6,7},{7,0},{8,9},{9,10},{10,1... | collective-permute-start | bytes 393224 | tf_op jit(solution)/shard_map/while/body/eval_jaxpr/ppermute | solution.py:22
  378.0 9.8 %collective-permute-start.5 = (bf16[2,256,2,64]{1,3,2,0:T(8,128)(2,1)S(1)}, bf16[2,256,2,64]{1,3,2,0:T(8,128)(2,1)S(1)}, u32[]{:S(2)}, u32[]{:S(2)}) collective-permute-start(bf16[2,256,2,64]{1,3,2,0:T(8,128)(2,1)S(1)} %fusion.92), channel_id=1, source_target_pairs={{0,1},{1,2},{2,3},{3,4},{4,5},{5,6},{6,7},{7,0},{8,9},{9,10},{10,1... | collective-permute-start | bytes 393224 | tf_op jit(solution)/shard_map/while/body/eval_jaxpr/ppermute | solution.py:22
  388.6 8.3 %all-to-all-start.5 = ((bf16[2,256,128]{2,0,1:T(2,128)(2,1)}), bf16[2,256,128]{2,0,1:T(2,128)(2,1)S(1)}, u32[]{:S(2)}, u32[]{:S(2)}) async-start(bf16[2,256,128]{2,0,1:T(2,128)(2,1)} %copy.122), calls=%async_computation.5 | async-start | bytes 262144 | tf_op jit(solution)/shard_map/all_to_all | solution.py:283
  397.0 8.3 %all-to-all-start.6 = ((bf16[2,256,128]{2,0,1:T(2,128)(2,1)}), bf16[2,256,128]{2,0,1:T(2,128)(2,1)S(1)}, u32[]{:S(2)}, u32[]{:S(2)}) async-start(bf16[2,256,128]{2,0,1:T(2,128)(2,1)} %copy.125), calls=%async_computation.6 | async-start | bytes 262144 | tf_op jit(solution)/shard_map/all_to_all | solution.py:290
  405.3 8.3 %all-to-all-start.7 = ((bf16[2,256,128]{2,0,1:T(2,128)(2,1)}), bf16[2,256,128]{2,0,1:T(2,128)(2,1)S(1)}, u32[]{:S(2)}, u32[]{:S(2)}) async-start(bf16[2,256,128]{2,0,1:T(2,128)(2,1)} %copy.128), calls=%async_computation.7 | async-start | bytes 262144 | tf_op jit(solution)/shard_map/all_to_all | solution.py:297
  408.6 109.6 %reduce-scatter.5.cloned.1.call-start = ((), (), s32[]{:S(2)}) async-start(), calls=%async_computation.15 | async-start | bytes 3244032 | tf_op jit(solution)/shard_map/reduce_scatter | solution.py:321
  416.2 246.5 %reduce-scatter.9.cloned.1.call-start = ((), (), s32[]{:S(2)}) async-start(), calls=%async_computation.17 | async-start | bytes 4325376 | tf_op jit(solution)/shard_map/reduce_scatter | solution.py:327
  420.0 385.2 %reduce-scatter.11.cloned.1.call-start = ((), (), s32[]{:S(2)}) async-start(), calls=%async_computation.18 | async-start | bytes 4325376 | tf_op jit(solution)/shard_map/reduce_scatter | solution.py:329
  (24 other events, 111.6 us)
Sparse Core Ops, SparseCore 0:
  11.0 58.1 all-gather.3
  72.2 55.3 all-gather.5
  130.6 55.7 all-gather.7
  236.8 134.4 reduce-scatter.6
  416.3 101.8 reduce-scatter.4
  521.0 141.6 reduce-scatter.8
  665.7 139.4 reduce-scatter.10
where the time goes:
time: 816 us; the launch traced here: 812 us
  waiting for transfers between devices  410 us (50%)
  starting transfers between devices  147 us (18%)
  blocking collectives  126 us (15%)
  local copies, waits for them, and re-layouts  45.9 us (6%)
  matrix products  28.5 us (3%)
  other arithmetic  26.9 us (3%)
  between operations  15.6 us (2%)
  loops' own time  12.1 us (1%)
    reduce_scatter x1, waiting for transfers between devices, on_device(): lax.psum_scatter(grad_up, ('head', 'blk'), scatter_dimension=0, tiled=True)  145 us
    reduce_scatter x1, waiting for transfers between devices, on_device(): lax.psum_scatter(grad_down, ('head', 'blk'), scatter_dimension=0, tiled=T...  142 us
    ppermute x30, starting transfers between devices, shifted(): return lax.ppermute(x, axis, pairs)  92.2 us
    unnamed x2, blocking collectives  81.9 us
    reduce_scatter x1, waiting for transfers between devices, on_device(): lax.psum_scatter(grad_project, ('head', 'blk'), scatter_dimension=0, tile...  44.7 us
    all_gather x1, blocking collectives, on_device(): lax.all_gather(output_weight, ('head', 'blk'), axis=0, tiled=True)  44.3 us
    ppermute x16, waiting for transfers between devices, from_behind(): return lax.ppermute(x, axis, [(i, (i + by) % peers) for i in range(peers)])  41.6 us
    ppermute x16, starting transfers between devices, from_behind(): return lax.ppermute(x, axis, [(i, (i + by) % peers) for i in range(peers)])  28 us
  transfers between devices with their start and end apart: 61, of which 26 were waited for; matrix products, arithmetic and copies ran while one was open for 11% of the time, Pallas kernels for 0%

commit v1 on v0

v1 whole, which is shorter than its diff:
```python
import functools

import jax
import jax.numpy as jnp
from jax import lax
from jax.experimental import pallas as pl
from jax.experimental.pallas import tpu as pltpu
from jax.sharding import PartitionSpec as P

H = 8
HD = 64
LANES = 128
EPSILON = 1e-05
NEG_FILL = -1e30
TILE_Q = 256

bf16 = jnp.bfloat16
f32 = jnp.float32
i32 = jnp.int32
BOTH = ("head", "blk")


def dot_nn(a, b):
    return lax.dot_general(a, b, (((1,), (0,)), ((), ())), preferred_element_type=f32)


def dot_nt(a, b):
    return lax.dot_general(a, b, (((1,), (1,)), ((), ())), preferred_element_type=f32)


def dot_tn(a, b):
    return lax.dot_general(a, b, (((0,), (0,)), ((), ())), preferred_element_type=f32)


def norm_forward(values, gain, shift):
    centred = values - jnp.mean(values, axis=-1, keepdims=True)
    variance = jnp.mean(centred * centred, axis=-1, keepdims=True)
    inverse_root = lax.rsqrt(variance + EPSILON)
    unit_value = centred * inverse_root
    return (unit_value * gain + shift, unit_value, inverse_root)


def norm_input_grad(upstream, unit_value, inverse_root, gain):
    scaled = upstream * gain
    inner = scaled - jnp.mean(scaled, axis=-1, keepdims=True)
    inner = inner - unit_value * jnp.mean(scaled * unit_value, axis=-1, keepdims=True)
    return inverse_root * inner


class AttentionShape:
    def __init__(self, blocks, part_rows, parts, run, stride):
        self.per_tile = max(1, TILE_Q // part_rows)
        self.tiles = blocks // self.per_tile
        self.tile = self.per_tile * part_rows
        self.part_rows = part_rows
        self.parts = parts
        self.run = run
        self.stride = stride
        self.span = self.tile * parts


def unpack_tile(packed_ref, tile, geo):
    half = geo.part_rows // 2
    pieces = []
    for i in range(geo.per_tile):
        packed = packed_ref[tile * geo.per_tile + i]
        pieces += [packed[:, :HD], packed[:, HD:]]
    return jnp.concatenate(pieces, axis=0)


def key_base(geo):
    rows = lax.broadcasted_iota(i32, (geo.tile, 1), 0)
    return (rows // geo.run) * geo.stride + rows % geo.run


def forward_kernel(geo, scal_ref, q_ref, kv_ref, bounds_ref, out_ref, ot_ref, lse_ref, kvt_ref):
    base = jnp.broadcast_to(key_base(geo), (geo.tile, geo.tile))
    for part in range(geo.parts):
        for tile in range(geo.tiles):
            kvt_ref[part, tile] = kv_ref[part, tile].T
    for tile in range(geo.tiles):
        q = unpack_tile(q_ref, tile, geo) * jnp.asarray(HD**-0.5, bf16)
        qz = jnp.concatenate([q, jnp.zeros_like(q)], axis=1)
        start = bounds_ref[tile, 0:1]
        last = bounds_ref[tile, 1:2]
        own = bounds_ref[tile, 2:3]

        def chunk(part, key_tile, carry, diagonal):
            run_max, run_sum, acc = carry
            offset = key_tile * geo.span + scal_ref[part]
            scores = dot_nt(kv_ref[part, key_tile], qz)
            allowed = (base >= start - offset) & (base <= last - offset)
            if diagonal:
                allowed = allowed | (base == own - offset)
            masked = jnp.where(allowed, scores, NEG_FILL)
            new_max = jnp.maximum(run_max, jnp.max(masked, axis=0, keepdims=True))
            factor = jnp.exp(run_max - new_max)
            probs = jnp.where(allowed, jnp.exp(masked - new_max), 0.0)
            new_sum = run_sum * factor + jnp.sum(probs, axis=0, keepdims=True)
            acc = acc * factor + dot_nn(kvt_ref[part, key_tile], probs.astype(bf16))
            return (new_max, new_sum, acc)

        carry = (
            jnp.full((1, geo.tile), NEG_FILL, f32),
            jnp.zeros((1, geo.tile), f32),
            jnp.zeros((2 * HD, geo.tile), f32),
        )
        for part in range(geo.parts):
            carry = chunk(part, tile, carry, True)

        def earlier(key_tile, carry):
            for part in range(geo.parts):
                carry = chunk(part, key_tile, carry, False)
            return carry

        carry = lax.fori_loop(scal_ref[geo.parts + tile], tile, earlier, carry)
        run_max, run_sum, acc = carry
        attended = acc[HD:] / run_sum
        ot_ref[tile] = attended
        lse_ref[tile] = jnp.broadcast_to(run_max + jnp.log(run_sum), (8, geo.tile))
        rows = attended.T
        half = geo.part_rows // 2
        for i in range(geo.per_tile):
            low = rows[2 * i * half : (2 * i + 1) * half]
            high = rows[(2 * i + 1) * half : (2 * i + 2) * half]
            out_ref[tile * geo.per_tile + i] = jnp.concatenate([low, high], axis=1).astype(bf16)


def backward_kernel(
    geo, scal_ref, q_ref, kv_ref, do_ref, bounds_ref, ot_ref, lse_ref, dq_ref, dkv_ref, kvt_ref
):
    base = jnp.broadcast_to(key_base(geo), (geo.tile, geo.tile))
    dkv_ref[...] = jnp.zeros_like(dkv_ref)
    for part in range(geo.parts):
        for tile in range(geo.tiles):
            kvt_ref[part, tile] = kv_ref[part, tile].T
    for tile in range(geo.tiles):
        q = unpack_tile(q_ref, tile, geo) * jnp.asarray(HD**-0.5, bf16)
        do = unpack_tile(do_ref, tile, geo)
        zeros = jnp.zeros_like(q)
        qz = jnp.concatenate([q, zeros], axis=1)
        doz = jnp.concatenate([zeros, do], axis=1)
        delta = jnp.sum(do.astype(f32).T * ot_ref[tile], axis=0, keepdims=True)
        log_total = lse_ref[tile, 0:1]
        start = bounds_ref[tile, 0:1]
        last = bounds_ref[tile, 1:2]
        own = bounds_ref[tile, 2:3]

        def chunk(part, key_tile, acc, diagonal):
            offset = key_tile * geo.span + scal_ref[part]
            keys = kv_ref[part, key_tile]
            scores = dot_nt(keys, qz)
            allowed = (base >= start - offset) & (base <= last - offset)
            if diagonal:
                allowed = allowed | (base == own - offset)
            probs = jnp.where(allowed, jnp.exp(scores - log_total), 0.0)
            grad_probs = dot_nt(keys, doz)
            grad_scores = (probs * (grad_probs - delta)).astype(bf16)
            dkv_ref[part, key_tile] += dot_nn(grad_scores, qz) + dot_nn(probs.astype(bf16), doz)
            return acc + dot_nn(kvt_ref[part, key_tile], grad_scores)

        acc = jnp.zeros((2 * HD, geo.tile), f32)
        for part in range(geo.parts):
            acc = chunk(part, tile, acc, True)

        def earlier(key_tile, acc):
            for part in range(geo.parts):
                acc = chunk(part, key_tile, acc, False)
            return acc

        acc = lax.fori_loop(scal_ref[geo.parts + tile], tile, earlier, acc)
        rows = (acc[:HD] * (HD**-0.5)).T
        half = geo.part_rows // 2
        for i in range(geo.per_tile):
            low = rows[2 * i * half : (2 * i + 1) * half]
            high = rows[(2 * i + 1) * half : (2 * i + 2) * half]
            dq_ref[tile * geo.per_tile + i] = jnp.concatenate([low, high], axis=1).astype(bf16)


def vmem_specs(count):
    return [pl.BlockSpec(memory_space=pltpu.VMEM)] * count


def attention_forward(geo, scalars, q, kv, bounds):
    return pl.pallas_call(
        functools.partial(forward_kernel, geo),
        out_shape=(
            jax.ShapeDtypeStruct(q.shape, bf16),
            jax.ShapeDtypeStruct((geo.tiles, HD, geo.tile), f32),
            jax.ShapeDtypeStruct((geo.tiles, 8, geo.tile), f32),
        ),
        in_specs=[pl.BlockSpec(memory_space=pltpu.SMEM)] + vmem_specs(3),
        out_specs=tuple(vmem_specs(3)),
        scratch_shapes=[pltpu.VMEM((geo.parts, geo.tiles, LANES, geo.tile), bf16)],
        compiler_params=pltpu.CompilerParams(vmem_limit_bytes=48 * 2**20),
        name="attention_forward",
    )(scalars, q, kv, bounds)


def attention_backward(geo, scalars, q, kv, do, bounds, ot, lse):
    return pl.pallas_call(
        functools.partial(backward_kernel, geo),
        out_shape=(
            jax.ShapeDtypeStruct(q.shape, bf16),
            jax.ShapeDtypeStruct(kv.shape, f32),
        ),
        in_specs=[pl.BlockSpec(memory_space=pltpu.SMEM)] + vmem_specs(6),
        out_specs=tuple(vmem_specs(2)),
        scratch_shapes=[pltpu.VMEM((geo.parts, geo.tiles, LANES, geo.tile), bf16)],
        compiler_params=pltpu.CompilerParams(vmem_limit_bytes=48 * 2**20),
        name="attention_backward",
    )(scalars, q, kv, do, bounds, ot, lse)


def gather_head(x):
    return lax.all_gather(x, "head", axis=0, tiled=False)


def exchange(x, axis):
    return lax.all_to_all(x, axis, split_axis=0, concat_axis=0, tiled=True)


def on_device(
    layer_input,
    segments,
    token_valid,
    attention_gain,
    attention_shift,
    project_weight,
    project_bias,
    output_weight,
    output_bias,
    feed_gain,
    feed_shift,
    up_weight,
    up_bias,
    down_weight,
    down_bias,
    cotangent,
):
    heads = lax.axis_size("head")
    blocks = lax.axis_size("blk")
    my_head = lax.axis_index("head")
    my_blk = lax.axis_index("blk")
    devices = heads * blocks
    seqs, _, sub, width = layer_input.shape
    hidden_width = up_weight.shape[1]
    hidden_slice = hidden_width // heads
    rows = sub * heads
    length = rows * blocks
    mine = seqs * sub
    tokens = seqs * rows
    local = H // heads
    cols = local * HD
    parts = blocks // (seqs * local)
    run = sub // parts
    part_rows = heads * run
    half = part_rows // 2
    w_rows = width // devices
    f_rows = hidden_width // devices
    geo = AttentionShape(blocks, part_rows, parts, run, sub)

    wp = project_weight.reshape(w_rows, 3, heads, local, HD)
    wq = wp[:, 0].transpose(1, 0, 2, 3).reshape(heads, w_rows, cols)
    wq = jnp.pad(wq, ((0, 0), (0, 0), (0, LANES - cols)))
    wkv = wp[:, 1:].transpose(2, 3, 0, 1, 4).reshape(heads, local * w_rows, LANES)
    small = [attention_gain, attention_shift, output_bias, feed_gain, feed_shift, down_bias]
    small += [project_bias, up_bias]
    counts = [v.shape[0] for v in small]
    small = jnp.concatenate(small)
    small_rows = -(-small.shape[0] // LANES)
    small = jnp.pad(small, (0, small_rows * LANES - small.shape[0])).reshape(1, small_rows, LANES)
    chunk = jnp.concatenate([wq, wkv, jnp.broadcast_to(small, (heads, small_rows, LANES))], axis=1)
    chunk_rows = chunk.shape[1]
    send = jnp.broadcast_to(chunk[:, None], (heads, blocks, chunk_rows, LANES))
    got = exchange(send.reshape(devices, chunk_rows, LANES), BOTH)
    w_groups = [
        got[:, i * w_rows : (i + 1) * w_rows].reshape(width, LANES) for i in range(1 + local)
    ]
    w_slice = jnp.concatenate(w_groups, axis=1)
    flat = got[:, (1 + local) * w_rows :].reshape(devices, small_rows * LANES).astype(f32)
    vectors = []
    at = 0
    for count in counts:
        vectors.append(flat[:, at : at + count].reshape(-1))
        at += count
    gain_one, shift_one, b_output, gain_two, shift_two, b_down, b_project, b_up = vectors

    x_mine = layer_input.reshape(mine, width)
    g_mine = cotangent.reshape(mine, width)
    x_all = gather_head(x_mine).reshape(heads, seqs, sub, width).transpose(1, 0, 2, 3)
    g_all = gather_head(g_mine).reshape(heads, seqs, sub, width).transpose(1, 0, 2, 3)
    x_all = x_all.reshape(tokens, width).astype(f32)
    g_all = g_all.reshape(tokens, width)

    up_parts = up_weight.reshape(w_rows, heads, hidden_slice).transpose(1, 0, 2)
    out_parts = jnp.broadcast_to(output_weight[None], (heads, w_rows, width))
    if hidden_slice == width:
        both = exchange(jnp.concatenate([up_parts, out_parts], axis=1), "head")
        shard = jnp.concatenate([both.reshape(2 * heads * w_rows, width), down_weight], axis=0)
        full = lax.all_gather(shard, "blk", axis=0, tiled=False)
        pair = full[:, : 2 * heads * w_rows].reshape(blocks, heads, 2, w_rows, width)
        w_up = pair[:, :, 0].transpose(1, 0, 2, 3).reshape(width, hidden_slice)
        w_out = pair[:, :, 1].transpose(1, 0, 2, 3).reshape(width, width)
        w_down = full[:, 2 * heads * w_rows :].reshape(hidden_slice, width)
    else:
        up_parts = lax.all_gather(exchange(up_parts, "head"), "blk", axis=0, tiled=False)
        out_parts = lax.all_gather(exchange(out_parts, "head"), "blk", axis=0, tiled=False)
        w_up = up_parts.transpose(1, 0, 2, 3).reshape(width, hidden_slice)
        w_out = out_parts.transpose(1, 0, 2, 3).reshape(width, width)
        w_down = lax.all_gather(down_weight, "blk", axis=0, tiled=True)

    n_one, u_one, rs_one = norm_forward(x_all, gain_one, shift_one)
    n_one = n_one.astype(bf16)
    qkv = dot_nn(n_one, w_slice)
    b_q = lax.dynamic_slice(b_project, (my_head * cols,), (cols,))
    b_v = lax.dynamic_slice(b_project, (width + my_head * cols,), (cols,))
    queries = (qkv[:, :cols] + b_q).astype(bf16)
    pairs = qkv[:, LANES:].reshape(tokens, local, 2, HD)
    b_pair = jnp.stack([jnp.zeros((local, HD), f32), b_v.reshape(local, HD)], axis=1)
    pairs = (pairs + b_pair).astype(bf16)
    queries = queries.reshape(seqs, heads, parts, run, local, HD).transpose(0, 4, 2, 1, 3, 5)
    queries = queries.reshape(blocks, 2, half, HD).transpose(0, 2, 1, 3).reshape(blocks, half, LANES)
    pairs = pairs.reshape(seqs, heads, parts, run, local, LANES).transpose(0, 4, 2, 1, 3, 5)
    pairs = pairs.reshape(blocks, part_rows, LANES)
    got = exchange(jnp.concatenate([queries, pairs], axis=1), "blk")
    q_task = got[:, :half]
    kv_parts = [got[:, half:]]
    for step in range(1, parts):
        around = [
            (t * parts + i, t * parts + (i + step) % parts)
            for t in range(blocks // parts)
            for i in range(parts)
        ]
        kv_parts.append(lax.ppermute(kv_parts[0], "blk", around))
    kv_task = jnp.stack(kv_parts).reshape(parts, geo.tiles, geo.tile, LANES)

    my_part = my_blk % parts
    my_seq = (my_blk // parts) // local
    seg = lax.dynamic_index_in_dim(segments, my_seq, 0, keepdims=False)
    valid = jnp.sum(lax.dynamic_index_in_dim(token_valid, my_seq, 0, keepdims=False))
    index = jnp.arange(blocks * part_rows, dtype=i32)
    own = (index // run) * sub + my_part * run + index % run
    own_seg = lax.dynamic_index_in_dim(seg.reshape(length // sub, parts, run), my_part, 1, False)
    start = jnp.sum((seg[None, :] < own_seg.reshape(-1)[:, None]).astype(i32), axis=1)
    last = jnp.minimum(own, valid - 1)
    bounds = jnp.stack([start, last, own]).reshape(3, geo.tiles, geo.tile).transpose(1, 0, 2)
    bounds = jnp.pad(bounds, ((0, 0), (0, 5), (0, 0)))
    first_seg = seg.reshape(geo.tiles, geo.span)[:, :1]
    first_tile = jnp.sum((seg[None, :] < first_seg).astype(i32), axis=1) // geo.span
    part_at = ((my_part - jnp.arange(parts, dtype=i32)) % parts) * run
    scalars = jnp.concatenate([part_at, first_tile])

    o_task, ot, lse = attention_forward(geo, scalars, q_task, kv_task, bounds)

    got = exchange(o_task, "blk")
    mixed = got.reshape(seqs, local, parts, half, 2, HD).transpose(0, 1, 2, 4, 3, 5)
    mixed = mixed.reshape(seqs, local, parts, heads, run, HD).transpose(0, 3, 2, 4, 1, 5)
    mixed = mixed.reshape(tokens, cols)
    mixed_all = lax.all_gather(mixed, "head", axis=1, tiled=True)

    middle = x_all + dot_nn(mixed_all, w_out) + b_output
    n_two, u_two, rs_two = norm_forward(middle, gain_two, shift_two)
    n_two = n_two.astype(bf16)
    b_up_slice = lax.dynamic_slice(b_up, (my_head * hidden_slice,), (hidden_slice,))
    hidden = dot_nn(n_two, w_up) + b_up_slice
    sigma = jax.nn.sigmoid(1.702 * hidden)
    activated = (hidden * sigma).astype(bf16)
    feed = dot_nn(activated, w_down)
    grad_act = dot_nt(g_all, w_down)
    grad_hidden = (grad_act * (sigma + 1.702 * hidden * sigma * (1.0 - sigma))).astype(bf16)
    grad_two = dot_nt(grad_hidden, w_up)

    def to_owners(partial):
        partial = partial.astype(bf16).reshape(seqs, heads, sub, width).transpose(1, 0, 2, 3)
        return exchange(partial.reshape(heads, mine, width), "head")

    def my_tokens(values):
        values = values.reshape(seqs, heads, sub, values.shape[-1])
        values = lax.dynamic_index_in_dim(values, my_head, 1, keepdims=False)
        return values.reshape(mine, values.shape[-1])

    grad_two_mine = jnp.sum(to_owners(grad_two).astype(f32), axis=0)
    grad_middle = g_mine.astype(f32) + norm_input_grad(
        grad_two_mine, my_tokens(u_two), my_tokens(rs_two), gain_two
    )
    grad_branch = grad_middle.astype(bf16)
    grad_mixed = dot_nt(grad_branch, w_out).astype(bf16)
    grad_mixed = grad_mixed.reshape(seqs, parts, run, heads, local, HD).transpose(3, 0, 4, 1, 2, 5)
    grad_mixed = grad_mixed.reshape(heads, blocks, run // 2 * LANES // HD // 2 * 2, HD)
    grad_mixed = grad_mixed.reshape(devices, run * HD // LANES, LANES)
    got = exchange(grad_mixed, BOTH)
    do_task = got.reshape(heads, blocks, run, HD).transpose(1, 0, 2, 3)
    do_task = do_task.reshape(blocks, 2, half, HD).transpose(0, 2, 1, 3)
    do_task = do_task.reshape(blocks, half, LANES)

    feed_mine = jnp.sum(to_owners(feed).astype(f32), axis=0)
    layer_output = my_tokens(middle) + feed_mine + b_down

    grad_down = dot_tn(activated, g_all).astype(bf16).reshape(blocks, -1, width)
    grad_up = dot_tn(n_two, grad_hidden).astype(bf16)
    grad_up = grad_up.reshape(heads, blocks, w_rows, hidden_slice).transpose(1, 0, 2, 3)
    branch_all = gather_head(grad_branch).reshape(heads, seqs, sub, width).transpose(1, 0, 2, 3)
    grad_out = dot_tn(mixed, branch_all.reshape(tokens, width)).astype(bf16)

    def over_blocks(partial):
        return lax.psum_scatter(partial, "blk", scatter_dimension=0, tiled=True)

    if hidden_slice == width:
        summed = over_blocks(
            jnp.concatenate(
                [grad_down.reshape(blocks, f_rows, width), grad_up.reshape(blocks, -1, width)],
                axis=1,
            ).reshape(-1, width)
        )
        own_down = summed[:f_rows]
        own_up = summed[f_rows:]
    else:
        own_down = over_blocks(grad_down.reshape(-1, width))
        own_up = over_blocks(grad_up.reshape(-1, hidden_slice))
    own_out = over_blocks(grad_out)
    own_up = exchange(own_up.reshape(heads, w_rows, hidden_slice), "head")
    own_up = own_up.transpose(1, 0, 2).reshape(w_rows, hidden_width)

    dq_task, dkv_task = attention_backward(geo, scalars, q_task, kv_task, do_task, bounds, ot, lse)
    dkv_task = dkv_task.reshape(parts, blocks, part_rows, LANES)
    dkv = dkv_task[0]
    for step in range(1, parts):
        around = [
            (t * parts + i, t * parts + (i - step) % parts)
            for t in range(blocks // parts)
            for i in range(parts)
        ]
        dkv = dkv + lax.ppermute(dkv_task[step].astype(bf16), "blk", around).astype(f32)
    dkv = dkv * 1.0
    got = exchange(jnp.concatenate([dq_task, dkv.astype(bf16)], axis=1), "blk")
    dq = got[:, :half].reshape(blocks, half, 2, HD).transpose(0, 2, 1, 3)
    dq = dq.reshape(seqs, local, parts, heads, run, HD).transpose(0, 3, 2, 4, 1, 5)
    dq = dq.reshape(tokens, cols)
    dkv = got[:, half:].reshape(seqs, local, parts, heads, run, LANES).transpose(0, 3, 2, 4, 1, 5)
    dkv = dkv.reshape(tokens, local * LANES)
    dq = jnp.pad(dq, ((0, 0), (0, LANES - cols)))
    d_proj = jnp.concatenate([dq, dkv], axis=1)

    grad_one = dot_nt(d_proj, w_slice)
    grad_one_mine = jnp.sum(to_owners(grad_one).astype(f32), axis=0)
    x_f32 = x_mine.astype(f32)
    input_grad = grad_middle + norm_input_grad(
        grad_one_mine, my_tokens(u_one), my_tokens(rs_one), gain_one
    )

    grad_w = dot_tn(n_one, d_proj).astype(bf16)
    col_sums = jnp.sum(d_proj.astype(f32), axis=0)
    bias_q = col_sums[:cols]
    bias_v = col_sums[LANES:].reshape(local, 2, HD)[:, 1].reshape(cols)
    bias_grad = jnp.zeros((2 * width,), f32)
    bias_grad = lax.dynamic_update_slice(bias_grad, bias_q, (my_head * cols,))
    bias_grad = lax.dynamic_update_slice(bias_grad, bias_v, (width + my_head * cols,))
    up_bias_grad = lax.dynamic_update_slice(
        jnp.zeros((hidden_width,), f32),
        jnp.sum(grad_hidden.astype(f32), axis=0),
        (my_head * hidden_slice,),
    )
    tiny = [
        jnp.sum(grad_one * u_one, axis=0),
        jnp.sum(grad_one, axis=0),
        jnp.sum(grad_branch.astype(f32), axis=0),
        jnp.sum(grad_two * u_two, axis=0),
        jnp.sum(grad_two, axis=0),
        jnp.sum(g_mine.astype(f32), axis=0),
        bias_grad,
        up_bias_grad,
    ]
    tiny = jnp.concatenate([v.reshape(devices, -1) for v in tiny], axis=1)
    high = tiny.astype(bf16)
    low = (tiny - high.astype(f32)).astype(bf16)
    tiny = jnp.concatenate([high, low], axis=1)
    tiny_rows = -(-tiny.shape[1] // LANES)
    tiny = jnp.pad(tiny, ((0, 0), (0, tiny_rows * LANES - tiny.shape[1])))
    tiny = tiny.reshape(devices, tiny_rows, LANES)
    grad_w = [
        grad_w[:, i * LANES : (i + 1) * LANES].reshape(devices, w_rows, LANES)
        for i in range(1 + local)
    ]
    got = exchange(jnp.concatenate(grad_w + [tiny], axis=1), BOTH)
    got = got.astype(f32)
    n_w = (1 + local) * w_rows
    own_w = jnp.sum(got[:, :n_w].reshape(heads, blocks, n_w, LANES), axis=1)
    own_q = own_w[:, :w_rows, :cols].transpose(1, 0, 2).reshape(w_rows, width)
    own_kv = own_w[:, w_rows:].reshape(heads, local, w_rows, 2, HD)
    own_kv = own_kv.transpose(2, 3, 0, 1, 4).reshape(w_rows, 2 * width)
    own_w = jnp.concatenate([own_q, own_kv], axis=1)
    summed = jnp.sum(got[:, n_w:].reshape(devices, -1), axis=0)
    total = sum(counts)
    summed = summed[:total] + summed[total : 2 * total]
    owned = []
    at = 0
    for count in counts:
        owned.append(summed[at : at + count])
        at += count

    return (
        layer_output.astype(bf16).reshape(layer_input.shape),
        input_grad.astype(bf16).reshape(layer_input.shape),
        owned[0],
        owned[1],
        own_w,
        owned[6],
        own_out.astype(f32),
        owned[2],
        owned[3],
        owned[4],
        own_up.astype(f32),
        owned[7],
        own_down.astype(f32),
        owned[5],
    )


def solution(mesh):
    tokens = P(None, "blk", "head", None)
    vector = P(BOTH)
    matrix = P(BOTH, None)
    return jax.shard_map(
        on_device,
        mesh=mesh,
        in_specs=(
            tokens,
            P(),
            P(),
            vector,
            vector,
            matrix,
            vector,
            matrix,
            vector,
            vector,
            vector,
            matrix,
            vector,
            matrix,
            vector,
            tokens,
        ),
        out_specs=(
            tokens,
            tokens,
            vector,
            vector,
            matrix,
            vector,
            matrix,
            vector,
            vector,
            vector,
            matrix,
            vector,
            matrix,
            vector,
        ),
        check_vma=False,
    )
```

time: 816 us -> 272 us (0.33)
  waiting for transfers between devices: 410 us -> 77.5 us
  starting transfers between devices: 147 us -> 44.4 us
  blocking collectives: 126 us -> 41.8 us
  matrix products: 28.5 us -> 11 us
  Pallas kernels: 0 us -> 16.8 us
  loops' own time: 12.1 us -> 0 us
    reduce_scatter x4 -> x2, waiting for transfers between devices: 332 us -> 33.3 us  [over_blocks(): return lax.psum_scatter(partial, 'blk', scatter_dimension=0, tiled=True)]
    ppermute x46 -> x2, starting transfers between devices: 120 us -> 0.56 us  [the longest x1 0.38 us: on_device(): lax.ppermute(dkv_task[step].astype(bf16), 'blk', around).astype(f32)]
    unnamed x2 -> x0, blocking collectives: 81.9 us -> none
    ppermute x46 -> x2, waiting for transfers between devices: 41.7 us -> 1.91 us  [the longest x1 1.29 us: on_device(): kv_parts.append(lax.ppermute(kv_parts[0], 'blk', around))]
    while x30 -> x0, local copies, waits for them, and re-layouts: 19.7 us -> none
    dot_general x19 -> x12, matrix products: 28.5 us -> 11 us  [the longest x4 4.21 us: dot_nt(): lax.dot_general(a, b, (((1,), (1,)), ((), ())), preferred_element_type=f32)]
    all_to_all x8 -> x11, starting transfers between devices: 26.6 us -> 43.7 us  [exchange(): return lax.all_to_all(x, axis, split_axis=0, concat_axis=0, tiled=True)]
    pallas_call x0 -> x2, Pallas kernels: none -> 16.8 us  [the longest x1 9.05 us: attention_forward(): pl.pallas_call(functools.partial(forward_kernel, geo), out_shape=(jax.Sha...]
  transfers between devices with their start and end apart: 61 -> 16, of which waited for: 26 -> 10; matrix products, arithmetic and copies ran while one was open for 11% -> 16% of each run, Pallas kernels for 0% -> 3%
where the time goes in v1:
time: 272 us
  waiting for transfers between devices  77.5 us (28%)
  starting transfers between devices  44.4 us (16%)
  local copies, waits for them, and re-layouts  43.3 us (16%)
  blocking collectives  41.8 us (15%)
  other arithmetic  21 us (8%)
  Pallas kernels  16.8 us (6%)
  between operations  15.7 us (6%)
  matrix products  11 us (4%)
    all_to_all x11, starting transfers between devices, exchange(): return lax.all_to_all(x, axis, split_axis=0, concat_axis=0, tiled=True)  43.7 us
    all_to_all x11, waiting for transfers between devices, exchange(): return lax.all_to_all(x, axis, split_axis=0, concat_axis=0, tiled=True)  42.2 us
    reduce_scatter x2, waiting for transfers between devices, over_blocks(): return lax.psum_scatter(partial, 'blk', scatter_dimension=0, tiled=True)  33.3 us
    all_gather x3, blocking collectives, gather_head(): return lax.all_gather(x, 'head', axis=0, tiled=False)  30.9 us
    all_gather x1, blocking collectives, on_device(): mixed_all = lax.all_gather(mixed, 'head', axis=1, tiled=True)  10.9 us
    pallas_call x1, Pallas kernels, attention_forward(): pl.pallas_call(functools.partial(forward_kernel, geo), out_shape=(jax.Sha...  9.05 us
    pallas_call x1, Pallas kernels, attention_backward(): pl.pallas_call(functools.partial(backward_kernel, geo), out_shape=(jax.Sh...  7.77 us
  transfers between devices with their start and end apart: 16, of which 10 were waited for; matrix products, arithmetic and copies ran while one was open for 16% of the time, Pallas kernels for 3%

profile of v1, /device:TPU:0, one launch (start us, length us, event | category | flops | bytes accessed | tf_op | source)
XLA Modules:
  0.0 271.5 jit_solution(13617430525331861100)
XLA Ops:
  7.2 0.9 reshape.843
  9.6 5.2 %all-to-all-start.3 = ((bf16[4,32,512]{2,1,0:T(8,128)(2,1)}), bf16[4,32,512]{2,1,0:T(8,128)(2,1)S(1)}, u32[]{:S(2)}, u32[]{:S(2)}) async-start(bf16[4,32,512]{2,1,0:T(8,128)(2,1)} %copy.135), calls=%async_computation.3 | async-start | bytes 262144 | tf_op jit(solution)/shard_map/all_to_all | solution.py:220
  14.8 0.9 reshape.826
  15.8 5.4 %concatenate.45 = bf16[192]{0:T(256)(128)(2,1)S(1)} concatenate(bf16[16]{0:T(256)(128)(2,1)} %param.19, bf16[16]{0:T(256)(128)(2,1)} %param.20, bf16[16]{0:T(256)(128)(2,1)} %param.24, bf16[16]{0:T(256)(128)(2,1)} %param.25, bf16[16]{0:T(256)(128)(2,1)} %param.26, bf16[16]{0:T(256)(128)(2,1)} %param.30, bf16[32]{0:T(256)(128)(2,1)} %param.22, bf16[64]{0:T(256)(128)(2,1)} %param.28), dimensions={0} | concatenate | bytes 768 | tf_op jit(solution)/shard_map/concatenate | solution.py:270
  21.5 10.6 %all_gather.19 = bf16[4,128,512]{2,1,0:T(8,128)(2,1)S(1)} all-gather(bf16[1,128,512]{2,1,0:T(8,128)(2,1)S(1)} %bitcast.280), channel_id=1, replica_groups=mesh['head'=4,'blk'=8] {'head'}, dimensions={0}, use_global_device_ids=true | all-gather | bytes 655360 | tf_op jit(solution)/shard_map/all_gather | solution.py:216
  32.6 0.9 broadcast_in_dim.14
  33.5 5.3 %all-to-all-start = ((bf16[32,50,128]{2,1,0:T(8,128)(2,1)}), bf16[32,50,128]{2,1,0:T(8,128)(2,1)S(1)}, u32[]{:S(2)}, u32[]{:S(2)}) async-start(bf16[32,50,128]{2,1,0:T(8,128)(2,1)} %bitcast.10), calls=%async_computation | async-start | bytes 917504 | tf_op jit(solution)/shard_map/all_to_all | solution.py:220
  39.4 1.3 fusion.29
  40.7 1.3 fusion.4
  42.9 10.9 %all-to-all-done = bf16[32,50,128]{2,1,0:T(8,128)(2,1)S(1)} async-done(((bf16[32,50,128]{2,1,0:T(8,128)(2,1)}), bf16[32,50,128]{2,1,0:T(8,128)(2,1)S(1)}, u32[]{:S(2)}, u32[]{:S(2)}) %all-to-all-start) | async-done | bytes 409632 | tf_op jit(solution)/shard_map/all_to_all | solution.py:220
  57.8 3.5 %all-to-all-start.1 = ((bf16[8,192,128]{2,1,0:T(8,128)(2,1)}), bf16[8,192,128]{2,1,0:T(8,128)(2,1)S(1)}, u32[]{:S(2)}, u32[]{:S(2)}) async-start(bf16[8,192,128]{2,1,0:T(8,128)(2,1)} %pad_maximum_fusion.4), calls=%async_computation.1 | async-start | bytes 786432 | tf_op jit(solution)/shard_map/all_to_all | solution.py:220
  62.5 1.0 convert_reduce_fusion
  63.5 13.2 %all-to-all-done.1 = bf16[8,192,128]{2,1,0:T(8,128)(2,1)S(1)} async-done(((bf16[8,192,128]{2,1,0:T(8,128)(2,1)}), bf16[8,192,128]{2,1,0:T(8,128)(2,1)S(1)}, u32[]{:S(2)}, u32[]{:S(2)}) %all-to-all-start.1) | async-done | bytes 393248 | tf_op jit(solution)/shard_map/all_to_all | solution.py:220
  77.0 1.3 collective-permute-done
  78.4 9.1 %attention_forward.1 = (bf16[8,64,128]{2,1,0:T(8,128)(2,1)}, f32[4,64,256]{2,1,0:T(8,128)S(1)}, f32[4,8,256]{2,1,0:T(8,128)S(1)}) custom-call(s32[6]{0:T(128)S(1)} %pad_add_fusion.scal_ref, bf16[8,64,128]{2,1,0:T(8,128)(2,1)S(1)} %slice.219.q_ref, bf16[2,4,256,128]{3,2,1,0:T(8,128)(2,1)S(1)} %pad_maximum_fusion.1.kv_ref, s32[4,8,256]{2,1,0:T(8,128)S(1)} %pad.10.bounds_ref), custom_call_target="tpu_custom_call" | custom-call | tf_op jit(solution)/shard_map/attention_forward/pallas_call | solution.py:185
  87.4 3.4 %all-to-all-start.2 = ((bf16[8,64,128]{2,1,0:T(8,128)(2,1)}), bf16[8,64,128]{2,1,0:T(8,128)(2,1)S(1)}, u32[]{:S(2)}, u32[]{:S(2)}) async-start(bf16[8,64,128]{2,1,0:T(8,128)(2,1)} %get-tuple-element.19), calls=%async_computation.2 | async-start | bytes 262144 | tf_op jit(solution)/shard_map/all_to_all | solution.py:220
  90.8 10.4 %all_gather.23 = bf16[4,128,512]{2,1,0:T(8,128)(2,1)S(1)} all-gather(bf16[1,128,512]{2,1,0:T(8,128)(2,1)S(1)} %bitcast.245), channel_id=1, replica_groups=mesh['head'=4,'blk'=8] {'head'}, dimensions={0}, use_global_device_ids=true | all-gather | bytes 655360 | tf_op jit(solution)/shard_map/all_gather | solution.py:216
  101.2 0.8 copy.140
  103.1 10.9 %all_gather.20 = bf16[512,512]{1,0:T(8,128)(2,1)} all-gather(bf16[512,128]{1,0:T(8,128)(2,1)S(1)} %reshape.842), channel_id=1, replica_groups=mesh['head'=4,'blk'=8] {'head'}, dimensions={1}, use_global_device_ids=true | all-gather | bytes 655360 | tf_op jit(solution)/shard_map/all_gather | solution.py:360
  114.0 1.1 slice.228
  115.1 1.5 slice.221
  116.9 1.0 copy-done.7
  121.2 0.9 copy.141
  122.1 4.2 %all-to-all-start.5 = ((bf16[4,128,512]{2,1,0:T(8,128)(2,1)}), bf16[4,128,512]{2,1,0:T(8,128)(2,1)}, u32[]{:S(2)}, u32[]{:S(2)}) async-start(bf16[4,128,512]{2,1,0:T(8,128)(2,1)} %bitcast.241), calls=%async_computation.5 | async-start | bytes 1048576 | tf_op jit(solution)/shard_map/all_to_all | solution.py:220
  128.1 1.3 fusion.27
  129.4 3.5 %all-to-all-done.5 = bf16[4,128,512]{2,1,0:T(8,128)(2,1)} async-done(((bf16[4,128,512]{2,1,0:T(8,128)(2,1)}), bf16[4,128,512]{2,1,0:T(8,128)(2,1)}, u32[]{:S(2)}, u32[]{:S(2)}) %all-to-all-start.5) | async-done | bytes 524320 | tf_op jit(solution)/shard_map/all_to_all | solution.py:220
  132.9 1.1 convert_reduce_fusion.3
  135.0 1.7 convert_reduce_fusion.7
  136.7 1.3 convolution_convert_fusion.5
  138.0 0.9 reshape.858
  138.9 1.7 copy.173
  140.6 1.8 reshape_reshape.3
  142.4 5.2 %all-to-all-start.6 = ((bf16[32,16,128]{2,1,0:T(8,128)(2,1)}), bf16[32,16,128]{2,1,0:T(8,128)(2,1)S(1)}, u32[]{:S(2)}, u32[]{:S(2)}) async-start(bf16[32,16,128]{2,1,0:T(8,128)(2,1)} %reshape_reshape.3), calls=%async_computation.6 | async-start | bytes 262144 | tf_op jit(solution)/shard_map/all_to_all | solution.py:220
  147.7 1.8 convolution_convert_fusion.2
  149.5 0.8 copy.138
  150.8 1.3 mul.287
  152.0 3.8 %all-to-all-done.6 = bf16[32,16,128]{2,1,0:T(8,128)(2,1)S(1)} async-done(((bf16[32,16,128]{2,1,0:T(8,128)(2,1)}), bf16[32,16,128]{2,1,0:T(8,128)(2,1)S(1)}, u32[]{:S(2)}, u32[]{:S(2)}) %all-to-all-start.6) | async-done | bytes 131104 | tf_op jit(solution)/shard_map/all_to_all | solution.py:220
  155.8 0.9 reshape.859
  156.7 1.0 copy.144
  157.7 1.0 copy.145
  158.6 1.1 reshape.861.do_ref
  159.8 7.8 %attention_backward.1 = (bf16[8,64,128]{2,1,0:T(8,128)(2,1)S(1)}, f32[2,4,256,128]{3,2,1,0:T(8,128)S(1)}) custom-call(s32[6]{0:T(128)S(1)} %pad_add_fusion.scal_ref, bf16[8,64,128]{2,1,0:T(8,128)(2,1)S(1)} %slice.219.q_ref, bf16[2,4,256,128]{3,2,1,0:T(8,128)(2,1)S(1)} %pad_maximum_fusion.1.kv_ref, bf16[8,64,128]{2,1,0:T(8,128)(2,1)S(1)} %reshape.861.do_ref, ...), custom_call_target="tpu_custom_call" | custom-call | tf_op jit(solution)/shard_map/attention_backward/pallas_call | solution.py:201
  169.3 0.8 pad_maximum_fusion.5
  170.1 3.5 %all-to-all-start.7 = ((bf16[8,192,128]{2,1,0:T(8,128)(2,1)}), bf16[8,192,128]{2,1,0:T(8,128)(2,1)S(1)}, u32[]{:S(2)}, u32[]{:S(2)}) async-start(bf16[8,192,128]{2,1,0:T(8,128)(2,1)} %pad_maximum_fusion.5), calls=%async_computation.7 | async-start | bytes 786432 | tf_op jit(solution)/shard_map/all_to_all | solution.py:220
  173.6 1.7 convolution_convert_fusion.1
  175.4 1.1 pad_maximum_fusion
  176.8 9.9 %all_gather.24 = bf16[4,128,512]{2,1,0:T(8,128)(2,1)S(1)} all-gather(bf16[1,128,512]{2,1,0:T(8,128)(2,1)S(1)} %fusion.15), channel_id=1, replica_groups=mesh['head'=4,'blk'=8] {'head'}, dimensions={0}, use_global_device_ids=true | all-gather | bytes 655360 | tf_op jit(solution)/shard_map/all_gather | solution.py:216
  186.8 0.9 copy.152
  189.7 1.7 fusion.26
  191.5 0.9 copy.149
  192.4 3.5 %all-to-all-start.8 = ((bf16[4,128,512]{2,1,0:T(8,128)(2,1)}), bf16[4,128,512]{2,1,0:T(8,128)(2,1)S(1)}, u32[]{:S(2)}, u32[]{:S(2)}) async-start(bf16[4,128,512]{2,1,0:T(8,128)(2,1)} %bitcast.69), calls=%async_computation.8 | async-start | bytes 1048576 | tf_op jit(solution)/shard_map/all_to_all | solution.py:220
  197.9 5.4 %all-to-all-done.8 = bf16[4,128,512]{2,1,0:T(8,128)(2,1)S(1)} async-done(((bf16[4,128,512]{2,1,0:T(8,128)(2,1)}), bf16[4,128,512]{2,1,0:T(8,128)(2,1)S(1)}, u32[]{:S(2)}, u32[]{:S(2)}) %all-to-all-start.8) | async-done | bytes 524320 | tf_op jit(solution)/shard_map/all_to_all | solution.py:220
  203.3 3.5 %all-to-all-start.4 = ((bf16[4,128,512]{2,1,0:T(8,128)(2,1)}), bf16[4,128,512]{2,1,0:T(8,128)(2,1)S(1)}, u32[]{:S(2)}, u32[]{:S(2)}) async-start(bf16[4,128,512]{2,1,0:T(8,128)(2,1)} %bitcast.40), calls=%async_computation.4 | async-start | bytes 1048576 | tf_op jit(solution)/shard_map/all_to_all | solution.py:220
  207.1 1.1 multiply_reduce_fusion.4
  208.2 1.8 convert_reduce_fusion.6
  210.4 1.6 slice_convert_fusion.1
  212.0 1.5 all-to-all-done.4
  213.4 3.3 %all-to-all-start.10 = ((bf16[4,16,512]{2,1,0:T(8,128)(2,1)}), bf16[4,16,512]{2,1,0:T(8,128)(2,1)S(1)}, u32[]{:S(2)}, u32[]{:S(2)}) async-start(bf16[4,16,512]{2,1,0:T(8,128)(2,1)} %bitcast.89), calls=%async_computation.12 | async-start | bytes 131072 | tf_op jit(solution)/shard_map/all_to_all | solution.py:220
  216.7 0.8 pad_maximum_fusion.2
  217.6 4.0 %all-to-all-done.10 = bf16[4,16,512]{2,1,0:T(8,128)(2,1)S(1)} async-done(((bf16[4,16,512]{2,1,0:T(8,128)(2,1)}), bf16[4,16,512]{2,1,0:T(8,128)(2,1)S(1)}, u32[]{:S(2)}, u32[]{:S(2)}) %all-to-all-start.10) | async-done | bytes 65568 | tf_op jit(solution)/shard_map/all_to_all | solution.py:220
  221.5 3.4 %all-to-all-start.9 = ((bf16[32,51,128]{2,1,0:T(8,128)(2,1)}), bf16[32,51,128]{2,1,0:T(8,128)(2,1)S(1)}, u32[]{:S(2)}, u32[]{:S(2)}) async-start(bf16[32,51,128]{2,1,0:T(8,128)(2,1)} %pad_maximum_fusion.2), calls=%async_computation.9 | async-start | bytes 917504 | tf_op jit(solution)/shard_map/all_to_all | solution.py:220
  225.0 0.9 convolution_convert_fusion.4
  226.7 33.3 %reduce-scatter.3.cloned.1.call-done = bf16[16,512]{1,0:T(8,128)(2,1)} async-done(((bf16[128,512]{1,0:T(8,128)(2,1)}), bf16[16,512]{1,0:T(8,128)(2,1)}) %reduce-scatter.3.cloned.1.call-update) | async-done | bytes 16400 | tf_op jit(solution)/shard_map/reduce_scatter | solution.py:407
  260.0 1.3 convert_element_type.214
  (257 shorter events, 27.4 us)
Async XLA Ops:
  7.2 14.4 %copy-start.23 = (bf16[2,1,64,512]{3,2,1,0:T(8,128)(2,1)S(1)}, bf16[2,1,64,512]{3,2,1,0:T(8,128)(2,1)}, u32[]{:S(2)}) copy-start(bf16[2,1,64,512]{3,2,1,0:T(8,128)(2,1)} %param.16) | copy-start | bytes 393220
  9.6 23.0 %all-to-all-start.3 = ((bf16[4,32,512]{2,1,0:T(8,128)(2,1)}), bf16[4,32,512]{2,1,0:T(8,128)(2,1)S(1)}, u32[]{:S(2)}, u32[]{:S(2)}) async-start(bf16[4,32,512]{2,1,0:T(8,128)(2,1)} %copy.135), calls=%async_computation.3 | async-start | bytes 262144 | tf_op jit(solution)/shard_map/all_to_all | solution.py:220
  32.2 7.2 %copy-start.36 = (s32[2,2048]{1,0:T(2,128)S(1)}, s32[2,2048]{1,0:T(2,128)}, u32[]{:S(2)}) copy-start(s32[2,2048]{1,0:T(2,128)} %param.17) | copy-start | bytes 49156
  32.2 7.2 %copy-start.37 = (s32[2,2048]{1,0:T(2,128)S(1)}, s32[2,2048]{1,0:T(2,128)}, u32[]{:S(2)}) copy-start(s32[2,2048]{1,0:T(2,128)} %param.18) | copy-start | bytes 49156
  32.4 84.5 %copy-start = (f32[2,4,64,512]{3,2,1,0:T(8,128)}, f32[2,4,64,512]{3,2,1,0:T(8,128)S(1)}, u32[]{:S(2)}) copy-start(f32[2,4,64,512]{3,2,1,0:T(8,128)S(1)} %copy.124) | copy-start | bytes 3145732
  33.5 8.7 %copy-start.27 = (bf16[64,512]{1,0:T(8,128)(2,1)S(1)}, bf16[64,512]{1,0:T(8,128)(2,1)}, u32[]{:S(2)}) copy-start(bf16[64,512]{1,0:T(8,128)(2,1)} %param.29) | copy-start | bytes 196612
  33.5 20.3 %all-to-all-start = ((bf16[32,50,128]{2,1,0:T(8,128)(2,1)}), bf16[32,50,128]{2,1,0:T(8,128)(2,1)S(1)}, u32[]{:S(2)}, u32[]{:S(2)}) async-start(bf16[32,50,128]{2,1,0:T(8,128)(2,1)} %bitcast.10), calls=%async_computation | async-start | bytes 917504 | tf_op jit(solution)/shard_map/all_to_all | solution.py:220
  38.8 75.2 %all-gather.3.cloned.1.call-start = ((), (), s32[]{:S(2)}) async-start(), calls=%async_computation.15 | async-start | bytes 1769472 | tf_op jit(solution)/shard_map/all_gather | solution.py:301
  42.1 12.4 %copy-start.30 = (f32[512]{0:T(512)}, f32[512]{0:T(512)S(1)}, u32[]{:S(2)}) copy-start(f32[512]{0:T(512)S(1)} %rsqrt.39) | copy-start | bytes 6148
  42.1 12.3 %copy-start.32 = (f32[512]{0:T(512)}, f32[512]{0:T(512)S(1)}, u32[]{:S(2)}) copy-start(f32[512]{0:T(512)S(1)} %div.85) | copy-start | bytes 6148
  54.4 1.3 copy-start.16
  54.4 0.8 copy-start.24
  54.5 1.2 copy-start.25
  54.5 1.2 copy-start.26
  57.8 18.9 %all-to-all-start.1 = ((bf16[8,192,128]{2,1,0:T(8,128)(2,1)}), bf16[8,192,128]{2,1,0:T(8,128)(2,1)S(1)}, u32[]{:S(2)}, u32[]{:S(2)}) async-start(bf16[8,192,128]{2,1,0:T(8,128)(2,1)} %pad_maximum_fusion.4), calls=%async_computation.1 | async-start | bytes 786432 | tf_op jit(solution)/shard_map/all_to_all | solution.py:220
  61.3 29.5 %copy-start.8 = (bf16[2,1,64,512]{3,2,1,0:T(8,128)(2,1)S(1)}, bf16[2,1,64,512]{3,2,1,0:T(8,128)(2,1)}, u32[]{:S(2)}) copy-start(bf16[2,1,64,512]{3,2,1,0:T(8,128)(2,1)} %param.31) | copy-start | bytes 393220
  76.7 1.6 collective-permute-start
  87.4 15.0 %all-to-all-start.2 = ((bf16[8,64,128]{2,1,0:T(8,128)(2,1)}), bf16[8,64,128]{2,1,0:T(8,128)(2,1)S(1)}, u32[]{:S(2)}, u32[]{:S(2)}) async-start(bf16[8,64,128]{2,1,0:T(8,128)(2,1)} %get-tuple-element.19), calls=%async_computation.2 | async-start | bytes 262144 | tf_op jit(solution)/shard_map/all_to_all | solution.py:220
  103.1 13.6 %copy-start.11 = (bf16[512,128]{1,0:T(8,128)(2,1)}, bf16[512,128]{1,0:T(8,128)(2,1)S(1)}, u32[]{:S(2)}) copy-start(bf16[512,128]{1,0:T(8,128)(2,1)S(1)} %reshape.842) | copy-start | bytes 393220
  115.1 4.3 %copy-start.20 = (bf16[8,64,512]{2,1,0:T(8,128)(2,1)}, bf16[8,64,512]{2,1,0:T(8,128)(2,1)S(1)}, u32[]{:S(2)}) copy-start(bf16[8,64,512]{2,1,0:T(8,128)(2,1)S(1)} %slice.228) | copy-start | bytes 1572868
  116.8 1.2 copy-start.7
  116.9 3.8 %copy-start.2 = (bf16[4,8,16,512]{3,2,1,0:T(8,128)(2,1)}, bf16[4,8,16,512]{3,2,1,0:T(8,128)(2,1)S(1)}, u32[]{:S(2)}) copy-start(bf16[4,8,16,512]{3,2,1,0:T(8,128)(2,1)S(1)} %copy.136) | copy-start | bytes 1572868
  118.9 1.0 copy-start.18
  119.4 1.3 copy-start.13
  120.7 1.4 copy-start.5
  122.1 10.8 %all-to-all-start.5 = ((bf16[4,128,512]{2,1,0:T(8,128)(2,1)}), bf16[4,128,512]{2,1,0:T(8,128)(2,1)}, u32[]{:S(2)}, u32[]{:S(2)}) async-start(bf16[4,128,512]{2,1,0:T(8,128)(2,1)} %bitcast.241), calls=%async_computation.5 | async-start | bytes 1048576 | tf_op jit(solution)/shard_map/all_to_all | solution.py:220
  129.4 8.7 %copy-start.28 = (f32[2,1,64,1]{2,1,0,3:T(1,128)}, f32[2,1,64,1]{2,1,0,3:T(1,128)S(1)}, u32[]{:S(2)}) copy-start(f32[2,1,64,1]{2,1,0,3:T(1,128)S(1)} %get-tuple-element.85) | copy-start | bytes 1540
  134.9 7.5 %copy-start.41 = (f32[128]{0:T(128)}, f32[128]{0:T(128)S(1)}, u32[]{:S(2)}) copy-start(f32[128]{0:T(128)S(1)} %broadcast_multiply_fusion.5) | copy-start | bytes 1540
  135.0 7.4 %copy-start.38 = (f32[2,64]{1,0:T(2,128)}, f32[2,64]{1,0:T(2,128)S(1)}, u32[]{:S(2)}) copy-start(f32[2,64]{1,0:T(2,128)S(1)} %div.95) | copy-start | bytes 1540
  142.4 13.4 %all-to-all-start.6 = ((bf16[32,16,128]{2,1,0:T(8,128)(2,1)}), bf16[32,16,128]{2,1,0:T(8,128)(2,1)S(1)}, u32[]{:S(2)}, u32[]{:S(2)}) async-start(bf16[32,16,128]{2,1,0:T(8,128)(2,1)} %reshape_reshape.3), calls=%async_computation.6 | async-start | bytes 262144 | tf_op jit(solution)/shard_map/all_to_all | solution.py:220
  159.8 8.2 %copy-start.6 = (bf16[512,512]{1,0:T(8,128)(2,1)S(1)}, bf16[512,512]{1,0:T(8,128)(2,1)}, u32[]{:S(2)}) copy-start(bf16[512,512]{1,0:T(8,128)(2,1)} %copy-done.5) | copy-start | bytes 1572868
  167.6 1.6 collective-permute-start.1
  168.6 5.0 %copy-start.19 = (bf16[2,4,64,512]{3,2,1,0:T(8,128)(2,1)S(1)}, bf16[2,4,64,512]{3,2,1,0:T(8,128)(2,1)}, u32[]{:S(2)}) copy-start(bf16[2,4,64,512]{3,2,1,0:T(8,128)(2,1)} %copy.140) | copy-start | bytes 1572868
  170.1 17.5 %all-to-all-start.7 = ((bf16[8,192,128]{2,1,0:T(8,128)(2,1)}), bf16[8,192,128]{2,1,0:T(8,128)(2,1)S(1)}, u32[]{:S(2)}, u32[]{:S(2)}) async-start(bf16[8,192,128]{2,1,0:T(8,128)(2,1)} %pad_maximum_fusion.5), calls=%async_computation.7 | async-start | bytes 786432 | tf_op jit(solution)/shard_map/all_to_all | solution.py:220
  173.5 36.8 %reduce-scatter.5.cloned.1.call-start = ((), (), s32[]{:S(2)}) async-start(), calls=%async_computation.14 | async-start | bytes 1179648 | tf_op jit(solution)/shard_map/reduce_scatter | solution.py:407
  175.3 1.2 copy-start.35
  175.3 1.3 copy-start.3
  175.4 1.3 copy-start.9
  175.4 1.3 copy-start.42
  175.4 1.3 copy-start.43
  187.6 0.8 copy-start.10
  188.4 1.0 slice-start
  188.4 1.3 copy-start.1
  188.4 1.3 copy-start.31
  188.4 1.3 copy-start.33
  189.7 1.8 copy-start.14
  191.4 5.2 %copy-start.17 = (bf16[512,512]{1,0:T(8,128)(2,1)S(1)}, bf16[512,512]{1,0:T(8,128)(2,1)}, u32[]{:S(2)}) copy-start(bf16[512,512]{1,0:T(8,128)(2,1)} %copy-done.16) | copy-start | bytes 1572868
  191.5 5.1 %copy-start.15 = (bf16[512,384]{1,0:T(8,128)(2,1)S(1)}, bf16[512,384]{1,0:T(8,128)(2,1)}, u32[]{:S(2)}) copy-start(bf16[512,384]{1,0:T(8,128)(2,1)} %copy-done.14) | copy-start | bytes 1179652
  192.4 10.9 %all-to-all-start.8 = ((bf16[4,128,512]{2,1,0:T(8,128)(2,1)}), bf16[4,128,512]{2,1,0:T(8,128)(2,1)S(1)}, u32[]{:S(2)}, u32[]{:S(2)}) async-start(bf16[4,128,512]{2,1,0:T(8,128)(2,1)} %bitcast.69), calls=%async_computation.8 | async-start | bytes 1048576 | tf_op jit(solution)/shard_map/all_to_all | solution.py:220
  197.1 11.1 %copy-start.29 = (f32[2,1,64,1]{2,1,0,3:T(1,128)S(1)}, f32[2,1,64,1]{2,1,0,3:T(1,128)}, u32[]{:S(2)}) copy-start(f32[2,1,64,1]{2,1,0,3:T(1,128)} %copy-done.28) | copy-start | bytes 1540
  197.1 11.1 %copy-start.39 = (f32[2,64]{1,0:T(2,128)S(1)}, f32[2,64]{1,0:T(2,128)}, u32[]{:S(2)}) copy-start(f32[2,64]{1,0:T(2,128)} %copy-done.38) | copy-start | bytes 1540
  197.1 11.1 %copy-start.40 = (f32[2,64]{1,0:T(2,128)S(1)}, f32[2,64]{1,0:T(2,128)}, u32[]{:S(2)}) copy-start(f32[2,64]{1,0:T(2,128)} %fusion.54) | copy-start | bytes 1540
  203.3 10.1 %all-to-all-start.4 = ((bf16[4,128,512]{2,1,0:T(8,128)(2,1)}), bf16[4,128,512]{2,1,0:T(8,128)(2,1)S(1)}, u32[]{:S(2)}, u32[]{:S(2)}) async-start(bf16[4,128,512]{2,1,0:T(8,128)(2,1)} %bitcast.40), calls=%async_computation.4 | async-start | bytes 1048576 | tf_op jit(solution)/shard_map/all_to_all | solution.py:220
  206.8 9.9 %copy-start.21 = (bf16[512,128]{1,0:T(8,128)(2,1)S(1)}, bf16[512,128]{1,0:T(8,128)(2,1)}, u32[]{:S(2)}) copy-start(bf16[512,128]{1,0:T(8,128)(2,1)} %get-tuple-element.102) | copy-start | bytes 393220
  206.8 9.9 %copy-start.22 = (bf16[512,128]{1,0:T(8,128)(2,1)S(1)}, bf16[512,128]{1,0:T(8,128)(2,1)}, u32[]{:S(2)}) copy-start(bf16[512,128]{1,0:T(8,128)(2,1)} %get-tuple-element.103) | copy-start | bytes 393220
  210.1 14.9 %copy-start.4 = (bf16[2,4,64,512]{3,2,1,0:T(8,128)(2,1)S(1)}, bf16[2,4,64,512]{3,2,1,0:T(8,128)(2,1)}, u32[]{:S(2)}) copy-start(bf16[2,4,64,512]{3,2,1,0:T(8,128)(2,1)} %copy.152) | copy-start | bytes 1572868
  210.1 14.9 %copy-start.12 = (bf16[512,128]{1,0:T(8,128)(2,1)S(1)}, bf16[512,128]{1,0:T(8,128)(2,1)}, u32[]{:S(2)}) copy-start(bf16[512,128]{1,0:T(8,128)(2,1)} %copy-done.11) | copy-start | bytes 393220
  213.4 8.1 %all-to-all-start.10 = ((bf16[4,16,512]{2,1,0:T(8,128)(2,1)}), bf16[4,16,512]{2,1,0:T(8,128)(2,1)S(1)}, u32[]{:S(2)}, u32[]{:S(2)}) async-start(bf16[4,16,512]{2,1,0:T(8,128)(2,1)} %bitcast.89), calls=%async_computation.12 | async-start | bytes 131072 | tf_op jit(solution)/shard_map/all_to_all | solution.py:220
  216.7 9.3 %copy-start.34 = (f32[512]{0:T(512)S(1)}, f32[512]{0:T(512)}, u32[]{:S(2)}) copy-start(f32[512]{0:T(512)} %add.313) | copy-start | bytes 6148
  221.5 40.5 %all-to-all-start.9 = ((bf16[32,51,128]{2,1,0:T(8,128)(2,1)}), bf16[32,51,128]{2,1,0:T(8,128)(2,1)S(1)}, u32[]{:S(2)}, u32[]{:S(2)}) async-start(bf16[32,51,128]{2,1,0:T(8,128)(2,1)} %pad_maximum_fusion.2), calls=%async_computation.9 | async-start | bytes 917504 | tf_op jit(solution)/shard_map/all_to_all | solution.py:220
  224.9 35.1 %reduce-scatter.3.cloned.1.call-start = ((), (), s32[]{:S(2)}) async-start(), calls=%async_computation.13 | async-start | bytes 147456 | tf_op jit(solution)/shard_map/reduce_scatter | solution.py:407
Sparse Core Ops, SparseCore 0:
  43.0 29.5 all-gather.2
  176.7 32.2 reduce-scatter.4
  228.5 31.3 reduce-scatter.2

commit v2 on v1

--- a/solution.py
+++ b/solution.py
@@ -49,23 +49,25 @@
 
 class AttentionShape:
     def __init__(self, blocks, part_rows, parts, run, stride):
+        self.blocks = blocks
         self.per_tile = max(1, TILE_Q // part_rows)
         self.tiles = blocks // self.per_tile
         self.tile = self.per_tile * part_rows
         self.part_rows = part_rows
+        self.half = part_rows // 2
         self.parts = parts
         self.run = run
         self.stride = stride
         self.span = self.tile * parts
 
 
-def unpack_tile(packed_ref, tile, geo):
-    half = geo.part_rows // 2
-    pieces = []
-    for i in range(geo.per_tile):
-        packed = packed_ref[tile * geo.per_tile + i]
-        pieces += [packed[:, :HD], packed[:, HD:]]
-    return jnp.concatenate(pieces, axis=0)
+def unpack_rows(packed):
+    return jnp.concatenate([packed[:, :HD], packed[:, HD:]], axis=0)
+
+
+def pack_rows(rows):
+    half = rows.shape[0] // 2
+    return jnp.concatenate([rows[:half], rows[half:]], axis=1)
 
 
 def key_base(geo):
@@ -73,13 +75,22 @@
     return (rows // geo.run) * geo.stride + rows % geo.run
 
 
-def forward_kernel(geo, scal_ref, q_ref, kv_ref, bounds_ref, out_ref, ot_ref, lse_ref, kvt_ref):
+def task_tile(ref, geo, tile, first, count):
+    block = ref[pl.ds(tile * geo.per_tile, geo.per_tile), first : first + count, :]
+    return block.reshape(geo.per_tile * count, LANES)
+
+
+def forward_kernel(geo, scal_ref, *refs):
+    part_refs = refs[: geo.parts]
+    bounds_ref, out_ref, ot_ref, lse_ref, kvt_ref = refs[geo.parts :]
     base = jnp.broadcast_to(key_base(geo), (geo.tile, geo.tile))
     for part in range(geo.parts):
         for tile in range(geo.tiles):
-            kvt_ref[part, tile] = kv_ref[part, tile].T
+            keys = task_tile(part_refs[part], geo, tile, geo.half, geo.part_rows)
+            kvt_ref[part, tile] = keys.T
     for tile in range(geo.tiles):
-        q = unpack_tile(q_ref, tile, geo) * jnp.asarray(HD**-0.5, bf16)
+        q = unpack_rows(task_tile(part_refs[0], geo, tile, 0, geo.half))
+        q = q * jnp.asarray(HD**-0.5, bf16)
         qz = jnp.concatenate([q, jnp.zeros_like(q)], axis=1)
         start = bounds_ref[tile, 0:1]
         last = bounds_ref[tile, 1:2]
@@ -88,7 +99,8 @@
         def chunk(part, key_tile, carry, diagonal):
             run_max, run_sum, acc = carry
             offset = key_tile * geo.span + scal_ref[part]
-            scores = dot_nt(kv_ref[part, key_tile], qz)
+            keys = task_tile(part_refs[part], geo, key_tile, geo.half, geo.part_rows)
+            scores = dot_nt(keys, qz)
             allowed = (base >= start - offset) & (base <= last - offset)
             if diagonal:
                 allowed = allowed | (base == own - offset)
@@ -118,25 +130,26 @@
         attended = acc[HD:] / run_sum
         ot_ref[tile] = attended
         lse_ref[tile] = jnp.broadcast_to(run_max + jnp.log(run_sum), (8, geo.tile))
-        rows = attended.T
-        half = geo.part_rows // 2
+        packed = pack_rows(attended.T).astype(bf16)
         for i in range(geo.per_tile):
-            low = rows[2 * i * half : (2 * i + 1) * half]
-            high = rows[(2 * i + 1) * half : (2 * i + 2) * half]
-            out_ref[tile * geo.per_tile + i] = jnp.concatenate([low, high], axis=1).astype(bf16)
-
-
-def backward_kernel(
-    geo, scal_ref, q_ref, kv_ref, do_ref, bounds_ref, ot_ref, lse_ref, dq_ref, dkv_ref, kvt_ref
-):
+            out_ref[tile * geo.per_tile + i] = packed[i * geo.half : (i + 1) * geo.half]
+
+
+def backward_kernel(geo, do_tile, scal_ref, *refs):
+    part_refs = refs[: geo.parts]
+    do_ref, bounds_ref, ot_ref, lse_ref, dq_ref = refs[geo.parts : geo.parts + 5]
+    grad_refs = refs[geo.parts + 5 : 2 * geo.parts + 5]
+    acc_ref, kvt_ref = refs[2 * geo.parts + 5 :]
     base = jnp.broadcast_to(key_base(geo), (geo.tile, geo.tile))
-    dkv_ref[...] = jnp.zeros_like(dkv_ref)
+    acc_ref[...] = jnp.zeros_like(acc_ref)
     for part in range(geo.parts):
         for tile in range(geo.tiles):
-            kvt_ref[part, tile] = kv_ref[part, tile].T
+            keys = task_tile(part_refs[part], geo, tile, geo.half, geo.part_rows)
+            kvt_ref[part, tile] = keys.T
     for tile in range(geo.tiles):
-        q = unpack_tile(q_ref, tile, geo) * jnp.asarray(HD**-0.5, bf16)
-        do = unpack_tile(do_ref, tile, geo)
+        q = unpack_rows(task_tile(part_refs[0], geo, tile, 0, geo.half))
+        q = q * jnp.asarray(HD**-0.5, bf16)
+        do = unpack_rows(do_tile(do_ref, geo, tile))
         zeros = jnp.zeros_like(q)
         qz = jnp.concatenate([q, zeros], axis=1)
         doz = jnp.concatenate([zeros, do], axis=1)
@@ -148,7 +161,7 @@
 
         def chunk(part, key_tile, acc, diagonal):
             offset = key_tile * geo.span + scal_ref[part]
-            keys = kv_ref[part, key_tile]
+            keys = task_tile(part_refs[part], geo, key_tile, geo.half, geo.part_rows)
             scores = dot_nt(keys, qz)
             allowed = (base >= start - offset) & (base <= last - offset)
             if diagonal:
@@ -156,7 +169,7 @@
             probs = jnp.where(allowed, jnp.exp(scores - log_total), 0.0)
             grad_probs = dot_nt(keys, doz)
             grad_scores = (probs * (grad_probs - delta)).astype(bf16)
-            dkv_ref[part, key_tile] += dot_nn(grad_scores, qz) + dot_nn(probs.astype(bf16), doz)
+            acc_ref[part, key_tile] += dot_nn(grad_scores, qz) + dot_nn(probs.astype(bf16), doz)
             return acc + dot_nn(kvt_ref[part, key_tile], grad_scores)
 
         acc = jnp.zeros((2 * HD, geo.tile), f32)
@@ -169,47 +182,109 @@
             return acc
 
         acc = lax.fori_loop(scal_ref[geo.parts + tile], tile, earlier, acc)
-        rows = (acc[:HD] * (HD**-0.5)).T
-        half = geo.part_rows // 2
+        packed = pack_rows((acc[:HD] * (HD**-0.5)).T).astype(bf16)
         for i in range(geo.per_tile):
-            low = rows[2 * i * half : (2 * i + 1) * half]
-            high = rows[(2 * i + 1) * half : (2 * i + 2) * half]
-            dq_ref[tile * geo.per_tile + i] = jnp.concatenate([low, high], axis=1).astype(bf16)
-
-
-def vmem_specs(count):
-    return [pl.BlockSpec(memory_space=pltpu.VMEM)] * count
-
-
-def attention_forward(geo, scalars, q, kv, bounds):
+            dq_ref[tile * geo.per_tile + i] = packed[i * geo.half : (i + 1) * geo.half]
+    for part in range(geo.parts):
+        for tile in range(geo.tiles):
+            for i in range(geo.per_tile):
+                rows = acc_ref[part, tile, i * geo.part_rows : (i + 1) * geo.part_rows]
+                grad_refs[part][tile * geo.per_tile + i] = rows.astype(grad_refs[part].dtype)
+
+
+VMEM_LIMIT = 16 * 2**20
+
+
+def far(shape, dtype):
+    return (pltpu.HBM(shape, dtype),)
+
+
+def local_call(kernel, name, scalars, arrays, outs, scratch=(), flops=10**8):
     return pl.pallas_call(
+        kernel,
+        out_shape=tuple(o[0] if len(o) == 1 else jax.ShapeDtypeStruct(*o) for o in outs),
+        in_specs=[pl.BlockSpec(memory_space=pltpu.SMEM)]
+        + [pl.BlockSpec(memory_space=pltpu.VMEM)] * len(arrays),
+        out_specs=tuple([pl.BlockSpec(memory_space=pltpu.VMEM)] * len(outs)),
+        scratch_shapes=list(scratch),
+        compiler_params=pltpu.CompilerParams(vmem_limit_bytes=VMEM_LIMIT),
+        cost_estimate=pl.CostEstimate(flops=flops, bytes_accessed=10**6, transcendentals=0),
+        name=name,
+    )(scalars, *arrays)
+
+
+def attention_forward(geo, scalars, part_arrays, bounds):
+    return local_call(
         functools.partial(forward_kernel, geo),
-        out_shape=(
-            jax.ShapeDtypeStruct(q.shape, bf16),
-            jax.ShapeDtypeStruct((geo.tiles, HD, geo.tile), f32),
-            jax.ShapeDtypeStruct((geo.tiles, 8, geo.tile), f32),
-        ),
-        in_specs=[pl.BlockSpec(memory_space=pltpu.SMEM)] + vmem_specs(3),
-        out_specs=tuple(vmem_specs(3)),
-        scratch_shapes=[pltpu.VMEM((geo.parts, geo.tiles, LANES, geo.tile), bf16)],
-        compiler_params=pltpu.CompilerParams(vmem_limit_bytes=48 * 2**20),
-        name="attention_forward",
-    )(scalars, q, kv, bounds)
-
-
-def attention_backward(geo, scalars, q, kv, do, bounds, ot, lse):
-    return pl.pallas_call(
-        functools.partial(backward_kernel, geo),
-        out_shape=(
-            jax.ShapeDtypeStruct(q.shape, bf16),
-            jax.ShapeDtypeStruct(kv.shape, f32),
-        ),
-        in_specs=[pl.BlockSpec(memory_space=pltpu.SMEM)] + vmem_specs(6),
-        out_specs=tuple(vmem_specs(2)),
-        scratch_shapes=[pltpu.VMEM((geo.parts, geo.tiles, LANES, geo.tile), bf16)],
-        compiler_params=pltpu.CompilerParams(vmem_limit_bytes=48 * 2**20),
-        name="attention_backward",
-    )(scalars, q, kv, do, bounds, ot, lse)
+        "attention_forward",
+        scalars,
+        [*part_arrays, bounds],
+        [
+            ((geo.blocks, geo.half, LANES), bf16),
+            far((geo.tiles, HD, geo.tile), f32),
+            far((geo.tiles, 8, geo.tile), f32),
+        ],
+        [pltpu.VMEM((geo.parts, geo.tiles, LANES, geo.tile), bf16)],
+        flops=30 * 10**9,
+    )
+
+
+def attention_backward(geo, do_tile, scalars, part_arrays, do, bounds, ot, lse):
+    grads = [((geo.blocks, geo.part_rows, LANES), f32)]
+    grads += [((geo.blocks, geo.part_rows, LANES), bf16)] * (geo.parts - 1)
+    return local_call(
+        functools.partial(backward_kernel, geo, do_tile),
+        "attention_backward",
+        scalars,
+        [*part_arrays, do, bounds, ot, lse],
+        [((geo.blocks, geo.half, LANES), bf16), *grads],
+        [
+            pltpu.VMEM((geo.parts, geo.tiles, geo.tile, LANES), f32),
+            pltpu.VMEM((geo.parts, geo.tiles, LANES, geo.tile), bf16),
+        ],
+        flops=30 * 10**9,
+    )
+
+
+def do_tile_grouped(do_ref, geo, tile):
+    heads = do_ref.shape[0] // geo.blocks
+    pieces = []
+    for i in range(geo.per_tile):
+        for head in range(heads):
+            pieces.append(do_ref[head * geo.blocks + tile * geo.per_tile + i])
+    return jnp.concatenate(pieces, axis=0)
+
+
+def do_tile_plain(do_ref, geo, tile):
+    return task_tile(do_ref, geo, tile, 0, geo.half)
+
+
+def query_positions(blocks, heads, run, sub, part, geo):
+    half = run // 2
+    block = jnp.arange(blocks, dtype=i32).reshape(geo.tiles, 1, geo.per_tile, 1, 1)
+    upper = jnp.arange(2, dtype=i32).reshape(1, 2, 1, 1, 1)
+    head = jnp.arange(heads, dtype=i32).reshape(1, 1, 1, heads, 1)
+    row = jnp.arange(half, dtype=i32).reshape(1, 1, 1, 1, half)
+    at = block * (heads * sub) + head * sub + part * run + upper * half + row
+    return at.reshape(geo.tiles, 1, geo.tile)
+
+
+def attention_bounds(segments, token_valid, my_seq, my_part, geo, heads, sub):
+    seg = lax.dynamic_index_in_dim(segments, my_seq, 0, keepdims=False)
+    valid = jnp.sum(lax.dynamic_index_in_dim(token_valid, my_seq, 0, keepdims=False))
+    own = query_positions(geo.blocks, heads, geo.run, sub, my_part, geo)
+    half = geo.run // 2
+    own_seg = seg.reshape(geo.blocks * heads, geo.parts, geo.run)
+    own_seg = lax.dynamic_index_in_dim(own_seg, my_part, 1, keepdims=False)
+    own_seg = own_seg.reshape(geo.tiles, geo.per_tile, heads, 2, half).transpose(0, 3, 1, 2, 4)
+    own_seg = own_seg.reshape(-1, 1)
+    start = jnp.sum((seg[None, :] < own_seg).astype(i32), axis=1).reshape(geo.tiles, 1, geo.tile)
+    last = jnp.minimum(own, valid - 1)
+    bounds = jnp.concatenate([start, last, own, jnp.zeros((geo.tiles, 5, geo.tile), i32)], axis=1)
+    first_seg = seg.reshape(geo.tiles, geo.span)[:, :1]
+    first_tile = jnp.sum((seg[None, :] < first_seg).astype(i32), axis=1) // geo.span
+    part_at = ((my_part - jnp.arange(geo.parts, dtype=i32)) % geo.parts) * geo.run
+    return jnp.concatenate([part_at, first_tile]), bounds
 
 
 def gather_head(x):
@@ -220,7 +295,15 @@
     return lax.all_to_all(x, axis, split_axis=0, concat_axis=0, tiled=True)
 
 
-def on_device(
+def within_group(blocks, parts, step):
+    return [
+        (t * parts + i, t * parts + (i + step) % parts)
+        for t in range(blocks // parts)
+        for i in range(parts)
+    ]
+
+
+def on_device_general(
     layer_input,
     segments,
     token_valid,
@@ -319,43 +402,23 @@
     pairs = qkv[:, LANES:].reshape(tokens, local, 2, HD)
     b_pair = jnp.stack([jnp.zeros((local, HD), f32), b_v.reshape(local, HD)], axis=1)
     pairs = (pairs + b_pair).astype(bf16)
-    queries = queries.reshape(seqs, heads, parts, run, local, HD).transpose(0, 4, 2, 1, 3, 5)
-    queries = queries.reshape(blocks, 2, half, HD).transpose(0, 2, 1, 3).reshape(blocks, half, LANES)
+    queries = queries.reshape(seqs, heads, parts, 2, run // 2, local, HD)
+    queries = queries.transpose(0, 5, 2, 1, 4, 3, 6).reshape(blocks, half, LANES)
     pairs = pairs.reshape(seqs, heads, parts, run, local, LANES).transpose(0, 4, 2, 1, 3, 5)
     pairs = pairs.reshape(blocks, part_rows, LANES)
-    got = exchange(jnp.concatenate([queries, pairs], axis=1), "blk")
-    q_task = got[:, :half]
-    kv_parts = [got[:, half:]]
+    task = exchange(jnp.concatenate([queries, pairs], axis=1), "blk")
+    part_arrays = [task]
     for step in range(1, parts):
-        around = [
-            (t * parts + i, t * parts + (i + step) % parts)
-            for t in range(blocks // parts)
-            for i in range(parts)
-        ]
-        kv_parts.append(lax.ppermute(kv_parts[0], "blk", around))
-    kv_task = jnp.stack(kv_parts).reshape(parts, geo.tiles, geo.tile, LANES)
+        part_arrays.append(lax.ppermute(task, "blk", within_group(blocks, parts, step)))
 
     my_part = my_blk % parts
     my_seq = (my_blk // parts) // local
-    seg = lax.dynamic_index_in_dim(segments, my_seq, 0, keepdims=False)
-    valid = jnp.sum(lax.dynamic_index_in_dim(token_valid, my_seq, 0, keepdims=False))
-    index = jnp.arange(blocks * part_rows, dtype=i32)
-    own = (index // run) * sub + my_part * run + index % run
-    own_seg = lax.dynamic_index_in_dim(seg.reshape(length // sub, parts, run), my_part, 1, False)
-    start = jnp.sum((seg[None, :] < own_seg.reshape(-1)[:, None]).astype(i32), axis=1)
-    last = jnp.minimum(own, valid - 1)
-    bounds = jnp.stack([start, last, own]).reshape(3, geo.tiles, geo.tile).transpose(1, 0, 2)
-    bounds = jnp.pad(bounds, ((0, 0), (0, 5), (0, 0)))
-    first_seg = seg.reshape(geo.tiles, geo.span)[:, :1]
-    first_tile = jnp.sum((seg[None, :] < first_seg).astype(i32), axis=1) // geo.span
-    part_at = ((my_part - jnp.arange(parts, dtype=i32)) % parts) * run
-    scalars = jnp.concatenate([part_at, first_tile])
-
-    o_task, ot, lse = attention_forward(geo, scalars, q_task, kv_task, bounds)
+    scalars, bounds = attention_bounds(segments, token_valid, my_seq, my_part, geo, heads, sub)
+    o_task, ot, lse = attention_forward(geo, scalars, part_arrays, bounds)
 
     got = exchange(o_task, "blk")
-    mixed = got.reshape(seqs, local, parts, half, 2, HD).transpose(0, 1, 2, 4, 3, 5)
-    mixed = mixed.reshape(seqs, local, parts, heads, run, HD).transpose(0, 3, 2, 4, 1, 5)
+    mixed = got.reshape(seqs, local, parts, heads, run // 2, 2, HD)
+    mixed = mixed.transpose(0, 3, 2, 5, 4, 1, 6)
     mixed = mixed.reshape(tokens, cols)
     mixed_all = lax.all_gather(mixed, "head", axis=1, tiled=True)
 
@@ -386,13 +449,10 @@
     )
     grad_branch = grad_middle.astype(bf16)
     grad_mixed = dot_nt(grad_branch, w_out).astype(bf16)
-    grad_mixed = grad_mixed.reshape(seqs, parts, run, heads, local, HD).transpose(3, 0, 4, 1, 2, 5)
-    grad_mixed = grad_mixed.reshape(heads, blocks, run // 2 * LANES // HD // 2 * 2, HD)
-    grad_mixed = grad_mixed.reshape(devices, run * HD // LANES, LANES)
-    got = exchange(grad_mixed, BOTH)
-    do_task = got.reshape(heads, blocks, run, HD).transpose(1, 0, 2, 3)
-    do_task = do_task.reshape(blocks, 2, half, HD).transpose(0, 2, 1, 3)
-    do_task = do_task.reshape(blocks, half, LANES)
+    grad_mixed = grad_mixed.reshape(seqs, parts, 2, run // 2, heads, local, HD)
+    grad_mixed = grad_mixed.transpose(4, 0, 5, 1, 3, 2, 6).reshape(devices, run // 2, LANES)
+    got = exchange(grad_mixed, BOTH).reshape(heads, blocks, run // 2, LANES)
+    do_task = got.transpose(1, 0, 2, 3).reshape(blocks, half, LANES)
 
     feed_mine = jnp.sum(to_owners(feed).astype(f32), axis=0)
     layer_output = my_tokens(middle) + feed_mine + b_down
@@ -422,20 +482,15 @@
     own_up = exchange(own_up.reshape(heads, w_rows, hidden_slice), "head")
     own_up = own_up.transpose(1, 0, 2).reshape(w_rows, hidden_width)
 
-    dq_task, dkv_task = attention_backward(geo, scalars, q_task, kv_task, do_task, bounds, ot, lse)
-    dkv_task = dkv_task.reshape(parts, blocks, part_rows, LANES)
-    dkv = dkv_task[0]
+    dq_task, dkv, *others = attention_backward(
+        geo, do_tile_plain, scalars, part_arrays, do_task, bounds, ot, lse
+    )
     for step in range(1, parts):
-        around = [
-            (t * parts + i, t * parts + (i - step) % parts)
-            for t in range(blocks // parts)
-            for i in range(parts)
-        ]
-        dkv = dkv + lax.ppermute(dkv_task[step].astype(bf16), "blk", around).astype(f32)
-    dkv = dkv * 1.0
+        back = within_group(blocks, parts, -step)
+        dkv = dkv + lax.ppermute(others[step - 1], "blk", back).astype(f32)
     got = exchange(jnp.concatenate([dq_task, dkv.astype(bf16)], axis=1), "blk")
-    dq = got[:, :half].reshape(blocks, half, 2, HD).transpose(0, 2, 1, 3)
-    dq = dq.reshape(seqs, local, parts, heads, run, HD).transpose(0, 3, 2, 4, 1, 5)
+    dq = got[:, :half].reshape(seqs, local, parts, heads, run // 2, 2, HD)
+    dq = dq.transpose(0, 3, 2, 5, 4, 1, 6)
     dq = dq.reshape(tokens, cols)
     dkv = got[:, half:].reshape(seqs, local, parts, heads, run, LANES).transpose(0, 3, 2, 4, 1, 5)
     dkv = dkv.reshape(tokens, local * LANES)
@@ -517,6 +572,770 @@
     )
 
 
+class Sizes:
+    def __init__(self, heads, blocks, seqs, sub, width, hidden_width):
+        self.heads = heads
+        self.blocks = blocks
+        self.seqs = seqs
+        self.sub = sub
+        self.width = width
+        self.devices = heads * blocks
+        self.mine = seqs * sub
+        self.tokens = self.mine * heads
+        self.local = H // heads
+        self.parts = blocks // (seqs * self.local)
+        self.run = sub // self.parts
+        self.part_rows = heads * self.run
+        self.half = self.part_rows // 2
+        self.w_rows = width // self.devices
+        self.f_rows = hidden_width // self.devices
+        self.hidden_slice = hidden_width // heads
+        self.w_chunk = (1 + self.local) * self.w_rows
+        self.head_rows = self.blocks * self.w_rows
+        self.groups = blocks // self.parts
+
+    def fits(self):
+        return (
+            self.local == 2
+            and self.parts == 2
+            and self.run % 32 == 0
+            and self.w_rows == 16
+            and self.hidden_slice == self.width
+            and self.mine % 16 == 0
+            and self.f_rows % 16 == 0
+        )
+
+    def task(self, seq, local, part):
+        return (seq * self.local + local) * self.parts + part
+
+
+SMALL = 8
+
+
+def slot_head(sz, scal_ref, slot):
+    return lax.rem(scal_ref[0] - slot + sz.heads, sz.heads)
+
+
+def halves(first, second):
+    low = jnp.concatenate([first[:, :HD], second[:, :HD]], axis=1)
+    high = jnp.concatenate([first[:, HD:], second[:, HD:]], axis=1)
+    return low, high
+
+
+def staged(count, refs):
+    scratch = refs[len(refs) - count - 1 :]
+    held, sems = scratch[:count], scratch[count]
+    copies = [pltpu.make_async_copy(refs[i], held[i], sems.at[i]) for i in range(count)]
+    for copy in copies:
+        copy.start()
+    for copy in copies:
+        copy.wait()
+    return held
+
+
+def staged_call(kernel, name, scalars, arrays, outs, scratch=()):
+    return pl.pallas_call(
+        kernel,
+        out_shape=tuple(jax.ShapeDtypeStruct(*o) for o in outs),
+        in_specs=[pl.BlockSpec(memory_space=pltpu.SMEM)]
+        + [pl.BlockSpec(memory_space=pltpu.HBM)] * len(arrays),
+        out_specs=tuple([pl.BlockSpec(memory_space=pltpu.VMEM)] * len(outs)),
+        scratch_shapes=list(scratch)
+        + [pltpu.VMEM(v.shape, v.dtype) for v in arrays]
+        + [pltpu.SemaphoreType.DMA((len(arrays),))],
+        compiler_params=pltpu.CompilerParams(vmem_limit_bytes=63 * 2**20),
+        name=name,
+    )(scalars, *arrays)
+
+
+def pack_kernel(sz, scal_ref, *refs):
+    count = 1 + SMALL
+    send_ref, small_scr = refs[count : count + 2]
+    small_scr[...] = jnp.zeros_like(small_scr)
+    wp_ref, *small_refs = staged(count, refs)
+    for i, ref in enumerate(small_refs):
+        small_scr[i : i + 1, : ref.shape[1]] = ref[...].astype(f32)
+    small = small_scr[...].astype(bf16)
+    for head in range(sz.heads):
+        at = head * LANES
+        q = wp_ref[:, at : at + LANES]
+        k = wp_ref[:, sz.width + at : sz.width + at + LANES]
+        v = wp_ref[:, 2 * sz.width + at : 2 * sz.width + at + LANES]
+        low, high = halves(k, v)
+        chunk = jnp.concatenate([q, low, high], axis=0)
+        for blk in range(sz.blocks):
+            send_ref[head * sz.blocks + blk, : sz.w_chunk] = chunk
+            send_ref[head * sz.blocks + blk, sz.w_chunk :] = small
+
+
+def pack_more_kernel(sz, scal_ref, *refs):
+    tokens_ref, column_ref = refs[5:7]
+    x_ref, g_ref, up_ref, wo_ref, down_ref = staged(5, refs)
+    tokens_ref[: sz.mine] = x_ref[...]
+    tokens_ref[sz.mine :] = g_ref[...]
+    for head in range(sz.heads):
+        part = up_ref[:, head * sz.hidden_slice : (head + 1) * sz.hidden_slice]
+        column_ref[head * sz.w_rows : (head + 1) * sz.w_rows] = part
+    at = sz.heads * sz.w_rows
+    column_ref[at : at + sz.w_rows] = wo_ref[...]
+    column_ref[at + sz.w_rows :] = down_ref[...]
+
+
+def spread(small, per, offset, count):
+    lane = lax.broadcasted_iota(i32, (LANES, count), 0)
+    at = lax.broadcasted_iota(i32, (LANES, count), 1) + offset
+    pick = jnp.where(at % per == lane, 1.0, 0.0).astype(bf16)
+    wide = dot_nn(small, pick)
+    source = lax.broadcasted_iota(i32, wide.shape, 0) // SMALL
+    column = (lax.broadcasted_iota(i32, wide.shape, 1) + offset) // per
+    wide = jnp.where(source == column, wide, 0.0)
+    return jnp.sum(wide.reshape(-1, SMALL, count), axis=0)
+
+
+def collect(values, per, offset, rows, devices):
+    count = values.shape[1]
+    tall = jnp.broadcast_to(values[None], (devices, SMALL, count)).reshape(devices * SMALL, count)
+    row = lax.broadcasted_iota(i32, tall.shape, 0)
+    column = (lax.broadcasted_iota(i32, tall.shape, 1) + offset) // per
+    index = row % SMALL
+    keep = (row // SMALL == column) & (index >= rows[0]) & (index < rows[1])
+    tall = jnp.where(keep, tall, 0.0)
+    lane = lax.broadcasted_iota(i32, (count, LANES), 1)
+    at = lax.broadcasted_iota(i32, (count, LANES), 0) + offset
+    pick = jnp.where(at % per == lane, 1.0, 0.0).astype(bf16)
+    return dot_nn(tall.astype(bf16), pick)
+
+
+def source_blk(sz, scal_ref, group_slot, part_slot):
+    group = lax.rem(scal_ref[1] // sz.parts - group_slot + sz.groups, sz.groups)
+    part = lax.rem(scal_ref[1] % sz.parts - part_slot + sz.parts, sz.parts)
+    return group * sz.parts + part
+
+
+def project_kernel(sz, scal_ref, got_ref, *refs):
+    x_refs = refs[: sz.heads]
+    send_ref, w_ref, vec_ref = refs[sz.heads :]
+    head = scal_ref[0]
+    for i in range(1 + sz.local):
+        part = got_ref[:, i * sz.w_rows : (i + 1) * sz.w_rows, :]
+        w_ref[:, i * LANES : (i + 1) * LANES] = part.reshape(sz.width, LANES)
+    small = got_ref[:, sz.w_chunk :, :].astype(f32).reshape(-1, LANES).astype(bf16)
+    vec = spread(small, sz.w_rows, 0, sz.width)
+    per = 2 * sz.w_rows
+    b_q = spread(small, per, head * LANES, LANES)[6:7]
+    b_v = spread(small, per, sz.width + head * LANES, LANES)[6:7]
+    b_up = spread(small, 4 * sz.w_rows, head * sz.hidden_slice, sz.hidden_slice)
+    row = lax.broadcasted_iota(i32, vec.shape, 0)
+    vec = jnp.where(row == 7, b_up, vec)
+    vec_ref[...] = vec
+    zero = jnp.zeros((1, HD), f32)
+    bias = jnp.concatenate([b_q, zero, b_v[:, :HD], zero, b_v[:, HD:]], axis=1)
+    gain, shift = vec[0:1], vec[1:2]
+    for slot in range(sz.heads):
+        x = x_refs[slot][: sz.mine].astype(f32)
+        normed = norm_forward(x, gain, shift)[0].astype(bf16)
+        qkv = (dot_nn(normed, w_ref[...]) + bias).astype(bf16)
+        to = slot_head(sz, scal_ref, slot)
+        half_run = sz.run // 2
+        for seq in range(sz.seqs):
+            for part in range(sz.parts):
+                at = seq * sz.sub + part * sz.run
+                low, high = halves(qkv[at : at + half_run, :LANES], qkv[at + half_run : at + sz.run, :LANES])
+                packed = (low, high)
+                for local in range(sz.local):
+                    task = sz.task(seq, local, part)
+                    q_at = pl.multiple_of(to * half_run, half_run)
+                    send_ref[task, pl.ds(q_at, half_run)] = packed[local]
+                    kv_at = pl.multiple_of(sz.half + to * sz.run, sz.run)
+                    send_ref[task, pl.ds(kv_at, sz.run)] = qkv[
+                        at : at + sz.run, (1 + local) * LANES : (2 + local) * LANES
+                    ]
+
+
+def regroup_kernel(sz, scal_ref, *refs):
+    count = sz.parts * sz.groups
+    column_refs, pay_refs, down_ref = refs[:count], refs[count:-1], refs[-1]
+    for part_slot in range(sz.parts):
+        for group_slot in range(sz.groups):
+            ref = column_refs[part_slot * sz.groups + group_slot]
+            blk = source_blk(sz, scal_ref, group_slot, part_slot)
+            at = pl.multiple_of(blk * sz.f_rows, sz.f_rows)
+            first = sz.heads * sz.w_rows
+            down_ref[pl.ds(at, sz.f_rows)] = ref[first + sz.w_rows :]
+            up_at = pl.multiple_of(blk * sz.w_rows, sz.w_rows)
+            out_at = pl.multiple_of(sz.head_rows + blk * sz.w_rows, sz.w_rows)
+            for step, pay_ref in enumerate(pay_refs):
+                to = lax.rem(scal_ref[0] + step, sz.heads)
+                from_at = pl.multiple_of(to * sz.w_rows, sz.w_rows)
+                pay_ref[pl.ds(up_at, sz.w_rows)] = ref[pl.ds(from_at, sz.w_rows)]
+                pay_ref[pl.ds(out_at, sz.w_rows)] = ref[first : first + sz.w_rows]
+
+
+def output_weight_rows(sz, pay_refs):
+    rows = slice(sz.head_rows, 2 * sz.head_rows)
+    return jnp.concatenate([ref[rows] for ref in pay_refs], axis=0)
+
+
+def feed_kernel(sz, scal_ref, vec_ref, down_ref, *refs):
+    n = sz.heads
+    x_refs, pay_refs, m_refs = refs[:n], refs[n : 2 * n], refs[2 * n : 3 * n]
+    outs = refs[3 * n :]
+    part_refs, feed_refs = outs[:n], outs[n : 2 * n]
+    mid_ref, act_ref, dh_ref, n_ref, mix_own_ref, sum_ref, up_ref, mix_scr = outs[2 * n :]
+    for slot in range(n):
+        at = pl.multiple_of(slot_head(sz, scal_ref, slot) * sz.head_rows, sz.head_rows)
+        up_ref[pl.ds(at, sz.head_rows)] = pay_refs[slot][: sz.head_rows]
+    w_out = output_weight_rows(sz, pay_refs)
+    half_run = sz.run // 2
+    for slot in range(n):
+        for seq in range(sz.seqs):
+            for part in range(sz.parts):
+                first = m_refs[slot][sz.task(seq, 0, part)]
+                second = m_refs[slot][sz.task(seq, 1, part)]
+                low, high = halves(first, second)
+                for head in range(n):
+                    at = seq * sz.sub + part * sz.run
+                    cols = slice(slot * LANES, (slot + 1) * LANES)
+                    rows = slice(head * half_run, (head + 1) * half_run)
+                    mix_scr[head, at : at + half_run, cols] = low[rows]
+                    mix_scr[head, at + half_run : at + sz.run, cols] = high[rows]
+    w_down = down_ref[...]
+    b_out, gain, shift, b_up = vec_ref[2:3], vec_ref[3:4], vec_ref[4:5], vec_ref[7:8]
+    sums = jnp.zeros((3, sz.width), f32)
+    group = 2
+    for first in range(0, n, group):
+        slots = range(first, first + group)
+        x = jnp.concatenate([x_refs[s][: sz.mine] for s in slots], axis=0).astype(f32)
+        g = jnp.concatenate([x_refs[s][sz.mine :] for s in slots], axis=0)
+        mixed = jnp.concatenate([mix_scr[slot_head(sz, scal_ref, s)] for s in slots], axis=0)
+        middle = x + dot_nn(mixed, w_out) + b_out
+        normed, unit, _ = norm_forward(middle, gain, shift)
+        normed = normed.astype(bf16)
+        hidden = dot_nn(normed, up_ref[...]) + b_up
+        sigma = 1.0 / (1.0 + jnp.exp(-1.702 * hidden))
+        activated = (hidden * sigma).astype(bf16)
+        slope = sigma + 1.702 * hidden * sigma * (1.0 - sigma)
+        grad_hidden = (dot_nt(g, w_down) * slope).astype(bf16)
+        grad_two = dot_nt(grad_hidden, up_ref[...])
+        feed = dot_nn(activated, w_down)
+        sums = sums + jnp.concatenate(
+            [
+                jnp.sum(grad_two * unit, axis=0, keepdims=True),
+                jnp.sum(grad_two, axis=0, keepdims=True),
+                jnp.sum(grad_hidden.astype(f32), axis=0, keepdims=True),
+            ],
+            axis=0,
+        )
+        for i, s in enumerate(slots):
+            rows = slice(i * sz.mine, (i + 1) * sz.mine)
+            part_refs[s][...] = grad_two[rows].astype(part_refs[s].dtype)
+            feed_refs[s][...] = feed[rows].astype(feed_refs[s].dtype)
+            if s == 0:
+                mid_ref[...] = middle[rows]
+                mix_own_ref[...] = mixed[rows]
+            act_ref[s] = activated[rows]
+            dh_ref[s] = grad_hidden[rows]
+            n_ref[s] = normed[rows]
+    sum_ref[...] = jnp.concatenate([sums, jnp.zeros((5, sz.width), f32)], axis=0)
+
+
+def give_and_keep(sz, scal_ref, values, rows, keep_ref, give_ref):
+    part = scal_ref[1] % sz.parts
+    for blk in range(sz.blocks):
+        group = blk // sz.parts
+        piece = values(blk)
+        @pl.when(part == blk % sz.parts)
+        def _():
+            keep_ref[group] = piece
+
+        @pl.when(part != blk % sz.parts)
+        def _():
+            give_ref[group] = piece.astype(bf16)
+
+
+def feed_grad_kernel(sz, scal_ref, act_ref, dh_ref, n_ref, *refs):
+    g_refs = refs[: sz.heads]
+    keep_ref, give_ref = refs[sz.heads :]
+    g = jnp.concatenate([ref[sz.mine :] for ref in g_refs], axis=0)
+    act = act_ref[...].reshape(sz.tokens, sz.hidden_slice)
+    down = dot_tn(act, g)
+    up = dot_tn(n_ref[...].reshape(sz.tokens, sz.width), dh_ref[...].reshape(sz.tokens, sz.hidden_slice))
+
+    def piece(blk):
+        pieces = [down[blk * sz.f_rows : (blk + 1) * sz.f_rows]]
+        for head in range(sz.heads):
+            at = head * sz.head_rows + blk * sz.w_rows
+            pieces.append(up[at : at + sz.w_rows])
+        return jnp.concatenate(pieces, axis=0)
+
+    give_and_keep(sz, scal_ref, piece, sz.f_rows + sz.heads * sz.w_rows, keep_ref, give_ref)
+
+
+def part_sum_kernel(sz, scal_ref, *refs):
+    pairs, (own_ref, *piece_refs) = refs[: -sz.groups], refs[-sz.groups :]
+    for step in range(sz.groups):
+        to = lax.rem(scal_ref[1] // sz.parts + step, sz.groups)
+        at = 0
+        for keep_ref, got_ref in zip(pairs[::2], pairs[1::2]):
+            total = keep_ref[to] + got_ref[to].astype(f32)
+            ref = piece_refs[step - 1] if step else own_ref
+            ref[at : at + total.shape[0]] = total.astype(ref.dtype)
+            at += total.shape[0]
+
+
+def middle_grad_kernel(sz, scal_ref, vec_ref, mid_ref, tokens_ref, *refs):
+    n = sz.heads
+    pay_refs, part_refs = refs[:n], refs[n : 2 * n]
+    grad_ref, branch_ref, send_ref, sum_ref = refs[2 * n :]
+    w_out = output_weight_rows(sz, pay_refs)
+    upstream = part_refs[0][...]
+    for ref in part_refs[1:]:
+        upstream = upstream + ref[...].astype(f32)
+    gain, shift = vec_ref[3:4], vec_ref[4:5]
+    _, unit, root = norm_forward(mid_ref[...], gain, shift)
+    g = tokens_ref[sz.mine :].astype(f32)
+    grad = g + norm_input_grad(upstream, unit, root, gain)
+    grad_ref[...] = grad
+    branch = grad.astype(bf16)
+    branch_ref[...] = branch
+    sum_ref[...] = jnp.concatenate(
+        [
+            jnp.sum(branch.astype(f32), axis=0, keepdims=True),
+            jnp.sum(g, axis=0, keepdims=True),
+            jnp.zeros((6, sz.width), f32),
+        ],
+        axis=0,
+    )
+    mixed = dot_nt(branch, w_out).astype(bf16)
+    half_run = sz.run // 2
+    for slot in range(n):
+        to = slot_head(sz, scal_ref, slot)
+        for seq in range(sz.seqs):
+            for part in range(sz.parts):
+                at = seq * sz.sub + part * sz.run
+                cols = slice(slot * LANES, (slot + 1) * LANES)
+                packed = halves(mixed[at : at + half_run, cols], mixed[at + half_run : at + sz.run, cols])
+                for local in range(sz.local):
+                    send_ref[to * sz.blocks + sz.task(seq, local, part)] = packed[local]
+
+
+def out_grad_kernel(sz, scal_ref, mix_ref, branch_ref, keep_ref, give_ref):
+    grad = dot_tn(mix_ref[...], branch_ref[...])
+    part = scal_ref[1] % sz.parts
+    for slot in range(sz.heads):
+        head = slot_head(sz, scal_ref, slot)
+        to = pl.multiple_of(head * sz.w_rows, sz.w_rows)
+        for blk in range(sz.blocks):
+            at = slot * sz.head_rows + blk * sz.w_rows
+            piece = grad[at : at + sz.w_rows]
+
+            @pl.when(part == blk % sz.parts)
+            def _():
+                keep_ref[blk // sz.parts, pl.ds(to, sz.w_rows)] = piece
+
+            @pl.when(part != blk % sz.parts)
+            def _():
+                give_ref[blk // sz.parts, pl.ds(to, sz.w_rows)] = piece.astype(bf16)
+
+
+def norm_again_kernel(sz, scal_ref, vec_ref, *refs):
+    x_refs = refs[: sz.heads]
+    n_ref, u_ref = refs[sz.heads :]
+    gain, shift = vec_ref[0:1], vec_ref[1:2]
+    for slot in range(sz.heads):
+        normed, unit, _ = norm_forward(x_refs[slot][: sz.mine].astype(f32), gain, shift)
+        at = slice(slot * sz.mine, (slot + 1) * sz.mine)
+        n_ref[:, at] = normed.astype(bf16).T
+        u_ref[:, at] = unit.astype(bf16).T
+
+
+def project_grad_kernel(sz, scal_ref, sum_a_ref, sum_b_ref, got_ref, w_ref, n_ref, u_ref, *refs):
+    n = sz.heads
+    send_ref, d_scr = refs
+    half_run = sz.run // 2
+    for slot in range(n):
+        head = slot_head(sz, scal_ref, slot)
+        q_at = pl.multiple_of(head * half_run, half_run)
+        kv_at = pl.multiple_of(sz.half + head * sz.run, sz.run)
+        for seq in range(sz.seqs):
+            for part in range(sz.parts):
+                at = slot * sz.mine + seq * sz.sub + part * sz.run
+                first = got_ref[sz.task(seq, 0, part), pl.ds(q_at, half_run)]
+                second = got_ref[sz.task(seq, 1, part), pl.ds(q_at, half_run)]
+                low, high = halves(first, second)
+                d_scr[at : at + half_run, :LANES] = low
+                d_scr[at + half_run : at + sz.run, :LANES] = high
+                for local in range(sz.local):
+                    d_scr[at : at + sz.run, (1 + local) * LANES : (2 + local) * LANES] = got_ref[
+                        sz.task(seq, local, part), pl.ds(kv_at, sz.run)
+                    ]
+    d_proj = d_scr[...]
+    grad_w = dot_nn(n_ref[...], d_proj).astype(bf16)
+    weights = w_ref[...].astype(f32)
+    ones = jnp.ones((16, sz.tokens), bf16)
+    column = dot_nn(ones, d_proj)[:SMALL]
+    terms = [dot_nn(u_ref[...], d_proj) * weights, column[0:1] * weights]
+    ones = jnp.ones((16, (1 + sz.local) * LANES), bf16)
+    sums = []
+    for term in terms:
+        high = term.astype(bf16)
+        low = (term - high.astype(f32)).astype(bf16)
+        sums.append((dot_nt(ones, high) + dot_nt(ones, low))[0:1])
+    sums = jnp.concatenate(sums, axis=0)
+    for dev in range(sz.devices):
+        rows = slice(dev * sz.w_rows, (dev + 1) * sz.w_rows)
+        for i in range(1 + sz.local):
+            cols = slice(i * LANES, (i + 1) * LANES)
+            send_ref[dev, i * sz.w_rows : (i + 1) * sz.w_rows] = grad_w[rows, cols]
+    sum_q = column[:, :LANES]
+    sum_v = jnp.concatenate([column[:, LANES + HD : 2 * LANES], column[:, 2 * LANES + HD :]], axis=1)
+    wide = jnp.concatenate(
+        [sums, sum_b_ref[0:1], sum_a_ref[0:2], sum_b_ref[1:2], jnp.zeros((2, sz.width), f32)], axis=0
+    )
+    up_bias = jnp.broadcast_to(sum_a_ref[2:3], (SMALL, sz.width))
+    head = scal_ref[0]
+    per = sz.w_rows
+    at = sz.w_chunk
+    for low in (False, True):
+        def level(v):
+            high = v.astype(bf16).astype(f32)
+            return v - high if low else high
+
+        share = collect(level(wide), per, 0, (0, 6), sz.devices)
+        share += collect(level(sum_q), 2 * per, head * LANES, (6, 7), sz.devices)
+        share += collect(level(sum_v), 2 * per, sz.width + head * LANES, (6, 7), sz.devices)
+        share += collect(level(up_bias), 4 * per, head * sz.hidden_slice, (7, 8), sz.devices)
+        share = share.reshape(sz.devices, SMALL, LANES)
+        if low:
+            both = jnp.concatenate([kept, share], axis=1).astype(bf16)
+        kept = share
+    send_ref[:, at : at + 2 * SMALL, :] = both
+
+
+def input_partial_kernel(sz, scal_ref, d_ref, w_ref, *part_refs):
+    grad_one = dot_nt(d_ref[...], w_ref[...])
+    for slot, ref in enumerate(part_refs):
+        ref[...] = grad_one[slot * sz.mine : (slot + 1) * sz.mine].astype(ref.dtype)
+
+
+def input_grad_kernel(sz, scal_ref, vec_ref, grad_ref, x_ref, *refs):
+    out_ref = refs[sz.heads]
+    upstream = refs[0][...]
+    for ref in refs[1 : sz.heads]:
+        upstream = upstream + ref[...].astype(f32)
+    gain, shift = vec_ref[0:1], vec_ref[1:2]
+    _, unit, root = norm_forward(x_ref[: sz.mine].astype(f32), gain, shift)
+    out_ref[...] = (grad_ref[...] + norm_input_grad(upstream, unit, root, gain)).astype(bf16)
+
+
+def split_kernel(sz, scal_ref, own_ref, *refs):
+    n = sz.heads
+    got_refs, feed_refs, refs = refs[: sz.groups - 1], refs[sz.groups - 1 :][: n - 1], refs[-n - 1 :]
+    down_ref, piece_ref, *send_refs = refs
+
+    def total(rows):
+        value = own_ref[rows]
+        for ref in got_refs:
+            value = value + ref[rows].astype(f32)
+        return value
+
+    down_ref[...] = total(slice(0, sz.f_rows))
+    for slot in range(n):
+        to = slot_head(sz, scal_ref, slot)
+        at = pl.multiple_of(sz.f_rows + to * sz.w_rows, sz.w_rows)
+        up = total(pl.ds(at, sz.w_rows)).astype(bf16)
+        out = total(pl.ds(at + n * sz.w_rows, sz.w_rows))
+        ref = send_refs[slot - 1] if slot else piece_ref
+        base = sz.mine if slot else 0
+        if slot:
+            ref[: sz.mine] = feed_refs[slot - 1][...]
+        ref[base : base + sz.w_rows] = up
+        ref[base + sz.w_rows :] = out.astype(bf16)
+
+
+def final_kernel(sz, scal_ref, got_ref, *refs):
+    piece_refs, refs = refs[: sz.heads], refs[sz.heads :]
+    w_ref, up_ref, out_ref, *small_refs = refs
+    out = piece_refs[0][sz.w_rows :].astype(f32)
+    for ref in piece_refs[1:]:
+        out = out + ref[sz.mine + sz.w_rows :].astype(f32)
+    out_ref[...] = out
+    for slot in range(sz.heads):
+        at = pl.multiple_of(slot_head(sz, scal_ref, slot) * sz.hidden_slice, LANES)
+        base = sz.mine if slot else 0
+        piece = piece_refs[(sz.heads - slot) % sz.heads][base : base + sz.w_rows]
+        up_ref[:, pl.ds(at, sz.hidden_slice)] = piece.astype(f32)
+    for head in range(sz.heads):
+        total = jnp.zeros((sz.w_chunk, LANES), f32)
+        for blk in range(sz.blocks):
+            total = total + got_ref[head * sz.blocks + blk, : sz.w_chunk].astype(f32)
+        at = head * LANES
+        w_ref[:, at : at + LANES] = total[: sz.w_rows]
+        low, high = halves(total[sz.w_rows : 2 * sz.w_rows], total[2 * sz.w_rows :])
+        w_ref[:, sz.width + at : sz.width + at + LANES] = low
+        w_ref[:, 2 * sz.width + at : 2 * sz.width + at + LANES] = high
+    small = jnp.sum(got_ref[:, sz.w_chunk :, :].astype(f32), axis=0)
+    small = small[:SMALL] + small[SMALL:]
+    for i, ref in enumerate(small_refs):
+        ref[...] = small[i : i + 1, : ref.shape[1]]
+
+
+def on_device_fused(
+    sz,
+    layer_input,
+    segments,
+    token_valid,
+    attention_gain,
+    attention_shift,
+    project_weight,
+    project_bias,
+    output_weight,
+    output_bias,
+    feed_gain,
+    feed_shift,
+    up_weight,
+    up_bias,
+    down_weight,
+    down_bias,
+    cotangent,
+):
+    n = sz.heads
+    my_head = lax.axis_index("head")
+    my_blk = lax.axis_index("blk")
+    scal = jnp.stack([my_head, my_blk]).astype(i32)
+    geo = AttentionShape(sz.blocks, sz.part_rows, sz.parts, sz.run, sz.sub)
+    token_shape = (sz.mine, sz.width)
+
+    def call(kernel, name, arrays, outs, scratch=(), flops=10**8):
+        return local_call(functools.partial(kernel, sz), name, scal, arrays, outs, scratch, flops)
+
+    def around(x, step):
+        return lax.ppermute(x, "head", [(i, (i + step) % n) for i in range(n)])
+
+    def after(values, *earlier):
+        return lax.optimization_barrier((values, *earlier))[0]
+
+    def around_groups(x, step):
+        pairs = [
+            (g * sz.parts + p, (g + step) % sz.groups * sz.parts + p)
+            for g in range(sz.groups)
+            for p in range(sz.parts)
+        ]
+        return lax.ppermute(x, "blk", pairs)
+
+    def around_parts(x, step):
+        return lax.ppermute(x, "blk", within_group(sz.blocks, sz.parts, step))
+
+    x_mine = layer_input.reshape(token_shape)
+    g_mine = cotangent.reshape(token_shape)
+    small = [attention_gain, attention_shift, output_bias, feed_gain, feed_shift, down_bias]
+    small += [project_bias, up_bias]
+    column_rows = (n + 1) * sz.w_rows + sz.f_rows
+    (send,) = staged_call(
+        functools.partial(pack_kernel, sz),
+        "pack",
+        scal,
+        [project_weight, *[v.reshape(1, -1) for v in small]],
+        [((sz.devices, sz.w_chunk + SMALL, LANES), bf16)],
+        [pltpu.VMEM((SMALL, LANES), f32)],
+    )
+    got = lax.all_to_all(send, BOTH, split_axis=0, concat_axis=0, tiled=True)
+    own_tokens, column = staged_call(
+        functools.partial(pack_more_kernel, sz),
+        "pack_more",
+        after(scal, send),
+        [x_mine, g_mine, up_weight, output_weight, down_weight],
+        [((2 * sz.mine, sz.width), bf16), ((column_rows, sz.width), bf16)],
+    )
+    x_slots = [own_tokens] + [around(own_tokens, d) for d in range(1, n)]
+    columns = [column] + [around_groups(column, d) for d in range(1, sz.groups)]
+
+    my_part = my_blk % sz.parts
+    my_seq = (my_blk // sz.parts) // sz.local
+    scalars, bounds = attention_bounds(
+        segments, token_valid, my_seq, my_part, geo, sz.heads, sz.sub
+    )
+    got = after(got, scalars, bounds, *columns)
+    send, w_slice, vec = call(
+        project_kernel,
+        "project",
+        [got, *x_slots],
+        [
+            ((sz.blocks, sz.half + sz.part_rows, LANES), bf16),
+            far((sz.width, (1 + sz.local) * LANES), bf16),
+            far((SMALL, sz.width), f32),
+        ],
+        flops=30 * 10**9,
+    )
+    columns += [around_parts(after(v, send), d) for d in range(1, sz.parts) for v in columns]
+    *pays, w_down = call(
+        regroup_kernel,
+        "regroup",
+        columns,
+        [far((2 * sz.head_rows, sz.width), bf16)]
+        + [((2 * sz.head_rows, sz.width), bf16)] * (n - 1)
+        + [far((sz.width, sz.width), bf16)],
+    )
+    pays = [pays[0]] + [around(pays[d], d) for d in range(1, n)]
+    turned = far((sz.width, sz.tokens), bf16)
+    n_one, u_one = call(
+        norm_again_kernel, "norm_again", [vec, *x_slots], [turned, turned]
+    )
+    task = exchange(send, "blk")
+    task = after(task, w_down, n_one)
+    others = [around_parts(task, step) for step in range(1, sz.parts)]
+    o_task, ot, lse = attention_forward(geo, scalars, [task, *others], bounds)
+    mixed = exchange(o_task, "blk")
+    m_slots = [mixed] + [around(mixed, d) for d in range(1, n)]
+
+    outs = call(
+        feed_kernel,
+        "feed",
+        [vec, w_down, *x_slots, *pays, *m_slots],
+        [far(token_shape, f32)]
+        + [(token_shape, bf16)] * (n - 1)
+        + [far(token_shape, f32)]
+        + [far(token_shape, bf16)] * (n - 1)
+        + [far(token_shape, f32)]
+        + [((n, sz.mine, sz.hidden_slice), bf16)] * 2
+        + [((n, *token_shape), bf16), far(token_shape, bf16), far((SMALL, sz.width), f32)],
+        [
+            pltpu.VMEM((sz.width, sz.hidden_slice), bf16),
+            pltpu.VMEM((n, *token_shape), bf16),
+        ],
+        flops=30 * 10**9,
+    )
+    grad_two, feed = outs[:n], outs[n : 2 * n]
+    middle, activated, grad_hidden, n_two, mixed_own, feed_sums = outs[2 * n :]
+    grad_two = [grad_two[0]] + [around(grad_two[d], -d) for d in range(1, n)]
+
+    def shared(rows):
+        shape = (sz.groups, rows, sz.width)
+        return [far(shape, f32), far(shape, bf16)]
+
+    keep, give = call(
+        feed_grad_kernel,
+        "feed_grad",
+        [activated, grad_hidden, n_two, *x_slots],
+        shared(sz.f_rows + n * sz.w_rows),
+    )
+    grad_two[0] = after(grad_two[0], keep)
+
+    grad_middle, branch, send, branch_sums = call(
+        middle_grad_kernel,
+        "middle_grad",
+        [vec, middle, own_tokens, *pays, *grad_two],
+        [
+            far(token_shape, f32),
+            far(token_shape, bf16),
+            ((sz.devices, sz.run // 2, LANES), bf16),
+            far((SMALL, sz.width), f32),
+        ],
+        flops=30 * 10**9,
+    )
+    do_task = exchange(send, BOTH)
+    given = around_parts(give, 1)
+    keep_out, give = call(
+        out_grad_kernel,
+        "out_grad",
+        [mixed_own, after(branch, send)],
+        shared(n * sz.w_rows),
+    )
+    rows = sz.f_rows + 2 * n * sz.w_rows
+    w_sum = call(
+        part_sum_kernel,
+        "part_sum",
+        [keep, given, keep_out, around_parts(give, 1)],
+        [far((rows, sz.width), f32)] + [((rows, sz.width), bf16)] * (sz.groups - 1),
+    )
+    w_pieces = [around_groups(w_sum[d], d) for d in range(1, sz.groups)]
+    dq, dkv, *dkv_others = attention_backward(
+        geo, do_tile_grouped, scalars, [task, *others], do_task, bounds, ot, lse
+    )
+    dkv_others[0] = after(dkv_others[0], *w_pieces)
+    for step in range(1, sz.parts):
+        back = within_group(sz.blocks, sz.parts, -step)
+        dkv = dkv + lax.ppermute(dkv_others[step - 1], "blk", back).astype(f32)
+    send = jnp.concatenate([dq, dkv.astype(bf16)], axis=1)
+    got = exchange(send, "blk")
+    down_grad, piece, *rest = call(
+        split_kernel,
+        "split",
+        [after(w_sum[0], send), *w_pieces, *feed[1:]],
+        [((sz.f_rows, sz.width), f32), far((2 * sz.w_rows, sz.width), bf16)]
+        + [far((sz.mine + 2 * sz.w_rows, sz.width), bf16)] * (n - 1),
+    )
+    rest = [around(v, -d - 1) for d, v in enumerate(rest)]
+    got = after(got, *rest)
+    send, d_proj = call(
+        project_grad_kernel,
+        "project_grad",
+        [feed_sums, branch_sums, got, w_slice, n_one, u_one],
+        [
+            ((sz.devices, sz.w_chunk + 2 * SMALL, LANES), bf16),
+            far((sz.tokens, (1 + sz.local) * LANES), bf16),
+        ],
+        flops=30 * 10**9,
+    )
+    got = exchange(send, BOTH)
+    outs = call(
+        input_partial_kernel,
+        "input_partial",
+        [d_proj, w_slice],
+        [(token_shape, f32)] + [(token_shape, bf16)] * (n - 1),
+    )
+    grad_one = [outs[0]] + [around(outs[d], -d) for d in range(1, n)]
+    (input_grad,) = call(
+        input_grad_kernel,
+        "input_grad",
+        [vec, grad_middle, own_tokens, *grad_one],
+        [(token_shape, bf16)],
+    )
+    layer_output = middle + feed[0] + vec[5:6]
+    for v in rest:
+        layer_output = layer_output + v[: sz.mine].astype(f32)
+    layer_output = layer_output.astype(bf16)
+    w_grad, up_grad, out_grad, *owned = call(
+        final_kernel,
+        "final",
+        [got, piece, *rest],
+        [
+            ((sz.w_rows, 3 * sz.width), f32),
+            ((sz.w_rows, n * sz.hidden_slice), f32),
+            ((sz.w_rows, sz.width), f32),
+        ]
+        + [((1, v.shape[0]), f32) for v in small],
+    )
+    owned = [v.reshape(-1) for v in owned]
+    return (
+        layer_output.reshape(layer_input.shape),
+        input_grad.reshape(layer_input.shape),
+        owned[0],
+        owned[1],
+        w_grad,
+        owned[6],
+        out_grad,
+        owned[2],
+        owned[3],
+        owned[4],
+        up_grad,
+        owned[7],
+        down_grad,
+        owned[5],
+    )
+
+
+def on_device(*arguments):
+    layer_input, up_weight = arguments[0], arguments[11]
+    seqs, _, sub, width = layer_input.shape
+    sz = Sizes(
+        lax.axis_size("head"), lax.axis_size("blk"), seqs, sub, width, up_weight.shape[1]
+    )
+    if sz.fits():
+        return on_device_fused(sz, *arguments)
+    return on_device_general(*arguments)
+
+
 def solution(mesh):
     tokens = P(None, "blk", "head", None)
     vector = P(BOTH)

time: 272 us -> 182 us (0.67)
  blocking collectives: 41.8 us -> 0 us
  local copies, waits for them, and re-layouts: 43.3 us -> 8.49 us
  Pallas kernels: 16.8 us -> 49.3 us
  waiting for transfers between devices: 77.5 us -> 47.5 us
  starting transfers between devices: 44.4 us -> 70 us
  other arithmetic: 21 us -> 4.33 us
  between operations: 15.7 us -> 1.98 us
  matrix products: 11 us -> 0 us
    ppermute x2 -> x32, starting transfers between devices: 0.56 us -> 43.3 us  [the longest x18 27.6 us: around(): return lax.ppermute(x, 'head', [(i, (i + step) % n) for i in range(n)])]
    all_gather x4 -> x0, blocking collectives: 41.8 us -> none  [the longest x3 30.9 us: gather_head(): return lax.all_gather(x, 'head', axis=0, tiled=False)]
    ppermute x2 -> x32, waiting for transfers between devices: 1.91 us -> 36.1 us  [the longest x18 27.9 us: around(): return lax.ppermute(x, 'head', [(i, (i + step) % n) for i in range(n)])]
    reduce_scatter x2 -> x0, waiting for transfers between devices: 33.3 us -> none  [over_blocks(): return lax.psum_scatter(partial, 'blk', scatter_dimension=0, tiled=True)]
    pallas_call x2 -> x17, Pallas kernels: 16.8 us -> 49.3 us  [the longest x15 44.3 us: local_call(): pl.pallas_call(kernel, out_shape=tuple((o[0] if len(o) == 1 else jax.Shap...]
    all_to_all x11 -> x5, waiting for transfers between devices: 42.2 us -> 10.5 us  [exchange(): return lax.all_to_all(x, axis, split_axis=0, concat_axis=0, tiled=True)]
    all_to_all x11 -> x5, starting transfers between devices: 43.7 us -> 23.1 us  [exchange(): return lax.all_to_all(x, axis, split_axis=0, concat_axis=0, tiled=True)]
    reshape x38 -> x3, local copies, waits for them, and re-layouts: 12.6 us -> 0.18 us  [the longest x1 0.09 us: attention_bounds(): own_seg = seg.reshape(geo.blocks * heads, geo.parts, geo.run)]
  transfers between devices with their start and end apart: 16 -> 38, of which waited for: 10 -> 17; matrix products, arithmetic and copies ran while one was open for 16% -> 3% of each run, Pallas kernels for 3% -> 18%
where the time goes in v2:
time: 182 us
  starting transfers between devices  70 us (38%)
  Pallas kernels  49.3 us (27%)
  waiting for transfers between devices  47.5 us (26%)
  local copies, waits for them, and re-layouts  8.49 us (5%)
  other arithmetic  4.33 us (2%)
  between operations  1.98 us (1%)
    pallas_call x15, Pallas kernels, local_call(): pl.pallas_call(kernel, out_shape=tuple((o[0] if len(o) == 1 else jax.Shap...  44.3 us
    ppermute x18, waiting for transfers between devices, around(): return lax.ppermute(x, 'head', [(i, (i + step) % n) for i in range(n)])  27.9 us
    ppermute x18, starting transfers between devices, around(): return lax.ppermute(x, 'head', [(i, (i + step) % n) for i in range(n)])  27.6 us
    all_to_all x5, starting transfers between devices, exchange(): return lax.all_to_all(x, axis, split_axis=0, concat_axis=0, tiled=True)  23.1 us
    ppermute x6, starting transfers between devices, around_groups(): return lax.ppermute(x, 'blk', pairs)  14.7 us
    all_to_all x5, waiting for transfers between devices, exchange(): return lax.all_to_all(x, axis, split_axis=0, concat_axis=0, tiled=True)  10.5 us
    unnamed x74, local copies, waits for them, and re-layouts  6.49 us
    ppermute x6, waiting for transfers between devices, around_groups(): return lax.ppermute(x, 'blk', pairs)  6.3 us
  transfers between devices with their start and end apart: 38, of which 17 were waited for; matrix products, arithmetic and copies ran while one was open for 3% of the time, Pallas kernels for 18%

profile of v2, /device:TPU:0, one launch (start us, length us, event | category | flops | bytes accessed | tf_op | source)
XLA Modules:
  0.0 181.6 jit_solution(3983514163875783297)
XLA Ops:
  1.3 2.4 %pack.1 = bf16[32,56,128]{2,1,0:T(8,128)(2,1)} custom-call(s32[2]{0:T(128)} %pad_add_fusion.scal_ref, bf16[16,1536]{1,0:T(8,128)(2,1)} %refs_0_.1, bf16[1,16]{1,0:T(2,128)(2,1)} %bitcast.41, bf16[1,16]{1,0:T(2,128)(2,1)} %bitcast.42, bf16[1,16]{1,0:T(2,128)(2,1)} %bitcast.43, bf16[1,16]{1,0:T(2,128)(2,1)} %bitcast.44, bf16[1,16]{1,0:T(2,128)(2,1)} %bitcast.45, ...), custom_call_target="tpu_custom_call" | custom-call | tf_op jit(solution)/shard_map/pack/pallas_call | solution.py:637
  3.7 2.6 %pack_more.1 = (bf16[256,512]{1,0:T(8,128)(2,1)}, bf16[144,512]{1,0:T(8,128)(2,1)}) custom-call(s32[2]{0:T(128)} %pad_add_fusion.scal_ref, bf16[128,512]{1,0:T(8,128)(2,1)} %bitcast.32, bf16[128,512]{1,0:T(8,128)(2,1)} %bitcast.33, bf16[16,2048]{1,0:T(8,128)(2,1)} %refs_2_.1, bf16[16,512]{1,0:T(8,128)(2,1)} %refs_3_.1, bf16[64,512]{1,0:T(8,128)(2,1)} %refs_4_.1), custom_call_target="tpu_custom_call" | custom-call | tf_op jit(solution)/shard_map/pack_more/pallas_call | solution.py:637
  6.4 3.1 %collective-permute-start = (bf16[144,512]{1,0:T(8,128)(2,1)}, bf16[144,512]{1,0:T(8,128)(2,1)S(1)}, u32[]{:S(2)}, u32[]{:S(2)}) collective-permute-start(bf16[144,512]{1,0:T(8,128)(2,1)} %get-tuple-element.98.refs_0_), channel_id=1, source_target_pairs={{0,2},{1,3},{2,4},{3,5},{4,6},{5,7},{6,0},{7,1},{8,10},{9,11},{10,... | collective-permute-start | bytes 442376 | tf_op jit(solution)/shard_map/ppermute | solution.py:1124
  9.5 2.6 %collective-permute-start.1 = (bf16[144,512]{1,0:T(8,128)(2,1)}, bf16[144,512]{1,0:T(8,128)(2,1)S(1)}, u32[]{:S(2)}, u32[]{:S(2)}) collective-permute-start(bf16[144,512]{1,0:T(8,128)(2,1)} %get-tuple-element.98.refs_0_), channel_id=1, source_target_pairs={{0,4},{1,5},{2,6},{3,7},{4,0},{5,1},{6,2},{7,3},{8,12},{9,13},{10,... | collective-permute-start | bytes 442376 | tf_op jit(solution)/shard_map/ppermute | solution.py:1124
  12.0 3.6 %all-to-all-start = ((bf16[32,56,128]{2,1,0:T(8,128)(2,1)}), bf16[32,56,128]{2,1,0:T(8,128)(2,1)S(1)}, u32[]{:S(2)}, u32[]{:S(2)}) async-start(bf16[32,56,128]{2,1,0:T(8,128)(2,1)} %pack.1), calls=%async_computation | async-start | bytes 917504 | tf_op jit(solution)/shard_map/all_to_all | solution.py:1142
  15.6 1.8 %collective-permute-start.3 = (bf16[256,512]{1,0:T(8,128)(2,1)}, bf16[256,512]{1,0:T(8,128)(2,1)S(1)}, u32[]{:S(2)}, u32[]{:S(2)}) collective-permute-start(bf16[256,512]{1,0:T(8,128)(2,1)} %get-tuple-element.95.refs_0_.tokens_ref.x_ref), channel_id=1, source_target_pairs={{0,8},{8,16},{16,24},{24,0},{1,9},{9,17},{17,25},{25,1},{2,10},{10... | collective-permute-start | bytes 786440 | tf_op jit(solution)/shard_map/ppermute | solution.py:1113
  17.5 1.5 collective-permute-start.4
  18.9 1.5 collective-permute-start.5
  24.1 1.0 convert_reduce_fusion
  25.2 3.4 %collective-permute-start.2 = (bf16[144,512]{1,0:T(8,128)(2,1)S(1)}, bf16[144,512]{1,0:T(8,128)(2,1)S(1)}, u32[]{:S(2)}, u32[]{:S(2)}) collective-permute-start(bf16[144,512]{1,0:T(8,128)(2,1)S(1)} %copy-done.9), channel_id=1, source_target_pairs={{0,6},{1,7},{2,0},{3,1},{4,2},{5,3},{6,4},{7,5},{8,14},{9,15},{10,... | collective-permute-start | bytes 442376 | tf_op jit(solution)/shard_map/ppermute | solution.py:1124
  28.7 4.0 %collective-permute-done.2.refs_3_ = bf16[144,512]{1,0:T(8,128)(2,1)S(1)} collective-permute-done((bf16[144,512]{1,0:T(8,128)(2,1)S(1)}, bf16[144,512]{1,0:T(8,128)(2,1)S(1)}, u32[]{:S(2)}, u32[]{:S(2)}) %collective-permute-start.2) | collective-permute-done | bytes 147488 | tf_op jit(solution)/shard_map/ppermute | solution.py:1124
  32.7 0.9 all-to-all-done.got_ref
  33.6 1.6 collective-permute-done.4.refs_2_
  35.3 2.2 %project.1 = (bf16[8,192,128]{2,1,0:T(8,128)(2,1)}, bf16[512,384]{1,0:T(8,128)(2,1)}, f32[8,512]{1,0:T(8,128)}) custom-call(s32[2]{0:T(128)S(1)} %copy-done.15, bf16[32,56,128]{2,1,0:T(8,128)(2,1)S(1)} %all-to-all-done.got_ref, bf16[256,512]{1,0:T(8,128)(2,1)S(1)} %copy-done.1, bf16[256,512]{1,0:T(8,128)(2,1)S(1)} %collective-permute-done.3.refs_1_, ...), custom_call_target="tpu_custom_call" | custom-call | flops 30000001024 | bytes 1000000 | tf_op jit(solution)/shard_map/project/pallas_call | solution.py:203
  37.5 4.5 %all-to-all-start.1 = ((bf16[8,192,128]{2,1,0:T(8,128)(2,1)}), bf16[8,192,128]{2,1,0:T(8,128)(2,1)S(1)}, u32[]{:S(2)}, u32[]{:S(2)}) async-start(bf16[8,192,128]{2,1,0:T(8,128)(2,1)} %get-tuple-element.97), calls=%async_computation.1 | async-start | bytes 786432 | tf_op jit(solution)/shard_map/all_to_all | solution.py:295
  43.7 2.2 %norm_again.1 = (bf16[512,512]{1,0:T(8,128)(2,1)}, bf16[512,512]{1,0:T(8,128)(2,1)}) custom-call(s32[2]{0:T(128)S(1)} %copy-done.15, f32[8,512]{1,0:T(8,128)S(1)} %copy-done.13, bf16[256,512]{1,0:T(8,128)(2,1)S(1)} %copy-done.1, bf16[256,512]{1,0:T(8,128)(2,1)S(1)} %collective-permute-done.3.refs_1_, bf16[256,512]{1,0:T(8,128)(2,1)S(1)} %collective-permute-done.4.refs_2_, ...), custom_call_target="tpu_custom_call" | custom-call | flops 100000000 | bytes 1000000 | tf_op jit(solution)/shard_map/norm_again/pallas_call | solution.py:203
  45.9 1.6 regroup.1
  48.2 6.3 %all-to-all-done.1.refs_0_ = bf16[8,192,128]{2,1,0:T(8,128)(2,1)S(1)} async-done(((bf16[8,192,128]{2,1,0:T(8,128)(2,1)}), bf16[8,192,128]{2,1,0:T(8,128)(2,1)S(1)}, u32[]{:S(2)}, u32[]{:S(2)}) %all-to-all-start.1) | async-done | bytes 393248 | tf_op jit(solution)/shard_map/all_to_all | solution.py:295
  54.5 1.3 collective-permute-start.10
  56.2 9.1 %attention_forward.1 = (bf16[8,64,128]{2,1,0:T(8,128)(2,1)}, f32[4,64,256]{2,1,0:T(8,128)}, f32[4,8,256]{2,1,0:T(8,128)}) custom-call(s32[6]{0:T(128)S(1)} %pad_add_fusion.1.scal_ref, bf16[8,192,128]{2,1,0:T(8,128)(2,1)S(1)} %all-to-all-done.1.refs_0_, bf16[8,192,128]{2,1,0:T(8,128)(2,1)S(1)} %collective-permute-done.13.refs_1_, ...), custom_call_target="tpu_custom_call" | custom-call | flops 30000001024 | bytes 1000000 | tf_op jit(solution)/shard_map/attention_forward/pallas_call | solution.py:203
  65.3 3.4 %all-to-all-start.2 = ((bf16[8,64,128]{2,1,0:T(8,128)(2,1)}), bf16[8,64,128]{2,1,0:T(8,128)(2,1)S(1)}, u32[]{:S(2)}, u32[]{:S(2)}) async-start(bf16[8,64,128]{2,1,0:T(8,128)(2,1)} %get-tuple-element.109), calls=%async_computation.2 | async-start | bytes 262144 | tf_op jit(solution)/shard_map/all_to_all | solution.py:295
  68.7 1.2 collective-permute-start.11
  69.9 1.5 collective-permute-start.12
  71.5 4.0 %all-to-all-done.2.refs_8_ = bf16[8,64,128]{2,1,0:T(8,128)(2,1)S(1)} async-done(((bf16[8,64,128]{2,1,0:T(8,128)(2,1)}), bf16[8,64,128]{2,1,0:T(8,128)(2,1)S(1)}, u32[]{:S(2)}, u32[]{:S(2)}) %all-to-all-start.2) | async-done | bytes 131104 | tf_op jit(solution)/shard_map/all_to_all | solution.py:295
  75.4 1.2 collective-permute-start.14
  77.3 2.2 %collective-permute-start.16 = (bf16[8,64,128]{2,1,0:T(8,128)(2,1)S(1)}, bf16[8,64,128]{2,1,0:T(8,128)(2,1)S(1)}, u32[]{:S(2)}, u32[]{:S(2)}) collective-permute-start(bf16[8,64,128]{2,1,0:T(8,128)(2,1)S(1)} %all-to-all-done.2.refs_8_), channel_id=1, source_target_pairs={{0,24},{8,0},{16,8},{24,16},{1,25},{9,1},{17,9},{25,17},{2,26},{10... | collective-permute-start | bytes 393224 | tf_op jit(solution)/shard_map/ppermute | solution.py:1113
  79.5 3.3 %collective-permute-done.14.refs_9_ = bf16[8,64,128]{2,1,0:T(8,128)(2,1)S(1)} collective-permute-done((bf16[8,64,128]{2,1,0:T(8,128)(2,1)S(1)}, bf16[8,64,128]{2,1,0:T(8,128)(2,1)S(1)}, u32[]{:S(2)}, u32[]{:S(2)}) %collective-permute-start.14) | collective-permute-done | bytes 131104 | tf_op jit(solution)/shard_map/ppermute | solution.py:1113
  82.8 1.3 collective-permute-done.15.refs_10_
  84.1 4.3 %feed.1 = (f32[128,512]{1,0:T(8,128)}, bf16[128,512]{1,0:T(8,128)(2,1)S(1)}, bf16[128,512]{1,0:T(8,128)(2,1)S(1)}, bf16[128,512]{1,0:T(8,128)(2,1)S(1)}, f32[128...) custom-call(s32[2]{0:T(128)S(1)} %copy-done.15, ...), custom_call_target="tpu_custom_call" | custom-call | flops 30000001024 | bytes 1000000 | tf_op jit(solution)/shard_map/feed/pallas_call | solution.py:203
  88.4 6.0 %collective-permute-start.18 = (bf16[128,512]{1,0:T(8,128)(2,1)S(1)}, bf16[128,512]{1,0:T(8,128)(2,1)S(1)}, u32[]{:S(2)}, u32[]{:S(2)}) collective-permute-start(bf16[128,512]{1,0:T(8,128)(2,1)S(1)} %get-tuple-element.120), channel_id=1, source_target_pairs={{0,24},{8,0},{16,8},{24,16},{1,25},{9,1},{17,9},{25,17},{2,26},{10... | collective-permute-start | bytes 393224 | tf_op jit(solution)/shard_map/ppermute | solution.py:1113
  94.4 1.4 collective-permute-start.19
  95.8 2.6 %feed_grad.1 = (f32[4,128,512]{2,1,0:T(8,128)}, bf16[4,128,512]{2,1,0:T(8,128)(2,1)}) custom-call(s32[2]{0:T(128)S(1)} %copy-done.15, bf16[4,128,512]{2,1,0:T(8,128)(2,1)S(1)} %get-tuple-element.112.act_ref, bf16[4,128,512]{2,1,0:T(8,128)(2,1)S(1)} %get-tuple-element.113.dh_ref, bf16[4,128,512]{2,1,0:T(8,128)(2,1)S(1)} %get-tuple-element.114.n_ref, ...), custom_call_target="tpu_custom_call" | custom-call | flops 100000000 | bytes 1000000 | tf_op jit(solution)/shard_map/feed_grad/pallas_call | solution.py:203
  98.4 3.8 %collective-permute-done.19.refs_6_ = bf16[128,512]{1,0:T(8,128)(2,1)S(1)} collective-permute-done((bf16[128,512]{1,0:T(8,128)(2,1)S(1)}, bf16[128,512]{1,0:T(8,128)(2,1)S(1)}, u32[]{:S(2)}, u32[]{:S(2)}) %collective-permute-start.19) | collective-permute-done | bytes 131104 | tf_op jit(solution)/shard_map/ppermute | solution.py:1113
  102.2 2.4 %middle_grad.1 = (f32[128,512]{1,0:T(8,128)}, bf16[128,512]{1,0:T(8,128)(2,1)}, bf16[32,16,128]{2,1,0:T(8,128)(2,1)}, f32[8,512]{1,0:T(8,128)}) custom-call(s32[2]{0:T(128)S(1)} %copy-done.15, f32[8,512]{1,0:T(8,128)S(1)} %copy-done.14, f32[128,512]{1,0:T(8,128)S(1)} %copy-done.8, bf16[256,512]{1,0:T(8,128)(2,1)S(1)} %copy-done.1, ...), custom_call_target="tpu_custom_call" | custom-call | flops 30000001024 | bytes 1000000 | tf_op jit(solution)/shard_map/middle_grad/pallas_call | solution.py:203
  104.6 0.9 copy-done.29
  105.5 2.0 %out_grad.1 = (f32[4,64,512]{2,1,0:T(8,128)}, bf16[4,64,512]{2,1,0:T(8,128)(2,1)}) custom-call(s32[2]{0:T(128)S(1)} %copy-done.15, bf16[128,512]{1,0:T(8,128)(2,1)S(1)} %copy-done.28, bf16[128,512]{1,0:T(8,128)(2,1)S(1)} %copy-done.29), custom_call_target="tpu_custom_call" | custom-call | flops 100000000 | bytes 1000000 | tf_op jit(solution)/shard_map/out_grad/pallas_call | solution.py:203
  107.5 4.3 %all-to-all-start.3 = ((bf16[32,16,128]{2,1,0:T(8,128)(2,1)}), bf16[32,16,128]{2,1,0:T(8,128)(2,1)S(1)}, u32[]{:S(2)}, u32[]{:S(2)}) async-start(bf16[32,16,128]{2,1,0:T(8,128)(2,1)} %get-tuple-element.124), calls=%async_computation.3 | async-start | bytes 262144 | tf_op jit(solution)/shard_map/all_to_all | solution.py:295
  111.8 1.0 copy-done.3
  112.8 1.6 part_sum.1
  114.5 1.8 collective-permute-start.22
  116.2 2.4 %collective-permute-start.23 = (bf16[192,512]{1,0:T(8,128)(2,1)}, bf16[192,512]{1,0:T(8,128)(2,1)S(1)}, u32[]{:S(2)}, u32[]{:S(2)}) collective-permute-start(bf16[192,512]{1,0:T(8,128)(2,1)} %get-tuple-element.135), channel_id=1, source_target_pairs={{0,4},{1,5},{2,6},{3,7},{4,0},{5,1},{6,2},{7,3},{8,12},{9,13},{10,... | collective-permute-start | bytes 589832 | tf_op jit(solution)/shard_map/ppermute | solution.py:1124
  118.7 1.4 collective-permute-start.24
  120.1 1.0 copy-done.21
  121.1 0.9 copy-done.31
  122.0 7.8 %attention_backward.1 = (bf16[8,64,128]{2,1,0:T(8,128)(2,1)S(1)}, f32[8,128,128]{2,1,0:T(8,128)S(1)}, bf16[8,128,128]{2,1,0:T(8,128)(2,1)S(1)}) custom-call(s32[6]{0:T(128)S(1)} %pad_add_fusion.1.scal_ref, bf16[8,192,128]{2,1,0:T(8,128)(2,1)S(1)} %all-to-all-done.1.refs_0_, bf16[8,192,128]{2,1,0:T(8,128)(2,1)S(1)} %copy-done.21, ...), custom_call_target="tpu_custom_call" | custom-call | flops 30000001024 | bytes 1000000 | tf_op jit(solution)/shard_map/attention_backward/pallas_call | solution.py:203
  129.8 2.3 %collective-permute-done.23.refs_1_ = bf16[192,512]{1,0:T(8,128)(2,1)S(1)} collective-permute-done((bf16[192,512]{1,0:T(8,128)(2,1)}, bf16[192,512]{1,0:T(8,128)(2,1)S(1)}, u32[]{:S(2)}, u32[]{:S(2)}) %collective-permute-start.23) | collective-permute-done | bytes 196640 | tf_op jit(solution)/shard_map/ppermute | solution.py:1124
  132.1 1.5 collective-permute-done.25
  133.8 0.8 pad_maximum_fusion
  134.6 7.2 %all-to-all-start.4 = ((bf16[8,192,128]{2,1,0:T(8,128)(2,1)}), bf16[8,192,128]{2,1,0:T(8,128)(2,1)S(1)}, u32[]{:S(2)}, u32[]{:S(2)}) async-start(bf16[8,192,128]{2,1,0:T(8,128)(2,1)} %pad_maximum_fusion), calls=%async_computation.4 | async-start | bytes 786432 | tf_op jit(solution)/shard_map/all_to_all | solution.py:295
  141.8 1.4 split.1
  143.2 2.4 %collective-permute-start.26 = (bf16[160,512]{1,0:T(8,128)(2,1)}, bf16[160,512]{1,0:T(8,128)(2,1)S(1)}, u32[]{:S(2)}, u32[]{:S(2)}) collective-permute-start(bf16[160,512]{1,0:T(8,128)(2,1)} %get-tuple-element.142), channel_id=1, source_target_pairs={{0,24},{8,0},{16,8},{24,16},{1,25},{9,1},{17,9},{25,17},{2,26},{10... | collective-permute-start | bytes 491528 | tf_op jit(solution)/shard_map/ppermute | solution.py:1113
  146.7 3.8 %collective-permute-done.26.refs_1_ = bf16[160,512]{1,0:T(8,128)(2,1)S(1)} collective-permute-done((bf16[160,512]{1,0:T(8,128)(2,1)}, bf16[160,512]{1,0:T(8,128)(2,1)S(1)}, u32[]{:S(2)}, u32[]{:S(2)}) %collective-permute-start.26) | collective-permute-done | bytes 163872 | tf_op jit(solution)/shard_map/ppermute | solution.py:1113
  150.5 5.2 %collective-permute-done.27.refs_2_ = bf16[160,512]{1,0:T(8,128)(2,1)S(1)} collective-permute-done((bf16[160,512]{1,0:T(8,128)(2,1)}, bf16[160,512]{1,0:T(8,128)(2,1)S(1)}, u32[]{:S(2)}, u32[]{:S(2)}) %collective-permute-start.27) | collective-permute-done | bytes 163872 | tf_op jit(solution)/shard_map/ppermute | solution.py:1113
  155.7 1.0 copy-done.18
  156.7 3.2 %project_grad.1 = (bf16[32,64,128]{2,1,0:T(8,128)(2,1)}, bf16[512,384]{1,0:T(8,128)(2,1)}) custom-call(s32[2]{0:T(128)S(1)} %copy-done.15, f32[8,512]{1,0:T(8,128)S(1)} %copy-done.33, f32[8,512]{1,0:T(8,128)S(1)} %copy-done.34, bf16[8,192,128]{2,1,0:T(8,128)(2,1)S(1)} %all-to-all-done.4.got_ref, bf16[512,384]{1,0:T(8,128)(2,1)S(1)} %copy-done.4, ...), custom_call_target="tpu_custom_call" | custom-call | flops 30000001024 | bytes 1000000 | tf_op jit(solution)/shard_map/project_grad/pallas_call | solution.py:203
  160.0 3.8 %all-to-all-start.5 = ((bf16[32,64,128]{2,1,0:T(8,128)(2,1)}), bf16[32,64,128]{2,1,0:T(8,128)(2,1)S(1)}, u32[]{:S(2)}, u32[]{:S(2)}) async-start(bf16[32,64,128]{2,1,0:T(8,128)(2,1)} %get-tuple-element.156), calls=%async_computation.5 | async-start | bytes 1048576 | tf_op jit(solution)/shard_map/all_to_all | solution.py:295
  163.8 1.0 input_partial.1
  164.8 2.7 %collective-permute-start.29 = (bf16[128,512]{1,0:T(8,128)(2,1)S(1)}, bf16[128,512]{1,0:T(8,128)(2,1)S(1)}, u32[]{:S(2)}, u32[]{:S(2)}) collective-permute-start(bf16[128,512]{1,0:T(8,128)(2,1)S(1)} %get-tuple-element.153), channel_id=1, source_target_pairs={{0,24},{8,0},{16,8},{24,16},{1,25},{9,1},{17,9},{25,17},{2,26},{10... | collective-permute-start | bytes 393224 | tf_op jit(solution)/shard_map/ppermute | solution.py:1113
  168.7 0.7 add_convert_fusion.1
  169.4 4.3 %collective-permute-done.29.refs_1_ = bf16[128,512]{1,0:T(8,128)(2,1)S(1)} collective-permute-done((bf16[128,512]{1,0:T(8,128)(2,1)S(1)}, bf16[128,512]{1,0:T(8,128)(2,1)S(1)}, u32[]{:S(2)}, u32[]{:S(2)}) %collective-permute-start.29) | collective-permute-done | bytes 131104 | tf_op jit(solution)/shard_map/ppermute | solution.py:1113
  173.7 3.5 %collective-permute-done.30.refs_2_ = bf16[128,512]{1,0:T(8,128)(2,1)S(1)} collective-permute-done((bf16[128,512]{1,0:T(8,128)(2,1)S(1)}, bf16[128,512]{1,0:T(8,128)(2,1)S(1)}, u32[]{:S(2)}, u32[]{:S(2)}) %collective-permute-start.30) | collective-permute-done | bytes 131104 | tf_op jit(solution)/shard_map/ppermute | solution.py:1113
  177.2 1.1 collective-permute-done.31.refs_3_
  178.4 1.5 input_grad.1
  180.2 1.3 final.1
  (136 shorter events, 10.1 us)
Async XLA Ops:
  0.6 19.8 %copy-start = (s32[2,2048]{1,0:T(2,128)S(1)}, s32[2,2048]{1,0:T(2,128)}, u32[]{:S(2)}) copy-start(s32[2,2048]{1,0:T(2,128)} %param.18) | copy-start | bytes 49156
  0.7 22.0 %copy-start.36 = (s32[2,2048]{1,0:T(2,128)S(1)}, s32[2,2048]{1,0:T(2,128)}, u32[]{:S(2)}) copy-start(s32[2,2048]{1,0:T(2,128)} %param.17) | copy-start | bytes 49156
  3.7 31.5 %copy-start.15 = (s32[2]{0:T(128)S(1)}, s32[2]{0:T(128)}, u32[]{:S(2)}) copy-start(s32[2]{0:T(128)} %pad_add_fusion.scal_ref) | copy-start | bytes 28
  6.4 18.9 %copy-start.9 = (bf16[144,512]{1,0:T(8,128)(2,1)S(1)}, bf16[144,512]{1,0:T(8,128)(2,1)}, u32[]{:S(2)}) copy-start(bf16[144,512]{1,0:T(8,128)(2,1)} %get-tuple-element.98.refs_0_) | copy-start | bytes 442372
  6.4 28.9 %copy-start.1 = (bf16[256,512]{1,0:T(8,128)(2,1)S(1)}, bf16[256,512]{1,0:T(8,128)(2,1)}, u32[]{:S(2)}) copy-start(bf16[256,512]{1,0:T(8,128)(2,1)} %get-tuple-element.95.refs_0_.tokens_ref.x_ref) | copy-start | bytes 786436
  6.4 18.8 %collective-permute-start = (bf16[144,512]{1,0:T(8,128)(2,1)}, bf16[144,512]{1,0:T(8,128)(2,1)S(1)}, u32[]{:S(2)}, u32[]{:S(2)}) collective-permute-start(bf16[144,512]{1,0:T(8,128)(2,1)} %get-tuple-element.98.refs_0_), channel_id=1, source_target_pairs={{0,2},{1,3},{2,4},{3,5},{4,6},{5,7},{6,0},{7,1},{8,10},{9,11},{10,... | collective-permute-start | bytes 442376 | tf_op jit(solution)/shard_map/ppermute | solution.py:1124
  9.5 19.3 %collective-permute-start.1 = (bf16[144,512]{1,0:T(8,128)(2,1)}, bf16[144,512]{1,0:T(8,128)(2,1)S(1)}, u32[]{:S(2)}, u32[]{:S(2)}) collective-permute-start(bf16[144,512]{1,0:T(8,128)(2,1)} %get-tuple-element.98.refs_0_), channel_id=1, source_target_pairs={{0,4},{1,5},{2,6},{3,7},{4,0},{5,1},{6,2},{7,3},{8,12},{9,13},{10,... | collective-permute-start | bytes 442376 | tf_op jit(solution)/shard_map/ppermute | solution.py:1124
  12.0 21.6 %all-to-all-start = ((bf16[32,56,128]{2,1,0:T(8,128)(2,1)}), bf16[32,56,128]{2,1,0:T(8,128)(2,1)S(1)}, u32[]{:S(2)}, u32[]{:S(2)}) async-start(bf16[32,56,128]{2,1,0:T(8,128)(2,1)} %pack.1), calls=%async_computation | async-start | bytes 917504 | tf_op jit(solution)/shard_map/all_to_all | solution.py:1142
  15.6 18.0 %collective-permute-start.3 = (bf16[256,512]{1,0:T(8,128)(2,1)}, bf16[256,512]{1,0:T(8,128)(2,1)S(1)}, u32[]{:S(2)}, u32[]{:S(2)}) collective-permute-start(bf16[256,512]{1,0:T(8,128)(2,1)} %get-tuple-element.95.refs_0_.tokens_ref.x_ref), channel_id=1, source_target_pairs={{0,8},{8,16},{16,24},{24,0},{1,9},{9,17},{17,25},{25,1},{2,10},{10... | collective-permute-start | bytes 786440 | tf_op jit(solution)/shard_map/ppermute | solution.py:1113
  17.5 17.8 %collective-permute-start.4 = (bf16[256,512]{1,0:T(8,128)(2,1)}, bf16[256,512]{1,0:T(8,128)(2,1)S(1)}, u32[]{:S(2)}, u32[]{:S(2)}) collective-permute-start(bf16[256,512]{1,0:T(8,128)(2,1)} %get-tuple-element.95.refs_0_.tokens_ref.x_ref), channel_id=1, source_target_pairs={{0,16},{8,24},{16,0},{24,8},{1,17},{9,25},{17,1},{25,9},{2,18},{10... | collective-permute-start | bytes 786440 | tf_op jit(solution)/shard_map/ppermute | solution.py:1113
  18.9 16.3 %collective-permute-start.5 = (bf16[256,512]{1,0:T(8,128)(2,1)}, bf16[256,512]{1,0:T(8,128)(2,1)S(1)}, u32[]{:S(2)}, u32[]{:S(2)}) collective-permute-start(bf16[256,512]{1,0:T(8,128)(2,1)} %get-tuple-element.95.refs_0_.tokens_ref.x_ref), channel_id=1, source_target_pairs={{0,24},{8,0},{16,8},{24,16},{1,25},{9,1},{17,9},{25,17},{2,26},{10... | collective-permute-start | bytes 786440 | tf_op jit(solution)/shard_map/ppermute | solution.py:1113
  25.2 7.5 %collective-permute-start.2 = (bf16[144,512]{1,0:T(8,128)(2,1)S(1)}, bf16[144,512]{1,0:T(8,128)(2,1)S(1)}, u32[]{:S(2)}, u32[]{:S(2)}) collective-permute-start(bf16[144,512]{1,0:T(8,128)(2,1)S(1)} %copy-done.9), channel_id=1, source_target_pairs={{0,6},{1,7},{2,0},{3,1},{4,2},{5,3},{6,4},{7,5},{8,14},{9,15},{10,... | collective-permute-start | bytes 442376 | tf_op jit(solution)/shard_map/ppermute | solution.py:1124
  37.5 17.0 %all-to-all-start.1 = ((bf16[8,192,128]{2,1,0:T(8,128)(2,1)}), bf16[8,192,128]{2,1,0:T(8,128)(2,1)S(1)}, u32[]{:S(2)}, u32[]{:S(2)}) async-start(bf16[8,192,128]{2,1,0:T(8,128)(2,1)} %get-tuple-element.97), calls=%async_computation.1 | async-start | bytes 786432 | tf_op jit(solution)/shard_map/all_to_all | solution.py:295
  42.0 3.9 %collective-permute-start.9 = (bf16[144,512]{1,0:T(8,128)(2,1)S(1)}, bf16[144,512]{1,0:T(8,128)(2,1)S(1)}, u32[]{:S(2)}, u32[]{:S(2)}) collective-permute-start(bf16[144,512]{1,0:T(8,128)(2,1)S(1)} %collective-permute-done.2.refs_3_), channel_id=1, source_target_pairs={{0,1},{1,0},{2,3},{3,2},{4,5},{5,4},{6,7},{7,6},{8,9},{9,8},{10,11... | collective-permute-start | bytes 442376 | tf_op jit(solution)/shard_map/ppermute | solution.py:1127
  42.5 3.4 %collective-permute-start.8 = (bf16[144,512]{1,0:T(8,128)(2,1)S(1)}, bf16[144,512]{1,0:T(8,128)(2,1)S(1)}, u32[]{:S(2)}, u32[]{:S(2)}) collective-permute-start(bf16[144,512]{1,0:T(8,128)(2,1)S(1)} %collective-permute-done.1.refs_2_), channel_id=1, source_target_pairs={{0,1},{1,0},{2,3},{3,2},{4,5},{5,4},{6,7},{7,6},{8,9},{9,8},{10,11... | collective-permute-start | bytes 442376 | tf_op jit(solution)/shard_map/ppermute | solution.py:1127
  42.5 3.4 %collective-permute-start.7 = (bf16[144,512]{1,0:T(8,128)(2,1)S(1)}, bf16[144,512]{1,0:T(8,128)(2,1)S(1)}, u32[]{:S(2)}, u32[]{:S(2)}) collective-permute-start(bf16[144,512]{1,0:T(8,128)(2,1)S(1)} %collective-permute-done.refs_1_), channel_id=1, source_target_pairs={{0,1},{1,0},{2,3},{3,2},{4,5},{5,4},{6,7},{7,6},{8,9},{9,8},{10,11... | collective-permute-start | bytes 442376 | tf_op jit(solution)/shard_map/ppermute | solution.py:1127
  43.0 2.9 %collective-permute-start.6 = (bf16[144,512]{1,0:T(8,128)(2,1)S(1)}, bf16[144,512]{1,0:T(8,128)(2,1)S(1)}, u32[]{:S(2)}, u32[]{:S(2)}) collective-permute-start(bf16[144,512]{1,0:T(8,128)(2,1)S(1)} %copy-done.9), channel_id=1, source_target_pairs={{0,1},{1,0},{2,3},{3,2},{4,5},{5,4},{6,7},{7,6},{8,9},{9,8},{10,11... | collective-permute-start | bytes 442376 | tf_op jit(solution)/shard_map/ppermute | solution.py:1127
  54.5 1.7 collective-permute-start.13
  54.5 29.6 %copy-start.19 = (bf16[512,512]{1,0:T(8,128)(2,1)S(1)}, bf16[512,512]{1,0:T(8,128)(2,1)}, u32[]{:S(2)}) copy-start(bf16[512,512]{1,0:T(8,128)(2,1)} %get-tuple-element.102.down_ref) | copy-start | bytes 1572868
  54.5 29.6 %copy-start.22 = (bf16[256,512]{1,0:T(8,128)(2,1)S(1)}, bf16[256,512]{1,0:T(8,128)(2,1)}, u32[]{:S(2)}) copy-start(bf16[256,512]{1,0:T(8,128)(2,1)} %get-tuple-element.103.refs_4_.refs_0_) | copy-start | bytes 786436
  54.5 22.8 %collective-permute-start.10 = (bf16[256,512]{1,0:T(8,128)(2,1)}, bf16[256,512]{1,0:T(8,128)(2,1)S(1)}, u32[]{:S(2)}, u32[]{:S(2)}) collective-permute-start(bf16[256,512]{1,0:T(8,128)(2,1)} %copy-done.27), channel_id=1, source_target_pairs={{0,8},{8,16},{16,24},{24,0},{1,9},{9,17},{17,25},{25,1},{2,10},{10... | collective-permute-start | bytes 786440 | tf_op jit(solution)/shard_map/ppermute | solution.py:1113
  56.2 9.1 %copy-start.20 = (bf16[8,192,128]{2,1,0:T(8,128)(2,1)}, bf16[8,192,128]{2,1,0:T(8,128)(2,1)S(1)}, u32[]{:S(2)}) copy-start(bf16[8,192,128]{2,1,0:T(8,128)(2,1)S(1)} %collective-permute-done.13.refs_1_) | copy-start | bytes 1179652
  65.3 10.1 %all-to-all-start.2 = ((bf16[8,64,128]{2,1,0:T(8,128)(2,1)}), bf16[8,64,128]{2,1,0:T(8,128)(2,1)S(1)}, u32[]{:S(2)}, u32[]{:S(2)}) async-start(bf16[8,64,128]{2,1,0:T(8,128)(2,1)} %get-tuple-element.109), calls=%async_computation.2 | async-start | bytes 262144 | tf_op jit(solution)/shard_map/all_to_all | solution.py:295
  68.7 10.8 %collective-permute-start.11 = (bf16[256,512]{1,0:T(8,128)(2,1)}, bf16[256,512]{1,0:T(8,128)(2,1)S(1)}, u32[]{:S(2)}, u32[]{:S(2)}) collective-permute-start(bf16[256,512]{1,0:T(8,128)(2,1)} %copy-done.26), channel_id=1, source_target_pairs={{0,16},{8,24},{16,0},{24,8},{1,17},{9,25},{17,1},{25,9},{2,18},{10... | collective-permute-start | bytes 786440 | tf_op jit(solution)/shard_map/ppermute | solution.py:1113
  69.9 9.6 %collective-permute-start.12 = (bf16[256,512]{1,0:T(8,128)(2,1)}, bf16[256,512]{1,0:T(8,128)(2,1)}, u32[]{:S(2)}, u32[]{:S(2)}) collective-permute-start(bf16[256,512]{1,0:T(8,128)(2,1)} %copy-done.25), channel_id=1, source_target_pairs={{0,24},{8,0},{16,8},{24,16},{1,25},{9,1},{17,9},{25,17},{2,26},{10... | collective-permute-start | bytes 786440 | tf_op jit(solution)/shard_map/ppermute | solution.py:1113
  75.4 7.4 %collective-permute-start.14 = (bf16[8,64,128]{2,1,0:T(8,128)(2,1)S(1)}, bf16[8,64,128]{2,1,0:T(8,128)(2,1)S(1)}, u32[]{:S(2)}, u32[]{:S(2)}) collective-permute-start(bf16[8,64,128]{2,1,0:T(8,128)(2,1)S(1)} %all-to-all-done.2.refs_8_), channel_id=1, source_target_pairs={{0,8},{8,16},{16,24},{24,0},{1,9},{9,17},{17,25},{25,1},{2,10},{10... | collective-permute-start | bytes 393224 | tf_op jit(solution)/shard_map/ppermute | solution.py:1113
  76.7 7.5 %collective-permute-start.15 = (bf16[8,64,128]{2,1,0:T(8,128)(2,1)S(1)}, bf16[8,64,128]{2,1,0:T(8,128)(2,1)S(1)}, u32[]{:S(2)}, u32[]{:S(2)}) collective-permute-start(bf16[8,64,128]{2,1,0:T(8,128)(2,1)S(1)} %all-to-all-done.2.refs_8_), channel_id=1, source_target_pairs={{0,16},{8,24},{16,0},{24,8},{1,17},{9,25},{17,1},{25,9},{2,18},{10... | collective-permute-start | bytes 393224 | tf_op jit(solution)/shard_map/ppermute | solution.py:1113
  77.3 6.8 %collective-permute-start.16 = (bf16[8,64,128]{2,1,0:T(8,128)(2,1)S(1)}, bf16[8,64,128]{2,1,0:T(8,128)(2,1)S(1)}, u32[]{:S(2)}, u32[]{:S(2)}) collective-permute-start(bf16[8,64,128]{2,1,0:T(8,128)(2,1)S(1)} %all-to-all-done.2.refs_8_), channel_id=1, source_target_pairs={{0,24},{8,0},{16,8},{24,16},{1,25},{9,1},{17,9},{25,17},{2,26},{10... | collective-permute-start | bytes 393224 | tf_op jit(solution)/shard_map/ppermute | solution.py:1113
  79.5 8.9 %copy-start.23 = (bf16[256,512]{1,0:T(8,128)(2,1)}, bf16[256,512]{1,0:T(8,128)(2,1)S(1)}, u32[]{:S(2)}) copy-start(bf16[256,512]{1,0:T(8,128)(2,1)S(1)} %collective-permute-done.11.refs_6_.refs_2_) | copy-start | bytes 786436
  88.4 10.0 %collective-permute-start.18 = (bf16[128,512]{1,0:T(8,128)(2,1)S(1)}, bf16[128,512]{1,0:T(8,128)(2,1)S(1)}, u32[]{:S(2)}, u32[]{:S(2)}) collective-permute-start(bf16[128,512]{1,0:T(8,128)(2,1)S(1)} %get-tuple-element.120), channel_id=1, source_target_pairs={{0,24},{8,0},{16,8},{24,16},{1,25},{9,1},{17,9},{25,17},{2,26},{10... | collective-permute-start | bytes 393224 | tf_op jit(solution)/shard_map/ppermute | solution.py:1113
  94.4 7.8 %collective-permute-start.19 = (bf16[128,512]{1,0:T(8,128)(2,1)S(1)}, bf16[128,512]{1,0:T(8,128)(2,1)S(1)}, u32[]{:S(2)}, u32[]{:S(2)}) collective-permute-start(bf16[128,512]{1,0:T(8,128)(2,1)S(1)} %get-tuple-element.121), channel_id=1, source_target_pairs={{0,16},{8,24},{16,0},{24,8},{1,17},{9,25},{17,1},{25,9},{2,18},{10... | collective-permute-start | bytes 393224 | tf_op jit(solution)/shard_map/ppermute | solution.py:1113
  95.8 6.4 %collective-permute-start.20 = (bf16[128,512]{1,0:T(8,128)(2,1)S(1)}, bf16[128,512]{1,0:T(8,128)(2,1)S(1)}, u32[]{:S(2)}, u32[]{:S(2)}) collective-permute-start(bf16[128,512]{1,0:T(8,128)(2,1)S(1)} %get-tuple-element.122), channel_id=1, source_target_pairs={{0,8},{8,16},{16,24},{24,0},{1,9},{9,17},{17,25},{25,1},{2,10},{10... | collective-permute-start | bytes 393224 | tf_op jit(solution)/shard_map/ppermute | solution.py:1113
  95.8 6.4 %copy-start.8 = (f32[128,512]{1,0:T(8,128)S(1)}, f32[128,512]{1,0:T(8,128)}, u32[]{:S(2)}) copy-start(f32[128,512]{1,0:T(8,128)} %get-tuple-element.110.mid_ref) | copy-start | bytes 786436
  95.8 6.4 %copy-start.14 = (f32[8,512]{1,0:T(8,128)S(1)}, f32[8,512]{1,0:T(8,128)}, u32[]{:S(2)}) copy-start(f32[8,512]{1,0:T(8,128)} %get-tuple-element.96.vec_ref) | copy-start | bytes 49156
  95.8 6.4 %copy-start.24 = (bf16[256,512]{1,0:T(8,128)(2,1)S(1)}, bf16[256,512]{1,0:T(8,128)(2,1)}, u32[]{:S(2)}) copy-start(bf16[256,512]{1,0:T(8,128)(2,1)} %copy-done.23) | copy-start | bytes 786436
  95.8 6.4 %copy-start.30 = (f32[128,512]{1,0:T(8,128)S(1)}, f32[128,512]{1,0:T(8,128)}, u32[]{:S(2)}) copy-start(f32[128,512]{1,0:T(8,128)} %get-tuple-element.119.refs_4_) | copy-start | bytes 786436
  98.4 13.4 %collective-permute-start.17 = (bf16[4,128,512]{2,1,0:T(8,128)(2,1)}, bf16[4,128,512]{2,1,0:T(8,128)(2,1)S(1)}, u32[]{:S(2)}, u32[]{:S(2)}) collective-permute-start(bf16[4,128,512]{2,1,0:T(8,128)(2,1)} %get-tuple-element.116), channel_id=1, source_target_pairs={{0,1},{1,0},{2,3},{3,2},{4,5},{5,4},{6,7},{7,6},{8,9},{9,8},{10,11... | collective-permute-start | bytes 1572872 | tf_op jit(solution)/shard_map/ppermute | solution.py:1127
  102.2 9.6 %copy-start.2 = (f32[4,128,512]{2,1,0:T(8,128)S(1)}, f32[4,128,512]{2,1,0:T(8,128)}, u32[]{:S(2)}) copy-start(f32[4,128,512]{2,1,0:T(8,128)} %get-tuple-element.115.refs_0_) | copy-start | bytes 3145732
  107.5 4.3 %collective-permute-start.21 = (bf16[4,64,512]{2,1,0:T(8,128)(2,1)}, bf16[4,64,512]{2,1,0:T(8,128)(2,1)S(1)}, u32[]{:S(2)}, u32[]{:S(2)}) collective-permute-start(bf16[4,64,512]{2,1,0:T(8,128)(2,1)} %get-tuple-element.127), channel_id=1, source_target_pairs={{0,1},{1,0},{2,3},{3,2},{4,5},{5,4},{6,7},{7,6},{8,9},{9,8},{10,11... | collective-permute-start | bytes 786440 | tf_op jit(solution)/shard_map/ppermute | solution.py:1127
  107.5 12.6 %all-to-all-start.3 = ((bf16[32,16,128]{2,1,0:T(8,128)(2,1)}), bf16[32,16,128]{2,1,0:T(8,128)(2,1)S(1)}, u32[]{:S(2)}, u32[]{:S(2)}) async-start(bf16[32,16,128]{2,1,0:T(8,128)(2,1)} %get-tuple-element.124), calls=%async_computation.3 | async-start | bytes 262144 | tf_op jit(solution)/shard_map/all_to_all | solution.py:295
  112.8 7.2 %copy-start.32 = (f32[4,8,256]{2,1,0:T(8,128)S(1)}, f32[4,8,256]{2,1,0:T(8,128)}, u32[]{:S(2)}) copy-start(f32[4,8,256]{2,1,0:T(8,128)} %get-tuple-element.130.refs_5_) | copy-start | bytes 98308
  114.5 15.4 %collective-permute-start.22 = (bf16[192,512]{1,0:T(8,128)(2,1)}, bf16[192,512]{1,0:T(8,128)(2,1)S(1)}, u32[]{:S(2)}, u32[]{:S(2)}) collective-permute-start(bf16[192,512]{1,0:T(8,128)(2,1)} %get-tuple-element.134), channel_id=1, source_target_pairs={{0,2},{1,3},{2,4},{3,5},{4,6},{5,7},{6,0},{7,1},{8,10},{9,11},{10,... | collective-permute-start | bytes 589832 | tf_op jit(solution)/shard_map/ppermute | solution.py:1124
  116.2 15.9 %collective-permute-start.23 = (bf16[192,512]{1,0:T(8,128)(2,1)}, bf16[192,512]{1,0:T(8,128)(2,1)S(1)}, u32[]{:S(2)}, u32[]{:S(2)}) collective-permute-start(bf16[192,512]{1,0:T(8,128)(2,1)} %get-tuple-element.135), channel_id=1, source_target_pairs={{0,4},{1,5},{2,6},{3,7},{4,0},{5,1},{6,2},{7,3},{8,12},{9,13},{10,... | collective-permute-start | bytes 589832 | tf_op jit(solution)/shard_map/ppermute | solution.py:1124
  118.7 13.4 %collective-permute-start.24 = (bf16[192,512]{1,0:T(8,128)(2,1)}, bf16[192,512]{1,0:T(8,128)(2,1)S(1)}, u32[]{:S(2)}, u32[]{:S(2)}) collective-permute-start(bf16[192,512]{1,0:T(8,128)(2,1)} %get-tuple-element.136), channel_id=1, source_target_pairs={{0,6},{1,7},{2,0},{3,1},{4,2},{5,3},{6,4},{7,5},{8,14},{9,15},{10,... | collective-permute-start | bytes 589832 | tf_op jit(solution)/shard_map/ppermute | solution.py:1124
  132.1 1.5 collective-permute-start.25
  133.7 8.0 %copy-start.5 = (f32[192,512]{1,0:T(8,128)S(1)}, f32[192,512]{1,0:T(8,128)}, u32[]{:S(2)}) copy-start(f32[192,512]{1,0:T(8,128)} %get-tuple-element.138.own_ref) | copy-start | bytes 1179652
  133.7 8.0 %copy-start.10 = (bf16[128,512]{1,0:T(8,128)(2,1)S(1)}, bf16[128,512]{1,0:T(8,128)(2,1)}, u32[]{:S(2)}) copy-start(bf16[128,512]{1,0:T(8,128)(2,1)} %get-tuple-element.139.refs_3_) | copy-start | bytes 393220
  133.7 8.0 %copy-start.11 = (bf16[128,512]{1,0:T(8,128)(2,1)S(1)}, bf16[128,512]{1,0:T(8,128)(2,1)}, u32[]{:S(2)}) copy-start(bf16[128,512]{1,0:T(8,128)(2,1)} %get-tuple-element.140.refs_4_) | copy-start | bytes 393220
  133.8 8.0 %copy-start.12 = (bf16[128,512]{1,0:T(8,128)(2,1)S(1)}, bf16[128,512]{1,0:T(8,128)(2,1)}, u32[]{:S(2)}) copy-start(bf16[128,512]{1,0:T(8,128)(2,1)} %get-tuple-element.141.refs_5_) | copy-start | bytes 393220
  134.5 21.1 %copy-start.4 = (bf16[512,384]{1,0:T(8,128)(2,1)S(1)}, bf16[512,384]{1,0:T(8,128)(2,1)}, u32[]{:S(2)}) copy-start(bf16[512,384]{1,0:T(8,128)(2,1)} %get-tuple-element.149.w_ref) | copy-start | bytes 1179652
  134.5 21.1 %copy-start.17 = (bf16[512,512]{1,0:T(8,128)(2,1)S(1)}, bf16[512,512]{1,0:T(8,128)(2,1)}, u32[]{:S(2)}) copy-start(bf16[512,512]{1,0:T(8,128)(2,1)} %get-tuple-element.107.n_ref) | copy-start | bytes 1572868
  134.5 21.1 %copy-start.33 = (f32[8,512]{1,0:T(8,128)S(1)}, f32[8,512]{1,0:T(8,128)}, u32[]{:S(2)}) copy-start(f32[8,512]{1,0:T(8,128)} %get-tuple-element.146.sum_a_ref) | copy-start | bytes 49156
  134.5 21.1 %copy-start.34 = (f32[8,512]{1,0:T(8,128)S(1)}, f32[8,512]{1,0:T(8,128)}, u32[]{:S(2)}) copy-start(f32[8,512]{1,0:T(8,128)} %get-tuple-element.147.sum_b_ref) | copy-start | bytes 49156
  134.6 21.1 %all-to-all-start.4 = ((bf16[8,192,128]{2,1,0:T(8,128)(2,1)}), bf16[8,192,128]{2,1,0:T(8,128)(2,1)S(1)}, u32[]{:S(2)}, u32[]{:S(2)}) async-start(bf16[8,192,128]{2,1,0:T(8,128)(2,1)} %pad_maximum_fusion), calls=%async_computation.4 | async-start | bytes 786432 | tf_op jit(solution)/shard_map/all_to_all | solution.py:295
  143.2 7.3 %collective-permute-start.26 = (bf16[160,512]{1,0:T(8,128)(2,1)}, bf16[160,512]{1,0:T(8,128)(2,1)S(1)}, u32[]{:S(2)}, u32[]{:S(2)}) collective-permute-start(bf16[160,512]{1,0:T(8,128)(2,1)} %get-tuple-element.142), channel_id=1, source_target_pairs={{0,24},{8,0},{16,8},{24,16},{1,25},{9,1},{17,9},{25,17},{2,26},{10... | collective-permute-start | bytes 491528 | tf_op jit(solution)/shard_map/ppermute | solution.py:1113
  145.6 10.0 %collective-permute-start.27 = (bf16[160,512]{1,0:T(8,128)(2,1)}, bf16[160,512]{1,0:T(8,128)(2,1)S(1)}, u32[]{:S(2)}, u32[]{:S(2)}) collective-permute-start(bf16[160,512]{1,0:T(8,128)(2,1)} %get-tuple-element.143), channel_id=1, source_target_pairs={{0,16},{8,24},{16,0},{24,8},{1,17},{9,25},{17,1},{25,9},{2,18},{10... | collective-permute-start | bytes 491528 | tf_op jit(solution)/shard_map/ppermute | solution.py:1113
  146.1 9.5 %collective-permute-start.28 = (bf16[160,512]{1,0:T(8,128)(2,1)}, bf16[160,512]{1,0:T(8,128)(2,1)S(1)}, u32[]{:S(2)}, u32[]{:S(2)}) collective-permute-start(bf16[160,512]{1,0:T(8,128)(2,1)} %get-tuple-element.144), channel_id=1, source_target_pairs={{0,8},{8,16},{16,24},{24,0},{1,9},{9,17},{17,25},{25,1},{2,10},{10... | collective-permute-start | bytes 491528 | tf_op jit(solution)/shard_map/ppermute | solution.py:1113
  160.0 8.7 %copy-start.35 = (f32[128,512]{1,0:T(8,128)S(1)}, f32[128,512]{1,0:T(8,128)}, u32[]{:S(2)}) copy-start(f32[128,512]{1,0:T(8,128)} %get-tuple-element.111) | copy-start | bytes 786436
  160.0 20.2 %all-to-all-start.5 = ((bf16[32,64,128]{2,1,0:T(8,128)(2,1)}), bf16[32,64,128]{2,1,0:T(8,128)(2,1)S(1)}, u32[]{:S(2)}, u32[]{:S(2)}) async-start(bf16[32,64,128]{2,1,0:T(8,128)(2,1)} %get-tuple-element.156), calls=%async_computation.5 | async-start | bytes 1048576 | tf_op jit(solution)/shard_map/all_to_all | solution.py:295
  163.8 14.6 %copy-start.7 = (f32[128,512]{1,0:T(8,128)S(1)}, f32[128,512]{1,0:T(8,128)}, u32[]{:S(2)}) copy-start(f32[128,512]{1,0:T(8,128)} %get-tuple-element.145.grad_ref) | copy-start | bytes 786436
  164.8 8.9 %collective-permute-start.29 = (bf16[128,512]{1,0:T(8,128)(2,1)S(1)}, bf16[128,512]{1,0:T(8,128)(2,1)S(1)}, u32[]{:S(2)}, u32[]{:S(2)}) collective-permute-start(bf16[128,512]{1,0:T(8,128)(2,1)S(1)} %get-tuple-element.153), channel_id=1, source_target_pairs={{0,24},{8,0},{16,8},{24,16},{1,25},{9,1},{17,9},{25,17},{2,26},{10... | collective-permute-start | bytes 393224 | tf_op jit(solution)/shard_map/ppermute | solution.py:1113
  167.6 9.7 %collective-permute-start.30 = (bf16[128,512]{1,0:T(8,128)(2,1)S(1)}, bf16[128,512]{1,0:T(8,128)(2,1)S(1)}, u32[]{:S(2)}, u32[]{:S(2)}) collective-permute-start(bf16[128,512]{1,0:T(8,128)(2,1)S(1)} %get-tuple-element.154), channel_id=1, source_target_pairs={{0,16},{8,24},{16,0},{24,8},{1,17},{9,25},{17,1},{25,9},{2,18},{10... | collective-permute-start | bytes 393224 | tf_op jit(solution)/shard_map/ppermute | solution.py:1113
  168.1 10.3 %collective-permute-start.31 = (bf16[128,512]{1,0:T(8,128)(2,1)S(1)}, bf16[128,512]{1,0:T(8,128)(2,1)S(1)}, u32[]{:S(2)}, u32[]{:S(2)}) collective-permute-start(bf16[128,512]{1,0:T(8,128)(2,1)S(1)} %get-tuple-element.155), channel_id=1, source_target_pairs={{0,8},{8,16},{16,24},{24,0},{1,9},{9,17},{17,25},{25,1},{2,10},{10... | collective-permute-start | bytes 393224 | tf_op jit(solution)/shard_map/ppermute | solution.py:1113
  168.7 11.5 %copy-start.16 = (bf16[32,512]{1,0:T(8,128)(2,1)S(1)}, bf16[32,512]{1,0:T(8,128)(2,1)}, u32[]{:S(2)}) copy-start(bf16[32,512]{1,0:T(8,128)(2,1)} %get-tuple-element.157.refs_0_) | copy-start | bytes 98308
  (11 other events, 25.2 us)

commit v3 on v2

--- a/solution.py
+++ b/solution.py
@@ -80,14 +80,20 @@
     return block.reshape(geo.per_tile * count, LANES)
 
 
+ONES = 16
+CHUNKS_AT_ONCE = 4
+
+
 def forward_kernel(geo, scal_ref, *refs):
     part_refs = refs[: geo.parts]
-    bounds_ref, out_ref, ot_ref, lse_ref, kvt_ref = refs[geo.parts :]
+    bounds_ref, out_ref, ot_ref, lse_ref, vt_ref = refs[geo.parts :]
     base = jnp.broadcast_to(key_base(geo), (geo.tile, geo.tile))
+    ones = jnp.ones((ONES, geo.tile), bf16)
     for part in range(geo.parts):
         for tile in range(geo.tiles):
             keys = task_tile(part_refs[part], geo, tile, geo.half, geo.part_rows)
-            kvt_ref[part, tile] = keys.T
+            vt_ref[part, tile, :ONES] = ones
+            vt_ref[part, tile, ONES:] = keys.T[HD:]
     for tile in range(geo.tiles):
         q = unpack_rows(task_tile(part_refs[0], geo, tile, 0, geo.half))
         q = q * jnp.asarray(HD**-0.5, bf16)
@@ -96,38 +102,47 @@
         last = bounds_ref[tile, 1:2]
         own = bounds_ref[tile, 2:3]
 
-        def chunk(part, key_tile, carry, diagonal):
-            run_max, run_sum, acc = carry
-            offset = key_tile * geo.span + scal_ref[part]
-            keys = task_tile(part_refs[part], geo, key_tile, geo.half, geo.part_rows)
-            scores = dot_nt(keys, qz)
-            allowed = (base >= start - offset) & (base <= last - offset)
-            if diagonal:
-                allowed = allowed | (base == own - offset)
-            masked = jnp.where(allowed, scores, NEG_FILL)
-            new_max = jnp.maximum(run_max, jnp.max(masked, axis=0, keepdims=True))
-            factor = jnp.exp(run_max - new_max)
-            probs = jnp.where(allowed, jnp.exp(masked - new_max), 0.0)
-            new_sum = run_sum * factor + jnp.sum(probs, axis=0, keepdims=True)
-            acc = acc * factor + dot_nn(kvt_ref[part, key_tile], probs.astype(bf16))
-            return (new_max, new_sum, acc)
+        def step(key_tiles, carry):
+            chunks = [(key_tile, part) for key_tile in key_tiles for part in range(geo.parts)]
+            for at in range(0, len(chunks), CHUNKS_AT_ONCE):
+                carry = some(chunks[at : at + CHUNKS_AT_ONCE], carry)
+            return carry
+
+        def some(chunks, carry):
+            run_max, acc = carry
+            masked = []
+            new_max = run_max
+            for key_tile, part in chunks:
+                offset = key_tile * geo.span + scal_ref[part]
+                keys = task_tile(part_refs[part], geo, key_tile, geo.half, geo.part_rows)
+                scores = dot_nt(keys, qz)
+                allowed = (base >= start - offset) & (base <= last - offset)
+                if key_tile == tile and part == 0:
+                    allowed = allowed | (base == own - offset)
+                masked.append(jnp.where(allowed, scores, NEG_FILL))
+                new_max = jnp.maximum(new_max, jnp.max(masked[-1], axis=0, keepdims=True))
+            acc = acc * jnp.exp(run_max - new_max)
+            for (key_tile, part), scores in zip(chunks, masked):
+                probs = jnp.exp(scores - new_max).astype(bf16)
+                acc = acc + dot_nn(vt_ref[part, key_tile], probs)
+            return (new_max, acc)
 
         carry = (
             jnp.full((1, geo.tile), NEG_FILL, f32),
-            jnp.zeros((1, geo.tile), f32),
-            jnp.zeros((2 * HD, geo.tile), f32),
+            jnp.zeros((ONES + HD, geo.tile), f32),
         )
-        for part in range(geo.parts):
-            carry = chunk(part, tile, carry, True)
-
-        def earlier(key_tile, carry):
-            for part in range(geo.parts):
-                carry = chunk(part, key_tile, carry, False)
-            return carry
-
-        carry = lax.fori_loop(scal_ref[geo.parts + tile], tile, earlier, carry)
-        run_max, run_sum, acc = carry
-        attended = acc[HD:] / run_sum
+        near = max(0, tile - 1)
+        carry = step(range(tile, near - 1, -1), carry)
+        if near:
+            carry = lax.cond(
+                scal_ref[geo.parts + tile] < near,
+                functools.partial(step, range(near)),
+                lambda same: same,
+                carry,
+            )
+        run_max, acc = carry
+        run_sum = acc[0:1]
+        attended = acc[ONES:] / run_sum
         ot_ref[tile] = attended
         lse_ref[tile] = jnp.broadcast_to(run_max + jnp.log(run_sum), (8, geo.tile))
         packed = pack_rows(attended.T).astype(bf16)
@@ -153,35 +168,42 @@
         zeros = jnp.zeros_like(q)
         qz = jnp.concatenate([q, zeros], axis=1)
         doz = jnp.concatenate([zeros, do], axis=1)
+        q_do = jnp.concatenate([qz, doz], axis=0)
         delta = jnp.sum(do.astype(f32).T * ot_ref[tile], axis=0, keepdims=True)
         log_total = lse_ref[tile, 0:1]
         start = bounds_ref[tile, 0:1]
         last = bounds_ref[tile, 1:2]
         own = bounds_ref[tile, 2:3]
 
-        def chunk(part, key_tile, acc, diagonal):
+        def chunk(part, key_tile, acc):
             offset = key_tile * geo.span + scal_ref[part]
             keys = task_tile(part_refs[part], geo, key_tile, geo.half, geo.part_rows)
             scores = dot_nt(keys, qz)
             allowed = (base >= start - offset) & (base <= last - offset)
-            if diagonal:
+            if key_tile == tile and part == 0:
                 allowed = allowed | (base == own - offset)
-            probs = jnp.where(allowed, jnp.exp(scores - log_total), 0.0)
+            probs = jnp.exp(jnp.where(allowed, scores, NEG_FILL) - log_total)
             grad_probs = dot_nt(keys, doz)
             grad_scores = (probs * (grad_probs - delta)).astype(bf16)
-            acc_ref[part, key_tile] += dot_nn(grad_scores, qz) + dot_nn(probs.astype(bf16), doz)
+            both = jnp.concatenate([grad_scores, probs.astype(bf16)], axis=1)
+            acc_ref[part, key_tile] += dot_nn(both, q_do)
             return acc + dot_nn(kvt_ref[part, key_tile], grad_scores)
 
-        acc = jnp.zeros((2 * HD, geo.tile), f32)
-        for part in range(geo.parts):
-            acc = chunk(part, tile, acc, True)
-
-        def earlier(key_tile, acc):
-            for part in range(geo.parts):
-                acc = chunk(part, key_tile, acc, False)
+        def step(key_tiles, acc):
+            for key_tile in key_tiles:
+                for part in range(geo.parts):
+                    acc = chunk(part, key_tile, acc)
             return acc
 
-        acc = lax.fori_loop(scal_ref[geo.parts + tile], tile, earlier, acc)
+        near = max(0, tile - 1)
+        acc = step(range(tile, near - 1, -1), jnp.zeros((2 * HD, geo.tile), f32))
+        if near:
+            acc = lax.cond(
+                scal_ref[geo.parts + tile] < near,
+                functools.partial(step, range(near)),
+                lambda same: same,
+                acc,
+            )
         packed = pack_rows((acc[:HD] * (HD**-0.5)).T).astype(bf16)
         for i in range(geo.per_tile):
             dq_ref[tile * geo.per_tile + i] = packed[i * geo.half : (i + 1) * geo.half]
@@ -199,7 +221,7 @@
     return (pltpu.HBM(shape, dtype),)
 
 
-def local_call(kernel, name, scalars, arrays, outs, scratch=(), flops=10**8):
+def local_call(kernel, name, scalars, arrays, outs, scratch=(), flops=10**8, limit=VMEM_LIMIT):
     return pl.pallas_call(
         kernel,
         out_shape=tuple(o[0] if len(o) == 1 else jax.ShapeDtypeStruct(*o) for o in outs),
@@ -207,10 +229,14 @@
         + [pl.BlockSpec(memory_space=pltpu.VMEM)] * len(arrays),
         out_specs=tuple([pl.BlockSpec(memory_space=pltpu.VMEM)] * len(outs)),
         scratch_shapes=list(scratch),
-        compiler_params=pltpu.CompilerParams(vmem_limit_bytes=VMEM_LIMIT),
+        compiler_params=pltpu.CompilerParams(vmem_limit_bytes=limit),
         cost_estimate=pl.CostEstimate(flops=flops, bytes_accessed=10**6, transcendentals=0),
         name=name,
     )(scalars, *arrays)
+
+
+def attention_limit(geo):
+    return VMEM_LIMIT if geo.parts == 2 else 3 * VMEM_LIMIT
 
 
 def attention_forward(geo, scalars, part_arrays, bounds):
@@ -224,8 +250,9 @@
             far((geo.tiles, HD, geo.tile), f32),
             far((geo.tiles, 8, geo.tile), f32),
         ],
-        [pltpu.VMEM((geo.parts, geo.tiles, LANES, geo.tile), bf16)],
+        [pltpu.VMEM((geo.parts, geo.tiles, ONES + HD, geo.tile), bf16)],
         flops=30 * 10**9,
+        limit=attention_limit(geo),
     )
 
 
@@ -243,6 +270,7 @@
             pltpu.VMEM((geo.parts, geo.tiles, LANES, geo.tile), bf16),
         ],
         flops=30 * 10**9,
+        limit=attention_limit(geo),
     )
 
 
@@ -612,8 +640,16 @@
 SMALL = 8
 
 
+def my_head_of(sz, scal_ref):
+    return scal_ref[0] // sz.blocks
+
+
+def my_blk_of(sz, scal_ref):
+    return lax.rem(scal_ref[0], sz.blocks)
+
+
 def slot_head(sz, scal_ref, slot):
-    return lax.rem(scal_ref[0] - slot + sz.heads, sz.heads)
+    return lax.rem(my_head_of(sz, scal_ref) - slot + sz.heads, sz.heads)
 
 
 def halves(first, second):
@@ -663,22 +699,20 @@
         v = wp_ref[:, 2 * sz.width + at : 2 * sz.width + at + LANES]
         low, high = halves(k, v)
         chunk = jnp.concatenate([q, low, high], axis=0)
-        for blk in range(sz.blocks):
-            send_ref[head * sz.blocks + blk, : sz.w_chunk] = chunk
-            send_ref[head * sz.blocks + blk, sz.w_chunk :] = small
-
-
-def pack_more_kernel(sz, scal_ref, *refs):
-    tokens_ref, column_ref = refs[5:7]
-    x_ref, g_ref, up_ref, wo_ref, down_ref = staged(5, refs)
-    tokens_ref[: sz.mine] = x_ref[...]
-    tokens_ref[sz.mine :] = g_ref[...]
-    for head in range(sz.heads):
-        part = up_ref[:, head * sz.hidden_slice : (head + 1) * sz.hidden_slice]
-        column_ref[head * sz.w_rows : (head + 1) * sz.w_rows] = part
-    at = sz.heads * sz.w_rows
-    column_ref[at : at + sz.w_rows] = wo_ref[...]
-    column_ref[at + sz.w_rows :] = down_ref[...]
+        for group in range(sz.groups):
+            send_ref[head * sz.groups + group, : sz.w_chunk] = chunk
+            send_ref[head * sz.groups + group, sz.w_chunk :] = small
+
+
+def pieces_kernel(sz, scal_ref, *refs):
+    piece_refs = refs[3 : 3 + sz.heads]
+    g_ref, up_ref, wo_ref = staged(3, refs)
+    for step, ref in enumerate(piece_refs):
+        to = lax.rem(my_head_of(sz, scal_ref) + step, sz.heads)
+        at = pl.multiple_of(to * sz.hidden_slice, LANES)
+        ref[: sz.mine] = g_ref[...]
+        ref[sz.mine : sz.mine + sz.w_rows] = up_ref[:, pl.ds(at, sz.hidden_slice)]
+        ref[sz.mine + sz.w_rows :] = wo_ref[...]
 
 
 def spread(small, per, offset, count):
@@ -707,19 +741,27 @@
 
 
 def source_blk(sz, scal_ref, group_slot, part_slot):
-    group = lax.rem(scal_ref[1] // sz.parts - group_slot + sz.groups, sz.groups)
-    part = lax.rem(scal_ref[1] % sz.parts - part_slot + sz.parts, sz.parts)
+    group = lax.rem(my_blk_of(sz, scal_ref) // sz.parts - group_slot + sz.groups, sz.groups)
+    part = lax.rem(my_blk_of(sz, scal_ref) % sz.parts - part_slot + sz.parts, sz.parts)
     return group * sz.parts + part
 
 
-def project_kernel(sz, scal_ref, got_ref, *refs):
+def project_kernel(sz, scal_ref, *refs):
+    got_refs, refs = refs[: sz.parts], refs[sz.parts :]
     x_refs = refs[: sz.heads]
-    send_ref, w_ref, vec_ref = refs[sz.heads :]
-    head = scal_ref[0]
-    for i in range(1 + sz.local):
-        part = got_ref[:, i * sz.w_rows : (i + 1) * sz.w_rows, :]
-        w_ref[:, i * LANES : (i + 1) * LANES] = part.reshape(sz.width, LANES)
-    small = got_ref[:, sz.w_chunk :, :].astype(f32).reshape(-1, LANES).astype(bf16)
+    send_ref, w_ref, vec_ref, small_scr = refs[sz.heads :]
+    head = my_head_of(sz, scal_ref)
+    for part_slot, ref in enumerate(got_refs):
+        part = lax.rem(my_blk_of(sz, scal_ref) + sz.parts - part_slot, sz.parts)
+        for src in range(sz.heads * sz.groups):
+            dev = src // sz.groups * sz.blocks + src % sz.groups * sz.parts + part
+            at = pl.multiple_of(dev * sz.w_rows, sz.w_rows)
+            for i in range(1 + sz.local):
+                piece = ref[src, i * sz.w_rows : (i + 1) * sz.w_rows]
+                w_ref[pl.ds(at, sz.w_rows), i * LANES : (i + 1) * LANES] = piece
+            at = pl.multiple_of(dev * SMALL, SMALL)
+            small_scr[pl.ds(at, SMALL)] = ref[src, sz.w_chunk :].astype(f32)
+    small = small_scr[...].astype(bf16)
     vec = spread(small, sz.w_rows, 0, sz.width)
     per = 2 * sz.w_rows
     b_q = spread(small, per, head * LANES, LANES)[6:7]
@@ -732,7 +774,7 @@
     bias = jnp.concatenate([b_q, zero, b_v[:, :HD], zero, b_v[:, HD:]], axis=1)
     gain, shift = vec[0:1], vec[1:2]
     for slot in range(sz.heads):
-        x = x_refs[slot][: sz.mine].astype(f32)
+        x = x_refs[slot][...].astype(f32)
         normed = norm_forward(x, gain, shift)[0].astype(bf16)
         qkv = (dot_nn(normed, w_ref[...]) + bias).astype(bf16)
         to = slot_head(sz, scal_ref, slot)
@@ -752,40 +794,32 @@
                     ]
 
 
-def regroup_kernel(sz, scal_ref, *refs):
-    count = sz.parts * sz.groups
-    column_refs, pay_refs, down_ref = refs[:count], refs[count:-1], refs[-1]
+def assemble_kernel(sz, scal_ref, *refs):
+    chunks = sz.parts * sz.groups
+    mixed_refs, down_refs = refs[:chunks], refs[chunks : 2 * chunks]
+    up_ref, wo_ref, down_ref = refs[2 * chunks :]
     for part_slot in range(sz.parts):
         for group_slot in range(sz.groups):
-            ref = column_refs[part_slot * sz.groups + group_slot]
+            i = part_slot * sz.groups + group_slot
             blk = source_blk(sz, scal_ref, group_slot, part_slot)
             at = pl.multiple_of(blk * sz.f_rows, sz.f_rows)
-            first = sz.heads * sz.w_rows
-            down_ref[pl.ds(at, sz.f_rows)] = ref[first + sz.w_rows :]
-            up_at = pl.multiple_of(blk * sz.w_rows, sz.w_rows)
-            out_at = pl.multiple_of(sz.head_rows + blk * sz.w_rows, sz.w_rows)
-            for step, pay_ref in enumerate(pay_refs):
-                to = lax.rem(scal_ref[0] + step, sz.heads)
-                from_at = pl.multiple_of(to * sz.w_rows, sz.w_rows)
-                pay_ref[pl.ds(up_at, sz.w_rows)] = ref[pl.ds(from_at, sz.w_rows)]
-                pay_ref[pl.ds(out_at, sz.w_rows)] = ref[first : first + sz.w_rows]
-
-
-def output_weight_rows(sz, pay_refs):
-    rows = slice(sz.head_rows, 2 * sz.head_rows)
-    return jnp.concatenate([ref[rows] for ref in pay_refs], axis=0)
-
-
-def feed_kernel(sz, scal_ref, vec_ref, down_ref, *refs):
+            down_ref[pl.ds(at, sz.f_rows)] = down_refs[i][...]
+            for slot in range(sz.heads):
+                head = slot_head(sz, scal_ref, slot)
+                at = pl.multiple_of(head * sz.head_rows + blk * sz.w_rows, sz.w_rows)
+                first = 2 * slot * sz.w_rows
+                up_ref[pl.ds(at, sz.w_rows)] = mixed_refs[i][first : first + sz.w_rows]
+                at = pl.multiple_of(slot * sz.head_rows + blk * sz.w_rows, sz.w_rows)
+                first += sz.w_rows
+                wo_ref[pl.ds(at, sz.w_rows)] = mixed_refs[i][first : first + sz.w_rows]
+
+
+def feed_kernel(sz, scal_ref, vec_ref, up_ref, wo_ref, down_ref, *refs):
     n = sz.heads
-    x_refs, pay_refs, m_refs = refs[:n], refs[n : 2 * n], refs[2 * n : 3 * n]
+    x_refs, g_refs, m_refs = refs[:n], refs[n : 2 * n], refs[2 * n : 3 * n]
     outs = refs[3 * n :]
     part_refs, feed_refs = outs[:n], outs[n : 2 * n]
-    mid_ref, act_ref, dh_ref, n_ref, mix_own_ref, sum_ref, up_ref, mix_scr = outs[2 * n :]
-    for slot in range(n):
-        at = pl.multiple_of(slot_head(sz, scal_ref, slot) * sz.head_rows, sz.head_rows)
-        up_ref[pl.ds(at, sz.head_rows)] = pay_refs[slot][: sz.head_rows]
-    w_out = output_weight_rows(sz, pay_refs)
+    mid_ref, act_ref, dh_ref, n_ref, mix_own_ref, sum_ref, mix_scr = outs[2 * n :]
     half_run = sz.run // 2
     for slot in range(n):
         for seq in range(sz.seqs):
@@ -805,10 +839,10 @@
     group = 2
     for first in range(0, n, group):
         slots = range(first, first + group)
-        x = jnp.concatenate([x_refs[s][: sz.mine] for s in slots], axis=0).astype(f32)
-        g = jnp.concatenate([x_refs[s][sz.mine :] for s in slots], axis=0)
+        x = jnp.concatenate([x_refs[s][...] for s in slots], axis=0).astype(f32)
+        g = jnp.concatenate([g_refs[s][: sz.mine] for s in slots], axis=0)
         mixed = jnp.concatenate([mix_scr[slot_head(sz, scal_ref, s)] for s in slots], axis=0)
-        middle = x + dot_nn(mixed, w_out) + b_out
+        middle = x + dot_nn(mixed, wo_ref[...]) + b_out
         normed, unit, _ = norm_forward(middle, gain, shift)
         normed = normed.astype(bf16)
         hidden = dot_nn(normed, up_ref[...]) + b_up
@@ -840,7 +874,7 @@
 
 
 def give_and_keep(sz, scal_ref, values, rows, keep_ref, give_ref):
-    part = scal_ref[1] % sz.parts
+    part = my_blk_of(sz, scal_ref) % sz.parts
     for blk in range(sz.blocks):
         group = blk // sz.parts
         piece = values(blk)
@@ -856,7 +890,7 @@
 def feed_grad_kernel(sz, scal_ref, act_ref, dh_ref, n_ref, *refs):
     g_refs = refs[: sz.heads]
     keep_ref, give_ref = refs[sz.heads :]
-    g = jnp.concatenate([ref[sz.mine :] for ref in g_refs], axis=0)
+    g = jnp.concatenate([ref[: sz.mine] for ref in g_refs], axis=0)
     act = act_ref[...].reshape(sz.tokens, sz.hidden_slice)
     down = dot_tn(act, g)
     up = dot_tn(n_ref[...].reshape(sz.tokens, sz.width), dh_ref[...].reshape(sz.tokens, sz.hidden_slice))
@@ -872,28 +906,29 @@
 
 
 def part_sum_kernel(sz, scal_ref, *refs):
-    pairs, (own_ref, *piece_refs) = refs[: -sz.groups], refs[-sz.groups :]
+    keep_ref, got_ref, keep_out_ref, got_out_ref, *refs = refs
+    down_refs, rest_refs = refs[: sz.groups], refs[sz.groups :]
+    rows = keep_ref.shape[1] - sz.f_rows
     for step in range(sz.groups):
-        to = lax.rem(scal_ref[1] // sz.parts + step, sz.groups)
-        at = 0
-        for keep_ref, got_ref in zip(pairs[::2], pairs[1::2]):
-            total = keep_ref[to] + got_ref[to].astype(f32)
-            ref = piece_refs[step - 1] if step else own_ref
-            ref[at : at + total.shape[0]] = total.astype(ref.dtype)
-            at += total.shape[0]
-
-
-def middle_grad_kernel(sz, scal_ref, vec_ref, mid_ref, tokens_ref, *refs):
+        to = lax.rem(my_blk_of(sz, scal_ref) // sz.parts + step, sz.groups)
+        total = keep_ref[to] + got_ref[to].astype(f32)
+        total_out = keep_out_ref[to] + got_out_ref[to].astype(f32)
+        dtype = rest_refs[step].dtype
+        down_refs[step][...] = total[: sz.f_rows].astype(dtype)
+        rest_refs[step][:rows] = total[sz.f_rows :].astype(dtype)
+        rest_refs[step][rows:] = total_out.astype(dtype)
+
+
+def middle_grad_kernel(sz, scal_ref, vec_ref, wo_ref, mid_ref, g_ref, mix_ref, *refs):
     n = sz.heads
-    pay_refs, part_refs = refs[:n], refs[n : 2 * n]
-    grad_ref, branch_ref, send_ref, sum_ref = refs[2 * n :]
-    w_out = output_weight_rows(sz, pay_refs)
+    part_refs = refs[:n]
+    grad_ref, branch_ref, send_ref, sum_ref, keep_ref, give_ref = refs[n:]
     upstream = part_refs[0][...]
     for ref in part_refs[1:]:
         upstream = upstream + ref[...].astype(f32)
     gain, shift = vec_ref[3:4], vec_ref[4:5]
     _, unit, root = norm_forward(mid_ref[...], gain, shift)
-    g = tokens_ref[sz.mine :].astype(f32)
+    g = g_ref[...].astype(f32)
     grad = g + norm_input_grad(upstream, unit, root, gain)
     grad_ref[...] = grad
     branch = grad.astype(bf16)
@@ -906,7 +941,7 @@
         ],
         axis=0,
     )
-    mixed = dot_nt(branch, w_out).astype(bf16)
+    mixed = dot_nt(branch, wo_ref[...]).astype(bf16)
     half_run = sz.run // 2
     for slot in range(n):
         to = slot_head(sz, scal_ref, slot)
@@ -917,11 +952,12 @@
                 packed = halves(mixed[at : at + half_run, cols], mixed[at + half_run : at + sz.run, cols])
                 for local in range(sz.local):
                     send_ref[to * sz.blocks + sz.task(seq, local, part)] = packed[local]
-
-
-def out_grad_kernel(sz, scal_ref, mix_ref, branch_ref, keep_ref, give_ref):
-    grad = dot_tn(mix_ref[...], branch_ref[...])
-    part = scal_ref[1] % sz.parts
+    out_grad(sz, scal_ref, mix_ref[...], branch, keep_ref, give_ref)
+
+
+def out_grad(sz, scal_ref, mixed, branch, keep_ref, give_ref):
+    grad = dot_tn(mixed, branch)
+    part = my_blk_of(sz, scal_ref) % sz.parts
     for slot in range(sz.heads):
         head = slot_head(sz, scal_ref, slot)
         to = pl.multiple_of(head * sz.w_rows, sz.w_rows)
@@ -943,34 +979,63 @@
     n_ref, u_ref = refs[sz.heads :]
     gain, shift = vec_ref[0:1], vec_ref[1:2]
     for slot in range(sz.heads):
-        normed, unit, _ = norm_forward(x_refs[slot][: sz.mine].astype(f32), gain, shift)
+        normed, unit, _ = norm_forward(x_refs[slot][...].astype(f32), gain, shift)
         at = slice(slot * sz.mine, (slot + 1) * sz.mine)
         n_ref[:, at] = normed.astype(bf16).T
         u_ref[:, at] = unit.astype(bf16).T
 
 
-def project_grad_kernel(sz, scal_ref, sum_a_ref, sum_b_ref, got_ref, w_ref, n_ref, u_ref, *refs):
-    n = sz.heads
-    send_ref, d_scr = refs
+def both_levels(values, *where):
+    high = values.astype(bf16).astype(f32)
+    return collect(high, *where) + collect(values - high, *where)
+
+
+def project_grad_kernel(sz, scal_ref, early_ref, *refs):
+    far_refs, (send_ref, d_out_ref), refs = refs[:4], refs[4:6], refs[6:]
+    got_ref, n_ref, u_ref, w_ref, d_ref, send_scr, sems = refs
+    copies = [
+        pltpu.make_async_copy(far_refs[i], ref, sems.at[i])
+        for i, ref in enumerate((got_ref, n_ref, u_ref, w_ref))
+    ]
+    n_w = sz.w_chunk
+    copies += [
+        pltpu.make_async_copy(d_ref, d_out_ref, sems.at[4]),
+        pltpu.make_async_copy(send_scr.at[:, :n_w], send_ref.at[:, :n_w], sems.at[5]),
+        pltpu.make_async_copy(send_scr.at[:, n_w:], send_ref.at[:, n_w:], sems.at[6]),
+    ]
+    for copy in copies[:4]:
+        copy.start()
+    head = my_head_of(sz, scal_ref)
     half_run = sz.run // 2
-    for slot in range(n):
-        head = slot_head(sz, scal_ref, slot)
-        q_at = pl.multiple_of(head * half_run, half_run)
-        kv_at = pl.multiple_of(sz.half + head * sz.run, sz.run)
+    copies[0].wait()
+    for slot in range(sz.heads):
+        to = slot_head(sz, scal_ref, slot)
+        q_at = pl.multiple_of(to * half_run, half_run)
+        kv_at = pl.multiple_of(sz.half + to * sz.run, sz.run)
         for seq in range(sz.seqs):
             for part in range(sz.parts):
                 at = slot * sz.mine + seq * sz.sub + part * sz.run
                 first = got_ref[sz.task(seq, 0, part), pl.ds(q_at, half_run)]
                 second = got_ref[sz.task(seq, 1, part), pl.ds(q_at, half_run)]
                 low, high = halves(first, second)
-                d_scr[at : at + half_run, :LANES] = low
-                d_scr[at + half_run : at + sz.run, :LANES] = high
+                d_ref[at : at + half_run, :LANES] = low
+                d_ref[at + half_run : at + sz.run, :LANES] = high
                 for local in range(sz.local):
-                    d_scr[at : at + sz.run, (1 + local) * LANES : (2 + local) * LANES] = got_ref[
+                    d_ref[at : at + sz.run, (1 + local) * LANES : (2 + local) * LANES] = got_ref[
                         sz.task(seq, local, part), pl.ds(kv_at, sz.run)
                     ]
-    d_proj = d_scr[...]
+    d_proj = d_ref[...]
+    copies[4].start()
+    copies[1].wait()
     grad_w = dot_nn(n_ref[...], d_proj).astype(bf16)
+    for dev in range(sz.devices):
+        rows = slice(dev * sz.w_rows, (dev + 1) * sz.w_rows)
+        for i in range(1 + sz.local):
+            cols = slice(i * LANES, (i + 1) * LANES)
+            send_scr[dev, i * sz.w_rows : (i + 1) * sz.w_rows] = grad_w[rows, cols]
+    copies[5].start()
+    copies[2].wait()
+    copies[3].wait()
     weights = w_ref[...].astype(f32)
     ones = jnp.ones((16, sz.tokens), bf16)
     column = dot_nn(ones, d_proj)[:SMALL]
@@ -981,35 +1046,25 @@
         high = term.astype(bf16)
         low = (term - high.astype(f32)).astype(bf16)
         sums.append((dot_nt(ones, high) + dot_nt(ones, low))[0:1])
-    sums = jnp.concatenate(sums, axis=0)
-    for dev in range(sz.devices):
-        rows = slice(dev * sz.w_rows, (dev + 1) * sz.w_rows)
-        for i in range(1 + sz.local):
-            cols = slice(i * LANES, (i + 1) * LANES)
-            send_ref[dev, i * sz.w_rows : (i + 1) * sz.w_rows] = grad_w[rows, cols]
+    wide = jnp.concatenate([*sums, jnp.zeros((SMALL - 2, sz.width), f32)], axis=0)
     sum_q = column[:, :LANES]
     sum_v = jnp.concatenate([column[:, LANES + HD : 2 * LANES], column[:, 2 * LANES + HD :]], axis=1)
-    wide = jnp.concatenate(
-        [sums, sum_b_ref[0:1], sum_a_ref[0:2], sum_b_ref[1:2], jnp.zeros((2, sz.width), f32)], axis=0
-    )
-    up_bias = jnp.broadcast_to(sum_a_ref[2:3], (SMALL, sz.width))
-    head = scal_ref[0]
     per = sz.w_rows
-    at = sz.w_chunk
-    for low in (False, True):
-        def level(v):
-            high = v.astype(bf16).astype(f32)
-            return v - high if low else high
-
-        share = collect(level(wide), per, 0, (0, 6), sz.devices)
-        share += collect(level(sum_q), 2 * per, head * LANES, (6, 7), sz.devices)
-        share += collect(level(sum_v), 2 * per, sz.width + head * LANES, (6, 7), sz.devices)
-        share += collect(level(up_bias), 4 * per, head * sz.hidden_slice, (7, 8), sz.devices)
-        share = share.reshape(sz.devices, SMALL, LANES)
-        if low:
-            both = jnp.concatenate([kept, share], axis=1).astype(bf16)
-        kept = share
-    send_ref[:, at : at + 2 * SMALL, :] = both
+    small = (
+        early_ref[...]
+        + both_levels(wide, per, 0, (0, 2), sz.devices)
+        + both_levels(sum_q, 2 * per, head * LANES, (6, 7), sz.devices)
+        + both_levels(sum_v, 2 * per, sz.width + head * LANES, (6, 7), sz.devices)
+    )
+    send_scr[:, n_w:, :] = two_levels(small.reshape(sz.devices, SMALL, LANES))
+    copies[6].start()
+    for copy in copies[4:]:
+        copy.wait()
+
+
+def two_levels(small):
+    high = small.astype(bf16).astype(f32)
+    return jnp.concatenate([high, small - high], axis=-2).astype(bf16)
 
 
 def input_partial_kernel(sz, scal_ref, d_ref, w_ref, *part_refs):
@@ -1024,14 +1079,25 @@
     for ref in refs[1 : sz.heads]:
         upstream = upstream + ref[...].astype(f32)
     gain, shift = vec_ref[0:1], vec_ref[1:2]
-    _, unit, root = norm_forward(x_ref[: sz.mine].astype(f32), gain, shift)
+    _, unit, root = norm_forward(x_ref[...].astype(f32), gain, shift)
     out_ref[...] = (grad_ref[...] + norm_input_grad(upstream, unit, root, gain)).astype(bf16)
 
 
-def split_kernel(sz, scal_ref, own_ref, *refs):
+def split_kernel(sz, scal_ref, sum_a_ref, sum_b_ref, own_ref, *refs):
     n = sz.heads
-    got_refs, feed_refs, refs = refs[: sz.groups - 1], refs[sz.groups - 1 :][: n - 1], refs[-n - 1 :]
-    down_ref, piece_ref, *send_refs = refs
+    early_ref, refs = refs[-1], refs[:-1]
+    wide = jnp.concatenate(
+        [sum_a_ref[0:2], sum_b_ref[0:1], sum_a_ref[0:2], sum_b_ref[1:2], sum_a_ref[2:3]]
+        + [jnp.zeros((1, sz.width), f32)],
+        axis=0,
+    )
+    up_bias = jnp.broadcast_to(sum_a_ref[2:3], (SMALL, sz.width))
+    at = my_head_of(sz, scal_ref) * sz.hidden_slice
+    early_ref[...] = both_levels(wide, sz.w_rows, 0, (2, 6), sz.devices) + both_levels(
+        up_bias, 4 * sz.w_rows, at, (7, 8), sz.devices
+    )
+    got_refs, feed_refs, refs = refs[: sz.groups - 1], refs[sz.groups - 1 :][: n - 1], refs[-n:]
+    piece_ref, *send_refs = refs
 
     def total(rows):
         value = own_ref[rows]
@@ -1039,10 +1105,9 @@
             value = value + ref[rows].astype(f32)
         return value
 
-    down_ref[...] = total(slice(0, sz.f_rows))
     for slot in range(n):
         to = slot_head(sz, scal_ref, slot)
-        at = pl.multiple_of(sz.f_rows + to * sz.w_rows, sz.w_rows)
+        at = pl.multiple_of(to * sz.w_rows, sz.w_rows)
         up = total(pl.ds(at, sz.w_rows)).astype(bf16)
         out = total(pl.ds(at + n * sz.w_rows, sz.w_rows))
         ref = send_refs[slot - 1] if slot else piece_ref
@@ -1080,6 +1145,10 @@
         ref[...] = small[i : i + 1, : ref.shape[1]]
 
 
+BLK = ("group", "part")
+ALL = ("head", "group", "part")
+
+
 def on_device_fused(
     sz,
     layer_input,
@@ -1101,8 +1170,8 @@
 ):
     n = sz.heads
     my_head = lax.axis_index("head")
-    my_blk = lax.axis_index("blk")
-    scal = jnp.stack([my_head, my_blk]).astype(i32)
+    my_blk = lax.axis_index(BLK)
+    scal = (my_head * sz.blocks + my_blk).astype(i32).reshape(1)
     geo = AttentionShape(sz.blocks, sz.part_rows, sz.parts, sz.run, sz.sub)
     token_shape = (sz.mine, sz.width)
 
@@ -1121,77 +1190,78 @@
             for g in range(sz.groups)
             for p in range(sz.parts)
         ]
-        return lax.ppermute(x, "blk", pairs)
+        return lax.ppermute(x, BLK, pairs)
 
     def around_parts(x, step):
-        return lax.ppermute(x, "blk", within_group(sz.blocks, sz.parts, step))
+        return lax.ppermute(x, BLK, within_group(sz.blocks, sz.parts, step))
 
     x_mine = layer_input.reshape(token_shape)
     g_mine = cotangent.reshape(token_shape)
     small = [attention_gain, attention_shift, output_bias, feed_gain, feed_shift, down_bias]
     small += [project_bias, up_bias]
-    column_rows = (n + 1) * sz.w_rows + sz.f_rows
     (send,) = staged_call(
         functools.partial(pack_kernel, sz),
         "pack",
         scal,
         [project_weight, *[v.reshape(1, -1) for v in small]],
-        [((sz.devices, sz.w_chunk + SMALL, LANES), bf16)],
+        [((n * sz.groups, sz.w_chunk + SMALL, LANES), bf16)],
         [pltpu.VMEM((SMALL, LANES), f32)],
     )
-    got = lax.all_to_all(send, BOTH, split_axis=0, concat_axis=0, tiled=True)
-    own_tokens, column = staged_call(
-        functools.partial(pack_more_kernel, sz),
-        "pack_more",
+    got = exchange(send, ("head", "group"))
+    x_slots = [x_mine] + [around(after(x_mine, send), d) for d in range(1, n)]
+    pieces = staged_call(
+        functools.partial(pieces_kernel, sz),
+        "pieces",
         after(scal, send),
-        [x_mine, g_mine, up_weight, output_weight, down_weight],
-        [((2 * sz.mine, sz.width), bf16), ((column_rows, sz.width), bf16)],
-    )
-    x_slots = [own_tokens] + [around(own_tokens, d) for d in range(1, n)]
-    columns = [column] + [around_groups(column, d) for d in range(1, sz.groups)]
+        [g_mine, up_weight, output_weight],
+        [((sz.mine + 2 * sz.w_rows, sz.width), bf16)] * n,
+    )
+    g_slots = [pieces[0]] + [around(after(pieces[d], x_slots[1]), d) for d in range(1, n)]
+    got_parts = [got] + [around_parts(got, d) for d in range(1, sz.parts)]
 
     my_part = my_blk % sz.parts
     my_seq = (my_blk // sz.parts) // sz.local
     scalars, bounds = attention_bounds(
         segments, token_valid, my_seq, my_part, geo, sz.heads, sz.sub
     )
-    got = after(got, scalars, bounds, *columns)
+    got_parts[0] = after(got_parts[0], scalars, bounds, *pieces)
     send, w_slice, vec = call(
         project_kernel,
         "project",
-        [got, *x_slots],
+        [*got_parts, *x_slots],
         [
             ((sz.blocks, sz.half + sz.part_rows, LANES), bf16),
             far((sz.width, (1 + sz.local) * LANES), bf16),
             far((SMALL, sz.width), f32),
         ],
+        [pltpu.VMEM((sz.devices * SMALL, LANES), f32)],
         flops=30 * 10**9,
     )
-    columns += [around_parts(after(v, send), d) for d in range(1, sz.parts) for v in columns]
-    *pays, w_down = call(
-        regroup_kernel,
-        "regroup",
-        columns,
-        [far((2 * sz.head_rows, sz.width), bf16)]
-        + [((2 * sz.head_rows, sz.width), bf16)] * (n - 1)
-        + [far((sz.width, sz.width), bf16)],
-    )
-    pays = [pays[0]] + [around(pays[d], d) for d in range(1, n)]
+    column = jnp.concatenate([v[sz.mine :] for v in g_slots], axis=0)
+    columns = [column] + [around_groups(column, d) for d in range(1, sz.groups)]
+    downs = [after(down_weight, x_slots[1])]
+    downs += [around_groups(downs[0], d) for d in range(1, sz.groups)]
+    task = exchange(send, BLK)
+    task = after(task, column, *downs)
+    others = [around_parts(task, step) for step in range(1, sz.parts)]
+    o_task, ot, lse = attention_forward(geo, scalars, [task, *others], bounds)
+    o_task = after(o_task, *columns)
+    columns += [around_parts(after(v, o_task), d) for d in range(1, sz.parts) for v in columns]
+    downs += [around_parts(after(v, o_task), d) for d in range(1, sz.parts) for v in downs]
+    square = ((sz.width, sz.width), bf16)
+    w_up, w_out, w_down = call(assemble_kernel, "assemble", [*columns, *downs], [square] * 3)
+    mixed = exchange(o_task, BLK)
     turned = far((sz.width, sz.tokens), bf16)
     n_one, u_one = call(
-        norm_again_kernel, "norm_again", [vec, *x_slots], [turned, turned]
-    )
-    task = exchange(send, "blk")
-    task = after(task, w_down, n_one)
-    others = [around_parts(task, step) for step in range(1, sz.parts)]
-    o_task, ot, lse = attention_forward(geo, scalars, [task, *others], bounds)
-    mixed = exchange(o_task, "blk")
+        norm_again_kernel, "norm_again", [after(vec, o_task), *x_slots], [turned, turned]
+    )
+    mixed = after(mixed, n_one)
     m_slots = [mixed] + [around(mixed, d) for d in range(1, n)]
 
     outs = call(
         feed_kernel,
         "feed",
-        [vec, w_down, *x_slots, *pays, *m_slots],
+        [vec, w_up, w_out, w_down, *x_slots, *g_slots, *m_slots],
         [far(token_shape, f32)]
         + [(token_shape, bf16)] * (n - 1)
         + [far(token_shape, f32)]
@@ -1200,7 +1270,6 @@
         + [((n, sz.mine, sz.hidden_slice), bf16)] * 2
         + [((n, *token_shape), bf16), far(token_shape, bf16), far((SMALL, sz.width), f32)],
         [
-            pltpu.VMEM((sz.width, sz.hidden_slice), bf16),
             pltpu.VMEM((n, *token_shape), bf16),
         ],
         flops=30 * 10**9,
@@ -1216,38 +1285,37 @@
     keep, give = call(
         feed_grad_kernel,
         "feed_grad",
-        [activated, grad_hidden, n_two, *x_slots],
+        [activated, grad_hidden, n_two, *g_slots],
         shared(sz.f_rows + n * sz.w_rows),
     )
     grad_two[0] = after(grad_two[0], keep)
 
-    grad_middle, branch, send, branch_sums = call(
+    grad_middle, branch, send, branch_sums, keep_out, give_out = call(
         middle_grad_kernel,
         "middle_grad",
-        [vec, middle, own_tokens, *pays, *grad_two],
+        [vec, w_out, middle, g_mine, mixed_own, *grad_two],
         [
             far(token_shape, f32),
             far(token_shape, bf16),
             ((sz.devices, sz.run // 2, LANES), bf16),
             far((SMALL, sz.width), f32),
+            *shared(n * sz.w_rows),
         ],
         flops=30 * 10**9,
     )
-    do_task = exchange(send, BOTH)
+    do_task = exchange(send, ALL)
     given = around_parts(give, 1)
-    keep_out, give = call(
-        out_grad_kernel,
-        "out_grad",
-        [mixed_own, after(branch, send)],
-        shared(n * sz.w_rows),
-    )
-    rows = sz.f_rows + 2 * n * sz.w_rows
-    w_sum = call(
+    down_shape, rest_shape = (sz.f_rows, sz.width), (2 * n * sz.w_rows, sz.width)
+    sums = call(
         part_sum_kernel,
         "part_sum",
-        [keep, given, keep_out, around_parts(give, 1)],
-        [far((rows, sz.width), f32)] + [((rows, sz.width), bf16)] * (sz.groups - 1),
-    )
+        [keep, given, keep_out, around_parts(give_out, 1)],
+        [far(down_shape, f32)]
+        + [far(down_shape, bf16)] * (sz.groups - 1)
+        + [far(rest_shape, f32)]
+        + [(rest_shape, bf16)] * (sz.groups - 1),
+    )
+    down_sum, w_sum = sums[: sz.groups], sums[sz.groups :]
     w_pieces = [around_groups(w_sum[d], d) for d in range(1, sz.groups)]
     dq, dkv, *dkv_others = attention_backward(
         geo, do_tile_grouped, scalars, [task, *others], do_task, bounds, ot, lse
@@ -1255,29 +1323,42 @@
     dkv_others[0] = after(dkv_others[0], *w_pieces)
     for step in range(1, sz.parts):
         back = within_group(sz.blocks, sz.parts, -step)
-        dkv = dkv + lax.ppermute(dkv_others[step - 1], "blk", back).astype(f32)
+        dkv = dkv + lax.ppermute(dkv_others[step - 1], BLK, back).astype(f32)
     send = jnp.concatenate([dq, dkv.astype(bf16)], axis=1)
-    got = exchange(send, "blk")
-    down_grad, piece, *rest = call(
+    got = exchange(send, BLK)
+    piece, *rest = call(
         split_kernel,
         "split",
-        [after(w_sum[0], send), *w_pieces, *feed[1:]],
-        [((sz.f_rows, sz.width), f32), far((2 * sz.w_rows, sz.width), bf16)]
-        + [far((sz.mine + 2 * sz.w_rows, sz.width), bf16)] * (n - 1),
-    )
+        [feed_sums, branch_sums, after(w_sum[0], send), *w_pieces, *feed[1:]],
+        [far((2 * sz.w_rows, sz.width), bf16)]
+        + [far((sz.mine + 2 * sz.w_rows, sz.width), bf16)] * (n - 1)
+        + [far((sz.devices * SMALL, LANES), f32)],
+    )
+    early = rest.pop()
     rest = [around(v, -d - 1) for d, v in enumerate(rest)]
     got = after(got, *rest)
-    send, d_proj = call(
-        project_grad_kernel,
-        "project_grad",
-        [feed_sums, branch_sums, got, w_slice, n_one, u_one],
-        [
-            ((sz.devices, sz.w_chunk + 2 * SMALL, LANES), bf16),
-            far((sz.tokens, (1 + sz.local) * LANES), bf16),
+    wide = (1 + sz.local) * LANES
+    send_shape = (sz.devices, sz.w_chunk + 2 * SMALL, LANES)
+    send, d_proj = pl.pallas_call(
+        functools.partial(project_grad_kernel, sz),
+        out_shape=(pltpu.HBM(send_shape, bf16), pltpu.HBM((sz.tokens, wide), bf16)),
+        in_specs=[pl.BlockSpec(memory_space=pltpu.SMEM), pl.BlockSpec(memory_space=pltpu.VMEM)]
+        + [pl.BlockSpec(memory_space=pltpu.HBM)] * 4,
+        out_specs=tuple([pl.BlockSpec(memory_space=pltpu.HBM)] * 2),
+        scratch_shapes=[
+            pltpu.VMEM(got.shape, bf16),
+            pltpu.VMEM((sz.width, sz.tokens), bf16),
+            pltpu.VMEM((sz.width, sz.tokens), bf16),
+            pltpu.VMEM((sz.width, wide), bf16),
+            pltpu.VMEM((sz.tokens, wide), bf16),
+            pltpu.VMEM(send_shape, bf16),
+            pltpu.SemaphoreType.DMA((7,)),
         ],
-        flops=30 * 10**9,
-    )
-    got = exchange(send, BOTH)
+        compiler_params=pltpu.CompilerParams(vmem_limit_bytes=63 * 2**20),
+        cost_estimate=pl.CostEstimate(flops=30 * 10**9, bytes_accessed=10**6, transcendentals=0),
+        name="project_grad",
+    )(scal, early, got, n_one, u_one, w_slice)
+    got = exchange(send, ALL)
     outs = call(
         input_partial_kernel,
         "input_partial",
@@ -1285,10 +1366,13 @@
         [(token_shape, f32)] + [(token_shape, bf16)] * (n - 1),
     )
     grad_one = [outs[0]] + [around(outs[d], -d) for d in range(1, n)]
+    down_grad = down_sum[0]
+    for d in range(1, sz.groups):
+        down_grad = down_grad + around_groups(after(down_sum[d], grad_one[1]), d).astype(f32)
     (input_grad,) = call(
         input_grad_kernel,
         "input_grad",
-        [vec, grad_middle, own_tokens, *grad_one],
+        [vec, grad_middle, x_mine, *grad_one],
         [(token_shape, bf16)],
     )
     layer_output = middle + feed[0] + vec[5:6]
@@ -1325,57 +1409,29 @@
     )
 
 
-def on_device(*arguments):
-    layer_input, up_weight = arguments[0], arguments[11]
-    seqs, _, sub, width = layer_input.shape
-    sz = Sizes(
-        lax.axis_size("head"), lax.axis_size("blk"), seqs, sub, width, up_weight.shape[1]
-    )
-    if sz.fits():
-        return on_device_fused(sz, *arguments)
-    return on_device_general(*arguments)
-
-
 def solution(mesh):
-    tokens = P(None, "blk", "head", None)
-    vector = P(BOTH)
-    matrix = P(BOTH, None)
-    return jax.shard_map(
-        on_device,
-        mesh=mesh,
-        in_specs=(
-            tokens,
-            P(),
-            P(),
-            vector,
-            vector,
-            matrix,
-            vector,
-            matrix,
-            vector,
-            vector,
-            vector,
-            matrix,
-            vector,
-            matrix,
-            vector,
-            tokens,
-        ),
-        out_specs=(
-            tokens,
-            tokens,
-            vector,
-            vector,
-            matrix,
-            vector,
-            matrix,
-            vector,
-            vector,
-            vector,
-            matrix,
-            vector,
-            matrix,
-            vector,
-        ),
-        check_vma=False,
-    )
+    heads, blocks = mesh.shape["head"], mesh.shape["blk"]
+
+    def layer(*arguments):
+        layer_input, up_weight = arguments[0], arguments[11]
+        seqs, _, tokens, width = layer_input.shape
+        sz = Sizes(heads, blocks, seqs, tokens // heads, width, up_weight.shape[1])
+        if sz.fits():
+            split = (heads, blocks // sz.parts, sz.parts)
+            inner = jax.sharding.Mesh(mesh.devices.reshape(split), ALL)
+            body, blk, everywhere = functools.partial(on_device_fused, sz), BLK, ALL
+        else:
+            inner, body, blk, everywhere = mesh, on_device_general, "blk", BOTH
+        rows = P(None, blk, "head", None)
+        vector, matrix = P(everywhere), P(everywhere, None)
+        weights = (vector, vector, matrix, vector, matrix, vector)
+        weights += (vector, vector, matrix, vector, matrix, vector)
+        return jax.shard_map(
+            body,
+            mesh=inner,
+            in_specs=(rows, P(), P(), *weights, rows),
+            out_specs=(rows, rows, *weights),
+            check_vma=False,
+        )(*arguments)
+
+    return layer

time: 182 us -> 166 us (0.912)
  Pallas kernels: 49.3 us -> 36.3 us
  starting transfers between devices: 70 us -> 78.3 us
  waiting for transfers between devices: 47.5 us -> 39.7 us
  local copies, waits for them, and re-layouts: 8.49 us -> 3.45 us
    pallas_call x15 -> x13, Pallas kernels: 44.3 us -> 28.2 us  [local_call(): pl.pallas_call(kernel, out_shape=tuple((o[0] if len(o) == 1 else jax.Shap...]
    ppermute x14 -> x25, starting transfers between devices: 15.7 us -> 26.1 us  [the longest x12 23.4 us: around_groups(): return lax.ppermute(x, BLK, pairs)]
    all_to_all x5 -> x6, waiting for transfers between devices: 10.5 us -> 2.87 us  [exchange(): return lax.all_to_all(x, axis, split_axis=0, concat_axis=0, tiled=True)]
    all_to_all x5 -> x6, starting transfers between devices: 23.1 us -> 29.7 us  [exchange(): return lax.all_to_all(x, axis, split_axis=0, concat_axis=0, tiled=True)]
    ppermute x14 -> x25, waiting for transfers between devices: 8.27 us -> 14 us  [the longest x12 12.3 us: around_groups(): return lax.ppermute(x, BLK, pairs)]
    ppermute x18, starting transfers between devices: 27.6 us -> 22.5 us  [around(): return lax.ppermute(x, 'head', [(i, (i + step) % n) for i in range(n)])]
    ppermute x18, waiting for transfers between devices: 27.9 us -> 22.8 us  [around(): return lax.ppermute(x, 'head', [(i, (i + step) % n) for i in range(n)])]
    pallas_call x0 -> x1, Pallas kernels: none -> 4.59 us  [on_device_fused(): pl.pallas_call(functools.partial(project_grad_kernel, sz), out_shape=(plt...]
  transfers between devices with their start and end apart: 38 -> 49, of which waited for: 17 -> 18; matrix products, arithmetic and copies ran while one was open for 3% -> 4% of each run, Pallas kernels for 18% -> 14%
where the time goes in v3:
time: 166 us; the launch traced here: 165 us
  starting transfers between devices  78.3 us (47%)
  waiting for transfers between devices  39.7 us (24%)
  Pallas kernels  36.3 us (22%)
  other arithmetic  5.86 us (4%)
  local copies, waits for them, and re-layouts  3.45 us (2%)
  between operations  1.88 us (1%)
    all_to_all x6, starting transfers between devices, exchange(): return lax.all_to_all(x, axis, split_axis=0, concat_axis=0, tiled=True)  29.7 us
    pallas_call x13, Pallas kernels, local_call(): pl.pallas_call(kernel, out_shape=tuple((o[0] if len(o) == 1 else jax.Shap...  28.2 us
    ppermute x12, starting transfers between devices, around_groups(): return lax.ppermute(x, BLK, pairs)  23.4 us
    ppermute x18, waiting for transfers between devices, around(): return lax.ppermute(x, 'head', [(i, (i + step) % n) for i in range(n)])  22.8 us
    ppermute x18, starting transfers between devices, around(): return lax.ppermute(x, 'head', [(i, (i + step) % n) for i in range(n)])  22.5 us
    ppermute x12, waiting for transfers between devices, around_groups(): return lax.ppermute(x, BLK, pairs)  12.3 us
    pallas_call x1, Pallas kernels, on_device_fused(): pl.pallas_call(functools.partial(project_grad_kernel, sz), out_shape=(plt...  4.59 us
    pallas_call x2, Pallas kernels, staged_call(): pl.pallas_call(kernel, out_shape=tuple((jax.ShapeDtypeStruct(*o) for o in...  3.51 us
  transfers between devices with their start and end apart: 49, of which 18 were waited for; matrix products, arithmetic and copies ran while one was open for 4% of the time, Pallas kernels for 14%

profile of v3, /device:TPU:0, one launch (start us, length us, event | category | flops | bytes accessed | tf_op | source)
XLA Modules:
  0.0 165.5 jit_solution(2418742616962638151)
XLA Ops:
  0.7 1.7 %pack.1 = bf16[16,56,128]{2,1,0:T(8,128)(2,1)} custom-call(s32[1]{0:T(128)} %bitcast.scal_ref, bf16[16,1536]{1,0:T(8,128)(2,1)} %refs_0_.1, bf16[1,16]{1,0:T(2,128)(2,1)} %bitcast.47, bf16[1,16]{1,0:T(2,128)(2,1)} %bitcast.48, bf16[1,16]{1,0:T(2,128)(2,1)} %bitcast.49, bf16[1,16]{1,0:T(2,128)(2,1)} %bitcast.50, bf16[1,16]{1,0:T(2,128)(2,1)} %bitcast.51, ...), custom_call_target="tpu_custom_call" | custom-call | tf_op jit(solution)/shard_map/pack/pallas_call | solution.py:673
  2.4 8.3 %all-to-all-start = ((bf16[16,56,128]{2,1,0:T(8,128)(2,1)}), bf16[16,56,128]{2,1,0:T(8,128)(2,1)S(1)}, u32[]{:S(2)}, u32[]{:S(2)}) async-start(bf16[16,56,128]{2,1,0:T(8,128)(2,1)} %pack.1), calls=%async_computation | async-start | bytes 458752 | tf_op jit(solution)/shard_map/all_to_all | solution.py:323
  10.7 1.9 %collective-permute-start.1 = (bf16[128,512]{1,0:T(8,128)(2,1)}, bf16[128,512]{1,0:T(8,128)(2,1)S(1)}, u32[]{:S(2)}, u32[]{:S(2)}) collective-permute-start(bf16[128,512]{1,0:T(8,128)(2,1)} %bitcast.30), channel_id=1, source_target_pairs={{0,8},{8,16},{16,24},{24,0},{1,9},{9,17},{17,25},{25,1},{2,10},{10... | collective-permute-start | bytes 393224 | tf_op jit(solution)/shard_map/ppermute | solution.py:1182
  12.6 1.5 collective-permute-start.2
  14.1 1.5 collective-permute-start.3
  16.1 2.0 %fusion.2 = (s32[2048]{0:T(1024)S(1)}, s32[1,2048]{1,0:T(1,128)S(1)}, s32[]{:T(128)}) fusion(s32[]{:T(128)} %broadcast.160, s32[2,2048]{1,0:T(2,128)} %param.17, s32[]{:T(128)S(6)} %select_n.38, s32[2,2048]{1,0:T(2,128)} %param.18), kind=kLoop, calls=%fused_computation.29 | loop fusion | flops 2047 | bytes 32780 | tf_op jit(solution)/shard_map/jit(dynamic_index_in_dim)/dynamic_slice | solution.py:301
  20.0 1.0 convert_reduce_fusion
  21.1 1.8 %pieces.1 = (bf16[160,512]{1,0:T(8,128)(2,1)}, bf16[160,512]{1,0:T(8,128)(2,1)}, bf16[160,512]{1,0:T(8,128)(2,1)}, bf16[160,512]{1,0:T(8,128)(2,1)}) custom-call(s32[1]{0:T(128)} %bitcast.scal_ref, bf16[128,512]{1,0:T(8,128)(2,1)} %bitcast.37, bf16[16,2048]{1,0:T(8,128)(2,1)} %refs_1_.1, bf16[16,512]{1,0:T(8,128)(2,1)} %refs_2_.1), custom_call_target="tpu_custom_call" | custom-call | tf_op jit(solution)/shard_map/pieces/pallas_call | solution.py:673
  23.1 2.8 %project.1 = (bf16[8,192,128]{2,1,0:T(8,128)(2,1)}, bf16[512,384]{1,0:T(8,128)(2,1)}, f32[8,512]{1,0:T(8,128)}) custom-call(s32[1]{0:T(128)} %bitcast.scal_ref, bf16[16,56,128]{2,1,0:T(8,128)(2,1)S(1)} %all-to-all-done.refs_0_, bf16[16,56,128]{2,1,0:T(8,128)(2,1)} %collective-permute-done.refs_1_, bf16[128,512]{1,0:T(8,128)(2,1)S(1)} %bitcast.33, ...), custom_call_target="tpu_custom_call" | custom-call | flops 30000001024 | bytes 1000000 | tf_op jit(solution)/shard_map/project/pallas_call | solution.py:225
  25.9 4.6 %all-to-all-start.1 = ((bf16[8,192,128]{2,1,0:T(8,128)(2,1)}), bf16[8,192,128]{2,1,0:T(8,128)(2,1)S(1)}, u32[]{:S(2)}, u32[]{:S(2)}) async-start(bf16[8,192,128]{2,1,0:T(8,128)(2,1)} %get-tuple-element.120), calls=%async_computation.1 | async-start | bytes 786432 | tf_op jit(solution)/shard_map/all_to_all | solution.py:323
  30.5 0.6 collective-permute-start.4
  31.7 2.4 %collective-permute-start.6 = (bf16[160,512]{1,0:T(8,128)(2,1)S(1)}, bf16[160,512]{1,0:T(8,128)(2,1)S(1)}, u32[]{:S(2)}, u32[]{:S(2)}) collective-permute-start(bf16[160,512]{1,0:T(8,128)(2,1)S(1)} %copy-done.26), channel_id=1, source_target_pairs={{0,24},{8,0},{16,8},{24,16},{1,25},{9,1},{17,9},{25,17},{2,26},{10... | collective-permute-start | bytes 491528 | tf_op jit(solution)/shard_map/ppermute | solution.py:1182
  34.1 2.0 %collective-permute-start.10 = (bf16[64,512]{1,0:T(8,128)(2,1)S(1)}, bf16[64,512]{1,0:T(8,128)(2,1)S(1)}, u32[]{:S(2)}, u32[]{:S(2)}) collective-permute-start(bf16[64,512]{1,0:T(8,128)(2,1)S(1)} %copy-done.14), channel_id=1, source_target_pairs={{0,2},{1,3},{2,4},{3,5},{4,6},{5,7},{6,0},{7,1},{8,10},{9,11},{10,... | collective-permute-start | bytes 196616 | tf_op jit(solution)/shard_map/ppermute | solution.py:1193
  36.1 2.4 %collective-permute-start.11 = (bf16[64,512]{1,0:T(8,128)(2,1)S(1)}, bf16[64,512]{1,0:T(8,128)(2,1)S(1)}, u32[]{:S(2)}, u32[]{:S(2)}) collective-permute-start(bf16[64,512]{1,0:T(8,128)(2,1)S(1)} %copy-done.14), channel_id=1, source_target_pairs={{0,4},{1,5},{2,6},{3,7},{4,0},{5,1},{6,2},{7,3},{8,12},{9,13},{10,... | collective-permute-start | bytes 196616 | tf_op jit(solution)/shard_map/ppermute | solution.py:1193
  38.5 3.8 %collective-permute-start.12 = (bf16[64,512]{1,0:T(8,128)(2,1)S(1)}, bf16[64,512]{1,0:T(8,128)(2,1)S(1)}, u32[]{:S(2)}, u32[]{:S(2)}) collective-permute-start(bf16[64,512]{1,0:T(8,128)(2,1)S(1)} %copy-done.14), channel_id=1, source_target_pairs={{0,6},{1,7},{2,0},{3,1},{4,2},{5,3},{6,4},{7,5},{8,14},{9,15},{10,... | collective-permute-start | bytes 196616 | tf_op jit(solution)/shard_map/ppermute | solution.py:1193
  42.4 1.5 collective-permute-done.10.refs_9_
  43.9 3.9 %collective-permute-done.11.refs_10_ = bf16[64,512]{1,0:T(8,128)(2,1)S(1)} collective-permute-done((bf16[64,512]{1,0:T(8,128)(2,1)S(1)}, bf16[64,512]{1,0:T(8,128)(2,1)S(1)}, u32[]{:S(2)}, u32[]{:S(2)}) %collective-permute-start.11) | collective-permute-done | bytes 65568 | tf_op jit(solution)/shard_map/ppermute | solution.py:1193
  47.8 1.5 collective-permute-start.7
  49.3 1.3 collective-permute-start.8
  50.6 1.1 collective-permute-start.9
  51.7 5.1 %attention_forward.1 = (bf16[8,64,128]{2,1,0:T(8,128)(2,1)}, f32[4,64,256]{2,1,0:T(8,128)}, f32[4,8,256]{2,1,0:T(8,128)}) custom-call(s32[6]{0:T(128)S(1)} %pad_add_fusion.scal_ref, bf16[8,192,128]{2,1,0:T(8,128)(2,1)S(1)} %all-to-all-done.1.refs_0_, bf16[8,192,128]{2,1,0:T(8,128)(2,1)S(1)} %collective-permute-done.13.refs_1_, ...), custom_call_target="tpu_custom_call" | custom-call | flops 30000001024 | bytes 1000000 | tf_op jit(solution)/shard_map/attention_forward/pallas_call | solution.py:225
  56.8 4.4 %collective-permute-done.8.refs_2_ = bf16[128,512]{1,0:T(8,128)(2,1)S(1)} collective-permute-done((bf16[128,512]{1,0:T(8,128)(2,1)S(1)}, bf16[128,512]{1,0:T(8,128)(2,1)S(1)}, u32[]{:S(2)}, u32[]{:S(2)}) %collective-permute-start.8) | collective-permute-done | bytes 131104 | tf_op jit(solution)/shard_map/ppermute | solution.py:1193
  61.2 4.6 %all-to-all-start.2 = ((bf16[8,64,128]{2,1,0:T(8,128)(2,1)}), bf16[8,64,128]{2,1,0:T(8,128)(2,1)S(1)}, u32[]{:S(2)}, u32[]{:S(2)}) async-start(bf16[8,64,128]{2,1,0:T(8,128)(2,1)} %get-tuple-element.124), calls=%async_computation.2 | async-start | bytes 262144 | tf_op jit(solution)/shard_map/all_to_all | solution.py:323
  68.6 1.6 norm_again.1
  70.2 2.3 %all-to-all-done.2.refs_8_ = bf16[8,64,128]{2,1,0:T(8,128)(2,1)S(1)} async-done(((bf16[8,64,128]{2,1,0:T(8,128)(2,1)}), bf16[8,64,128]{2,1,0:T(8,128)(2,1)S(1)}, u32[]{:S(2)}, u32[]{:S(2)}) %all-to-all-start.2) | async-done | bytes 131104 | tf_op jit(solution)/shard_map/all_to_all | solution.py:323
  73.7 2.4 %collective-permute-start.24 = (bf16[8,64,128]{2,1,0:T(8,128)(2,1)S(1)}, bf16[8,64,128]{2,1,0:T(8,128)(2,1)S(1)}, u32[]{:S(2)}, u32[]{:S(2)}) collective-permute-start(bf16[8,64,128]{2,1,0:T(8,128)(2,1)S(1)} %all-to-all-done.2.refs_8_), channel_id=1, source_target_pairs={{0,24},{8,0},{16,8},{24,16},{1,25},{9,1},{17,9},{25,17},{2,26},{10... | collective-permute-start | bytes 393224 | tf_op jit(solution)/shard_map/ppermute | solution.py:1182
  76.2 3.6 %collective-permute-done.22.refs_9_ = bf16[8,64,128]{2,1,0:T(8,128)(2,1)S(1)} collective-permute-done((bf16[8,64,128]{2,1,0:T(8,128)(2,1)S(1)}, bf16[8,64,128]{2,1,0:T(8,128)(2,1)S(1)}, u32[]{:S(2)}, u32[]{:S(2)}) %collective-permute-start.22) | collective-permute-done | bytes 131104 | tf_op jit(solution)/shard_map/ppermute | solution.py:1182
  79.9 0.8 collective-permute-done.23.refs_10_
  80.6 3.3 %feed.1 = (f32[128,512]{1,0:T(8,128)}, bf16[128,512]{1,0:T(8,128)(2,1)S(1)}, bf16[128,512]{1,0:T(8,128)(2,1)S(1)}, bf16[128,512]{1,0:T(8,128)(2,1)S(1)}, f32[128...) custom-call(s32[1]{0:T(128)} %bitcast.scal_ref, ...), custom_call_target="tpu_custom_call" | custom-call | flops 30000001024 | bytes 1000000 | tf_op jit(solution)/shard_map/feed/pallas_call | solution.py:225
  84.0 2.4 %collective-permute-start.25 = (bf16[128,512]{1,0:T(8,128)(2,1)S(1)}, bf16[128,512]{1,0:T(8,128)(2,1)S(1)}, u32[]{:S(2)}, u32[]{:S(2)}) collective-permute-start(bf16[128,512]{1,0:T(8,128)(2,1)S(1)} %get-tuple-element.149), channel_id=1, source_target_pairs={{0,24},{8,0},{16,8},{24,16},{1,25},{9,1},{17,9},{25,17},{2,26},{10... | collective-permute-start | bytes 393224 | tf_op jit(solution)/shard_map/ppermute | solution.py:1182
  86.4 0.8 collective-permute-start.26
  87.2 2.0 %feed_grad.1 = (f32[4,128,512]{2,1,0:T(8,128)}, bf16[4,128,512]{2,1,0:T(8,128)(2,1)}) custom-call(s32[1]{0:T(128)} %bitcast.scal_ref, bf16[4,128,512]{2,1,0:T(8,128)(2,1)S(1)} %get-tuple-element.144.act_ref, bf16[4,128,512]{2,1,0:T(8,128)(2,1)S(1)} %get-tuple-element.145.dh_ref, bf16[4,128,512]{2,1,0:T(8,128)(2,1)S(1)} %get-tuple-element.146.n_ref, ...), custom_call_target="tpu_custom_call" | custom-call | flops 100000000 | bytes 1000000 | tf_op jit(solution)/shard_map/feed_grad/pallas_call | solution.py:225
  89.3 0.8 collective-permute-done.25.refs_1_
  90.1 1.3 collective-permute-done.26.refs_2_
  91.3 1.7 %collective-permute-done.27.refs_3_ = bf16[128,512]{1,0:T(8,128)(2,1)S(1)} collective-permute-done((bf16[128,512]{1,0:T(8,128)(2,1)S(1)}, bf16[128,512]{1,0:T(8,128)(2,1)S(1)}, u32[]{:S(2)}, u32[]{:S(2)}) %collective-permute-start.27) | collective-permute-done | bytes 131104 | tf_op jit(solution)/shard_map/ppermute | solution.py:1182
  93.1 2.0 %middle_grad.1 = (f32[128,512]{1,0:T(8,128)}, bf16[128,512]{1,0:T(8,128)(2,1)}, bf16[32,16,128]{2,1,0:T(8,128)(2,1)}, f32[8,512]{1,0:T(8,128)}, f32[4,64,512]{2,1,0:T(8,128)}, /*index=5*/bf16[4,64,512]{2,1,0:T(8,128)(2,1)}) custom-call(s32[1]{0:T(128)} %bitcast.scal_ref, f32[8,512]{1,0:T(8,128)S(1)} %copy-done.13, ...), custom_call_target="tpu_custom_call" | custom-call | flops 30000001024 | bytes 1000000 | tf_op jit(solution)/shard_map/middle_grad/pallas_call | solution.py:225
  95.1 3.0 %all-to-all-start.3 = ((bf16[32,16,128]{2,1,0:T(8,128)(2,1)}), bf16[32,16,128]{2,1,0:T(8,128)(2,1)S(1)}, u32[]{:S(2)}, u32[]{:S(2)}) async-start(bf16[32,16,128]{2,1,0:T(8,128)(2,1)} %get-tuple-element.157), calls=%async_computation.3 | async-start | bytes 262144 | tf_op jit(solution)/shard_map/all_to_all | solution.py:323
  98.2 1.0 copy-done.1
  99.2 1.0 part_sum.1
  100.2 1.8 %collective-permute-start.30 = (bf16[128,512]{1,0:T(8,128)(2,1)}, bf16[128,512]{1,0:T(8,128)(2,1)S(1)}, u32[]{:S(2)}, u32[]{:S(2)}) collective-permute-start(bf16[128,512]{1,0:T(8,128)(2,1)} %get-tuple-element.163), channel_id=1, source_target_pairs={{0,2},{1,3},{2,4},{3,5},{4,6},{5,7},{6,0},{7,1},{8,10},{9,11},{10,... | collective-permute-start | bytes 393224 | tf_op jit(solution)/shard_map/ppermute | solution.py:1193
  102.0 2.4 %collective-permute-start.31 = (bf16[128,512]{1,0:T(8,128)(2,1)}, bf16[128,512]{1,0:T(8,128)(2,1)S(1)}, u32[]{:S(2)}, u32[]{:S(2)}) collective-permute-start(bf16[128,512]{1,0:T(8,128)(2,1)} %get-tuple-element.164), channel_id=1, source_target_pairs={{0,4},{1,5},{2,6},{3,7},{4,0},{5,1},{6,2},{7,3},{8,12},{9,13},{10,... | collective-permute-start | bytes 393224 | tf_op jit(solution)/shard_map/ppermute | solution.py:1193
  104.4 1.4 collective-permute-start.32
  106.3 0.9 copy-done.21
  107.3 6.5 %attention_backward.1 = (bf16[8,64,128]{2,1,0:T(8,128)(2,1)S(1)}, f32[8,128,128]{2,1,0:T(8,128)S(1)}, bf16[8,128,128]{2,1,0:T(8,128)(2,1)S(1)}) custom-call(s32[6]{0:T(128)S(1)} %pad_add_fusion.scal_ref, bf16[8,192,128]{2,1,0:T(8,128)(2,1)S(1)} %all-to-all-done.1.refs_0_, bf16[8,192,128]{2,1,0:T(8,128)(2,1)S(1)} %copy-done.19, ...), custom_call_target="tpu_custom_call" | custom-call | flops 30000001024 | bytes 1000000 | tf_op jit(solution)/shard_map/attention_backward/pallas_call | solution.py:225
  114.2 1.2 collective-permute-done.33
  115.6 0.8 pad_maximum_fusion
  116.4 5.4 %all-to-all-start.4 = ((bf16[8,192,128]{2,1,0:T(8,128)(2,1)}), bf16[8,192,128]{2,1,0:T(8,128)(2,1)}, u32[]{:S(2)}, u32[]{:S(2)}) async-start(bf16[8,192,128]{2,1,0:T(8,128)(2,1)} %pad_maximum_fusion), calls=%async_computation.4 | async-start | bytes 786432 | tf_op jit(solution)/shard_map/all_to_all | solution.py:323
  121.8 1.3 split.1
  123.1 2.4 %collective-permute-start.34 = (bf16[160,512]{1,0:T(8,128)(2,1)}, bf16[160,512]{1,0:T(8,128)(2,1)S(1)}, u32[]{:S(2)}, u32[]{:S(2)}) collective-permute-start(bf16[160,512]{1,0:T(8,128)(2,1)} %get-tuple-element.171), channel_id=1, source_target_pairs={{0,24},{8,0},{16,8},{24,16},{1,25},{9,1},{17,9},{25,17},{2,26},{10... | collective-permute-start | bytes 491528 | tf_op jit(solution)/shard_map/ppermute | solution.py:1182
  126.1 0.6 collective-permute-start.36
  126.6 3.8 %collective-permute-done.34.refs_1_ = bf16[160,512]{1,0:T(8,128)(2,1)S(1)} collective-permute-done((bf16[160,512]{1,0:T(8,128)(2,1)}, bf16[160,512]{1,0:T(8,128)(2,1)S(1)}, u32[]{:S(2)}, u32[]{:S(2)}) %collective-permute-start.34) | collective-permute-done | bytes 163872 | tf_op jit(solution)/shard_map/ppermute | solution.py:1182
  130.4 5.2 %collective-permute-done.35.refs_2_ = bf16[160,512]{1,0:T(8,128)(2,1)S(1)} collective-permute-done((bf16[160,512]{1,0:T(8,128)(2,1)}, bf16[160,512]{1,0:T(8,128)(2,1)S(1)}, u32[]{:S(2)}, u32[]{:S(2)}) %collective-permute-start.35) | collective-permute-done | bytes 163872 | tf_op jit(solution)/shard_map/ppermute | solution.py:1182
  135.6 4.6 %project_grad.1 = (bf16[32,64,128]{2,1,0:T(8,128)(2,1)}, bf16[512,384]{1,0:T(8,128)(2,1)}) custom-call(s32[1]{0:T(128)} %bitcast.scal_ref, f32[256,128]{1,0:T(8,128)} %get-tuple-element.175.early_ref, bf16[8,192,128]{2,1,0:T(8,128)(2,1)} %all-to-all-done.4.refs_0_, bf16[512,512]{1,0:T(8,128)(2,1)} %get-tuple-element.137.refs_1_, ...), custom_call_target="tpu_custom_call" | custom-call | flops 30000001024 | bytes 1000000 | tf_op jit(solution)/shard_map/project_grad/pallas_call | solution.py:1342
  140.2 3.8 %all-to-all-start.5 = ((bf16[32,64,128]{2,1,0:T(8,128)(2,1)}), bf16[32,64,128]{2,1,0:T(8,128)(2,1)S(1)}, u32[]{:S(2)}, u32[]{:S(2)}) async-start(bf16[32,64,128]{2,1,0:T(8,128)(2,1)} %get-tuple-element.184), calls=%async_computation.5 | async-start | bytes 1048576 | tf_op jit(solution)/shard_map/all_to_all | solution.py:323
  144.6 2.7 %collective-permute-start.37 = (bf16[128,512]{1,0:T(8,128)(2,1)S(1)}, bf16[128,512]{1,0:T(8,128)(2,1)S(1)}, u32[]{:S(2)}, u32[]{:S(2)}) collective-permute-start(bf16[128,512]{1,0:T(8,128)(2,1)S(1)} %get-tuple-element.181), channel_id=1, source_target_pairs={{0,24},{8,0},{16,8},{24,16},{1,25},{9,1},{17,9},{25,17},{2,26},{10... | collective-permute-start | bytes 393224 | tf_op jit(solution)/shard_map/ppermute | solution.py:1182
  148.4 5.6 %collective-permute-done.37.refs_1_ = bf16[128,512]{1,0:T(8,128)(2,1)S(1)} collective-permute-done((bf16[128,512]{1,0:T(8,128)(2,1)S(1)}, bf16[128,512]{1,0:T(8,128)(2,1)S(1)}, u32[]{:S(2)}, u32[]{:S(2)}) %collective-permute-start.37) | collective-permute-done | bytes 131104 | tf_op jit(solution)/shard_map/ppermute | solution.py:1182
  154.1 1.8 %collective-permute-start.40 = (bf16[64,512]{1,0:T(8,128)(2,1)S(1)}, bf16[64,512]{1,0:T(8,128)(2,1)S(1)}, u32[]{:S(2)}, u32[]{:S(2)}) collective-permute-start(bf16[64,512]{1,0:T(8,128)(2,1)S(1)} %copy-done.31), channel_id=1, source_target_pairs={{0,2},{1,3},{2,4},{3,5},{4,6},{5,7},{6,0},{7,1},{8,10},{9,11},{10,... | collective-permute-start | bytes 196616 | tf_op jit(solution)/shard_map/ppermute | solution.py:1193
  155.9 3.0 %collective-permute-start.41 = (bf16[64,512]{1,0:T(8,128)(2,1)S(1)}, bf16[64,512]{1,0:T(8,128)(2,1)S(1)}, u32[]{:S(2)}, u32[]{:S(2)}) collective-permute-start(bf16[64,512]{1,0:T(8,128)(2,1)S(1)} %copy-done.30), channel_id=1, source_target_pairs={{0,4},{1,5},{2,6},{3,7},{4,0},{5,1},{6,2},{7,3},{8,12},{9,13},{10,... | collective-permute-start | bytes 196616 | tf_op jit(solution)/shard_map/ppermute | solution.py:1193
  158.9 0.9 collective-permute-start.42
  159.8 0.7 add_convert_fusion.1
  160.5 1.0 input_grad.1
  161.5 2.1 %collective-permute-done.41 = bf16[64,512]{1,0:T(8,128)(2,1)S(1)} collective-permute-done((bf16[64,512]{1,0:T(8,128)(2,1)S(1)}, bf16[64,512]{1,0:T(8,128)(2,1)S(1)}, u32[]{:S(2)}, u32[]{:S(2)}) %collective-permute-start.41) | collective-permute-done | bytes 65568 | tf_op jit(solution)/shard_map/ppermute | solution.py:1193
  164.0 0.7 convert_add_fusion
  164.7 0.8 final.1
  (151 shorter events, 10.3 us)
Async XLA Ops:
  0.6 22.4 %copy-start.2 = (bf16[2,1,64,512]{3,2,1,0:T(8,128)(2,1)S(1)}, bf16[2,1,64,512]{3,2,1,0:T(8,128)(2,1)}, u32[]{:S(2)}) copy-start(bf16[2,1,64,512]{3,2,1,0:T(8,128)(2,1)} %param.16) | copy-start | bytes 393220
  2.4 18.7 %all-to-all-start = ((bf16[16,56,128]{2,1,0:T(8,128)(2,1)}), bf16[16,56,128]{2,1,0:T(8,128)(2,1)S(1)}, u32[]{:S(2)}, u32[]{:S(2)}) async-start(bf16[16,56,128]{2,1,0:T(8,128)(2,1)} %pack.1), calls=%async_computation | async-start | bytes 458752 | tf_op jit(solution)/shard_map/all_to_all | solution.py:323
  10.7 12.3 %collective-permute-start.1 = (bf16[128,512]{1,0:T(8,128)(2,1)}, bf16[128,512]{1,0:T(8,128)(2,1)S(1)}, u32[]{:S(2)}, u32[]{:S(2)}) collective-permute-start(bf16[128,512]{1,0:T(8,128)(2,1)} %bitcast.30), channel_id=1, source_target_pairs={{0,8},{8,16},{16,24},{24,0},{1,9},{9,17},{17,25},{25,1},{2,10},{10... | collective-permute-start | bytes 393224 | tf_op jit(solution)/shard_map/ppermute | solution.py:1182
  12.6 10.4 %collective-permute-start.2 = (bf16[128,512]{1,0:T(8,128)(2,1)}, bf16[128,512]{1,0:T(8,128)(2,1)S(1)}, u32[]{:S(2)}, u32[]{:S(2)}) collective-permute-start(bf16[128,512]{1,0:T(8,128)(2,1)} %bitcast.31), channel_id=1, source_target_pairs={{0,16},{8,24},{16,0},{24,8},{1,17},{9,25},{17,1},{25,9},{2,18},{10... | collective-permute-start | bytes 393224 | tf_op jit(solution)/shard_map/ppermute | solution.py:1182
  14.1 8.9 %collective-permute-start.3 = (bf16[128,512]{1,0:T(8,128)(2,1)}, bf16[128,512]{1,0:T(8,128)(2,1)S(1)}, u32[]{:S(2)}, u32[]{:S(2)}) collective-permute-start(bf16[128,512]{1,0:T(8,128)(2,1)} %bitcast.32), channel_id=1, source_target_pairs={{0,24},{8,0},{16,8},{24,16},{1,25},{9,1},{17,9},{25,17},{2,26},{10... | collective-permute-start | bytes 393224 | tf_op jit(solution)/shard_map/ppermute | solution.py:1182
  21.1 2.0 %collective-permute-start = (bf16[16,56,128]{2,1,0:T(8,128)(2,1)S(1)}, bf16[16,56,128]{2,1,0:T(8,128)(2,1)}, u32[]{:S(2)}, u32[]{:S(2)}) collective-permute-start(bf16[16,56,128]{2,1,0:T(8,128)(2,1)S(1)} %all-to-all-done.refs_0_), channel_id=1, source_target_pairs={{0,1},{1,0},{2,3},{3,2},{4,5},{5,4},{6,7},{7,6},{8,9},{9,8},{10,11... | collective-permute-start | bytes 688136 | tf_op jit(solution)/shard_map/ppermute | solution.py:1196
  23.0 7.5 %copy-start.28 = (bf16[160,512]{1,0:T(8,128)(2,1)S(1)}, bf16[160,512]{1,0:T(8,128)(2,1)}, u32[]{:S(2)}) copy-start(bf16[160,512]{1,0:T(8,128)(2,1)} %get-tuple-element.117) | copy-start | bytes 491524
  23.0 8.1 %copy-start.27 = (bf16[160,512]{1,0:T(8,128)(2,1)S(1)}, bf16[160,512]{1,0:T(8,128)(2,1)}, u32[]{:S(2)}) copy-start(bf16[160,512]{1,0:T(8,128)(2,1)} %get-tuple-element.118) | copy-start | bytes 491524
  23.0 8.7 %copy-start.26 = (bf16[160,512]{1,0:T(8,128)(2,1)S(1)}, bf16[160,512]{1,0:T(8,128)(2,1)}, u32[]{:S(2)}) copy-start(bf16[160,512]{1,0:T(8,128)(2,1)} %get-tuple-element.119) | copy-start | bytes 491524
  23.0 11.1 %copy-start.8 = (bf16[160,512]{1,0:T(8,128)(2,1)S(1)}, bf16[160,512]{1,0:T(8,128)(2,1)}, u32[]{:S(2)}) copy-start(bf16[160,512]{1,0:T(8,128)(2,1)} %get-tuple-element.110.refs_4_.refs_0_) | copy-start | bytes 491524
  23.0 11.1 %copy-start.14 = (bf16[64,512]{1,0:T(8,128)(2,1)S(1)}, bf16[64,512]{1,0:T(8,128)(2,1)}, u32[]{:S(2)}) copy-start(bf16[64,512]{1,0:T(8,128)(2,1)} %refs_8_) | copy-start | bytes 196612
  25.9 21.9 %all-to-all-start.1 = ((bf16[8,192,128]{2,1,0:T(8,128)(2,1)}), bf16[8,192,128]{2,1,0:T(8,128)(2,1)S(1)}, u32[]{:S(2)}, u32[]{:S(2)}) async-start(bf16[8,192,128]{2,1,0:T(8,128)(2,1)} %get-tuple-element.120), calls=%async_computation.1 | async-start | bytes 786432 | tf_op jit(solution)/shard_map/all_to_all | solution.py:323
  30.5 8.0 %collective-permute-start.4 = (bf16[160,512]{1,0:T(8,128)(2,1)S(1)}, bf16[160,512]{1,0:T(8,128)(2,1)S(1)}, u32[]{:S(2)}, u32[]{:S(2)}) collective-permute-start(bf16[160,512]{1,0:T(8,128)(2,1)S(1)} %copy-done.28), channel_id=1, source_target_pairs={{0,8},{8,16},{16,24},{24,0},{1,9},{9,17},{17,25},{25,1},{2,10},{10... | collective-permute-start | bytes 491528 | tf_op jit(solution)/shard_map/ppermute | solution.py:1182
  31.2 11.2 %collective-permute-start.5 = (bf16[160,512]{1,0:T(8,128)(2,1)S(1)}, bf16[160,512]{1,0:T(8,128)(2,1)S(1)}, u32[]{:S(2)}, u32[]{:S(2)}) collective-permute-start(bf16[160,512]{1,0:T(8,128)(2,1)S(1)} %copy-done.27), channel_id=1, source_target_pairs={{0,16},{8,24},{16,0},{24,8},{1,17},{9,25},{17,1},{25,9},{2,18},{10... | collective-permute-start | bytes 491528 | tf_op jit(solution)/shard_map/ppermute | solution.py:1182
  31.7 10.6 %collective-permute-start.6 = (bf16[160,512]{1,0:T(8,128)(2,1)S(1)}, bf16[160,512]{1,0:T(8,128)(2,1)S(1)}, u32[]{:S(2)}, u32[]{:S(2)}) collective-permute-start(bf16[160,512]{1,0:T(8,128)(2,1)S(1)} %copy-done.26), channel_id=1, source_target_pairs={{0,24},{8,0},{16,8},{24,16},{1,25},{9,1},{17,9},{25,17},{2,26},{10... | collective-permute-start | bytes 491528 | tf_op jit(solution)/shard_map/ppermute | solution.py:1182
  34.1 9.8 %collective-permute-start.10 = (bf16[64,512]{1,0:T(8,128)(2,1)S(1)}, bf16[64,512]{1,0:T(8,128)(2,1)S(1)}, u32[]{:S(2)}, u32[]{:S(2)}) collective-permute-start(bf16[64,512]{1,0:T(8,128)(2,1)S(1)} %copy-done.14), channel_id=1, source_target_pairs={{0,2},{1,3},{2,4},{3,5},{4,6},{5,7},{6,0},{7,1},{8,10},{9,11},{10,... | collective-permute-start | bytes 196616 | tf_op jit(solution)/shard_map/ppermute | solution.py:1193
  36.1 11.7 %collective-permute-start.11 = (bf16[64,512]{1,0:T(8,128)(2,1)S(1)}, bf16[64,512]{1,0:T(8,128)(2,1)S(1)}, u32[]{:S(2)}, u32[]{:S(2)}) collective-permute-start(bf16[64,512]{1,0:T(8,128)(2,1)S(1)} %copy-done.14), channel_id=1, source_target_pairs={{0,4},{1,5},{2,6},{3,7},{4,0},{5,1},{6,2},{7,3},{8,12},{9,13},{10,... | collective-permute-start | bytes 196616 | tf_op jit(solution)/shard_map/ppermute | solution.py:1193
  38.5 9.2 %collective-permute-start.12 = (bf16[64,512]{1,0:T(8,128)(2,1)S(1)}, bf16[64,512]{1,0:T(8,128)(2,1)S(1)}, u32[]{:S(2)}, u32[]{:S(2)}) collective-permute-start(bf16[64,512]{1,0:T(8,128)(2,1)S(1)} %copy-done.14), channel_id=1, source_target_pairs={{0,6},{1,7},{2,0},{3,1},{4,2},{5,3},{6,4},{7,5},{8,14},{9,15},{10,... | collective-permute-start | bytes 196616 | tf_op jit(solution)/shard_map/ppermute | solution.py:1193
  42.4 26.2 %copy-start.13 = (f32[8,512]{1,0:T(8,128)S(1)}, f32[8,512]{1,0:T(8,128)}, u32[]{:S(2)}) copy-start(f32[8,512]{1,0:T(8,128)} %get-tuple-element.136.vec_ref) | copy-start | bytes 49156
  47.8 3.9 %collective-permute-start.13 = (bf16[8,192,128]{2,1,0:T(8,128)(2,1)S(1)}, bf16[8,192,128]{2,1,0:T(8,128)(2,1)S(1)}, u32[]{:S(2)}, u32[]{:S(2)}) collective-permute-start(bf16[8,192,128]{2,1,0:T(8,128)(2,1)S(1)} %all-to-all-done.1.refs_0_), channel_id=1, source_target_pairs={{0,1},{1,0},{2,3},{3,2},{4,5},{5,4},{6,7},{7,6},{8,9},{9,8},{10,11... | collective-permute-start | bytes 1179656 | tf_op jit(solution)/shard_map/ppermute | solution.py:1196
  47.8 9.1 %collective-permute-start.7 = (bf16[128,512]{1,0:T(8,128)(2,1)S(1)}, bf16[128,512]{1,0:T(8,128)(2,1)S(1)}, u32[]{:S(2)}, u32[]{:S(2)}) collective-permute-start(bf16[128,512]{1,0:T(8,128)(2,1)S(1)} %pad_maximum_fusion.1.refs_0_), channel_id=1, source_target_pairs={{0,2},{1,3},{2,4},{3,5},{4,6},{5,7},{6,0},{7,1},{8,10},{9,11},{10,... | collective-permute-start | bytes 393224 | tf_op jit(solution)/shard_map/ppermute | solution.py:1193
  49.3 11.9 %collective-permute-start.8 = (bf16[128,512]{1,0:T(8,128)(2,1)S(1)}, bf16[128,512]{1,0:T(8,128)(2,1)S(1)}, u32[]{:S(2)}, u32[]{:S(2)}) collective-permute-start(bf16[128,512]{1,0:T(8,128)(2,1)S(1)} %pad_maximum_fusion.1.refs_0_), channel_id=1, source_target_pairs={{0,4},{1,5},{2,6},{3,7},{4,0},{5,1},{6,2},{7,3},{8,12},{9,13},{10,... | collective-permute-start | bytes 393224 | tf_op jit(solution)/shard_map/ppermute | solution.py:1193
  50.6 10.6 %collective-permute-start.9 = (bf16[128,512]{1,0:T(8,128)(2,1)S(1)}, bf16[128,512]{1,0:T(8,128)(2,1)S(1)}, u32[]{:S(2)}, u32[]{:S(2)}) collective-permute-start(bf16[128,512]{1,0:T(8,128)(2,1)S(1)} %pad_maximum_fusion.1.refs_0_), channel_id=1, source_target_pairs={{0,6},{1,7},{2,0},{3,1},{4,2},{5,3},{6,4},{7,5},{8,14},{9,15},{10,... | collective-permute-start | bytes 393224 | tf_op jit(solution)/shard_map/ppermute | solution.py:1193
  61.2 11.4 %all-to-all-start.2 = ((bf16[8,64,128]{2,1,0:T(8,128)(2,1)}), bf16[8,64,128]{2,1,0:T(8,128)(2,1)S(1)}, u32[]{:S(2)}, u32[]{:S(2)}) async-start(bf16[8,64,128]{2,1,0:T(8,128)(2,1)} %get-tuple-element.124), calls=%async_computation.2 | async-start | bytes 262144 | tf_op jit(solution)/shard_map/all_to_all | solution.py:323
  65.8 1.5 collective-permute-start.19
  66.3 6.8 %collective-permute-start.17 = (bf16[128,512]{1,0:T(8,128)(2,1)S(1)}, bf16[128,512]{1,0:T(8,128)(2,1)S(1)}, u32[]{:S(2)}, u32[]{:S(2)}) collective-permute-start(bf16[128,512]{1,0:T(8,128)(2,1)S(1)} %collective-permute-done.9.refs_3_), channel_id=1, source_target_pairs={{0,1},{1,0},{2,3},{3,2},{4,5},{5,4},{6,7},{7,6},{8,9},{9,8},{10,11... | collective-permute-start | bytes 393224 | tf_op jit(solution)/shard_map/ppermute | solution.py:1196
  66.3 7.4 %collective-permute-start.16 = (bf16[128,512]{1,0:T(8,128)(2,1)S(1)}, bf16[128,512]{1,0:T(8,128)(2,1)S(1)}, u32[]{:S(2)}, u32[]{:S(2)}) collective-permute-start(bf16[128,512]{1,0:T(8,128)(2,1)S(1)} %collective-permute-done.8.refs_2_), channel_id=1, source_target_pairs={{0,1},{1,0},{2,3},{3,2},{4,5},{5,4},{6,7},{7,6},{8,9},{9,8},{10,11... | collective-permute-start | bytes 393224 | tf_op jit(solution)/shard_map/ppermute | solution.py:1196
  66.8 1.3 collective-permute-start.20
  66.8 1.4 collective-permute-start.21
  67.3 5.3 %collective-permute-start.18 = (bf16[64,512]{1,0:T(8,128)(2,1)S(1)}, bf16[64,512]{1,0:T(8,128)(2,1)S(1)}, u32[]{:S(2)}, u32[]{:S(2)}) collective-permute-start(bf16[64,512]{1,0:T(8,128)(2,1)S(1)} %copy-done.14), channel_id=1, source_target_pairs={{0,1},{1,0},{2,3},{3,2},{4,5},{5,4},{6,7},{7,6},{8,9},{9,8},{10,11... | collective-permute-start | bytes 196616 | tf_op jit(solution)/shard_map/ppermute | solution.py:1196
  68.1 8.0 %collective-permute-start.15 = (bf16[128,512]{1,0:T(8,128)(2,1)S(1)}, bf16[128,512]{1,0:T(8,128)(2,1)S(1)}, u32[]{:S(2)}, u32[]{:S(2)}) collective-permute-start(bf16[128,512]{1,0:T(8,128)(2,1)S(1)} %collective-permute-done.7.refs_1_), channel_id=1, source_target_pairs={{0,1},{1,0},{2,3},{3,2},{4,5},{5,4},{6,7},{7,6},{8,9},{9,8},{10,11... | collective-permute-start | bytes 393224 | tf_op jit(solution)/shard_map/ppermute | solution.py:1196
  68.3 7.8 %collective-permute-start.14 = (bf16[128,512]{1,0:T(8,128)(2,1)S(1)}, bf16[128,512]{1,0:T(8,128)(2,1)S(1)}, u32[]{:S(2)}, u32[]{:S(2)}) collective-permute-start(bf16[128,512]{1,0:T(8,128)(2,1)S(1)} %pad_maximum_fusion.1.refs_0_), channel_id=1, source_target_pairs={{0,1},{1,0},{2,3},{3,2},{4,5},{5,4},{6,7},{7,6},{8,9},{9,8},{10,11... | collective-permute-start | bytes 393224 | tf_op jit(solution)/shard_map/ppermute | solution.py:1196
  72.6 7.3 %collective-permute-start.22 = (bf16[8,64,128]{2,1,0:T(8,128)(2,1)S(1)}, bf16[8,64,128]{2,1,0:T(8,128)(2,1)S(1)}, u32[]{:S(2)}, u32[]{:S(2)}) collective-permute-start(bf16[8,64,128]{2,1,0:T(8,128)(2,1)S(1)} %all-to-all-done.2.refs_8_), channel_id=1, source_target_pairs={{0,8},{8,16},{16,24},{24,0},{1,9},{9,17},{17,25},{25,1},{2,10},{10... | collective-permute-start | bytes 393224 | tf_op jit(solution)/shard_map/ppermute | solution.py:1182
  73.2 7.5 %collective-permute-start.23 = (bf16[8,64,128]{2,1,0:T(8,128)(2,1)S(1)}, bf16[8,64,128]{2,1,0:T(8,128)(2,1)S(1)}, u32[]{:S(2)}, u32[]{:S(2)}) collective-permute-start(bf16[8,64,128]{2,1,0:T(8,128)(2,1)S(1)} %all-to-all-done.2.refs_8_), channel_id=1, source_target_pairs={{0,16},{8,24},{16,0},{24,8},{1,17},{9,25},{17,1},{25,9},{2,18},{10... | collective-permute-start | bytes 393224 | tf_op jit(solution)/shard_map/ppermute | solution.py:1182
  73.7 6.9 %collective-permute-start.24 = (bf16[8,64,128]{2,1,0:T(8,128)(2,1)S(1)}, bf16[8,64,128]{2,1,0:T(8,128)(2,1)S(1)}, u32[]{:S(2)}, u32[]{:S(2)}) collective-permute-start(bf16[8,64,128]{2,1,0:T(8,128)(2,1)S(1)} %all-to-all-done.2.refs_8_), channel_id=1, source_target_pairs={{0,24},{8,0},{16,8},{24,16},{1,25},{9,1},{17,9},{25,17},{2,26},{10... | collective-permute-start | bytes 393224 | tf_op jit(solution)/shard_map/ppermute | solution.py:1182
  84.0 6.1 %collective-permute-start.25 = (bf16[128,512]{1,0:T(8,128)(2,1)S(1)}, bf16[128,512]{1,0:T(8,128)(2,1)S(1)}, u32[]{:S(2)}, u32[]{:S(2)}) collective-permute-start(bf16[128,512]{1,0:T(8,128)(2,1)S(1)} %get-tuple-element.149), channel_id=1, source_target_pairs={{0,24},{8,0},{16,8},{24,16},{1,25},{9,1},{17,9},{25,17},{2,26},{10... | collective-permute-start | bytes 393224 | tf_op jit(solution)/shard_map/ppermute | solution.py:1182
  86.4 5.0 %collective-permute-start.26 = (bf16[128,512]{1,0:T(8,128)(2,1)S(1)}, bf16[128,512]{1,0:T(8,128)(2,1)S(1)}, u32[]{:S(2)}, u32[]{:S(2)}) collective-permute-start(bf16[128,512]{1,0:T(8,128)(2,1)S(1)} %get-tuple-element.150), channel_id=1, source_target_pairs={{0,16},{8,24},{16,0},{24,8},{1,17},{9,25},{17,1},{25,9},{2,18},{10... | collective-permute-start | bytes 393224 | tf_op jit(solution)/shard_map/ppermute | solution.py:1182
  87.2 5.9 %collective-permute-start.27 = (bf16[128,512]{1,0:T(8,128)(2,1)S(1)}, bf16[128,512]{1,0:T(8,128)(2,1)S(1)}, u32[]{:S(2)}, u32[]{:S(2)}) collective-permute-start(bf16[128,512]{1,0:T(8,128)(2,1)S(1)} %get-tuple-element.151), channel_id=1, source_target_pairs={{0,8},{8,16},{16,24},{24,0},{1,9},{9,17},{17,25},{25,1},{2,10},{10... | collective-permute-start | bytes 393224 | tf_op jit(solution)/shard_map/ppermute | solution.py:1182
  89.3 8.9 %collective-permute-start.28 = (bf16[4,128,512]{2,1,0:T(8,128)(2,1)}, bf16[4,128,512]{2,1,0:T(8,128)(2,1)S(1)}, u32[]{:S(2)}, u32[]{:S(2)}) collective-permute-start(bf16[4,128,512]{2,1,0:T(8,128)(2,1)} %get-tuple-element.153), channel_id=1, source_target_pairs={{0,1},{1,0},{2,3},{3,2},{4,5},{5,4},{6,7},{7,6},{8,9},{9,8},{10,11... | collective-permute-start | bytes 1572872 | tf_op jit(solution)/shard_map/ppermute | solution.py:1196
  95.1 3.0 %collective-permute-start.29 = (bf16[4,64,512]{2,1,0:T(8,128)(2,1)}, bf16[4,64,512]{2,1,0:T(8,128)(2,1)S(1)}, u32[]{:S(2)}, u32[]{:S(2)}) collective-permute-start(bf16[4,64,512]{2,1,0:T(8,128)(2,1)} %get-tuple-element.155), channel_id=1, source_target_pairs={{0,1},{1,0},{2,3},{3,2},{4,5},{5,4},{6,7},{7,6},{8,9},{9,8},{10,11... | collective-permute-start | bytes 786440 | tf_op jit(solution)/shard_map/ppermute | solution.py:1196
  95.1 11.2 %all-to-all-start.3 = ((bf16[32,16,128]{2,1,0:T(8,128)(2,1)}), bf16[32,16,128]{2,1,0:T(8,128)(2,1)S(1)}, u32[]{:S(2)}, u32[]{:S(2)}) async-start(bf16[32,16,128]{2,1,0:T(8,128)(2,1)} %get-tuple-element.157), calls=%async_computation.3 | async-start | bytes 262144 | tf_op jit(solution)/shard_map/all_to_all | solution.py:323
  99.2 7.1 %copy-start.19 = (bf16[8,192,128]{2,1,0:T(8,128)(2,1)S(1)}, bf16[8,192,128]{2,1,0:T(8,128)(2,1)}, u32[]{:S(2)}) copy-start(bf16[8,192,128]{2,1,0:T(8,128)(2,1)} %copy-done.18) | copy-start | bytes 1179652
  99.2 7.1 %copy-start.23 = (f32[4,8,256]{2,1,0:T(8,128)S(1)}, f32[4,8,256]{2,1,0:T(8,128)}, u32[]{:S(2)}) copy-start(f32[4,8,256]{2,1,0:T(8,128)} %get-tuple-element.159.refs_5_) | copy-start | bytes 98308
  100.2 13.6 %collective-permute-start.30 = (bf16[128,512]{1,0:T(8,128)(2,1)}, bf16[128,512]{1,0:T(8,128)(2,1)S(1)}, u32[]{:S(2)}, u32[]{:S(2)}) collective-permute-start(bf16[128,512]{1,0:T(8,128)(2,1)} %get-tuple-element.163), channel_id=1, source_target_pairs={{0,2},{1,3},{2,4},{3,5},{4,6},{5,7},{6,0},{7,1},{8,10},{9,11},{10,... | collective-permute-start | bytes 393224 | tf_op jit(solution)/shard_map/ppermute | solution.py:1193
  102.0 11.8 %collective-permute-start.31 = (bf16[128,512]{1,0:T(8,128)(2,1)}, bf16[128,512]{1,0:T(8,128)(2,1)S(1)}, u32[]{:S(2)}, u32[]{:S(2)}) collective-permute-start(bf16[128,512]{1,0:T(8,128)(2,1)} %get-tuple-element.164), channel_id=1, source_target_pairs={{0,4},{1,5},{2,6},{3,7},{4,0},{5,1},{6,2},{7,3},{8,12},{9,13},{10,... | collective-permute-start | bytes 393224 | tf_op jit(solution)/shard_map/ppermute | solution.py:1193
  104.4 9.4 %collective-permute-start.32 = (bf16[128,512]{1,0:T(8,128)(2,1)S(1)}, bf16[128,512]{1,0:T(8,128)(2,1)S(1)}, u32[]{:S(2)}, u32[]{:S(2)}) collective-permute-start(bf16[128,512]{1,0:T(8,128)(2,1)S(1)} %get-tuple-element.165), channel_id=1, source_target_pairs={{0,6},{1,7},{2,0},{3,1},{4,2},{5,3},{6,4},{7,5},{8,14},{9,15},{10,... | collective-permute-start | bytes 393224 | tf_op jit(solution)/shard_map/ppermute | solution.py:1193
  113.8 1.6 collective-permute-start.33
  115.5 6.2 %copy-start.7 = (f32[128,512]{1,0:T(8,128)S(1)}, f32[128,512]{1,0:T(8,128)}, u32[]{:S(2)}) copy-start(f32[128,512]{1,0:T(8,128)} %get-tuple-element.167.own_ref) | copy-start | bytes 786436
  116.4 19.2 %all-to-all-start.4 = ((bf16[8,192,128]{2,1,0:T(8,128)(2,1)}), bf16[8,192,128]{2,1,0:T(8,128)(2,1)}, u32[]{:S(2)}, u32[]{:S(2)}) async-start(bf16[8,192,128]{2,1,0:T(8,128)(2,1)} %pad_maximum_fusion), calls=%async_computation.4 | async-start | bytes 786432 | tf_op jit(solution)/shard_map/all_to_all | solution.py:323
  123.1 7.3 %collective-permute-start.34 = (bf16[160,512]{1,0:T(8,128)(2,1)}, bf16[160,512]{1,0:T(8,128)(2,1)S(1)}, u32[]{:S(2)}, u32[]{:S(2)}) collective-permute-start(bf16[160,512]{1,0:T(8,128)(2,1)} %get-tuple-element.171), channel_id=1, source_target_pairs={{0,24},{8,0},{16,8},{24,16},{1,25},{9,1},{17,9},{25,17},{2,26},{10... | collective-permute-start | bytes 491528 | tf_op jit(solution)/shard_map/ppermute | solution.py:1182
  125.5 10.0 %collective-permute-start.35 = (bf16[160,512]{1,0:T(8,128)(2,1)}, bf16[160,512]{1,0:T(8,128)(2,1)S(1)}, u32[]{:S(2)}, u32[]{:S(2)}) collective-permute-start(bf16[160,512]{1,0:T(8,128)(2,1)} %get-tuple-element.172), channel_id=1, source_target_pairs={{0,16},{8,24},{16,0},{24,8},{1,17},{9,25},{17,1},{25,9},{2,18},{10... | collective-permute-start | bytes 491528 | tf_op jit(solution)/shard_map/ppermute | solution.py:1182
  126.1 9.5 %collective-permute-start.36 = (bf16[160,512]{1,0:T(8,128)(2,1)}, bf16[160,512]{1,0:T(8,128)(2,1)S(1)}, u32[]{:S(2)}, u32[]{:S(2)}) collective-permute-start(bf16[160,512]{1,0:T(8,128)(2,1)} %get-tuple-element.173), channel_id=1, source_target_pairs={{0,8},{8,16},{16,24},{24,0},{1,9},{9,17},{17,25},{25,1},{2,10},{10... | collective-permute-start | bytes 491528 | tf_op jit(solution)/shard_map/ppermute | solution.py:1182
  140.2 13.9 %copy-start.31 = (bf16[64,512]{1,0:T(8,128)(2,1)S(1)}, bf16[64,512]{1,0:T(8,128)(2,1)}, u32[]{:S(2)}) copy-start(bf16[64,512]{1,0:T(8,128)(2,1)} %get-tuple-element.198) | copy-start | bytes 196612
  140.2 15.7 %copy-start.30 = (bf16[64,512]{1,0:T(8,128)(2,1)S(1)}, bf16[64,512]{1,0:T(8,128)(2,1)}, u32[]{:S(2)}) copy-start(bf16[64,512]{1,0:T(8,128)(2,1)} %get-tuple-element.200) | copy-start | bytes 196612
  140.2 18.7 %copy-start.29 = (bf16[64,512]{1,0:T(8,128)(2,1)S(1)}, bf16[64,512]{1,0:T(8,128)(2,1)}, u32[]{:S(2)}) copy-start(bf16[64,512]{1,0:T(8,128)(2,1)} %get-tuple-element.202) | copy-start | bytes 196612
  140.2 19.5 %copy-start.24 = (f32[128,512]{1,0:T(8,128)S(1)}, f32[128,512]{1,0:T(8,128)}, u32[]{:S(2)}) copy-start(f32[128,512]{1,0:T(8,128)} %get-tuple-element.140) | copy-start | bytes 786436
  140.2 24.5 %all-to-all-start.5 = ((bf16[32,64,128]{2,1,0:T(8,128)(2,1)}), bf16[32,64,128]{2,1,0:T(8,128)(2,1)S(1)}, u32[]{:S(2)}, u32[]{:S(2)}) async-start(bf16[32,64,128]{2,1,0:T(8,128)(2,1)} %get-tuple-element.184), calls=%async_computation.5 | async-start | bytes 1048576 | tf_op jit(solution)/shard_map/all_to_all | solution.py:323
  144.1 16.4 %copy-start.6 = (f32[128,512]{1,0:T(8,128)S(1)}, f32[128,512]{1,0:T(8,128)}, u32[]{:S(2)}) copy-start(f32[128,512]{1,0:T(8,128)} %get-tuple-element.174.grad_ref) | copy-start | bytes 786436
  144.6 9.5 %collective-permute-start.37 = (bf16[128,512]{1,0:T(8,128)(2,1)S(1)}, bf16[128,512]{1,0:T(8,128)(2,1)S(1)}, u32[]{:S(2)}, u32[]{:S(2)}) collective-permute-start(bf16[128,512]{1,0:T(8,128)(2,1)S(1)} %get-tuple-element.181), channel_id=1, source_target_pairs={{0,24},{8,0},{16,8},{24,16},{1,25},{9,1},{17,9},{25,17},{2,26},{10... | collective-permute-start | bytes 393224 | tf_op jit(solution)/shard_map/ppermute | solution.py:1182
  147.3 13.2 %collective-permute-start.38 = (bf16[128,512]{1,0:T(8,128)(2,1)S(1)}, bf16[128,512]{1,0:T(8,128)(2,1)S(1)}, u32[]{:S(2)}, u32[]{:S(2)}) collective-permute-start(bf16[128,512]{1,0:T(8,128)(2,1)S(1)} %get-tuple-element.182), channel_id=1, source_target_pairs={{0,16},{8,24},{16,0},{24,8},{1,17},{9,25},{17,1},{25,9},{2,18},{10... | collective-permute-start | bytes 393224 | tf_op jit(solution)/shard_map/ppermute | solution.py:1182
  147.9 12.6 %collective-permute-start.39 = (bf16[128,512]{1,0:T(8,128)(2,1)S(1)}, bf16[128,512]{1,0:T(8,128)(2,1)S(1)}, u32[]{:S(2)}, u32[]{:S(2)}) collective-permute-start(bf16[128,512]{1,0:T(8,128)(2,1)S(1)} %get-tuple-element.183), channel_id=1, source_target_pairs={{0,8},{8,16},{16,24},{24,0},{1,9},{9,17},{17,25},{25,1},{2,10},{10... | collective-permute-start | bytes 393224 | tf_op jit(solution)/shard_map/ppermute | solution.py:1182
  154.1 7.4 %collective-permute-start.40 = (bf16[64,512]{1,0:T(8,128)(2,1)S(1)}, bf16[64,512]{1,0:T(8,128)(2,1)S(1)}, u32[]{:S(2)}, u32[]{:S(2)}) collective-permute-start(bf16[64,512]{1,0:T(8,128)(2,1)S(1)} %copy-done.31), channel_id=1, source_target_pairs={{0,2},{1,3},{2,4},{3,5},{4,6},{5,7},{6,0},{7,1},{8,10},{9,11},{10,... | collective-permute-start | bytes 196616 | tf_op jit(solution)/shard_map/ppermute | solution.py:1193
  155.9 7.7 %collective-permute-start.41 = (bf16[64,512]{1,0:T(8,128)(2,1)S(1)}, bf16[64,512]{1,0:T(8,128)(2,1)S(1)}, u32[]{:S(2)}, u32[]{:S(2)}) collective-permute-start(bf16[64,512]{1,0:T(8,128)(2,1)S(1)} %copy-done.30), channel_id=1, source_target_pairs={{0,4},{1,5},{2,6},{3,7},{4,0},{5,1},{6,2},{7,3},{8,12},{9,13},{10,... | collective-permute-start | bytes 196616 | tf_op jit(solution)/shard_map/ppermute | solution.py:1193
  158.9 5.1 %collective-permute-start.42 = (bf16[64,512]{1,0:T(8,128)(2,1)S(1)}, bf16[64,512]{1,0:T(8,128)(2,1)S(1)}, u32[]{:S(2)}, u32[]{:S(2)}) collective-permute-start(bf16[64,512]{1,0:T(8,128)(2,1)S(1)} %copy-done.29), channel_id=1, source_target_pairs={{0,6},{1,7},{2,0},{3,1},{4,2},{5,3},{6,4},{7,5},{8,14},{9,15},{10,... | collective-permute-start | bytes 196616 | tf_op jit(solution)/shard_map/ppermute | solution.py:1193
  (17 other events, 83.0 us)

commit v4 on v3

--- a/solution.py
+++ b/solution.py
@@ -214,6 +214,25 @@
                 grad_refs[part][tile * geo.per_tile + i] = rows.astype(grad_refs[part].dtype)
 
 
+COST = {
+    "assemble": 100000000,
+    "attention_backward": 30000000000,
+    "attention_forward": 30000000000,
+    "feed": 30000000000,
+    "feed_grad": 100000000,
+    "final": 100000000,
+    "fold": 30000000000,
+    "input_grad": 100000000,
+    "input_partial": 30000000000,
+    "middle_grad": 30000000000,
+    "norm_again": 100000000,
+    "part_sum": 30000000000,
+    "project": 30000000000,
+    "project_grad": 30000000000,
+    "split": 100000000,
+}
+
+
 VMEM_LIMIT = 16 * 2**20
 
 
@@ -221,7 +240,7 @@
     return (pltpu.HBM(shape, dtype),)
 
 
-def local_call(kernel, name, scalars, arrays, outs, scratch=(), flops=10**8, limit=VMEM_LIMIT):
+def local_call(kernel, name, scalars, arrays, outs, scratch=(), limit=VMEM_LIMIT):
     return pl.pallas_call(
         kernel,
         out_shape=tuple(o[0] if len(o) == 1 else jax.ShapeDtypeStruct(*o) for o in outs),
@@ -230,7 +249,7 @@
         out_specs=tuple([pl.BlockSpec(memory_space=pltpu.VMEM)] * len(outs)),
         scratch_shapes=list(scratch),
         compiler_params=pltpu.CompilerParams(vmem_limit_bytes=limit),
-        cost_estimate=pl.CostEstimate(flops=flops, bytes_accessed=10**6, transcendentals=0),
+        cost_estimate=pl.CostEstimate(flops=COST.get(name, 10**8), bytes_accessed=10**6, transcendentals=0),
         name=name,
     )(scalars, *arrays)
 
@@ -251,7 +270,6 @@
             far((geo.tiles, 8, geo.tile), f32),
         ],
         [pltpu.VMEM((geo.parts, geo.tiles, ONES + HD, geo.tile), bf16)],
-        flops=30 * 10**9,
         limit=attention_limit(geo),
     )
 
@@ -269,7 +287,6 @@
             pltpu.VMEM((geo.parts, geo.tiles, geo.tile, LANES), f32),
             pltpu.VMEM((geo.parts, geo.tiles, LANES, geo.tile), bf16),
         ],
-        flops=30 * 10**9,
         limit=attention_limit(geo),
     )
 
@@ -991,17 +1008,23 @@
 
 
 def project_grad_kernel(sz, scal_ref, early_ref, *refs):
-    far_refs, (send_ref, d_out_ref), refs = refs[:4], refs[4:6], refs[6:]
-    got_ref, n_ref, u_ref, w_ref, d_ref, send_scr, sems = refs
+    far_refs, (keep_ref, give_ref), refs = refs[:4], refs[4:6], refs[6:]
+    part_refs, refs = refs[: sz.heads], refs[sz.heads :]
+    got_ref, n_ref, u_ref, w_ref, d_ref, send_scr, own_scr, part_scr, sems = refs
     copies = [
         pltpu.make_async_copy(far_refs[i], ref, sems.at[i])
         for i, ref in enumerate((got_ref, n_ref, u_ref, w_ref))
     ]
     n_w = sz.w_chunk
+    mine = lax.rem(my_blk_of(sz, scal_ref), sz.parts)
     copies += [
-        pltpu.make_async_copy(d_ref, d_out_ref, sems.at[4]),
-        pltpu.make_async_copy(send_scr.at[:, :n_w], send_ref.at[:, :n_w], sems.at[5]),
-        pltpu.make_async_copy(send_scr.at[:, n_w:], send_ref.at[:, n_w:], sems.at[6]),
+        pltpu.make_async_copy(send_scr.at[:, sz.parts - 1 - mine], give_ref, sems.at[4]),
+        pltpu.make_async_copy(send_scr.at[:, mine], keep_ref, sems.at[5]),
+        pltpu.make_async_copy(own_scr, part_refs[0], sems.at[6]),
+    ]
+    copies += [
+        pltpu.make_async_copy(part_scr.at[s - 1], part_refs[s], sems.at[6 + s])
+        for s in range(1, sz.heads)
     ]
     for copy in copies[:4]:
         copy.start()
@@ -1025,15 +1048,14 @@
                         sz.task(seq, local, part), pl.ds(kv_at, sz.run)
                     ]
     d_proj = d_ref[...]
-    copies[4].start()
     copies[1].wait()
     grad_w = dot_nn(n_ref[...], d_proj).astype(bf16)
     for dev in range(sz.devices):
         rows = slice(dev * sz.w_rows, (dev + 1) * sz.w_rows)
         for i in range(1 + sz.local):
             cols = slice(i * LANES, (i + 1) * LANES)
-            send_scr[dev, i * sz.w_rows : (i + 1) * sz.w_rows] = grad_w[rows, cols]
-    copies[5].start()
+            to = (dev // sz.parts, dev % sz.parts)
+            send_scr[*to, i * sz.w_rows : (i + 1) * sz.w_rows] = grad_w[rows, cols]
     copies[2].wait()
     copies[3].wait()
     weights = w_ref[...].astype(f32)
@@ -1056,8 +1078,15 @@
         + both_levels(sum_q, 2 * per, head * LANES, (6, 7), sz.devices)
         + both_levels(sum_v, 2 * per, sz.width + head * LANES, (6, 7), sz.devices)
     )
-    send_scr[:, n_w:, :] = two_levels(small.reshape(sz.devices, SMALL, LANES))
-    copies[6].start()
+    small = two_levels(small.reshape(-1, sz.parts, SMALL, LANES))
+    send_scr[:, :, n_w:, :] = small
+    copies[4].start()
+    copies[5].start()
+    grad_one = dot_nt(d_proj, w_ref[...])
+    own_scr[...] = grad_one[: sz.mine]
+    part_scr[...] = grad_one[sz.mine :].astype(bf16).reshape(part_scr.shape)
+    for copy in copies[6:]:
+        copy.start()
     for copy in copies[4:]:
         copy.wait()
 
@@ -1067,10 +1096,11 @@
     return jnp.concatenate([high, small - high], axis=-2).astype(bf16)
 
 
-def input_partial_kernel(sz, scal_ref, d_ref, w_ref, *part_refs):
-    grad_one = dot_nt(d_ref[...], w_ref[...])
-    for slot, ref in enumerate(part_refs):
-        ref[...] = grad_one[slot * sz.mine : (slot + 1) * sz.mine].astype(ref.dtype)
+def fold_kernel(sz, scal_ref, keep_ref, got_ref, send_ref):
+    n_w = sz.w_chunk
+    total = keep_ref[...].astype(f32) + got_ref[...].astype(f32)
+    send_ref[:, :n_w] = total[:, :n_w].astype(bf16)
+    send_ref[:, n_w:] = two_levels(total[:, n_w : n_w + SMALL] + total[:, n_w + SMALL :])
 
 
 def input_grad_kernel(sz, scal_ref, vec_ref, grad_ref, x_ref, *refs):
@@ -1132,8 +1162,8 @@
         up_ref[:, pl.ds(at, sz.hidden_slice)] = piece.astype(f32)
     for head in range(sz.heads):
         total = jnp.zeros((sz.w_chunk, LANES), f32)
-        for blk in range(sz.blocks):
-            total = total + got_ref[head * sz.blocks + blk, : sz.w_chunk].astype(f32)
+        for group in range(sz.groups):
+            total = total + got_ref[head * sz.groups + group, : sz.w_chunk].astype(f32)
         at = head * LANES
         w_ref[:, at : at + LANES] = total[: sz.w_rows]
         low, high = halves(total[sz.w_rows : 2 * sz.w_rows], total[2 * sz.w_rows :])
@@ -1175,8 +1205,9 @@
     geo = AttentionShape(sz.blocks, sz.part_rows, sz.parts, sz.run, sz.sub)
     token_shape = (sz.mine, sz.width)
 
-    def call(kernel, name, arrays, outs, scratch=(), flops=10**8):
-        return local_call(functools.partial(kernel, sz), name, scal, arrays, outs, scratch, flops)
+    def call(kernel, name, arrays, outs, scratch=(), limit=VMEM_LIMIT):
+        kernel = functools.partial(kernel, sz)
+        return local_call(kernel, name, scal, arrays, outs, scratch, limit)
 
     def around(x, step):
         return lax.ppermute(x, "head", [(i, (i + step) % n) for i in range(n)])
@@ -1224,7 +1255,7 @@
     scalars, bounds = attention_bounds(
         segments, token_valid, my_seq, my_part, geo, sz.heads, sz.sub
     )
-    got_parts[0] = after(got_parts[0], scalars, bounds, *pieces)
+    got_parts[0] = after(got_parts[0], scalars, bounds)
     send, w_slice, vec = call(
         project_kernel,
         "project",
@@ -1235,7 +1266,6 @@
             far((SMALL, sz.width), f32),
         ],
         [pltpu.VMEM((sz.devices * SMALL, LANES), f32)],
-        flops=30 * 10**9,
     )
     column = jnp.concatenate([v[sz.mine :] for v in g_slots], axis=0)
     columns = [column] + [around_groups(column, d) for d in range(1, sz.groups)]
@@ -1245,7 +1275,6 @@
     task = after(task, column, *downs)
     others = [around_parts(task, step) for step in range(1, sz.parts)]
     o_task, ot, lse = attention_forward(geo, scalars, [task, *others], bounds)
-    o_task = after(o_task, *columns)
     columns += [around_parts(after(v, o_task), d) for d in range(1, sz.parts) for v in columns]
     downs += [around_parts(after(v, o_task), d) for d in range(1, sz.parts) for v in downs]
     square = ((sz.width, sz.width), bf16)
@@ -1255,7 +1284,7 @@
     n_one, u_one = call(
         norm_again_kernel, "norm_again", [after(vec, o_task), *x_slots], [turned, turned]
     )
-    mixed = after(mixed, n_one)
+    mixed = after(mixed, n_one, *columns)
     m_slots = [mixed] + [around(mixed, d) for d in range(1, n)]
 
     outs = call(
@@ -1272,7 +1301,6 @@
         [
             pltpu.VMEM((n, *token_shape), bf16),
         ],
-        flops=30 * 10**9,
     )
     grad_two, feed = outs[:n], outs[n : 2 * n]
     middle, activated, grad_hidden, n_two, mixed_own, feed_sums = outs[2 * n :]
@@ -1288,7 +1316,6 @@
         [activated, grad_hidden, n_two, *g_slots],
         shared(sz.f_rows + n * sz.w_rows),
     )
-    grad_two[0] = after(grad_two[0], keep)
 
     grad_middle, branch, send, branch_sums, keep_out, give_out = call(
         middle_grad_kernel,
@@ -1301,7 +1328,6 @@
             far((SMALL, sz.width), f32),
             *shared(n * sz.w_rows),
         ],
-        flops=30 * 10**9,
     )
     do_task = exchange(send, ALL)
     given = around_parts(give, 1)
@@ -1336,39 +1362,43 @@
     )
     early = rest.pop()
     rest = [around(v, -d - 1) for d, v in enumerate(rest)]
-    got = after(got, *rest)
+    got = after(got, rest[0], rest[2])
     wide = (1 + sz.local) * LANES
-    send_shape = (sz.devices, sz.w_chunk + 2 * SMALL, LANES)
-    send, d_proj = pl.pallas_call(
+    send_shape = (n * sz.groups, sz.w_chunk + 2 * SMALL, LANES)
+    keep, give, *outs = pl.pallas_call(
         functools.partial(project_grad_kernel, sz),
-        out_shape=(pltpu.HBM(send_shape, bf16), pltpu.HBM((sz.tokens, wide), bf16)),
+        out_shape=(
+            pltpu.HBM(send_shape, bf16),
+            pltpu.HBM(send_shape, bf16),
+            pltpu.HBM(token_shape, f32),
+            *[pltpu.HBM(token_shape, bf16)] * (n - 1),
+        ),
         in_specs=[pl.BlockSpec(memory_space=pltpu.SMEM), pl.BlockSpec(memory_space=pltpu.VMEM)]
         + [pl.BlockSpec(memory_space=pltpu.HBM)] * 4,
-        out_specs=tuple([pl.BlockSpec(memory_space=pltpu.HBM)] * 2),
+        out_specs=tuple([pl.BlockSpec(memory_space=pltpu.HBM)] * (2 + n)),
         scratch_shapes=[
             pltpu.VMEM(got.shape, bf16),
             pltpu.VMEM((sz.width, sz.tokens), bf16),
             pltpu.VMEM((sz.width, sz.tokens), bf16),
             pltpu.VMEM((sz.width, wide), bf16),
             pltpu.VMEM((sz.tokens, wide), bf16),
-            pltpu.VMEM(send_shape, bf16),
-            pltpu.SemaphoreType.DMA((7,)),
+            pltpu.VMEM((send_shape[0], sz.parts, *send_shape[1:]), bf16),
+            pltpu.VMEM(token_shape, f32),
+            pltpu.VMEM((n - 1, *token_shape), bf16),
+            pltpu.SemaphoreType.DMA((6 + n,)),
         ],
         compiler_params=pltpu.CompilerParams(vmem_limit_bytes=63 * 2**20),
-        cost_estimate=pl.CostEstimate(flops=30 * 10**9, bytes_accessed=10**6, transcendentals=0),
+        cost_estimate=pl.CostEstimate(
+            flops=COST["project_grad"], bytes_accessed=10**6, transcendentals=0
+        ),
         name="project_grad",
     )(scal, early, got, n_one, u_one, w_slice)
-    got = exchange(send, ALL)
-    outs = call(
-        input_partial_kernel,
-        "input_partial",
-        [d_proj, w_slice],
-        [(token_shape, f32)] + [(token_shape, bf16)] * (n - 1),
-    )
+    (send,) = call(fold_kernel, "fold", [keep, around_parts(give, 1)], [(send_shape, bf16)])
+    got = exchange(send, ("head", "group"))
     grad_one = [outs[0]] + [around(outs[d], -d) for d in range(1, n)]
     down_grad = down_sum[0]
     for d in range(1, sz.groups):
-        down_grad = down_grad + around_groups(after(down_sum[d], grad_one[1]), d).astype(f32)
+        down_grad = down_grad + around_groups(after(down_sum[d], outs[1]), d).astype(f32)
     (input_grad,) = call(
         input_grad_kernel,
         "input_grad",

time: 166 us -> 159 us (0.958)
  waiting for transfers between devices: 39.7 us -> 33.9 us
  Pallas kernels: 36.3 us -> 33.7 us
  local copies, waits for them, and re-layouts: 3.45 us -> 5.13 us
    ppermute x12, waiting for transfers between devices: 12.3 us -> 6.27 us  [around_groups(): return lax.ppermute(x, BLK, pairs)]
    pallas_call x13, Pallas kernels: 28.2 us -> 25.2 us  [local_call(): pl.pallas_call(kernel, out_shape=tuple((o[0] if len(o) == 1 else jax.Shap...]
    ppermute x12, starting transfers between devices: 23.4 us -> 21.5 us  [around_groups(): return lax.ppermute(x, BLK, pairs)]
  transfers between devices with their start and end apart: 49 -> 50, of which waited for: 18 -> 19; matrix products, arithmetic and copies ran while one was open for 4% -> 4% of each run, Pallas kernels for 14% -> 13%
where the time goes in v4:
time: 159 us; the launch traced here: 158 us
  starting transfers between devices  77.4 us (49%)
  waiting for transfers between devices  33.9 us (21%)
  Pallas kernels  33.7 us (21%)
  other arithmetic  5.85 us (4%)
  local copies, waits for them, and re-layouts  5.13 us (3%)
  between operations  1.81 us (1%)
    all_to_all x6, starting transfers between devices, exchange(): return lax.all_to_all(x, axis, split_axis=0, concat_axis=0, tiled=True)  30.6 us
    pallas_call x13, Pallas kernels, local_call(): pl.pallas_call(kernel, out_shape=tuple((o[0] if len(o) == 1 else jax.Shap...  25.2 us
    ppermute x18, starting transfers between devices, around(): return lax.ppermute(x, 'head', [(i, (i + step) % n) for i in range(n)])  23 us
    ppermute x18, waiting for transfers between devices, around(): return lax.ppermute(x, 'head', [(i, (i + step) % n) for i in range(n)])  21.8 us
    ppermute x12, starting transfers between devices, around_groups(): return lax.ppermute(x, BLK, pairs)  21.5 us
    ppermute x12, waiting for transfers between devices, around_groups(): return lax.ppermute(x, BLK, pairs)  6.27 us
    pallas_call x1, Pallas kernels, on_device_fused(): pl.pallas_call(functools.partial(project_grad_kernel, sz), out_shape=(plt...  4.99 us
    pallas_call x2, Pallas kernels, staged_call(): pl.pallas_call(kernel, out_shape=tuple((jax.ShapeDtypeStruct(*o) for o in...  3.55 us
  transfers between devices with their start and end apart: 50, of which 19 were waited for; matrix products, arithmetic and copies ran while one was open for 4% of the time, Pallas kernels for 13%

profile of v4, /device:TPU:0, one launch (start us, length us, event | category | flops | bytes accessed | tf_op | source)
XLA Modules:
  0.0 157.9 jit_solution(5957339067233263200)
XLA Ops:
  0.7 1.7 %pack.1 = bf16[16,56,128]{2,1,0:T(8,128)(2,1)} custom-call(s32[1]{0:T(128)} %bitcast.scal_ref, bf16[16,1536]{1,0:T(8,128)(2,1)} %refs_0_.1, bf16[1,16]{1,0:T(2,128)(2,1)} %bitcast.47, bf16[1,16]{1,0:T(2,128)(2,1)} %bitcast.48, bf16[1,16]{1,0:T(2,128)(2,1)} %bitcast.49, bf16[1,16]{1,0:T(2,128)(2,1)} %bitcast.50, bf16[1,16]{1,0:T(2,128)(2,1)} %bitcast.51, ...), custom_call_target="tpu_custom_call" | custom-call | tf_op jit(solution)/shard_map/pack/pallas_call | solution.py:690
  2.4 8.3 %all-to-all-start = ((bf16[16,56,128]{2,1,0:T(8,128)(2,1)}), bf16[16,56,128]{2,1,0:T(8,128)(2,1)S(1)}, u32[]{:S(2)}, u32[]{:S(2)}) async-start(bf16[16,56,128]{2,1,0:T(8,128)(2,1)} %pack.1), calls=%async_computation | async-start | bytes 458752 | tf_op jit(solution)/shard_map/all_to_all | solution.py:340
  10.7 1.9 %collective-permute-start.1 = (bf16[128,512]{1,0:T(8,128)(2,1)}, bf16[128,512]{1,0:T(8,128)(2,1)S(1)}, u32[]{:S(2)}, u32[]{:S(2)}) collective-permute-start(bf16[128,512]{1,0:T(8,128)(2,1)} %bitcast.30), channel_id=1, source_target_pairs={{0,8},{8,16},{16,24},{24,0},{1,9},{9,17},{17,25},{25,1},{2,10},{10... | collective-permute-start | bytes 393224 | tf_op jit(solution)/shard_map/ppermute | solution.py:1213
  12.7 1.5 collective-permute-start.2
  14.1 1.5 collective-permute-start.3
  16.1 2.0 %fusion.2 = (s32[2048]{0:T(1024)S(1)}, s32[1,2048]{1,0:T(1,128)S(1)}, s32[]{:T(128)}) fusion(s32[]{:T(128)} %broadcast.160, s32[2,2048]{1,0:T(2,128)} %param.17, s32[]{:T(128)S(6)} %select_n.38, s32[2,2048]{1,0:T(2,128)} %param.18), kind=kLoop, calls=%fused_computation.29 | loop fusion | flops 2047 | bytes 32780 | tf_op jit(solution)/shard_map/jit(dynamic_index_in_dim)/dynamic_slice | solution.py:318
  20.0 1.0 convert_reduce_fusion
  21.8 0.8 collective-permute-done.refs_1_
  22.6 1.8 %project.1 = (bf16[8,192,128]{2,1,0:T(8,128)(2,1)}, bf16[512,384]{1,0:T(8,128)(2,1)}, f32[8,512]{1,0:T(8,128)}) custom-call(s32[1]{0:T(128)} %bitcast.scal_ref, bf16[16,56,128]{2,1,0:T(8,128)(2,1)S(1)} %all-to-all-done.refs_0_, bf16[16,56,128]{2,1,0:T(8,128)(2,1)S(1)} %collective-permute-done.refs_1_, bf16[128,512]{1,0:T(8,128)(2,1)S(1)} %bitcast.33, ...), custom_call_target="tpu_custom_call" | custom-call | flops 30000001024 | bytes 1000000 | tf_op jit(solution)/shard_map/project/pallas_call | solution.py:244
  24.4 4.5 %all-to-all-start.1 = ((bf16[8,192,128]{2,1,0:T(8,128)(2,1)}), bf16[8,192,128]{2,1,0:T(8,128)(2,1)S(1)}, u32[]{:S(2)}, u32[]{:S(2)}) async-start(bf16[8,192,128]{2,1,0:T(8,128)(2,1)} %get-tuple-element.118), calls=%async_computation.1 | async-start | bytes 786432 | tf_op jit(solution)/shard_map/all_to_all | solution.py:340
  28.9 1.8 %pieces.1 = (bf16[160,512]{1,0:T(8,128)(2,1)}, bf16[160,512]{1,0:T(8,128)(2,1)}, bf16[160,512]{1,0:T(8,128)(2,1)}, bf16[160,512]{1,0:T(8,128)(2,1)}) custom-call(s32[1]{0:T(128)} %bitcast.scal_ref, bf16[128,512]{1,0:T(8,128)(2,1)} %bitcast.37, bf16[16,2048]{1,0:T(8,128)(2,1)} %refs_1_.1, bf16[16,512]{1,0:T(8,128)(2,1)} %refs_2_.1), custom_call_target="tpu_custom_call" | custom-call | tf_op jit(solution)/shard_map/pieces/pallas_call | solution.py:690
  31.9 2.4 %collective-permute-start.6 = (bf16[160,512]{1,0:T(8,128)(2,1)}, bf16[160,512]{1,0:T(8,128)(2,1)S(1)}, u32[]{:S(2)}, u32[]{:S(2)}) collective-permute-start(bf16[160,512]{1,0:T(8,128)(2,1)} %get-tuple-element.117), channel_id=1, source_target_pairs={{0,24},{8,0},{16,8},{24,16},{1,25},{9,1},{17,9},{25,17},{2,26},{10... | collective-permute-start | bytes 491528 | tf_op jit(solution)/shard_map/ppermute | solution.py:1213
  34.3 0.8 slice.28
  35.0 2.0 %collective-permute-start.10 = (bf16[64,512]{1,0:T(8,128)(2,1)}, bf16[64,512]{1,0:T(8,128)(2,1)S(1)}, u32[]{:S(2)}, u32[]{:S(2)}) collective-permute-start(bf16[64,512]{1,0:T(8,128)(2,1)} %refs_8_), channel_id=1, source_target_pairs={{0,2},{1,3},{2,4},{3,5},{4,6},{5,7},{6,0},{7,1},{8,10},{9,11},{10,... | collective-permute-start | bytes 196616 | tf_op jit(solution)/shard_map/ppermute | solution.py:1224
  37.1 2.4 %collective-permute-start.11 = (bf16[64,512]{1,0:T(8,128)(2,1)}, bf16[64,512]{1,0:T(8,128)(2,1)S(1)}, u32[]{:S(2)}, u32[]{:S(2)}) collective-permute-start(bf16[64,512]{1,0:T(8,128)(2,1)} %refs_8_), channel_id=1, source_target_pairs={{0,4},{1,5},{2,6},{3,7},{4,0},{5,1},{6,2},{7,3},{8,12},{9,13},{10,... | collective-permute-start | bytes 196616 | tf_op jit(solution)/shard_map/ppermute | solution.py:1224
  39.4 3.4 %collective-permute-start.12 = (bf16[64,512]{1,0:T(8,128)(2,1)}, bf16[64,512]{1,0:T(8,128)(2,1)S(1)}, u32[]{:S(2)}, u32[]{:S(2)}) collective-permute-start(bf16[64,512]{1,0:T(8,128)(2,1)} %refs_8_), channel_id=1, source_target_pairs={{0,6},{1,7},{2,0},{3,1},{4,2},{5,3},{6,4},{7,5},{8,14},{9,15},{10,... | collective-permute-start | bytes 196616 | tf_op jit(solution)/shard_map/ppermute | solution.py:1224
  42.9 3.2 %collective-permute-done.11.refs_10_ = bf16[64,512]{1,0:T(8,128)(2,1)S(1)} collective-permute-done((bf16[64,512]{1,0:T(8,128)(2,1)}, bf16[64,512]{1,0:T(8,128)(2,1)S(1)}, u32[]{:S(2)}, u32[]{:S(2)}) %collective-permute-start.11) | collective-permute-done | bytes 65568 | tf_op jit(solution)/shard_map/ppermute | solution.py:1224
  46.2 2.9 %collective-permute-start.9 = (bf16[128,512]{1,0:T(8,128)(2,1)S(1)}, bf16[128,512]{1,0:T(8,128)(2,1)S(1)}, u32[]{:S(2)}, u32[]{:S(2)}) collective-permute-start(bf16[128,512]{1,0:T(8,128)(2,1)S(1)} %pad_maximum_fusion.1.refs_0_), channel_id=1, source_target_pairs={{0,6},{1,7},{2,0},{3,1},{4,2},{5,3},{6,4},{7,5},{8,14},{9,15},{10,... | collective-permute-start | bytes 393224 | tf_op jit(solution)/shard_map/ppermute | solution.py:1224
  49.7 3.9 %attention_forward.1 = (bf16[8,64,128]{2,1,0:T(8,128)(2,1)}, f32[4,64,256]{2,1,0:T(8,128)}, f32[4,8,256]{2,1,0:T(8,128)}) custom-call(s32[6]{0:T(128)S(1)} %pad_add_fusion.scal_ref, bf16[8,192,128]{2,1,0:T(8,128)(2,1)S(1)} %all-to-all-done.1.refs_0_, bf16[8,192,128]{2,1,0:T(8,128)(2,1)S(1)} %collective-permute-done.13.refs_1_, ...), custom_call_target="tpu_custom_call" | custom-call | flops 30000001024 | bytes 1000000 | tf_op jit(solution)/shard_map/attention_forward/pallas_call | solution.py:244
  53.6 5.7 %all-to-all-start.2 = ((bf16[8,64,128]{2,1,0:T(8,128)(2,1)}), bf16[8,64,128]{2,1,0:T(8,128)(2,1)S(1)}, u32[]{:S(2)}, u32[]{:S(2)}) async-start(bf16[8,64,128]{2,1,0:T(8,128)(2,1)} %get-tuple-element.121), calls=%async_computation.2 | async-start | bytes 262144 | tf_op jit(solution)/shard_map/all_to_all | solution.py:340
  59.8 1.6 %collective-permute-done.8.refs_2_ = bf16[128,512]{1,0:T(8,128)(2,1)S(1)} collective-permute-done((bf16[128,512]{1,0:T(8,128)(2,1)S(1)}, bf16[128,512]{1,0:T(8,128)(2,1)S(1)}, u32[]{:S(2)}, u32[]{:S(2)}) %collective-permute-start.8) | collective-permute-done | bytes 131104 | tf_op jit(solution)/shard_map/ppermute | solution.py:1224
  62.5 1.6 %norm_again.1 = (bf16[512,512]{1,0:T(8,128)(2,1)}, bf16[512,512]{1,0:T(8,128)(2,1)}) custom-call(s32[1]{0:T(128)} %bitcast.scal_ref, f32[8,512]{1,0:T(8,128)S(1)} %copy-done.11, bf16[128,512]{1,0:T(8,128)(2,1)S(1)} %bitcast.34, bf16[128,512]{1,0:T(8,128)(2,1)S(1)} %collective-permute-done.1.refs_3_.refs_1_, ...), custom_call_target="tpu_custom_call" | custom-call | flops 100000000 | bytes 1000000 | tf_op jit(solution)/shard_map/norm_again/pallas_call | solution.py:244
  64.2 1.9 %all-to-all-done.2.refs_8_ = bf16[8,64,128]{2,1,0:T(8,128)(2,1)S(1)} async-done(((bf16[8,64,128]{2,1,0:T(8,128)(2,1)}), bf16[8,64,128]{2,1,0:T(8,128)(2,1)S(1)}, u32[]{:S(2)}, u32[]{:S(2)}) %all-to-all-start.2) | async-done | bytes 131104 | tf_op jit(solution)/shard_map/all_to_all | solution.py:340
  67.2 2.4 %collective-permute-start.24 = (bf16[8,64,128]{2,1,0:T(8,128)(2,1)S(1)}, bf16[8,64,128]{2,1,0:T(8,128)(2,1)S(1)}, u32[]{:S(2)}, u32[]{:S(2)}) collective-permute-start(bf16[8,64,128]{2,1,0:T(8,128)(2,1)S(1)} %all-to-all-done.2.refs_8_), channel_id=1, source_target_pairs={{0,24},{8,0},{16,8},{24,16},{1,25},{9,1},{17,9},{25,17},{2,26},{10... | collective-permute-start | bytes 393224 | tf_op jit(solution)/shard_map/ppermute | solution.py:1213
  71.2 1.0 assemble.1
  72.2 1.2 collective-permute-done.22.refs_9_
  73.4 0.8 collective-permute-done.23.refs_10_
  74.2 3.3 %feed.1 = (f32[128,512]{1,0:T(8,128)}, bf16[128,512]{1,0:T(8,128)(2,1)S(1)}, bf16[128,512]{1,0:T(8,128)(2,1)S(1)}, bf16[128,512]{1,0:T(8,128)(2,1)S(1)}, f32[128...) custom-call(s32[1]{0:T(128)} %bitcast.scal_ref, ...), custom_call_target="tpu_custom_call" | custom-call | flops 30000001024 | bytes 1000000 | tf_op jit(solution)/shard_map/feed/pallas_call | solution.py:244
  77.5 2.3 %collective-permute-start.25 = (bf16[128,512]{1,0:T(8,128)(2,1)S(1)}, bf16[128,512]{1,0:T(8,128)(2,1)S(1)}, u32[]{:S(2)}, u32[]{:S(2)}) collective-permute-start(bf16[128,512]{1,0:T(8,128)(2,1)S(1)} %get-tuple-element.141), channel_id=1, source_target_pairs={{0,24},{8,0},{16,8},{24,16},{1,25},{9,1},{17,9},{25,17},{2,26},{10... | collective-permute-start | bytes 393224 | tf_op jit(solution)/shard_map/ppermute | solution.py:1213
  79.9 0.8 collective-permute-start.26
  80.7 2.1 %feed_grad.1 = (f32[4,128,512]{2,1,0:T(8,128)}, bf16[4,128,512]{2,1,0:T(8,128)(2,1)}) custom-call(s32[1]{0:T(128)} %bitcast.scal_ref, bf16[4,128,512]{2,1,0:T(8,128)(2,1)S(1)} %get-tuple-element.145.act_ref, bf16[4,128,512]{2,1,0:T(8,128)(2,1)S(1)} %get-tuple-element.146.dh_ref, bf16[4,128,512]{2,1,0:T(8,128)(2,1)S(1)} %get-tuple-element.147.n_ref, ...), custom_call_target="tpu_custom_call" | custom-call | flops 100000000 | bytes 1000000 | tf_op jit(solution)/shard_map/feed_grad/pallas_call | solution.py:244
  82.8 0.9 collective-permute-done.25.refs_1_
  83.7 1.1 collective-permute-done.26.refs_2_
  84.8 1.7 %collective-permute-done.27.refs_3_ = bf16[128,512]{1,0:T(8,128)(2,1)S(1)} collective-permute-done((bf16[128,512]{1,0:T(8,128)(2,1)S(1)}, bf16[128,512]{1,0:T(8,128)(2,1)S(1)}, u32[]{:S(2)}, u32[]{:S(2)}) %collective-permute-start.27) | collective-permute-done | bytes 131104 | tf_op jit(solution)/shard_map/ppermute | solution.py:1213
  86.6 2.0 %middle_grad.1 = (f32[128,512]{1,0:T(8,128)}, bf16[128,512]{1,0:T(8,128)(2,1)}, bf16[32,16,128]{2,1,0:T(8,128)(2,1)}, f32[8,512]{1,0:T(8,128)}, f32[4,64,512]{2,1,0:T(8,128)}, /*index=5*/bf16[4,64,512]{2,1,0:T(8,128)(2,1)}) custom-call(s32[1]{0:T(128)} %bitcast.scal_ref, f32[8,512]{1,0:T(8,128)S(1)} %copy-done.11, ...), custom_call_target="tpu_custom_call" | custom-call | flops 30000001024 | bytes 1000000 | tf_op jit(solution)/shard_map/middle_grad/pallas_call | solution.py:244
  88.7 2.6 %all-to-all-start.3 = ((bf16[32,16,128]{2,1,0:T(8,128)(2,1)}), bf16[32,16,128]{2,1,0:T(8,128)(2,1)S(1)}, u32[]{:S(2)}, u32[]{:S(2)}) async-start(bf16[32,16,128]{2,1,0:T(8,128)(2,1)} %get-tuple-element.153), calls=%async_computation.3 | async-start | bytes 262144 | tf_op jit(solution)/shard_map/all_to_all | solution.py:340
  91.3 1.0 copy-done.16
  92.3 0.9 part_sum.1
  93.3 1.8 %collective-permute-start.30 = (bf16[128,512]{1,0:T(8,128)(2,1)S(1)}, bf16[128,512]{1,0:T(8,128)(2,1)S(1)}, u32[]{:S(2)}, u32[]{:S(2)}) collective-permute-start(bf16[128,512]{1,0:T(8,128)(2,1)S(1)} %get-tuple-element.159), channel_id=1, source_target_pairs={{0,2},{1,3},{2,4},{3,5},{4,6},{5,7},{6,0},{7,1},{8,10},{9,11},{10,... | collective-permute-start | bytes 393224 | tf_op jit(solution)/shard_map/ppermute | solution.py:1224
  95.0 2.4 %collective-permute-start.31 = (bf16[128,512]{1,0:T(8,128)(2,1)S(1)}, bf16[128,512]{1,0:T(8,128)(2,1)S(1)}, u32[]{:S(2)}, u32[]{:S(2)}) collective-permute-start(bf16[128,512]{1,0:T(8,128)(2,1)S(1)} %get-tuple-element.160), channel_id=1, source_target_pairs={{0,4},{1,5},{2,6},{3,7},{4,0},{5,1},{6,2},{7,3},{8,12},{9,13},{10,... | collective-permute-start | bytes 393224 | tf_op jit(solution)/shard_map/ppermute | solution.py:1224
  97.4 1.4 collective-permute-start.32
  99.4 0.9 copy-done.19
  100.4 4.7 %attention_backward.1 = (bf16[8,64,128]{2,1,0:T(8,128)(2,1)S(1)}, f32[8,128,128]{2,1,0:T(8,128)S(1)}, bf16[8,128,128]{2,1,0:T(8,128)(2,1)S(1)}) custom-call(s32[6]{0:T(128)S(1)} %pad_add_fusion.scal_ref, bf16[8,192,128]{2,1,0:T(8,128)(2,1)S(1)} %all-to-all-done.1.refs_0_, bf16[8,192,128]{2,1,0:T(8,128)(2,1)S(1)} %collective-permute-done.13.refs_1_, ...), custom_call_target="tpu_custom_call" | custom-call | flops 30000001024 | bytes 1000000 | tf_op jit(solution)/shard_map/attention_backward/pallas_call | solution.py:244
  105.1 1.4 collective-permute-done.31.refs_1_
  106.6 1.4 collective-permute-done.33
  108.2 0.8 pad_maximum_fusion
  109.0 5.6 %all-to-all-start.4 = ((bf16[8,192,128]{2,1,0:T(8,128)(2,1)}), bf16[8,192,128]{2,1,0:T(8,128)(2,1)}, u32[]{:S(2)}, u32[]{:S(2)}) async-start(bf16[8,192,128]{2,1,0:T(8,128)(2,1)} %pad_maximum_fusion), calls=%async_computation.4 | async-start | bytes 786432 | tf_op jit(solution)/shard_map/all_to_all | solution.py:340
  114.6 1.4 split.1
  116.0 2.4 %collective-permute-start.34 = (bf16[160,512]{1,0:T(8,128)(2,1)}, bf16[160,512]{1,0:T(8,128)(2,1)S(1)}, u32[]{:S(2)}, u32[]{:S(2)}) collective-permute-start(bf16[160,512]{1,0:T(8,128)(2,1)} %get-tuple-element.167), channel_id=1, source_target_pairs={{0,24},{8,0},{16,8},{24,16},{1,25},{9,1},{17,9},{25,17},{2,26},{10... | collective-permute-start | bytes 491528 | tf_op jit(solution)/shard_map/ppermute | solution.py:1213
  118.4 4.8 %collective-permute-done.34.refs_1_ = bf16[160,512]{1,0:T(8,128)(2,1)S(1)} collective-permute-done((bf16[160,512]{1,0:T(8,128)(2,1)}, bf16[160,512]{1,0:T(8,128)(2,1)S(1)}, u32[]{:S(2)}, u32[]{:S(2)}) %collective-permute-start.34) | collective-permute-done | bytes 163872 | tf_op jit(solution)/shard_map/ppermute | solution.py:1213
  123.2 4.0 %collective-permute-done.36.refs_3_ = bf16[160,512]{1,0:T(8,128)(2,1)S(1)} collective-permute-done((bf16[160,512]{1,0:T(8,128)(2,1)}, bf16[160,512]{1,0:T(8,128)(2,1)S(1)}, u32[]{:S(2)}, u32[]{:S(2)}) %collective-permute-start.36) | collective-permute-done | bytes 163872 | tf_op jit(solution)/shard_map/ppermute | solution.py:1213
  127.2 5.0 %project_grad.1 = (bf16[16,64,128]{2,1,0:T(8,128)(2,1)}, bf16[16,64,128]{2,1,0:T(8,128)(2,1)}, f32[128,512]{1,0:T(8,128)}, bf16[128,512]{1,0:T(8,128)(2,1)}, bf1...) custom-call(s32[1]{0:T(128)} %bitcast.scal_ref, f32[256,128]{1,0:T(8,128)} %get-tuple-element.171.early_ref, ...), custom_call_target="tpu_custom_call" | custom-call | flops 30000001024 | bytes 1000000 | tf_op jit(solution)/shard_map/project_grad/pallas_call | solution.py:1368
  132.3 1.5 collective-permute-start.35
  134.6 2.4 %collective-permute-start.42 = (bf16[64,512]{1,0:T(8,128)(2,1)}, bf16[64,512]{1,0:T(8,128)(2,1)S(1)}, u32[]{:S(2)}, u32[]{:S(2)}) collective-permute-start(bf16[64,512]{1,0:T(8,128)(2,1)} %get-tuple-element.196), channel_id=1, source_target_pairs={{0,4},{1,5},{2,6},{3,7},{4,0},{5,1},{6,2},{7,3},{8,12},{9,13},{10,... | collective-permute-start | bytes 196616 | tf_op jit(solution)/shard_map/ppermute | solution.py:1224
  136.9 1.5 collective-permute-start.43
  138.4 0.9 copy-done.18
  139.4 0.8 fold.1
  140.2 3.9 %all-to-all-start.5 = ((bf16[16,64,128]{2,1,0:T(8,128)(2,1)}), bf16[16,64,128]{2,1,0:T(8,128)(2,1)S(1)}, u32[]{:S(2)}, u32[]{:S(2)}) async-start(bf16[16,64,128]{2,1,0:T(8,128)(2,1)} %fold.1), calls=%async_computation.5 | async-start | bytes 524288 | tf_op jit(solution)/shard_map/all_to_all | solution.py:340
  144.1 0.7 add_convert_fusion.1
  144.9 2.8 %collective-permute-start.37 = (bf16[128,512]{1,0:T(8,128)(2,1)S(1)}, bf16[128,512]{1,0:T(8,128)(2,1)S(1)}, u32[]{:S(2)}, u32[]{:S(2)}) collective-permute-start(bf16[128,512]{1,0:T(8,128)(2,1)S(1)} %copy-done.26), channel_id=1, source_target_pairs={{0,24},{8,0},{16,8},{24,16},{1,25},{9,1},{17,9},{25,17},{2,26},{10... | collective-permute-start | bytes 393224 | tf_op jit(solution)/shard_map/ppermute | solution.py:1213
  149.6 3.0 %collective-permute-done.37.refs_1_ = bf16[128,512]{1,0:T(8,128)(2,1)S(1)} collective-permute-done((bf16[128,512]{1,0:T(8,128)(2,1)S(1)}, bf16[128,512]{1,0:T(8,128)(2,1)S(1)}, u32[]{:S(2)}, u32[]{:S(2)}) %collective-permute-start.37) | collective-permute-done | bytes 131104 | tf_op jit(solution)/shard_map/ppermute | solution.py:1213
  152.6 3.6 %collective-permute-done.38.refs_2_ = bf16[128,512]{1,0:T(8,128)(2,1)S(1)} collective-permute-done((bf16[128,512]{1,0:T(8,128)(2,1)S(1)}, bf16[128,512]{1,0:T(8,128)(2,1)S(1)}, u32[]{:S(2)}, u32[]{:S(2)}) %collective-permute-start.38) | collective-permute-done | bytes 131104 | tf_op jit(solution)/shard_map/ppermute | solution.py:1213
  156.2 1.0 input_grad.1
  157.1 0.8 final.1
  (143 shorter events, 12.3 us)
Async XLA Ops:
  0.6 21.9 %copy-start = (bf16[2,1,64,512]{3,2,1,0:T(8,128)(2,1)S(1)}, bf16[2,1,64,512]{3,2,1,0:T(8,128)(2,1)}, u32[]{:S(2)}) copy-start(bf16[2,1,64,512]{3,2,1,0:T(8,128)(2,1)} %param.16) | copy-start | bytes 393220
  2.4 18.7 %all-to-all-start = ((bf16[16,56,128]{2,1,0:T(8,128)(2,1)}), bf16[16,56,128]{2,1,0:T(8,128)(2,1)S(1)}, u32[]{:S(2)}, u32[]{:S(2)}) async-start(bf16[16,56,128]{2,1,0:T(8,128)(2,1)} %pack.1), calls=%async_computation | async-start | bytes 458752 | tf_op jit(solution)/shard_map/all_to_all | solution.py:340
  10.7 10.5 %collective-permute-start.1 = (bf16[128,512]{1,0:T(8,128)(2,1)}, bf16[128,512]{1,0:T(8,128)(2,1)S(1)}, u32[]{:S(2)}, u32[]{:S(2)}) collective-permute-start(bf16[128,512]{1,0:T(8,128)(2,1)} %bitcast.30), channel_id=1, source_target_pairs={{0,8},{8,16},{16,24},{24,0},{1,9},{9,17},{17,25},{25,1},{2,10},{10... | collective-permute-start | bytes 393224 | tf_op jit(solution)/shard_map/ppermute | solution.py:1213
  12.7 9.2 %collective-permute-start.2 = (bf16[128,512]{1,0:T(8,128)(2,1)}, bf16[128,512]{1,0:T(8,128)(2,1)S(1)}, u32[]{:S(2)}, u32[]{:S(2)}) collective-permute-start(bf16[128,512]{1,0:T(8,128)(2,1)} %bitcast.31), channel_id=1, source_target_pairs={{0,16},{8,24},{16,0},{24,8},{1,17},{9,25},{17,1},{25,9},{2,18},{10... | collective-permute-start | bytes 393224 | tf_op jit(solution)/shard_map/ppermute | solution.py:1213
  14.1 7.7 %collective-permute-start.3 = (bf16[128,512]{1,0:T(8,128)(2,1)}, bf16[128,512]{1,0:T(8,128)(2,1)S(1)}, u32[]{:S(2)}, u32[]{:S(2)}) collective-permute-start(bf16[128,512]{1,0:T(8,128)(2,1)} %bitcast.32), channel_id=1, source_target_pairs={{0,24},{8,0},{16,8},{24,16},{1,25},{9,1},{17,9},{25,17},{2,26},{10... | collective-permute-start | bytes 393224 | tf_op jit(solution)/shard_map/ppermute | solution.py:1213
  21.1 1.5 collective-permute-start
  24.4 21.8 %all-to-all-start.1 = ((bf16[8,192,128]{2,1,0:T(8,128)(2,1)}), bf16[8,192,128]{2,1,0:T(8,128)(2,1)S(1)}, u32[]{:S(2)}, u32[]{:S(2)}) async-start(bf16[8,192,128]{2,1,0:T(8,128)(2,1)} %get-tuple-element.118), calls=%async_computation.1 | async-start | bytes 786432 | tf_op jit(solution)/shard_map/all_to_all | solution.py:340
  30.7 8.7 %collective-permute-start.4 = (bf16[160,512]{1,0:T(8,128)(2,1)}, bf16[160,512]{1,0:T(8,128)(2,1)S(1)}, u32[]{:S(2)}, u32[]{:S(2)}) collective-permute-start(bf16[160,512]{1,0:T(8,128)(2,1)} %get-tuple-element.113), channel_id=1, source_target_pairs={{0,8},{8,16},{16,24},{24,0},{1,9},{9,17},{17,25},{25,1},{2,10},{10... | collective-permute-start | bytes 491528 | tf_op jit(solution)/shard_map/ppermute | solution.py:1213
  31.4 11.5 %collective-permute-start.5 = (bf16[160,512]{1,0:T(8,128)(2,1)}, bf16[160,512]{1,0:T(8,128)(2,1)S(1)}, u32[]{:S(2)}, u32[]{:S(2)}) collective-permute-start(bf16[160,512]{1,0:T(8,128)(2,1)} %get-tuple-element.115), channel_id=1, source_target_pairs={{0,16},{8,24},{16,0},{24,8},{1,17},{9,25},{17,1},{25,9},{2,18},{10... | collective-permute-start | bytes 491528 | tf_op jit(solution)/shard_map/ppermute | solution.py:1213
  31.9 10.9 %collective-permute-start.6 = (bf16[160,512]{1,0:T(8,128)(2,1)}, bf16[160,512]{1,0:T(8,128)(2,1)S(1)}, u32[]{:S(2)}, u32[]{:S(2)}) collective-permute-start(bf16[160,512]{1,0:T(8,128)(2,1)} %get-tuple-element.117), channel_id=1, source_target_pairs={{0,24},{8,0},{16,8},{24,16},{1,25},{9,1},{17,9},{25,17},{2,26},{10... | collective-permute-start | bytes 491528 | tf_op jit(solution)/shard_map/ppermute | solution.py:1213
  35.0 7.8 %collective-permute-start.10 = (bf16[64,512]{1,0:T(8,128)(2,1)}, bf16[64,512]{1,0:T(8,128)(2,1)S(1)}, u32[]{:S(2)}, u32[]{:S(2)}) collective-permute-start(bf16[64,512]{1,0:T(8,128)(2,1)} %refs_8_), channel_id=1, source_target_pairs={{0,2},{1,3},{2,4},{3,5},{4,6},{5,7},{6,0},{7,1},{8,10},{9,11},{10,... | collective-permute-start | bytes 196616 | tf_op jit(solution)/shard_map/ppermute | solution.py:1224
  37.1 9.1 %collective-permute-start.11 = (bf16[64,512]{1,0:T(8,128)(2,1)}, bf16[64,512]{1,0:T(8,128)(2,1)S(1)}, u32[]{:S(2)}, u32[]{:S(2)}) collective-permute-start(bf16[64,512]{1,0:T(8,128)(2,1)} %refs_8_), channel_id=1, source_target_pairs={{0,4},{1,5},{2,6},{3,7},{4,0},{5,1},{6,2},{7,3},{8,12},{9,13},{10,... | collective-permute-start | bytes 196616 | tf_op jit(solution)/shard_map/ppermute | solution.py:1224
  39.4 6.7 %collective-permute-start.12 = (bf16[64,512]{1,0:T(8,128)(2,1)}, bf16[64,512]{1,0:T(8,128)(2,1)S(1)}, u32[]{:S(2)}, u32[]{:S(2)}) collective-permute-start(bf16[64,512]{1,0:T(8,128)(2,1)} %refs_8_), channel_id=1, source_target_pairs={{0,6},{1,7},{2,0},{3,1},{4,2},{5,3},{6,4},{7,5},{8,14},{9,15},{10,... | collective-permute-start | bytes 196616 | tf_op jit(solution)/shard_map/ppermute | solution.py:1224
  42.9 19.7 %copy-start.11 = (f32[8,512]{1,0:T(8,128)S(1)}, f32[8,512]{1,0:T(8,128)}, u32[]{:S(2)}) copy-start(f32[8,512]{1,0:T(8,128)} %get-tuple-element.133.vec_ref) | copy-start | bytes 49156
  46.1 3.6 %collective-permute-start.13 = (bf16[8,192,128]{2,1,0:T(8,128)(2,1)S(1)}, bf16[8,192,128]{2,1,0:T(8,128)(2,1)S(1)}, u32[]{:S(2)}, u32[]{:S(2)}) collective-permute-start(bf16[8,192,128]{2,1,0:T(8,128)(2,1)S(1)} %all-to-all-done.1.refs_0_), channel_id=1, source_target_pairs={{0,1},{1,0},{2,3},{3,2},{4,5},{5,4},{6,7},{7,6},{8,9},{9,8},{10,11... | collective-permute-start | bytes 1179656 | tf_op jit(solution)/shard_map/ppermute | solution.py:1227
  46.2 13.2 %collective-permute-start.9 = (bf16[128,512]{1,0:T(8,128)(2,1)S(1)}, bf16[128,512]{1,0:T(8,128)(2,1)S(1)}, u32[]{:S(2)}, u32[]{:S(2)}) collective-permute-start(bf16[128,512]{1,0:T(8,128)(2,1)S(1)} %pad_maximum_fusion.1.refs_0_), channel_id=1, source_target_pairs={{0,6},{1,7},{2,0},{3,1},{4,2},{5,3},{6,4},{7,5},{8,14},{9,15},{10,... | collective-permute-start | bytes 393224 | tf_op jit(solution)/shard_map/ppermute | solution.py:1224
  49.1 12.3 %collective-permute-start.8 = (bf16[128,512]{1,0:T(8,128)(2,1)S(1)}, bf16[128,512]{1,0:T(8,128)(2,1)S(1)}, u32[]{:S(2)}, u32[]{:S(2)}) collective-permute-start(bf16[128,512]{1,0:T(8,128)(2,1)S(1)} %pad_maximum_fusion.1.refs_0_), channel_id=1, source_target_pairs={{0,4},{1,5},{2,6},{3,7},{4,0},{5,1},{6,2},{7,3},{8,12},{9,13},{10,... | collective-permute-start | bytes 393224 | tf_op jit(solution)/shard_map/ppermute | solution.py:1224
  49.1 12.3 %collective-permute-start.7 = (bf16[128,512]{1,0:T(8,128)(2,1)S(1)}, bf16[128,512]{1,0:T(8,128)(2,1)S(1)}, u32[]{:S(2)}, u32[]{:S(2)}) collective-permute-start(bf16[128,512]{1,0:T(8,128)(2,1)S(1)} %pad_maximum_fusion.1.refs_0_), channel_id=1, source_target_pairs={{0,2},{1,3},{2,4},{3,5},{4,6},{5,7},{6,0},{7,1},{8,10},{9,11},{10,... | collective-permute-start | bytes 393224 | tf_op jit(solution)/shard_map/ppermute | solution.py:1224
  53.6 12.5 %all-to-all-start.2 = ((bf16[8,64,128]{2,1,0:T(8,128)(2,1)}), bf16[8,64,128]{2,1,0:T(8,128)(2,1)S(1)}, u32[]{:S(2)}, u32[]{:S(2)}) async-start(bf16[8,64,128]{2,1,0:T(8,128)(2,1)} %get-tuple-element.121), calls=%async_computation.2 | async-start | bytes 262144 | tf_op jit(solution)/shard_map/all_to_all | solution.py:340
  59.3 3.1 %collective-permute-start.17 = (bf16[128,512]{1,0:T(8,128)(2,1)S(1)}, bf16[128,512]{1,0:T(8,128)(2,1)S(1)}, u32[]{:S(2)}, u32[]{:S(2)}) collective-permute-start(bf16[128,512]{1,0:T(8,128)(2,1)S(1)} %collective-permute-done.9.refs_3_), channel_id=1, source_target_pairs={{0,1},{1,0},{2,3},{3,2},{4,5},{5,4},{6,7},{7,6},{8,9},{9,8},{10,11... | collective-permute-start | bytes 393224 | tf_op jit(solution)/shard_map/ppermute | solution.py:1227
  61.4 2.7 %collective-permute-start.16 = (bf16[128,512]{1,0:T(8,128)(2,1)S(1)}, bf16[128,512]{1,0:T(8,128)(2,1)S(1)}, u32[]{:S(2)}, u32[]{:S(2)}) collective-permute-start(bf16[128,512]{1,0:T(8,128)(2,1)S(1)} %collective-permute-done.8.refs_2_), channel_id=1, source_target_pairs={{0,1},{1,0},{2,3},{3,2},{4,5},{5,4},{6,7},{7,6},{8,9},{9,8},{10,11... | collective-permute-start | bytes 393224 | tf_op jit(solution)/shard_map/ppermute | solution.py:1227
  61.4 2.7 %collective-permute-start.15 = (bf16[128,512]{1,0:T(8,128)(2,1)S(1)}, bf16[128,512]{1,0:T(8,128)(2,1)S(1)}, u32[]{:S(2)}, u32[]{:S(2)}) collective-permute-start(bf16[128,512]{1,0:T(8,128)(2,1)S(1)} %collective-permute-done.7.refs_1_), channel_id=1, source_target_pairs={{0,1},{1,0},{2,3},{3,2},{4,5},{5,4},{6,7},{7,6},{8,9},{9,8},{10,11... | collective-permute-start | bytes 393224 | tf_op jit(solution)/shard_map/ppermute | solution.py:1227
  61.9 2.2 %collective-permute-start.14 = (bf16[128,512]{1,0:T(8,128)(2,1)S(1)}, bf16[128,512]{1,0:T(8,128)(2,1)S(1)}, u32[]{:S(2)}, u32[]{:S(2)}) collective-permute-start(bf16[128,512]{1,0:T(8,128)(2,1)S(1)} %pad_maximum_fusion.1.refs_0_), channel_id=1, source_target_pairs={{0,1},{1,0},{2,3},{3,2},{4,5},{5,4},{6,7},{7,6},{8,9},{9,8},{10,11... | collective-permute-start | bytes 393224 | tf_op jit(solution)/shard_map/ppermute | solution.py:1227
  61.9 12.2 %copy-start.6 = (bf16[160,512]{1,0:T(8,128)(2,1)S(1)}, bf16[160,512]{1,0:T(8,128)(2,1)}, u32[]{:S(2)}) copy-start(bf16[160,512]{1,0:T(8,128)(2,1)} %get-tuple-element.111.refs_4_.refs_0_) | copy-start | bytes 491524
  61.9 7.6 %collective-permute-start.19 = (bf16[64,512]{1,0:T(8,128)(2,1)S(1)}, bf16[64,512]{1,0:T(8,128)(2,1)S(1)}, u32[]{:S(2)}, u32[]{:S(2)}) collective-permute-start(bf16[64,512]{1,0:T(8,128)(2,1)S(1)} %collective-permute-done.10.refs_9_), channel_id=1, source_target_pairs={{0,1},{1,0},{2,3},{3,2},{4,5},{5,4},{6,7},{7,6},{8,9},{9,8},{10,11... | collective-permute-start | bytes 196616 | tf_op jit(solution)/shard_map/ppermute | solution.py:1227
  62.4 7.1 %collective-permute-start.20 = (bf16[64,512]{1,0:T(8,128)(2,1)S(1)}, bf16[64,512]{1,0:T(8,128)(2,1)S(1)}, u32[]{:S(2)}, u32[]{:S(2)}) collective-permute-start(bf16[64,512]{1,0:T(8,128)(2,1)S(1)} %collective-permute-done.11.refs_10_), channel_id=1, source_target_pairs={{0,1},{1,0},{2,3},{3,2},{4,5},{5,4},{6,7},{7,6},{8,9},{9,8},{10,11... | collective-permute-start | bytes 196616 | tf_op jit(solution)/shard_map/ppermute | solution.py:1227
  66.1 7.3 %collective-permute-start.22 = (bf16[8,64,128]{2,1,0:T(8,128)(2,1)S(1)}, bf16[8,64,128]{2,1,0:T(8,128)(2,1)S(1)}, u32[]{:S(2)}, u32[]{:S(2)}) collective-permute-start(bf16[8,64,128]{2,1,0:T(8,128)(2,1)S(1)} %all-to-all-done.2.refs_8_), channel_id=1, source_target_pairs={{0,8},{8,16},{16,24},{24,0},{1,9},{9,17},{17,25},{25,1},{2,10},{10... | collective-permute-start | bytes 393224 | tf_op jit(solution)/shard_map/ppermute | solution.py:1213
  66.7 7.5 %collective-permute-start.23 = (bf16[8,64,128]{2,1,0:T(8,128)(2,1)S(1)}, bf16[8,64,128]{2,1,0:T(8,128)(2,1)S(1)}, u32[]{:S(2)}, u32[]{:S(2)}) collective-permute-start(bf16[8,64,128]{2,1,0:T(8,128)(2,1)S(1)} %all-to-all-done.2.refs_8_), channel_id=1, source_target_pairs={{0,16},{8,24},{16,0},{24,8},{1,17},{9,25},{17,1},{25,9},{2,18},{10... | collective-permute-start | bytes 393224 | tf_op jit(solution)/shard_map/ppermute | solution.py:1213
  67.2 7.0 %collective-permute-start.24 = (bf16[8,64,128]{2,1,0:T(8,128)(2,1)S(1)}, bf16[8,64,128]{2,1,0:T(8,128)(2,1)S(1)}, u32[]{:S(2)}, u32[]{:S(2)}) collective-permute-start(bf16[8,64,128]{2,1,0:T(8,128)(2,1)S(1)} %all-to-all-done.2.refs_8_), channel_id=1, source_target_pairs={{0,24},{8,0},{16,8},{24,16},{1,25},{9,1},{17,9},{25,17},{2,26},{10... | collective-permute-start | bytes 393224 | tf_op jit(solution)/shard_map/ppermute | solution.py:1213
  69.6 1.3 collective-permute-start.21
  69.6 1.6 %collective-permute-start.18 = (bf16[64,512]{1,0:T(8,128)(2,1)}, bf16[64,512]{1,0:T(8,128)(2,1)S(1)}, u32[]{:S(2)}, u32[]{:S(2)}) collective-permute-start(bf16[64,512]{1,0:T(8,128)(2,1)} %refs_8_), channel_id=1, source_target_pairs={{0,1},{1,0},{2,3},{3,2},{4,5},{5,4},{6,7},{7,6},{8,9},{9,8},{10,11... | collective-permute-start | bytes 196616 | tf_op jit(solution)/shard_map/ppermute | solution.py:1227
  77.5 6.2 %collective-permute-start.25 = (bf16[128,512]{1,0:T(8,128)(2,1)S(1)}, bf16[128,512]{1,0:T(8,128)(2,1)S(1)}, u32[]{:S(2)}, u32[]{:S(2)}) collective-permute-start(bf16[128,512]{1,0:T(8,128)(2,1)S(1)} %get-tuple-element.141), channel_id=1, source_target_pairs={{0,24},{8,0},{16,8},{24,16},{1,25},{9,1},{17,9},{25,17},{2,26},{10... | collective-permute-start | bytes 393224 | tf_op jit(solution)/shard_map/ppermute | solution.py:1213
  79.9 5.0 %collective-permute-start.26 = (bf16[128,512]{1,0:T(8,128)(2,1)S(1)}, bf16[128,512]{1,0:T(8,128)(2,1)S(1)}, u32[]{:S(2)}, u32[]{:S(2)}) collective-permute-start(bf16[128,512]{1,0:T(8,128)(2,1)S(1)} %get-tuple-element.142), channel_id=1, source_target_pairs={{0,16},{8,24},{16,0},{24,8},{1,17},{9,25},{17,1},{25,9},{2,18},{10... | collective-permute-start | bytes 393224 | tf_op jit(solution)/shard_map/ppermute | solution.py:1213
  80.7 5.9 %collective-permute-start.27 = (bf16[128,512]{1,0:T(8,128)(2,1)S(1)}, bf16[128,512]{1,0:T(8,128)(2,1)S(1)}, u32[]{:S(2)}, u32[]{:S(2)}) collective-permute-start(bf16[128,512]{1,0:T(8,128)(2,1)S(1)} %get-tuple-element.143), channel_id=1, source_target_pairs={{0,8},{8,16},{16,24},{24,0},{1,9},{9,17},{17,25},{25,1},{2,10},{10... | collective-permute-start | bytes 393224 | tf_op jit(solution)/shard_map/ppermute | solution.py:1213
  82.8 8.5 %collective-permute-start.28 = (bf16[4,128,512]{2,1,0:T(8,128)(2,1)}, bf16[4,128,512]{2,1,0:T(8,128)(2,1)S(1)}, u32[]{:S(2)}, u32[]{:S(2)}) collective-permute-start(bf16[4,128,512]{2,1,0:T(8,128)(2,1)} %get-tuple-element.149), channel_id=1, source_target_pairs={{0,1},{1,0},{2,3},{3,2},{4,5},{5,4},{6,7},{7,6},{8,9},{9,8},{10,11... | collective-permute-start | bytes 1572872 | tf_op jit(solution)/shard_map/ppermute | solution.py:1227
  88.7 2.6 %collective-permute-start.29 = (bf16[4,64,512]{2,1,0:T(8,128)(2,1)}, bf16[4,64,512]{2,1,0:T(8,128)(2,1)S(1)}, u32[]{:S(2)}, u32[]{:S(2)}) collective-permute-start(bf16[4,64,512]{2,1,0:T(8,128)(2,1)} %get-tuple-element.151), channel_id=1, source_target_pairs={{0,1},{1,0},{2,3},{3,2},{4,5},{5,4},{6,7},{7,6},{8,9},{9,8},{10,11... | collective-permute-start | bytes 786440 | tf_op jit(solution)/shard_map/ppermute | solution.py:1227
  88.7 10.8 %all-to-all-start.3 = ((bf16[32,16,128]{2,1,0:T(8,128)(2,1)}), bf16[32,16,128]{2,1,0:T(8,128)(2,1)S(1)}, u32[]{:S(2)}, u32[]{:S(2)}) async-start(bf16[32,16,128]{2,1,0:T(8,128)(2,1)} %get-tuple-element.153), calls=%async_computation.3 | async-start | bytes 262144 | tf_op jit(solution)/shard_map/all_to_all | solution.py:340
  92.3 7.1 %copy-start.21 = (f32[4,8,256]{2,1,0:T(8,128)S(1)}, f32[4,8,256]{2,1,0:T(8,128)}, u32[]{:S(2)}) copy-start(f32[4,8,256]{2,1,0:T(8,128)} %get-tuple-element.155.refs_5_) | copy-start | bytes 98308
  93.3 11.8 %collective-permute-start.30 = (bf16[128,512]{1,0:T(8,128)(2,1)S(1)}, bf16[128,512]{1,0:T(8,128)(2,1)S(1)}, u32[]{:S(2)}, u32[]{:S(2)}) collective-permute-start(bf16[128,512]{1,0:T(8,128)(2,1)S(1)} %get-tuple-element.159), channel_id=1, source_target_pairs={{0,2},{1,3},{2,4},{3,5},{4,6},{5,7},{6,0},{7,1},{8,10},{9,11},{10,... | collective-permute-start | bytes 393224 | tf_op jit(solution)/shard_map/ppermute | solution.py:1224
  95.0 11.5 %collective-permute-start.31 = (bf16[128,512]{1,0:T(8,128)(2,1)S(1)}, bf16[128,512]{1,0:T(8,128)(2,1)S(1)}, u32[]{:S(2)}, u32[]{:S(2)}) collective-permute-start(bf16[128,512]{1,0:T(8,128)(2,1)S(1)} %get-tuple-element.160), channel_id=1, source_target_pairs={{0,4},{1,5},{2,6},{3,7},{4,0},{5,1},{6,2},{7,3},{8,12},{9,13},{10,... | collective-permute-start | bytes 393224 | tf_op jit(solution)/shard_map/ppermute | solution.py:1224
  97.4 9.1 %collective-permute-start.32 = (bf16[128,512]{1,0:T(8,128)(2,1)S(1)}, bf16[128,512]{1,0:T(8,128)(2,1)S(1)}, u32[]{:S(2)}, u32[]{:S(2)}) collective-permute-start(bf16[128,512]{1,0:T(8,128)(2,1)S(1)} %get-tuple-element.161), channel_id=1, source_target_pairs={{0,6},{1,7},{2,0},{3,1},{4,2},{5,3},{6,4},{7,5},{8,14},{9,15},{10,... | collective-permute-start | bytes 393224 | tf_op jit(solution)/shard_map/ppermute | solution.py:1224
  106.5 1.5 collective-permute-start.33
  108.1 6.4 %copy-start.5 = (f32[128,512]{1,0:T(8,128)S(1)}, f32[128,512]{1,0:T(8,128)}, u32[]{:S(2)}) copy-start(f32[128,512]{1,0:T(8,128)} %get-tuple-element.163.own_ref) | copy-start | bytes 786436
  108.1 6.4 %copy-start.8 = (bf16[128,512]{1,0:T(8,128)(2,1)S(1)}, bf16[128,512]{1,0:T(8,128)(2,1)}, u32[]{:S(2)}) copy-start(bf16[128,512]{1,0:T(8,128)(2,1)} %get-tuple-element.164.refs_3_) | copy-start | bytes 393220
  108.1 6.4 %copy-start.9 = (bf16[128,512]{1,0:T(8,128)(2,1)S(1)}, bf16[128,512]{1,0:T(8,128)(2,1)}, u32[]{:S(2)}) copy-start(bf16[128,512]{1,0:T(8,128)(2,1)} %get-tuple-element.165.refs_4_) | copy-start | bytes 393220
  109.0 18.2 %all-to-all-start.4 = ((bf16[8,192,128]{2,1,0:T(8,128)(2,1)}), bf16[8,192,128]{2,1,0:T(8,128)(2,1)}, u32[]{:S(2)}, u32[]{:S(2)}) async-start(bf16[8,192,128]{2,1,0:T(8,128)(2,1)} %pad_maximum_fusion), calls=%async_computation.4 | async-start | bytes 786432 | tf_op jit(solution)/shard_map/all_to_all | solution.py:340
  116.0 7.2 %collective-permute-start.34 = (bf16[160,512]{1,0:T(8,128)(2,1)}, bf16[160,512]{1,0:T(8,128)(2,1)S(1)}, u32[]{:S(2)}, u32[]{:S(2)}) collective-permute-start(bf16[160,512]{1,0:T(8,128)(2,1)} %get-tuple-element.167), channel_id=1, source_target_pairs={{0,24},{8,0},{16,8},{24,16},{1,25},{9,1},{17,9},{25,17},{2,26},{10... | collective-permute-start | bytes 491528 | tf_op jit(solution)/shard_map/ppermute | solution.py:1213
  118.4 8.8 %collective-permute-start.36 = (bf16[160,512]{1,0:T(8,128)(2,1)}, bf16[160,512]{1,0:T(8,128)(2,1)S(1)}, u32[]{:S(2)}, u32[]{:S(2)}) collective-permute-start(bf16[160,512]{1,0:T(8,128)(2,1)} %get-tuple-element.169), channel_id=1, source_target_pairs={{0,8},{8,16},{16,24},{24,0},{1,9},{9,17},{17,25},{25,1},{2,10},{10... | collective-permute-start | bytes 491528 | tf_op jit(solution)/shard_map/ppermute | solution.py:1213
  132.2 6.2 %collective-permute-start.40 = (bf16[16,64,128]{2,1,0:T(8,128)(2,1)}, bf16[16,64,128]{2,1,0:T(8,128)(2,1)S(1)}, u32[]{:S(2)}, u32[]{:S(2)}) collective-permute-start(bf16[16,64,128]{2,1,0:T(8,128)(2,1)} %get-tuple-element.180), channel_id=1, source_target_pairs={{0,1},{1,0},{2,3},{3,2},{4,5},{5,4},{6,7},{7,6},{8,9},{9,8},{10,11... | collective-permute-start | bytes 786440 | tf_op jit(solution)/shard_map/ppermute | solution.py:1227
  132.3 11.8 %collective-permute-start.35 = (bf16[160,512]{1,0:T(8,128)(2,1)}, bf16[160,512]{1,0:T(8,128)(2,1)S(1)}, u32[]{:S(2)}, u32[]{:S(2)}) collective-permute-start(bf16[160,512]{1,0:T(8,128)(2,1)} %get-tuple-element.168), channel_id=1, source_target_pairs={{0,16},{8,24},{16,0},{24,8},{1,17},{9,25},{17,1},{25,9},{2,18},{10... | collective-permute-start | bytes 491528 | tf_op jit(solution)/shard_map/ppermute | solution.py:1213
  133.8 14.4 %collective-permute-start.41 = (bf16[64,512]{1,0:T(8,128)(2,1)}, bf16[64,512]{1,0:T(8,128)(2,1)S(1)}, u32[]{:S(2)}, u32[]{:S(2)}) collective-permute-start(bf16[64,512]{1,0:T(8,128)(2,1)} %get-tuple-element.194), channel_id=1, source_target_pairs={{0,2},{1,3},{2,4},{3,5},{4,6},{5,7},{6,0},{7,1},{8,10},{9,11},{10,... | collective-permute-start | bytes 196616 | tf_op jit(solution)/shard_map/ppermute | solution.py:1224
  134.6 14.3 %collective-permute-start.42 = (bf16[64,512]{1,0:T(8,128)(2,1)}, bf16[64,512]{1,0:T(8,128)(2,1)S(1)}, u32[]{:S(2)}, u32[]{:S(2)}) collective-permute-start(bf16[64,512]{1,0:T(8,128)(2,1)} %get-tuple-element.196), channel_id=1, source_target_pairs={{0,4},{1,5},{2,6},{3,7},{4,0},{5,1},{6,2},{7,3},{8,12},{9,13},{10,... | collective-permute-start | bytes 196616 | tf_op jit(solution)/shard_map/ppermute | solution.py:1224
  136.9 11.9 %collective-permute-start.43 = (bf16[64,512]{1,0:T(8,128)(2,1)}, bf16[64,512]{1,0:T(8,128)(2,1)S(1)}, u32[]{:S(2)}, u32[]{:S(2)}) collective-permute-start(bf16[64,512]{1,0:T(8,128)(2,1)} %get-tuple-element.198), channel_id=1, source_target_pairs={{0,6},{1,7},{2,0},{3,1},{4,2},{5,3},{6,4},{7,5},{8,14},{9,15},{10,... | collective-permute-start | bytes 196616 | tf_op jit(solution)/shard_map/ppermute | solution.py:1224
  140.2 7.6 %copy-start.25 = (bf16[128,512]{1,0:T(8,128)(2,1)S(1)}, bf16[128,512]{1,0:T(8,128)(2,1)}, u32[]{:S(2)}) copy-start(bf16[128,512]{1,0:T(8,128)(2,1)} %get-tuple-element.177) | copy-start | bytes 393220
  140.2 8.1 %copy-start.24 = (bf16[128,512]{1,0:T(8,128)(2,1)S(1)}, bf16[128,512]{1,0:T(8,128)(2,1)}, u32[]{:S(2)}) copy-start(bf16[128,512]{1,0:T(8,128)(2,1)} %get-tuple-element.178) | copy-start | bytes 393220
  140.2 8.7 %copy-start.23 = (f32[64,512]{1,0:T(8,128)S(1)}, f32[64,512]{1,0:T(8,128)}, u32[]{:S(2)}) copy-start(f32[64,512]{1,0:T(8,128)} %get-tuple-element.192) | copy-start | bytes 393220
  140.2 16.0 %copy-start.1 = (bf16[2,1,64,512]{3,2,1,0:T(8,128)(2,1)S(1)}, bf16[2,1,64,512]{3,2,1,0:T(8,128)(2,1)}, u32[]{:S(2)}) copy-start(bf16[2,1,64,512]{3,2,1,0:T(8,128)(2,1)} %param.16) | copy-start | bytes 393220
  140.2 16.0 %copy-start.3 = (f32[128,512]{1,0:T(8,128)S(1)}, f32[128,512]{1,0:T(8,128)}, u32[]{:S(2)}) copy-start(f32[128,512]{1,0:T(8,128)} %get-tuple-element.170.grad_ref) | copy-start | bytes 786436
  140.2 16.0 %copy-start.4 = (f32[128,512]{1,0:T(8,128)S(1)}, f32[128,512]{1,0:T(8,128)}, u32[]{:S(2)}) copy-start(f32[128,512]{1,0:T(8,128)} %get-tuple-element.175.refs_0_) | copy-start | bytes 786436
  140.2 16.9 %all-to-all-start.5 = ((bf16[16,64,128]{2,1,0:T(8,128)(2,1)}), bf16[16,64,128]{2,1,0:T(8,128)(2,1)S(1)}, u32[]{:S(2)}, u32[]{:S(2)}) async-start(bf16[16,64,128]{2,1,0:T(8,128)(2,1)} %fold.1), calls=%async_computation.5 | async-start | bytes 524288 | tf_op jit(solution)/shard_map/all_to_all | solution.py:340
  144.9 12.2 %copy-start.12 = (bf16[32,512]{1,0:T(8,128)(2,1)S(1)}, bf16[32,512]{1,0:T(8,128)(2,1)}, u32[]{:S(2)}) copy-start(bf16[32,512]{1,0:T(8,128)(2,1)} %get-tuple-element.181.refs_0_) | copy-start | bytes 98308
  144.9 7.7 %collective-permute-start.37 = (bf16[128,512]{1,0:T(8,128)(2,1)S(1)}, bf16[128,512]{1,0:T(8,128)(2,1)S(1)}, u32[]{:S(2)}, u32[]{:S(2)}) collective-permute-start(bf16[128,512]{1,0:T(8,128)(2,1)S(1)} %copy-done.26), channel_id=1, source_target_pairs={{0,24},{8,0},{16,8},{24,16},{1,25},{9,1},{17,9},{25,17},{2,26},{10... | collective-permute-start | bytes 393224 | tf_op jit(solution)/shard_map/ppermute | solution.py:1213
  147.7 8.4 %collective-permute-start.38 = (bf16[128,512]{1,0:T(8,128)(2,1)S(1)}, bf16[128,512]{1,0:T(8,128)(2,1)S(1)}, u32[]{:S(2)}, u32[]{:S(2)}) collective-permute-start(bf16[128,512]{1,0:T(8,128)(2,1)S(1)} %copy-done.25), channel_id=1, source_target_pairs={{0,16},{8,24},{16,0},{24,8},{1,17},{9,25},{17,1},{25,9},{2,18},{10... | collective-permute-start | bytes 393224 | tf_op jit(solution)/shard_map/ppermute | solution.py:1213
  148.3 7.8 %collective-permute-start.39 = (bf16[128,512]{1,0:T(8,128)(2,1)S(1)}, bf16[128,512]{1,0:T(8,128)(2,1)S(1)}, u32[]{:S(2)}, u32[]{:S(2)}) collective-permute-start(bf16[128,512]{1,0:T(8,128)(2,1)S(1)} %copy-done.24), channel_id=1, source_target_pairs={{0,8},{8,16},{16,24},{24,0},{1,9},{9,17},{17,25},{25,1},{2,10},{10... | collective-permute-start | bytes 393224 | tf_op jit(solution)/shard_map/ppermute | solution.py:1213
  (13 other events, 59.9 us)

commit v5 on v4

--- a/solution.py
+++ b/solution.py
@@ -195,7 +195,7 @@
                     acc = chunk(part, key_tile, acc)
             return acc
 
-        near = max(0, tile - 1)
+        near = max(0, tile - 1) if geo.parts > 2 else 0
         acc = step(range(tile, near - 1, -1), jnp.zeros((2 * HD, geo.tile), f32))
         if near:
             acc = lax.cond(
@@ -1362,7 +1362,7 @@
     )
     early = rest.pop()
     rest = [around(v, -d - 1) for d, v in enumerate(rest)]
-    got = after(got, rest[0], rest[2])
+    got = after(got, rest[0], rest[1])
     wide = (1 + sz.local) * LANES
     send_shape = (n * sz.groups, sz.w_chunk + 2 * SMALL, LANES)
     keep, give, *outs = pl.pallas_call(

time: 159 us -> 159 us (level)
  Pallas kernels: 33.7 us -> 36.2 us
  waiting for transfers between devices: 33.9 us -> 31.8 us
    ppermute x18, waiting for transfers between devices: 21.8 us -> 18.8 us  [around(): return lax.ppermute(x, 'head', [(i, (i + step) % n) for i in range(n)])]
    pallas_call x13, Pallas kernels: 25.2 us -> 27.7 us  [local_call(): pl.pallas_call(kernel, out_shape=tuple((o[0] if len(o) == 1 else jax.Shap...]
    all_to_all x6, waiting for transfers between devices: 2.52 us -> 4.48 us  [exchange(): return lax.all_to_all(x, axis, split_axis=0, concat_axis=0, tiled=True)]
    all_to_all x6, starting transfers between devices: 30.6 us -> 28.9 us  [exchange(): return lax.all_to_all(x, axis, split_axis=0, concat_axis=0, tiled=True)]
  transfers between devices with their start and end apart: 50 -> 50, of which waited for: 19 -> 20; matrix products, arithmetic and copies ran while one was open for 4% -> 4% of each run, Pallas kernels for 13% -> 15%
where the time goes in v5:
time: 159 us; the launch traced here: 158 us
  starting transfers between devices  76.8 us (48%)
  Pallas kernels  36.2 us (23%)
  waiting for transfers between devices  31.8 us (20%)
  other arithmetic  5.85 us (4%)
  local copies, waits for them, and re-layouts  5.13 us (3%)
  between operations  1.81 us (1%)
    all_to_all x6, starting transfers between devices, exchange(): return lax.all_to_all(x, axis, split_axis=0, concat_axis=0, tiled=True)  28.9 us
    pallas_call x13, Pallas kernels, local_call(): pl.pallas_call(kernel, out_shape=tuple((o[0] if len(o) == 1 else jax.Shap...  27.7 us
    ppermute x18, starting transfers between devices, around(): return lax.ppermute(x, 'head', [(i, (i + step) % n) for i in range(n)])  23.7 us
    ppermute x12, starting transfers between devices, around_groups(): return lax.ppermute(x, BLK, pairs)  21.8 us
    ppermute x18, waiting for transfers between devices, around(): return lax.ppermute(x, 'head', [(i, (i + step) % n) for i in range(n)])  18.8 us
    ppermute x12, waiting for transfers between devices, around_groups(): return lax.ppermute(x, BLK, pairs)  5.38 us
    pallas_call x1, Pallas kernels, on_device_fused(): pl.pallas_call(functools.partial(project_grad_kernel, sz), out_shape=(plt...  4.99 us
    all_to_all x6, waiting for transfers between devices, exchange(): return lax.all_to_all(x, axis, split_axis=0, concat_axis=0, tiled=True)  4.48 us
  transfers between devices with their start and end apart: 50, of which 20 were waited for; matrix products, arithmetic and copies ran while one was open for 4% of the time, Pallas kernels for 15%

profile of v5, /device:TPU:0, one launch (start us, length us, event | category | flops | bytes accessed | tf_op | source)
XLA Modules:
  0.0 157.6 jit_solution(16298245990306517176)
XLA Ops:
  0.7 1.7 %pack.1 = bf16[16,56,128]{2,1,0:T(8,128)(2,1)} custom-call(s32[1]{0:T(128)} %bitcast.scal_ref, bf16[16,1536]{1,0:T(8,128)(2,1)} %refs_0_.1, bf16[1,16]{1,0:T(2,128)(2,1)} %bitcast.47, bf16[1,16]{1,0:T(2,128)(2,1)} %bitcast.48, bf16[1,16]{1,0:T(2,128)(2,1)} %bitcast.49, bf16[1,16]{1,0:T(2,128)(2,1)} %bitcast.50, bf16[1,16]{1,0:T(2,128)(2,1)} %bitcast.51, ...), custom_call_target="tpu_custom_call" | custom-call | tf_op jit(solution)/shard_map/pack/pallas_call | solution.py:690
  2.4 8.3 %all-to-all-start = ((bf16[16,56,128]{2,1,0:T(8,128)(2,1)}), bf16[16,56,128]{2,1,0:T(8,128)(2,1)S(1)}, u32[]{:S(2)}, u32[]{:S(2)}) async-start(bf16[16,56,128]{2,1,0:T(8,128)(2,1)} %pack.1), calls=%async_computation | async-start | bytes 458752 | tf_op jit(solution)/shard_map/all_to_all | solution.py:340
  10.7 1.9 %collective-permute-start.1 = (bf16[128,512]{1,0:T(8,128)(2,1)}, bf16[128,512]{1,0:T(8,128)(2,1)S(1)}, u32[]{:S(2)}, u32[]{:S(2)}) collective-permute-start(bf16[128,512]{1,0:T(8,128)(2,1)} %bitcast.30), channel_id=1, source_target_pairs={{0,8},{8,16},{16,24},{24,0},{1,9},{9,17},{17,25},{25,1},{2,10},{10... | collective-permute-start | bytes 393224 | tf_op jit(solution)/shard_map/ppermute | solution.py:1213
  12.7 1.5 collective-permute-start.2
  14.1 1.5 collective-permute-start.3
  16.1 2.0 %fusion.2 = (s32[2048]{0:T(1024)S(1)}, s32[1,2048]{1,0:T(1,128)S(1)}, s32[]{:T(128)}) fusion(s32[]{:T(128)} %broadcast.160, s32[2,2048]{1,0:T(2,128)} %param.17, s32[]{:T(128)S(6)} %select_n.38, s32[2,2048]{1,0:T(2,128)} %param.18), kind=kLoop, calls=%fused_computation.29 | loop fusion | flops 2047 | bytes 32780 | tf_op jit(solution)/shard_map/jit(dynamic_index_in_dim)/dynamic_slice | solution.py:318
  20.0 1.0 convert_reduce_fusion
  21.8 0.8 collective-permute-done.refs_1_
  22.6 1.8 %project.1 = (bf16[8,192,128]{2,1,0:T(8,128)(2,1)}, bf16[512,384]{1,0:T(8,128)(2,1)}, f32[8,512]{1,0:T(8,128)}) custom-call(s32[1]{0:T(128)} %bitcast.scal_ref, bf16[16,56,128]{2,1,0:T(8,128)(2,1)S(1)} %all-to-all-done.refs_0_, bf16[16,56,128]{2,1,0:T(8,128)(2,1)S(1)} %collective-permute-done.refs_1_, bf16[128,512]{1,0:T(8,128)(2,1)S(1)} %bitcast.33, ...), custom_call_target="tpu_custom_call" | custom-call | flops 30000001024 | bytes 1000000 | tf_op jit(solution)/shard_map/project/pallas_call | solution.py:244
  24.4 4.5 %all-to-all-start.1 = ((bf16[8,192,128]{2,1,0:T(8,128)(2,1)}), bf16[8,192,128]{2,1,0:T(8,128)(2,1)S(1)}, u32[]{:S(2)}, u32[]{:S(2)}) async-start(bf16[8,192,128]{2,1,0:T(8,128)(2,1)} %get-tuple-element.118), calls=%async_computation.1 | async-start | bytes 786432 | tf_op jit(solution)/shard_map/all_to_all | solution.py:340
  28.9 1.8 %pieces.1 = (bf16[160,512]{1,0:T(8,128)(2,1)}, bf16[160,512]{1,0:T(8,128)(2,1)}, bf16[160,512]{1,0:T(8,128)(2,1)}, bf16[160,512]{1,0:T(8,128)(2,1)}) custom-call(s32[1]{0:T(128)} %bitcast.scal_ref, bf16[128,512]{1,0:T(8,128)(2,1)} %bitcast.37, bf16[16,2048]{1,0:T(8,128)(2,1)} %refs_1_.1, bf16[16,512]{1,0:T(8,128)(2,1)} %refs_2_.1), custom_call_target="tpu_custom_call" | custom-call | tf_op jit(solution)/shard_map/pieces/pallas_call | solution.py:690
  31.9 2.4 %collective-permute-start.6 = (bf16[160,512]{1,0:T(8,128)(2,1)}, bf16[160,512]{1,0:T(8,128)(2,1)S(1)}, u32[]{:S(2)}, u32[]{:S(2)}) collective-permute-start(bf16[160,512]{1,0:T(8,128)(2,1)} %get-tuple-element.117), channel_id=1, source_target_pairs={{0,24},{8,0},{16,8},{24,16},{1,25},{9,1},{17,9},{25,17},{2,26},{10... | collective-permute-start | bytes 491528 | tf_op jit(solution)/shard_map/ppermute | solution.py:1213
  34.3 0.8 slice.28
  35.0 2.0 %collective-permute-start.10 = (bf16[64,512]{1,0:T(8,128)(2,1)}, bf16[64,512]{1,0:T(8,128)(2,1)S(1)}, u32[]{:S(2)}, u32[]{:S(2)}) collective-permute-start(bf16[64,512]{1,0:T(8,128)(2,1)} %refs_8_), channel_id=1, source_target_pairs={{0,2},{1,3},{2,4},{3,5},{4,6},{5,7},{6,0},{7,1},{8,10},{9,11},{10,... | collective-permute-start | bytes 196616 | tf_op jit(solution)/shard_map/ppermute | solution.py:1224
  37.1 2.4 %collective-permute-start.11 = (bf16[64,512]{1,0:T(8,128)(2,1)}, bf16[64,512]{1,0:T(8,128)(2,1)S(1)}, u32[]{:S(2)}, u32[]{:S(2)}) collective-permute-start(bf16[64,512]{1,0:T(8,128)(2,1)} %refs_8_), channel_id=1, source_target_pairs={{0,4},{1,5},{2,6},{3,7},{4,0},{5,1},{6,2},{7,3},{8,12},{9,13},{10,... | collective-permute-start | bytes 196616 | tf_op jit(solution)/shard_map/ppermute | solution.py:1224
  39.4 3.4 %collective-permute-start.12 = (bf16[64,512]{1,0:T(8,128)(2,1)}, bf16[64,512]{1,0:T(8,128)(2,1)S(1)}, u32[]{:S(2)}, u32[]{:S(2)}) collective-permute-start(bf16[64,512]{1,0:T(8,128)(2,1)} %refs_8_), channel_id=1, source_target_pairs={{0,6},{1,7},{2,0},{3,1},{4,2},{5,3},{6,4},{7,5},{8,14},{9,15},{10,... | collective-permute-start | bytes 196616 | tf_op jit(solution)/shard_map/ppermute | solution.py:1224
  42.9 3.2 %collective-permute-done.11.refs_10_ = bf16[64,512]{1,0:T(8,128)(2,1)S(1)} collective-permute-done((bf16[64,512]{1,0:T(8,128)(2,1)}, bf16[64,512]{1,0:T(8,128)(2,1)S(1)}, u32[]{:S(2)}, u32[]{:S(2)}) %collective-permute-start.11) | collective-permute-done | bytes 65568 | tf_op jit(solution)/shard_map/ppermute | solution.py:1224
  46.2 2.9 %collective-permute-start.9 = (bf16[128,512]{1,0:T(8,128)(2,1)S(1)}, bf16[128,512]{1,0:T(8,128)(2,1)S(1)}, u32[]{:S(2)}, u32[]{:S(2)}) collective-permute-start(bf16[128,512]{1,0:T(8,128)(2,1)S(1)} %pad_maximum_fusion.1.refs_0_), channel_id=1, source_target_pairs={{0,6},{1,7},{2,0},{3,1},{4,2},{5,3},{6,4},{7,5},{8,14},{9,15},{10,... | collective-permute-start | bytes 393224 | tf_op jit(solution)/shard_map/ppermute | solution.py:1224
  49.7 5.1 %attention_forward.1 = (bf16[8,64,128]{2,1,0:T(8,128)(2,1)}, f32[4,64,256]{2,1,0:T(8,128)}, f32[4,8,256]{2,1,0:T(8,128)}) custom-call(s32[6]{0:T(128)S(1)} %pad_add_fusion.scal_ref, bf16[8,192,128]{2,1,0:T(8,128)(2,1)S(1)} %all-to-all-done.1.refs_0_, bf16[8,192,128]{2,1,0:T(8,128)(2,1)S(1)} %collective-permute-done.13.refs_1_, ...), custom_call_target="tpu_custom_call" | custom-call | flops 30000001024 | bytes 1000000 | tf_op jit(solution)/shard_map/attention_forward/pallas_call | solution.py:244
  54.8 4.1 %all-to-all-start.2 = ((bf16[8,64,128]{2,1,0:T(8,128)(2,1)}), bf16[8,64,128]{2,1,0:T(8,128)(2,1)S(1)}, u32[]{:S(2)}, u32[]{:S(2)}) async-start(bf16[8,64,128]{2,1,0:T(8,128)(2,1)} %get-tuple-element.121), calls=%async_computation.2 | async-start | bytes 262144 | tf_op jit(solution)/shard_map/all_to_all | solution.py:340
  59.5 1.9 %collective-permute-done.8.refs_2_ = bf16[128,512]{1,0:T(8,128)(2,1)S(1)} collective-permute-done((bf16[128,512]{1,0:T(8,128)(2,1)S(1)}, bf16[128,512]{1,0:T(8,128)(2,1)S(1)}, u32[]{:S(2)}, u32[]{:S(2)}) %collective-permute-start.8) | collective-permute-done | bytes 131104 | tf_op jit(solution)/shard_map/ppermute | solution.py:1224
  62.5 1.6 %norm_again.1 = (bf16[512,512]{1,0:T(8,128)(2,1)}, bf16[512,512]{1,0:T(8,128)(2,1)}) custom-call(s32[1]{0:T(128)} %bitcast.scal_ref, f32[8,512]{1,0:T(8,128)S(1)} %copy-done.11, bf16[128,512]{1,0:T(8,128)(2,1)S(1)} %bitcast.34, bf16[128,512]{1,0:T(8,128)(2,1)S(1)} %collective-permute-done.1.refs_3_.refs_1_, ...), custom_call_target="tpu_custom_call" | custom-call | flops 100000000 | bytes 1000000 | tf_op jit(solution)/shard_map/norm_again/pallas_call | solution.py:244
  64.2 1.6 %all-to-all-done.2.refs_8_ = bf16[8,64,128]{2,1,0:T(8,128)(2,1)S(1)} async-done(((bf16[8,64,128]{2,1,0:T(8,128)(2,1)}), bf16[8,64,128]{2,1,0:T(8,128)(2,1)S(1)}, u32[]{:S(2)}, u32[]{:S(2)}) %all-to-all-start.2) | async-done | bytes 131104 | tf_op jit(solution)/shard_map/all_to_all | solution.py:340
  66.3 2.9 %collective-permute-start.24 = (bf16[8,64,128]{2,1,0:T(8,128)(2,1)S(1)}, bf16[8,64,128]{2,1,0:T(8,128)(2,1)S(1)}, u32[]{:S(2)}, u32[]{:S(2)}) collective-permute-start(bf16[8,64,128]{2,1,0:T(8,128)(2,1)S(1)} %all-to-all-done.2.refs_8_), channel_id=1, source_target_pairs={{0,24},{8,0},{16,8},{24,16},{1,25},{9,1},{17,9},{25,17},{2,26},{10... | collective-permute-start | bytes 393224 | tf_op jit(solution)/shard_map/ppermute | solution.py:1213
  69.8 0.7 collective-permute-done.21.refs_15_
  70.9 1.0 assemble.1
  71.8 1.2 collective-permute-done.22.refs_9_
  73.5 3.3 %feed.1 = (f32[128,512]{1,0:T(8,128)}, bf16[128,512]{1,0:T(8,128)(2,1)S(1)}, bf16[128,512]{1,0:T(8,128)(2,1)S(1)}, bf16[128,512]{1,0:T(8,128)(2,1)S(1)}, f32[128...) custom-call(s32[1]{0:T(128)} %bitcast.scal_ref, ...), custom_call_target="tpu_custom_call" | custom-call | flops 30000001024 | bytes 1000000 | tf_op jit(solution)/shard_map/feed/pallas_call | solution.py:244
  76.9 2.6 %collective-permute-start.25 = (bf16[128,512]{1,0:T(8,128)(2,1)S(1)}, bf16[128,512]{1,0:T(8,128)(2,1)S(1)}, u32[]{:S(2)}, u32[]{:S(2)}) collective-permute-start(bf16[128,512]{1,0:T(8,128)(2,1)S(1)} %get-tuple-element.141), channel_id=1, source_target_pairs={{0,24},{8,0},{16,8},{24,16},{1,25},{9,1},{17,9},{25,17},{2,26},{10... | collective-permute-start | bytes 393224 | tf_op jit(solution)/shard_map/ppermute | solution.py:1213
  79.5 0.9 collective-permute-start.26
  80.4 2.1 %feed_grad.1 = (f32[4,128,512]{2,1,0:T(8,128)}, bf16[4,128,512]{2,1,0:T(8,128)(2,1)}) custom-call(s32[1]{0:T(128)} %bitcast.scal_ref, bf16[4,128,512]{2,1,0:T(8,128)(2,1)S(1)} %get-tuple-element.145.act_ref, bf16[4,128,512]{2,1,0:T(8,128)(2,1)S(1)} %get-tuple-element.146.dh_ref, bf16[4,128,512]{2,1,0:T(8,128)(2,1)S(1)} %get-tuple-element.147.n_ref, ...), custom_call_target="tpu_custom_call" | custom-call | flops 100000000 | bytes 1000000 | tf_op jit(solution)/shard_map/feed_grad/pallas_call | solution.py:244
  82.9 1.6 %collective-permute-done.26.refs_2_ = bf16[128,512]{1,0:T(8,128)(2,1)S(1)} collective-permute-done((bf16[128,512]{1,0:T(8,128)(2,1)S(1)}, bf16[128,512]{1,0:T(8,128)(2,1)S(1)}, u32[]{:S(2)}, u32[]{:S(2)}) %collective-permute-start.26) | collective-permute-done | bytes 131104 | tf_op jit(solution)/shard_map/ppermute | solution.py:1213
  84.5 1.8 %collective-permute-done.27.refs_3_ = bf16[128,512]{1,0:T(8,128)(2,1)S(1)} collective-permute-done((bf16[128,512]{1,0:T(8,128)(2,1)S(1)}, bf16[128,512]{1,0:T(8,128)(2,1)S(1)}, u32[]{:S(2)}, u32[]{:S(2)}) %collective-permute-start.27) | collective-permute-done | bytes 131104 | tf_op jit(solution)/shard_map/ppermute | solution.py:1213
  86.3 2.0 %middle_grad.1 = (f32[128,512]{1,0:T(8,128)}, bf16[128,512]{1,0:T(8,128)(2,1)}, bf16[32,16,128]{2,1,0:T(8,128)(2,1)}, f32[8,512]{1,0:T(8,128)}, f32[4,64,512]{2,1,0:T(8,128)}, /*index=5*/bf16[4,64,512]{2,1,0:T(8,128)(2,1)}) custom-call(s32[1]{0:T(128)} %bitcast.scal_ref, f32[8,512]{1,0:T(8,128)S(1)} %copy-done.11, ...), custom_call_target="tpu_custom_call" | custom-call | flops 30000001024 | bytes 1000000 | tf_op jit(solution)/shard_map/middle_grad/pallas_call | solution.py:244
  88.3 2.6 %all-to-all-start.3 = ((bf16[32,16,128]{2,1,0:T(8,128)(2,1)}), bf16[32,16,128]{2,1,0:T(8,128)(2,1)S(1)}, u32[]{:S(2)}, u32[]{:S(2)}) async-start(bf16[32,16,128]{2,1,0:T(8,128)(2,1)} %get-tuple-element.153), calls=%async_computation.3 | async-start | bytes 262144 | tf_op jit(solution)/shard_map/all_to_all | solution.py:340
  91.0 1.0 copy-done.16
  92.0 0.9 part_sum.1
  92.9 1.8 %collective-permute-start.30 = (bf16[128,512]{1,0:T(8,128)(2,1)S(1)}, bf16[128,512]{1,0:T(8,128)(2,1)S(1)}, u32[]{:S(2)}, u32[]{:S(2)}) collective-permute-start(bf16[128,512]{1,0:T(8,128)(2,1)S(1)} %get-tuple-element.159), channel_id=1, source_target_pairs={{0,2},{1,3},{2,4},{3,5},{4,6},{5,7},{6,0},{7,1},{8,10},{9,11},{10,... | collective-permute-start | bytes 393224 | tf_op jit(solution)/shard_map/ppermute | solution.py:1224
  94.7 2.4 %collective-permute-start.31 = (bf16[128,512]{1,0:T(8,128)(2,1)S(1)}, bf16[128,512]{1,0:T(8,128)(2,1)S(1)}, u32[]{:S(2)}, u32[]{:S(2)}) collective-permute-start(bf16[128,512]{1,0:T(8,128)(2,1)S(1)} %get-tuple-element.160), channel_id=1, source_target_pairs={{0,4},{1,5},{2,6},{3,7},{4,0},{5,1},{6,2},{7,3},{8,12},{9,13},{10,... | collective-permute-start | bytes 393224 | tf_op jit(solution)/shard_map/ppermute | solution.py:1224
  97.1 1.4 collective-permute-start.32
  99.1 0.9 copy-done.19
  100.1 5.9 %attention_backward.1 = (bf16[8,64,128]{2,1,0:T(8,128)(2,1)S(1)}, f32[8,128,128]{2,1,0:T(8,128)S(1)}, bf16[8,128,128]{2,1,0:T(8,128)(2,1)S(1)}) custom-call(s32[6]{0:T(128)S(1)} %pad_add_fusion.scal_ref, bf16[8,192,128]{2,1,0:T(8,128)(2,1)S(1)} %all-to-all-done.1.refs_0_, bf16[8,192,128]{2,1,0:T(8,128)(2,1)S(1)} %collective-permute-done.13.refs_1_, ...), custom_call_target="tpu_custom_call" | custom-call | flops 30000001024 | bytes 1000000 | tf_op jit(solution)/shard_map/attention_backward/pallas_call | solution.py:244
  106.4 1.3 collective-permute-done.33
  107.9 0.8 pad_maximum_fusion
  108.6 5.6 %all-to-all-start.4 = ((bf16[8,192,128]{2,1,0:T(8,128)(2,1)}), bf16[8,192,128]{2,1,0:T(8,128)(2,1)}, u32[]{:S(2)}, u32[]{:S(2)}) async-start(bf16[8,192,128]{2,1,0:T(8,128)(2,1)} %pad_maximum_fusion), calls=%async_computation.4 | async-start | bytes 786432 | tf_op jit(solution)/shard_map/all_to_all | solution.py:340
  114.3 1.4 split.1
  115.6 2.4 %collective-permute-start.34 = (bf16[160,512]{1,0:T(8,128)(2,1)}, bf16[160,512]{1,0:T(8,128)(2,1)S(1)}, u32[]{:S(2)}, u32[]{:S(2)}) collective-permute-start(bf16[160,512]{1,0:T(8,128)(2,1)} %get-tuple-element.167), channel_id=1, source_target_pairs={{0,24},{8,0},{16,8},{24,16},{1,25},{9,1},{17,9},{25,17},{2,26},{10... | collective-permute-start | bytes 491528 | tf_op jit(solution)/shard_map/ppermute | solution.py:1213
  118.6 3.9 %collective-permute-done.34.refs_1_ = bf16[160,512]{1,0:T(8,128)(2,1)S(1)} collective-permute-done((bf16[160,512]{1,0:T(8,128)(2,1)}, bf16[160,512]{1,0:T(8,128)(2,1)S(1)}, u32[]{:S(2)}, u32[]{:S(2)}) %collective-permute-start.34) | collective-permute-done | bytes 163872 | tf_op jit(solution)/shard_map/ppermute | solution.py:1213
  122.5 2.0 %collective-permute-done.35.refs_2_ = bf16[160,512]{1,0:T(8,128)(2,1)S(1)} collective-permute-done((bf16[160,512]{1,0:T(8,128)(2,1)}, bf16[160,512]{1,0:T(8,128)(2,1)S(1)}, u32[]{:S(2)}, u32[]{:S(2)}) %collective-permute-start.35) | collective-permute-done | bytes 163872 | tf_op jit(solution)/shard_map/ppermute | solution.py:1213
  124.6 2.3 %all-to-all-done.4.refs_0_ = bf16[8,192,128]{2,1,0:T(8,128)(2,1)} async-done(((bf16[8,192,128]{2,1,0:T(8,128)(2,1)}), bf16[8,192,128]{2,1,0:T(8,128)(2,1)}, u32[]{:S(2)}, u32[]{:S(2)}) %all-to-all-start.4) | async-done | bytes 393248 | tf_op jit(solution)/shard_map/all_to_all | solution.py:340
  126.9 5.0 %project_grad.1 = (bf16[16,64,128]{2,1,0:T(8,128)(2,1)}, bf16[16,64,128]{2,1,0:T(8,128)(2,1)}, f32[128,512]{1,0:T(8,128)}, bf16[128,512]{1,0:T(8,128)(2,1)}, bf1...) custom-call(s32[1]{0:T(128)} %bitcast.scal_ref, f32[256,128]{1,0:T(8,128)} %get-tuple-element.171.early_ref, ...), custom_call_target="tpu_custom_call" | custom-call | flops 30000001024 | bytes 1000000 | tf_op jit(solution)/shard_map/project_grad/pallas_call | solution.py:1368
  132.0 1.5 collective-permute-start.36
  133.5 1.0 collective-permute-start.41
  134.5 2.4 %collective-permute-start.42 = (bf16[64,512]{1,0:T(8,128)(2,1)}, bf16[64,512]{1,0:T(8,128)(2,1)S(1)}, u32[]{:S(2)}, u32[]{:S(2)}) collective-permute-start(bf16[64,512]{1,0:T(8,128)(2,1)} %get-tuple-element.196), channel_id=1, source_target_pairs={{0,4},{1,5},{2,6},{3,7},{4,0},{5,1},{6,2},{7,3},{8,12},{9,13},{10,... | collective-permute-start | bytes 196616 | tf_op jit(solution)/shard_map/ppermute | solution.py:1224
  136.9 1.5 collective-permute-start.43
  138.4 0.9 copy-done.18
  139.3 0.8 fold.1
  140.1 3.7 %all-to-all-start.5 = ((bf16[16,64,128]{2,1,0:T(8,128)(2,1)}), bf16[16,64,128]{2,1,0:T(8,128)(2,1)S(1)}, u32[]{:S(2)}, u32[]{:S(2)}) async-start(bf16[16,64,128]{2,1,0:T(8,128)(2,1)} %fold.1), calls=%async_computation.5 | async-start | bytes 524288 | tf_op jit(solution)/shard_map/all_to_all | solution.py:340
  143.8 0.7 add_convert_fusion.1
  144.6 2.8 %collective-permute-start.37 = (bf16[128,512]{1,0:T(8,128)(2,1)S(1)}, bf16[128,512]{1,0:T(8,128)(2,1)S(1)}, u32[]{:S(2)}, u32[]{:S(2)}) collective-permute-start(bf16[128,512]{1,0:T(8,128)(2,1)S(1)} %copy-done.26), channel_id=1, source_target_pairs={{0,24},{8,0},{16,8},{24,16},{1,25},{9,1},{17,9},{25,17},{2,26},{10... | collective-permute-start | bytes 393224 | tf_op jit(solution)/shard_map/ppermute | solution.py:1213
  149.2 3.3 %collective-permute-done.37.refs_1_ = bf16[128,512]{1,0:T(8,128)(2,1)S(1)} collective-permute-done((bf16[128,512]{1,0:T(8,128)(2,1)S(1)}, bf16[128,512]{1,0:T(8,128)(2,1)S(1)}, u32[]{:S(2)}, u32[]{:S(2)}) %collective-permute-start.37) | collective-permute-done | bytes 131104 | tf_op jit(solution)/shard_map/ppermute | solution.py:1213
  152.5 3.4 %collective-permute-done.38.refs_2_ = bf16[128,512]{1,0:T(8,128)(2,1)S(1)} collective-permute-done((bf16[128,512]{1,0:T(8,128)(2,1)S(1)}, bf16[128,512]{1,0:T(8,128)(2,1)S(1)}, u32[]{:S(2)}, u32[]{:S(2)}) %collective-permute-start.38) | collective-permute-done | bytes 131104 | tf_op jit(solution)/shard_map/ppermute | solution.py:1213
  155.9 1.0 input_grad.1
  156.8 0.8 final.1
  (143 shorter events, 11.9 us)
Async XLA Ops:
  0.6 21.9 %copy-start = (bf16[2,1,64,512]{3,2,1,0:T(8,128)(2,1)S(1)}, bf16[2,1,64,512]{3,2,1,0:T(8,128)(2,1)}, u32[]{:S(2)}) copy-start(bf16[2,1,64,512]{3,2,1,0:T(8,128)(2,1)} %param.16) | copy-start | bytes 393220
  2.4 18.7 %all-to-all-start = ((bf16[16,56,128]{2,1,0:T(8,128)(2,1)}), bf16[16,56,128]{2,1,0:T(8,128)(2,1)S(1)}, u32[]{:S(2)}, u32[]{:S(2)}) async-start(bf16[16,56,128]{2,1,0:T(8,128)(2,1)} %pack.1), calls=%async_computation | async-start | bytes 458752 | tf_op jit(solution)/shard_map/all_to_all | solution.py:340
  10.7 10.5 %collective-permute-start.1 = (bf16[128,512]{1,0:T(8,128)(2,1)}, bf16[128,512]{1,0:T(8,128)(2,1)S(1)}, u32[]{:S(2)}, u32[]{:S(2)}) collective-permute-start(bf16[128,512]{1,0:T(8,128)(2,1)} %bitcast.30), channel_id=1, source_target_pairs={{0,8},{8,16},{16,24},{24,0},{1,9},{9,17},{17,25},{25,1},{2,10},{10... | collective-permute-start | bytes 393224 | tf_op jit(solution)/shard_map/ppermute | solution.py:1213
  12.7 9.2 %collective-permute-start.2 = (bf16[128,512]{1,0:T(8,128)(2,1)}, bf16[128,512]{1,0:T(8,128)(2,1)S(1)}, u32[]{:S(2)}, u32[]{:S(2)}) collective-permute-start(bf16[128,512]{1,0:T(8,128)(2,1)} %bitcast.31), channel_id=1, source_target_pairs={{0,16},{8,24},{16,0},{24,8},{1,17},{9,25},{17,1},{25,9},{2,18},{10... | collective-permute-start | bytes 393224 | tf_op jit(solution)/shard_map/ppermute | solution.py:1213
  14.1 7.7 %collective-permute-start.3 = (bf16[128,512]{1,0:T(8,128)(2,1)}, bf16[128,512]{1,0:T(8,128)(2,1)S(1)}, u32[]{:S(2)}, u32[]{:S(2)}) collective-permute-start(bf16[128,512]{1,0:T(8,128)(2,1)} %bitcast.32), channel_id=1, source_target_pairs={{0,24},{8,0},{16,8},{24,16},{1,25},{9,1},{17,9},{25,17},{2,26},{10... | collective-permute-start | bytes 393224 | tf_op jit(solution)/shard_map/ppermute | solution.py:1213
  21.1 1.5 collective-permute-start
  24.4 21.8 %all-to-all-start.1 = ((bf16[8,192,128]{2,1,0:T(8,128)(2,1)}), bf16[8,192,128]{2,1,0:T(8,128)(2,1)S(1)}, u32[]{:S(2)}, u32[]{:S(2)}) async-start(bf16[8,192,128]{2,1,0:T(8,128)(2,1)} %get-tuple-element.118), calls=%async_computation.1 | async-start | bytes 786432 | tf_op jit(solution)/shard_map/all_to_all | solution.py:340
  30.7 8.7 %collective-permute-start.4 = (bf16[160,512]{1,0:T(8,128)(2,1)}, bf16[160,512]{1,0:T(8,128)(2,1)S(1)}, u32[]{:S(2)}, u32[]{:S(2)}) collective-permute-start(bf16[160,512]{1,0:T(8,128)(2,1)} %get-tuple-element.113), channel_id=1, source_target_pairs={{0,8},{8,16},{16,24},{24,0},{1,9},{9,17},{17,25},{25,1},{2,10},{10... | collective-permute-start | bytes 491528 | tf_op jit(solution)/shard_map/ppermute | solution.py:1213
  31.4 11.5 %collective-permute-start.5 = (bf16[160,512]{1,0:T(8,128)(2,1)}, bf16[160,512]{1,0:T(8,128)(2,1)S(1)}, u32[]{:S(2)}, u32[]{:S(2)}) collective-permute-start(bf16[160,512]{1,0:T(8,128)(2,1)} %get-tuple-element.115), channel_id=1, source_target_pairs={{0,16},{8,24},{16,0},{24,8},{1,17},{9,25},{17,1},{25,9},{2,18},{10... | collective-permute-start | bytes 491528 | tf_op jit(solution)/shard_map/ppermute | solution.py:1213
  31.9 10.9 %collective-permute-start.6 = (bf16[160,512]{1,0:T(8,128)(2,1)}, bf16[160,512]{1,0:T(8,128)(2,1)S(1)}, u32[]{:S(2)}, u32[]{:S(2)}) collective-permute-start(bf16[160,512]{1,0:T(8,128)(2,1)} %get-tuple-element.117), channel_id=1, source_target_pairs={{0,24},{8,0},{16,8},{24,16},{1,25},{9,1},{17,9},{25,17},{2,26},{10... | collective-permute-start | bytes 491528 | tf_op jit(solution)/shard_map/ppermute | solution.py:1213
  35.0 7.8 %collective-permute-start.10 = (bf16[64,512]{1,0:T(8,128)(2,1)}, bf16[64,512]{1,0:T(8,128)(2,1)S(1)}, u32[]{:S(2)}, u32[]{:S(2)}) collective-permute-start(bf16[64,512]{1,0:T(8,128)(2,1)} %refs_8_), channel_id=1, source_target_pairs={{0,2},{1,3},{2,4},{3,5},{4,6},{5,7},{6,0},{7,1},{8,10},{9,11},{10,... | collective-permute-start | bytes 196616 | tf_op jit(solution)/shard_map/ppermute | solution.py:1224
  37.1 9.1 %collective-permute-start.11 = (bf16[64,512]{1,0:T(8,128)(2,1)}, bf16[64,512]{1,0:T(8,128)(2,1)S(1)}, u32[]{:S(2)}, u32[]{:S(2)}) collective-permute-start(bf16[64,512]{1,0:T(8,128)(2,1)} %refs_8_), channel_id=1, source_target_pairs={{0,4},{1,5},{2,6},{3,7},{4,0},{5,1},{6,2},{7,3},{8,12},{9,13},{10,... | collective-permute-start | bytes 196616 | tf_op jit(solution)/shard_map/ppermute | solution.py:1224
  39.4 6.7 %collective-permute-start.12 = (bf16[64,512]{1,0:T(8,128)(2,1)}, bf16[64,512]{1,0:T(8,128)(2,1)S(1)}, u32[]{:S(2)}, u32[]{:S(2)}) collective-permute-start(bf16[64,512]{1,0:T(8,128)(2,1)} %refs_8_), channel_id=1, source_target_pairs={{0,6},{1,7},{2,0},{3,1},{4,2},{5,3},{6,4},{7,5},{8,14},{9,15},{10,... | collective-permute-start | bytes 196616 | tf_op jit(solution)/shard_map/ppermute | solution.py:1224
  42.9 19.7 %copy-start.11 = (f32[8,512]{1,0:T(8,128)S(1)}, f32[8,512]{1,0:T(8,128)}, u32[]{:S(2)}) copy-start(f32[8,512]{1,0:T(8,128)} %get-tuple-element.133.vec_ref) | copy-start | bytes 49156
  46.1 3.6 %collective-permute-start.13 = (bf16[8,192,128]{2,1,0:T(8,128)(2,1)S(1)}, bf16[8,192,128]{2,1,0:T(8,128)(2,1)S(1)}, u32[]{:S(2)}, u32[]{:S(2)}) collective-permute-start(bf16[8,192,128]{2,1,0:T(8,128)(2,1)S(1)} %all-to-all-done.1.refs_0_), channel_id=1, source_target_pairs={{0,1},{1,0},{2,3},{3,2},{4,5},{5,4},{6,7},{7,6},{8,9},{9,8},{10,11... | collective-permute-start | bytes 1179656 | tf_op jit(solution)/shard_map/ppermute | solution.py:1227
  46.2 12.8 %collective-permute-start.9 = (bf16[128,512]{1,0:T(8,128)(2,1)S(1)}, bf16[128,512]{1,0:T(8,128)(2,1)S(1)}, u32[]{:S(2)}, u32[]{:S(2)}) collective-permute-start(bf16[128,512]{1,0:T(8,128)(2,1)S(1)} %pad_maximum_fusion.1.refs_0_), channel_id=1, source_target_pairs={{0,6},{1,7},{2,0},{3,1},{4,2},{5,3},{6,4},{7,5},{8,14},{9,15},{10,... | collective-permute-start | bytes 393224 | tf_op jit(solution)/shard_map/ppermute | solution.py:1224
  49.1 12.3 %collective-permute-start.8 = (bf16[128,512]{1,0:T(8,128)(2,1)S(1)}, bf16[128,512]{1,0:T(8,128)(2,1)S(1)}, u32[]{:S(2)}, u32[]{:S(2)}) collective-permute-start(bf16[128,512]{1,0:T(8,128)(2,1)S(1)} %pad_maximum_fusion.1.refs_0_), channel_id=1, source_target_pairs={{0,4},{1,5},{2,6},{3,7},{4,0},{5,1},{6,2},{7,3},{8,12},{9,13},{10,... | collective-permute-start | bytes 393224 | tf_op jit(solution)/shard_map/ppermute | solution.py:1224
  49.1 12.3 %collective-permute-start.7 = (bf16[128,512]{1,0:T(8,128)(2,1)S(1)}, bf16[128,512]{1,0:T(8,128)(2,1)S(1)}, u32[]{:S(2)}, u32[]{:S(2)}) collective-permute-start(bf16[128,512]{1,0:T(8,128)(2,1)S(1)} %pad_maximum_fusion.1.refs_0_), channel_id=1, source_target_pairs={{0,2},{1,3},{2,4},{3,5},{4,6},{5,7},{6,0},{7,1},{8,10},{9,11},{10,... | collective-permute-start | bytes 393224 | tf_op jit(solution)/shard_map/ppermute | solution.py:1224
  54.8 10.9 %all-to-all-start.2 = ((bf16[8,64,128]{2,1,0:T(8,128)(2,1)}), bf16[8,64,128]{2,1,0:T(8,128)(2,1)S(1)}, u32[]{:S(2)}, u32[]{:S(2)}) async-start(bf16[8,64,128]{2,1,0:T(8,128)(2,1)} %get-tuple-element.121), calls=%async_computation.2 | async-start | bytes 262144 | tf_op jit(solution)/shard_map/all_to_all | solution.py:340
  59.0 3.5 %collective-permute-start.17 = (bf16[128,512]{1,0:T(8,128)(2,1)S(1)}, bf16[128,512]{1,0:T(8,128)(2,1)S(1)}, u32[]{:S(2)}, u32[]{:S(2)}) collective-permute-start(bf16[128,512]{1,0:T(8,128)(2,1)S(1)} %collective-permute-done.9.refs_3_), channel_id=1, source_target_pairs={{0,1},{1,0},{2,3},{3,2},{4,5},{5,4},{6,7},{7,6},{8,9},{9,8},{10,11... | collective-permute-start | bytes 393224 | tf_op jit(solution)/shard_map/ppermute | solution.py:1227
  61.4 2.7 %collective-permute-start.16 = (bf16[128,512]{1,0:T(8,128)(2,1)S(1)}, bf16[128,512]{1,0:T(8,128)(2,1)S(1)}, u32[]{:S(2)}, u32[]{:S(2)}) collective-permute-start(bf16[128,512]{1,0:T(8,128)(2,1)S(1)} %collective-permute-done.8.refs_2_), channel_id=1, source_target_pairs={{0,1},{1,0},{2,3},{3,2},{4,5},{5,4},{6,7},{7,6},{8,9},{9,8},{10,11... | collective-permute-start | bytes 393224 | tf_op jit(solution)/shard_map/ppermute | solution.py:1227
  61.4 2.7 %collective-permute-start.15 = (bf16[128,512]{1,0:T(8,128)(2,1)S(1)}, bf16[128,512]{1,0:T(8,128)(2,1)S(1)}, u32[]{:S(2)}, u32[]{:S(2)}) collective-permute-start(bf16[128,512]{1,0:T(8,128)(2,1)S(1)} %collective-permute-done.7.refs_1_), channel_id=1, source_target_pairs={{0,1},{1,0},{2,3},{3,2},{4,5},{5,4},{6,7},{7,6},{8,9},{9,8},{10,11... | collective-permute-start | bytes 393224 | tf_op jit(solution)/shard_map/ppermute | solution.py:1227
  61.9 2.2 %collective-permute-start.14 = (bf16[128,512]{1,0:T(8,128)(2,1)S(1)}, bf16[128,512]{1,0:T(8,128)(2,1)S(1)}, u32[]{:S(2)}, u32[]{:S(2)}) collective-permute-start(bf16[128,512]{1,0:T(8,128)(2,1)S(1)} %pad_maximum_fusion.1.refs_0_), channel_id=1, source_target_pairs={{0,1},{1,0},{2,3},{3,2},{4,5},{5,4},{6,7},{7,6},{8,9},{9,8},{10,11... | collective-permute-start | bytes 393224 | tf_op jit(solution)/shard_map/ppermute | solution.py:1227
  61.9 11.6 %copy-start.6 = (bf16[160,512]{1,0:T(8,128)(2,1)S(1)}, bf16[160,512]{1,0:T(8,128)(2,1)}, u32[]{:S(2)}) copy-start(bf16[160,512]{1,0:T(8,128)(2,1)} %get-tuple-element.111.refs_4_.refs_0_) | copy-start | bytes 491524
  61.9 7.3 %collective-permute-start.19 = (bf16[64,512]{1,0:T(8,128)(2,1)S(1)}, bf16[64,512]{1,0:T(8,128)(2,1)S(1)}, u32[]{:S(2)}, u32[]{:S(2)}) collective-permute-start(bf16[64,512]{1,0:T(8,128)(2,1)S(1)} %collective-permute-done.10.refs_9_), channel_id=1, source_target_pairs={{0,1},{1,0},{2,3},{3,2},{4,5},{5,4},{6,7},{7,6},{8,9},{9,8},{10,11... | collective-permute-start | bytes 196616 | tf_op jit(solution)/shard_map/ppermute | solution.py:1227
  62.4 6.8 %collective-permute-start.20 = (bf16[64,512]{1,0:T(8,128)(2,1)S(1)}, bf16[64,512]{1,0:T(8,128)(2,1)S(1)}, u32[]{:S(2)}, u32[]{:S(2)}) collective-permute-start(bf16[64,512]{1,0:T(8,128)(2,1)S(1)} %collective-permute-done.11.refs_10_), channel_id=1, source_target_pairs={{0,1},{1,0},{2,3},{3,2},{4,5},{5,4},{6,7},{7,6},{8,9},{9,8},{10,11... | collective-permute-start | bytes 196616 | tf_op jit(solution)/shard_map/ppermute | solution.py:1227
  65.8 7.3 %collective-permute-start.22 = (bf16[8,64,128]{2,1,0:T(8,128)(2,1)S(1)}, bf16[8,64,128]{2,1,0:T(8,128)(2,1)S(1)}, u32[]{:S(2)}, u32[]{:S(2)}) collective-permute-start(bf16[8,64,128]{2,1,0:T(8,128)(2,1)S(1)} %all-to-all-done.2.refs_8_), channel_id=1, source_target_pairs={{0,8},{8,16},{16,24},{24,0},{1,9},{9,17},{17,25},{25,1},{2,10},{10... | collective-permute-start | bytes 393224 | tf_op jit(solution)/shard_map/ppermute | solution.py:1213
  65.8 7.7 %collective-permute-start.23 = (bf16[8,64,128]{2,1,0:T(8,128)(2,1)S(1)}, bf16[8,64,128]{2,1,0:T(8,128)(2,1)S(1)}, u32[]{:S(2)}, u32[]{:S(2)}) collective-permute-start(bf16[8,64,128]{2,1,0:T(8,128)(2,1)S(1)} %all-to-all-done.2.refs_8_), channel_id=1, source_target_pairs={{0,16},{8,24},{16,0},{24,8},{1,17},{9,25},{17,1},{25,9},{2,18},{10... | collective-permute-start | bytes 393224 | tf_op jit(solution)/shard_map/ppermute | solution.py:1213
  66.3 7.2 %collective-permute-start.24 = (bf16[8,64,128]{2,1,0:T(8,128)(2,1)S(1)}, bf16[8,64,128]{2,1,0:T(8,128)(2,1)S(1)}, u32[]{:S(2)}, u32[]{:S(2)}) collective-permute-start(bf16[8,64,128]{2,1,0:T(8,128)(2,1)S(1)} %all-to-all-done.2.refs_8_), channel_id=1, source_target_pairs={{0,24},{8,0},{16,8},{24,16},{1,25},{9,1},{17,9},{25,17},{2,26},{10... | collective-permute-start | bytes 393224 | tf_op jit(solution)/shard_map/ppermute | solution.py:1213
  69.2 1.3 collective-permute-start.21
  69.3 1.6 %collective-permute-start.18 = (bf16[64,512]{1,0:T(8,128)(2,1)}, bf16[64,512]{1,0:T(8,128)(2,1)S(1)}, u32[]{:S(2)}, u32[]{:S(2)}) collective-permute-start(bf16[64,512]{1,0:T(8,128)(2,1)} %refs_8_), channel_id=1, source_target_pairs={{0,1},{1,0},{2,3},{3,2},{4,5},{5,4},{6,7},{7,6},{8,9},{9,8},{10,11... | collective-permute-start | bytes 196616 | tf_op jit(solution)/shard_map/ppermute | solution.py:1227
  76.9 6.0 %collective-permute-start.25 = (bf16[128,512]{1,0:T(8,128)(2,1)S(1)}, bf16[128,512]{1,0:T(8,128)(2,1)S(1)}, u32[]{:S(2)}, u32[]{:S(2)}) collective-permute-start(bf16[128,512]{1,0:T(8,128)(2,1)S(1)} %get-tuple-element.141), channel_id=1, source_target_pairs={{0,24},{8,0},{16,8},{24,16},{1,25},{9,1},{17,9},{25,17},{2,26},{10... | collective-permute-start | bytes 393224 | tf_op jit(solution)/shard_map/ppermute | solution.py:1213
  79.5 5.0 %collective-permute-start.26 = (bf16[128,512]{1,0:T(8,128)(2,1)S(1)}, bf16[128,512]{1,0:T(8,128)(2,1)S(1)}, u32[]{:S(2)}, u32[]{:S(2)}) collective-permute-start(bf16[128,512]{1,0:T(8,128)(2,1)S(1)} %get-tuple-element.142), channel_id=1, source_target_pairs={{0,16},{8,24},{16,0},{24,8},{1,17},{9,25},{17,1},{25,9},{2,18},{10... | collective-permute-start | bytes 393224 | tf_op jit(solution)/shard_map/ppermute | solution.py:1213
  80.4 5.9 %collective-permute-start.27 = (bf16[128,512]{1,0:T(8,128)(2,1)S(1)}, bf16[128,512]{1,0:T(8,128)(2,1)S(1)}, u32[]{:S(2)}, u32[]{:S(2)}) collective-permute-start(bf16[128,512]{1,0:T(8,128)(2,1)S(1)} %get-tuple-element.143), channel_id=1, source_target_pairs={{0,8},{8,16},{16,24},{24,0},{1,9},{9,17},{17,25},{25,1},{2,10},{10... | collective-permute-start | bytes 393224 | tf_op jit(solution)/shard_map/ppermute | solution.py:1213
  82.5 8.5 %collective-permute-start.28 = (bf16[4,128,512]{2,1,0:T(8,128)(2,1)}, bf16[4,128,512]{2,1,0:T(8,128)(2,1)S(1)}, u32[]{:S(2)}, u32[]{:S(2)}) collective-permute-start(bf16[4,128,512]{2,1,0:T(8,128)(2,1)} %get-tuple-element.149), channel_id=1, source_target_pairs={{0,1},{1,0},{2,3},{3,2},{4,5},{5,4},{6,7},{7,6},{8,9},{9,8},{10,11... | collective-permute-start | bytes 1572872 | tf_op jit(solution)/shard_map/ppermute | solution.py:1227
  88.3 2.6 %collective-permute-start.29 = (bf16[4,64,512]{2,1,0:T(8,128)(2,1)}, bf16[4,64,512]{2,1,0:T(8,128)(2,1)S(1)}, u32[]{:S(2)}, u32[]{:S(2)}) collective-permute-start(bf16[4,64,512]{2,1,0:T(8,128)(2,1)} %get-tuple-element.151), channel_id=1, source_target_pairs={{0,1},{1,0},{2,3},{3,2},{4,5},{5,4},{6,7},{7,6},{8,9},{9,8},{10,11... | collective-permute-start | bytes 786440 | tf_op jit(solution)/shard_map/ppermute | solution.py:1227
  88.3 10.8 %all-to-all-start.3 = ((bf16[32,16,128]{2,1,0:T(8,128)(2,1)}), bf16[32,16,128]{2,1,0:T(8,128)(2,1)S(1)}, u32[]{:S(2)}, u32[]{:S(2)}) async-start(bf16[32,16,128]{2,1,0:T(8,128)(2,1)} %get-tuple-element.153), calls=%async_computation.3 | async-start | bytes 262144 | tf_op jit(solution)/shard_map/all_to_all | solution.py:340
  92.0 7.1 %copy-start.21 = (f32[4,8,256]{2,1,0:T(8,128)S(1)}, f32[4,8,256]{2,1,0:T(8,128)}, u32[]{:S(2)}) copy-start(f32[4,8,256]{2,1,0:T(8,128)} %get-tuple-element.155.refs_5_) | copy-start | bytes 98308
  92.9 13.1 %collective-permute-start.30 = (bf16[128,512]{1,0:T(8,128)(2,1)S(1)}, bf16[128,512]{1,0:T(8,128)(2,1)S(1)}, u32[]{:S(2)}, u32[]{:S(2)}) collective-permute-start(bf16[128,512]{1,0:T(8,128)(2,1)S(1)} %get-tuple-element.159), channel_id=1, source_target_pairs={{0,2},{1,3},{2,4},{3,5},{4,6},{5,7},{6,0},{7,1},{8,10},{9,11},{10,... | collective-permute-start | bytes 393224 | tf_op jit(solution)/shard_map/ppermute | solution.py:1224
  94.7 11.5 %collective-permute-start.31 = (bf16[128,512]{1,0:T(8,128)(2,1)S(1)}, bf16[128,512]{1,0:T(8,128)(2,1)S(1)}, u32[]{:S(2)}, u32[]{:S(2)}) collective-permute-start(bf16[128,512]{1,0:T(8,128)(2,1)S(1)} %get-tuple-element.160), channel_id=1, source_target_pairs={{0,4},{1,5},{2,6},{3,7},{4,0},{5,1},{6,2},{7,3},{8,12},{9,13},{10,... | collective-permute-start | bytes 393224 | tf_op jit(solution)/shard_map/ppermute | solution.py:1224
  97.1 9.1 %collective-permute-start.32 = (bf16[128,512]{1,0:T(8,128)(2,1)S(1)}, bf16[128,512]{1,0:T(8,128)(2,1)S(1)}, u32[]{:S(2)}, u32[]{:S(2)}) collective-permute-start(bf16[128,512]{1,0:T(8,128)(2,1)S(1)} %get-tuple-element.161), channel_id=1, source_target_pairs={{0,6},{1,7},{2,0},{3,1},{4,2},{5,3},{6,4},{7,5},{8,14},{9,15},{10,... | collective-permute-start | bytes 393224 | tf_op jit(solution)/shard_map/ppermute | solution.py:1224
  106.2 1.5 collective-permute-start.33
  107.8 6.4 %copy-start.5 = (f32[128,512]{1,0:T(8,128)S(1)}, f32[128,512]{1,0:T(8,128)}, u32[]{:S(2)}) copy-start(f32[128,512]{1,0:T(8,128)} %get-tuple-element.163.own_ref) | copy-start | bytes 786436
  107.8 6.4 %copy-start.8 = (bf16[128,512]{1,0:T(8,128)(2,1)S(1)}, bf16[128,512]{1,0:T(8,128)(2,1)}, u32[]{:S(2)}) copy-start(bf16[128,512]{1,0:T(8,128)(2,1)} %get-tuple-element.164.refs_3_) | copy-start | bytes 393220
  107.8 6.4 %copy-start.9 = (bf16[128,512]{1,0:T(8,128)(2,1)S(1)}, bf16[128,512]{1,0:T(8,128)(2,1)}, u32[]{:S(2)}) copy-start(bf16[128,512]{1,0:T(8,128)(2,1)} %get-tuple-element.165.refs_4_) | copy-start | bytes 393220
  108.6 18.2 %all-to-all-start.4 = ((bf16[8,192,128]{2,1,0:T(8,128)(2,1)}), bf16[8,192,128]{2,1,0:T(8,128)(2,1)}, u32[]{:S(2)}, u32[]{:S(2)}) async-start(bf16[8,192,128]{2,1,0:T(8,128)(2,1)} %pad_maximum_fusion), calls=%async_computation.4 | async-start | bytes 786432 | tf_op jit(solution)/shard_map/all_to_all | solution.py:340
  115.6 6.9 %collective-permute-start.34 = (bf16[160,512]{1,0:T(8,128)(2,1)}, bf16[160,512]{1,0:T(8,128)(2,1)S(1)}, u32[]{:S(2)}, u32[]{:S(2)}) collective-permute-start(bf16[160,512]{1,0:T(8,128)(2,1)} %get-tuple-element.167), channel_id=1, source_target_pairs={{0,24},{8,0},{16,8},{24,16},{1,25},{9,1},{17,9},{25,17},{2,26},{10... | collective-permute-start | bytes 491528 | tf_op jit(solution)/shard_map/ppermute | solution.py:1213
  118.0 6.5 %collective-permute-start.35 = (bf16[160,512]{1,0:T(8,128)(2,1)}, bf16[160,512]{1,0:T(8,128)(2,1)S(1)}, u32[]{:S(2)}, u32[]{:S(2)}) collective-permute-start(bf16[160,512]{1,0:T(8,128)(2,1)} %get-tuple-element.168), channel_id=1, source_target_pairs={{0,16},{8,24},{16,0},{24,8},{1,17},{9,25},{17,1},{25,9},{2,18},{10... | collective-permute-start | bytes 491528 | tf_op jit(solution)/shard_map/ppermute | solution.py:1213
  131.9 6.5 %collective-permute-start.40 = (bf16[16,64,128]{2,1,0:T(8,128)(2,1)}, bf16[16,64,128]{2,1,0:T(8,128)(2,1)S(1)}, u32[]{:S(2)}, u32[]{:S(2)}) collective-permute-start(bf16[16,64,128]{2,1,0:T(8,128)(2,1)} %get-tuple-element.180), channel_id=1, source_target_pairs={{0,1},{1,0},{2,3},{3,2},{4,5},{5,4},{6,7},{7,6},{8,9},{9,8},{10,11... | collective-permute-start | bytes 786440 | tf_op jit(solution)/shard_map/ppermute | solution.py:1227
  132.0 11.9 %collective-permute-start.36 = (bf16[160,512]{1,0:T(8,128)(2,1)}, bf16[160,512]{1,0:T(8,128)(2,1)S(1)}, u32[]{:S(2)}, u32[]{:S(2)}) collective-permute-start(bf16[160,512]{1,0:T(8,128)(2,1)} %get-tuple-element.169), channel_id=1, source_target_pairs={{0,8},{8,16},{16,24},{24,0},{1,9},{9,17},{17,25},{25,1},{2,10},{10... | collective-permute-start | bytes 491528 | tf_op jit(solution)/shard_map/ppermute | solution.py:1213
  133.5 14.4 %collective-permute-start.41 = (bf16[64,512]{1,0:T(8,128)(2,1)}, bf16[64,512]{1,0:T(8,128)(2,1)S(1)}, u32[]{:S(2)}, u32[]{:S(2)}) collective-permute-start(bf16[64,512]{1,0:T(8,128)(2,1)} %get-tuple-element.194), channel_id=1, source_target_pairs={{0,2},{1,3},{2,4},{3,5},{4,6},{5,7},{6,0},{7,1},{8,10},{9,11},{10,... | collective-permute-start | bytes 196616 | tf_op jit(solution)/shard_map/ppermute | solution.py:1224
  134.5 14.0 %collective-permute-start.42 = (bf16[64,512]{1,0:T(8,128)(2,1)}, bf16[64,512]{1,0:T(8,128)(2,1)S(1)}, u32[]{:S(2)}, u32[]{:S(2)}) collective-permute-start(bf16[64,512]{1,0:T(8,128)(2,1)} %get-tuple-element.196), channel_id=1, source_target_pairs={{0,4},{1,5},{2,6},{3,7},{4,0},{5,1},{6,2},{7,3},{8,12},{9,13},{10,... | collective-permute-start | bytes 196616 | tf_op jit(solution)/shard_map/ppermute | solution.py:1224
  136.9 11.6 %collective-permute-start.43 = (bf16[64,512]{1,0:T(8,128)(2,1)}, bf16[64,512]{1,0:T(8,128)(2,1)S(1)}, u32[]{:S(2)}, u32[]{:S(2)}) collective-permute-start(bf16[64,512]{1,0:T(8,128)(2,1)} %get-tuple-element.198), channel_id=1, source_target_pairs={{0,6},{1,7},{2,0},{3,1},{4,2},{5,3},{6,4},{7,5},{8,14},{9,15},{10,... | collective-permute-start | bytes 196616 | tf_op jit(solution)/shard_map/ppermute | solution.py:1224
  140.1 7.3 %copy-start.25 = (bf16[128,512]{1,0:T(8,128)(2,1)S(1)}, bf16[128,512]{1,0:T(8,128)(2,1)}, u32[]{:S(2)}) copy-start(bf16[128,512]{1,0:T(8,128)(2,1)} %get-tuple-element.177) | copy-start | bytes 393220
  140.1 7.8 %copy-start.24 = (bf16[128,512]{1,0:T(8,128)(2,1)S(1)}, bf16[128,512]{1,0:T(8,128)(2,1)}, u32[]{:S(2)}) copy-start(bf16[128,512]{1,0:T(8,128)(2,1)} %get-tuple-element.178) | copy-start | bytes 393220
  140.1 8.4 %copy-start.23 = (f32[64,512]{1,0:T(8,128)S(1)}, f32[64,512]{1,0:T(8,128)}, u32[]{:S(2)}) copy-start(f32[64,512]{1,0:T(8,128)} %get-tuple-element.192) | copy-start | bytes 393220
  140.1 15.7 %copy-start.1 = (bf16[2,1,64,512]{3,2,1,0:T(8,128)(2,1)S(1)}, bf16[2,1,64,512]{3,2,1,0:T(8,128)(2,1)}, u32[]{:S(2)}) copy-start(bf16[2,1,64,512]{3,2,1,0:T(8,128)(2,1)} %param.16) | copy-start | bytes 393220
  140.1 15.7 %copy-start.3 = (f32[128,512]{1,0:T(8,128)S(1)}, f32[128,512]{1,0:T(8,128)}, u32[]{:S(2)}) copy-start(f32[128,512]{1,0:T(8,128)} %get-tuple-element.170.grad_ref) | copy-start | bytes 786436
  140.1 15.7 %copy-start.4 = (f32[128,512]{1,0:T(8,128)S(1)}, f32[128,512]{1,0:T(8,128)}, u32[]{:S(2)}) copy-start(f32[128,512]{1,0:T(8,128)} %get-tuple-element.175.refs_0_) | copy-start | bytes 786436
  140.1 16.7 %all-to-all-start.5 = ((bf16[16,64,128]{2,1,0:T(8,128)(2,1)}), bf16[16,64,128]{2,1,0:T(8,128)(2,1)S(1)}, u32[]{:S(2)}, u32[]{:S(2)}) async-start(bf16[16,64,128]{2,1,0:T(8,128)(2,1)} %fold.1), calls=%async_computation.5 | async-start | bytes 524288 | tf_op jit(solution)/shard_map/all_to_all | solution.py:340
  144.6 12.3 %copy-start.12 = (bf16[32,512]{1,0:T(8,128)(2,1)S(1)}, bf16[32,512]{1,0:T(8,128)(2,1)}, u32[]{:S(2)}) copy-start(bf16[32,512]{1,0:T(8,128)(2,1)} %get-tuple-element.181.refs_0_) | copy-start | bytes 98308
  144.6 7.9 %collective-permute-start.37 = (bf16[128,512]{1,0:T(8,128)(2,1)S(1)}, bf16[128,512]{1,0:T(8,128)(2,1)S(1)}, u32[]{:S(2)}, u32[]{:S(2)}) collective-permute-start(bf16[128,512]{1,0:T(8,128)(2,1)S(1)} %copy-done.26), channel_id=1, source_target_pairs={{0,24},{8,0},{16,8},{24,16},{1,25},{9,1},{17,9},{25,17},{2,26},{10... | collective-permute-start | bytes 393224 | tf_op jit(solution)/shard_map/ppermute | solution.py:1213
  147.4 8.5 %collective-permute-start.38 = (bf16[128,512]{1,0:T(8,128)(2,1)S(1)}, bf16[128,512]{1,0:T(8,128)(2,1)S(1)}, u32[]{:S(2)}, u32[]{:S(2)}) collective-permute-start(bf16[128,512]{1,0:T(8,128)(2,1)S(1)} %copy-done.25), channel_id=1, source_target_pairs={{0,16},{8,24},{16,0},{24,8},{1,17},{9,25},{17,1},{25,9},{2,18},{10... | collective-permute-start | bytes 393224 | tf_op jit(solution)/shard_map/ppermute | solution.py:1213
  147.9 8.0 %collective-permute-start.39 = (bf16[128,512]{1,0:T(8,128)(2,1)S(1)}, bf16[128,512]{1,0:T(8,128)(2,1)S(1)}, u32[]{:S(2)}, u32[]{:S(2)}) collective-permute-start(bf16[128,512]{1,0:T(8,128)(2,1)S(1)} %copy-done.24), channel_id=1, source_target_pairs={{0,8},{8,16},{16,24},{24,0},{1,9},{9,17},{17,25},{25,1},{2,10},{10... | collective-permute-start | bytes 393224 | tf_op jit(solution)/shard_map/ppermute | solution.py:1213
  (13 other events, 59.4 us)
